TPU v7x, 32 devices: a whole 2x2x4 slice. The times are simulated.
32 devices in a mesh: prompt: 4 (over y, x), resp: 8 (over z, core).
Axes of the slice: x: 2, y: 2, z: 4, core: 2. Of those that a mesh axis runs over, the one named last changes fastest.
Arguments:
- question_key_matrix: bfloat16 [8, 1024, 256], P('resp', 'prompt'), may hold values from -0.31835938 to 0.31835938
- prompt_values: bfloat16 [8, 1024, 256], P('resp', 'prompt'), may hold values from -6 to 6
- prompt_gates: float32 [8, 2, 1024], P('resp', None, 'prompt'), may hold values from -2.3 to 0, as said below
- resp_queries: bfloat16 [128, 512, 256], P(('prompt', 'resp')), may hold values from -0.31835938 to 0.31835938
- resp_keys: bfloat16 [128, 512, 256], P(('prompt', 'resp')), may hold values from -0.31835938 to 0.31835938
- response_value_rows: bfloat16 [128, 512, 256], P(('prompt', 'resp')), may hold values from -6 to 6
- resp_gates: float32 [128, 2, 512], P(('prompt', 'resp')), may hold values from -2.3 to 0, as said below
- resp_cotangent: bfloat16 [128, 512, 256], P(('prompt', 'resp')), may hold values from -0.59765625 to 0.59765625
- group_ids: int32 [128], P(('prompt', 'resp')), may hold values from 0 to 7, as said below
- resp_lengths: int32 [32, 4], P(('prompt', 'resp')), may hold values from 1 to 512, 1536 in all within a row
- loss_mask: int32 [128, 512], P(('prompt', 'resp')), may hold values 0 or 1
- advantages: int32 [128], P(('prompt', 'resp')), may hold values from -2048 to 2048
Outputs:
- resp_out: bfloat16 [128, 512, 256], P(('prompt', 'resp'))
- resp_dq: bfloat16 [128, 512, 256], P(('prompt', 'resp'))
- answer_key_derivative: bfloat16 [128, 512, 256], P(('prompt', 'resp'))
- resp_dv: bfloat16 [128, 512, 256], P(('prompt', 'resp'))
- prompt_dk: bfloat16 [8, 1024, 256], P('resp', 'prompt')
- prompt_dv: bfloat16 [8, 1024, 256], P('resp', 'prompt')
Inputs may be any that keep to these rules, and one draw needn't show every extreme that they name: `group_ids`: never falling along the responses; every prompt has at least one response. `resp_lengths`: the lengths of one device's 4 responses sum to 1536. `prompt_gates`: negative log decays. `resp_gates`: negative log decays.
All inputs are finite; a program needn't handle non-finite values. No bound on the sum of `loss_mask` on one device may be relied on, other than what follows from the above.
Results may differ from a plain program's by a relative error of at most 0.012.
Values may be sent and summed in bfloat16 or wider, within the bound.
No kernel may reach another device: no remote copies, remote signals or barrier semaphores. Data moves between devices by JAX's collectives and lax.ppermute only.
A program may use at most 64 MiB of HBM per device.

v0:
```python
import jax
import jax.numpy as jnp
from jax import lax
from jax.experimental import pallas as pl
from jax.experimental.pallas import tpu as pltpu
from jax.sharding import PartitionSpec as P

H = 2
DH = 128
HALF = 256
F32 = jnp.float32
BF16 = jnp.bfloat16
NEVER = -1e30
VMEM = pl.BlockSpec(memory_space=pltpu.VMEM)
ANY = pl.BlockSpec(memory_space=pl.ANY)
SMEM = pl.BlockSpec(memory_space=pltpu.SMEM)


def params(mebibytes=16):
    return pltpu.CompilerParams(vmem_limit_bytes=mebibytes * 1024 * 1024)


def mm(a, b):
    return lax.dot_general(a, b, (((1,), (0,)), ((), ())), preferred_element_type=F32)


def mm_nt(a, b):
    return lax.dot_general(a, b, (((1,), (1,)), ((), ())), preferred_element_type=F32)


def mm_tn(a, b):
    return lax.dot_general(a, b, (((0,), (0,)), ((), ())), preferred_element_type=F32)


def in_hbm(x):
    return pltpu.with_memory_space_constraint(x, pltpu.HBM)


def three_terms(x):
    high = x.astype(BF16)
    rest = x - high.astype(F32)
    middle = rest.astype(BF16)
    return high, middle, (rest - middle.astype(F32)).astype(BF16)


def lane_cumsum(x):
    rows, width = x.shape
    ones = lax.broadcasted_iota(jnp.int32, (128, 128), 0) <= lax.broadcasted_iota(jnp.int32, (128, 128), 1)
    terms = jnp.concatenate(three_terms(x), axis=0)
    starts = range(0, width, 128)
    sums = mm(jnp.concatenate([terms[:, b : b + 128] for b in starts], axis=0), ones.astype(F32).astype(BF16))
    parts = []
    before = jnp.zeros((rows, 1), F32)
    for b in range(len(starts)):
        at = 3 * rows * b
        part = sums[at : at + rows] + sums[at + rows : at + 2 * rows] + sums[at + 2 * rows : at + 3 * rows]
        part = part + before
        before = part[:, 127:128]
        parts.append(part)
    return jnp.concatenate(parts, axis=1)


def first_kernel(
    n, ids_ref, lens_ref, adv_ref, keys_hbm, values_hbm, pgates_hbm, gates_hbm, mask_hbm, q_hbm, c_hbm, k_hbm, v_hbm,
    *refs,
):
    msgs, (cols_ref, rows_ref, q, c, k_out, v_out) = refs[:n], refs[n : n + 6]
    keys, values, pgates, gates, mask, matrices, sems = refs[n + 6 :]
    pairs = [(pgates_hbm, pgates), (gates_hbm, gates), (mask_hbm, mask), (keys_hbm, keys), (values_hbm, values)]
    count = gates.shape[0]
    slots = gates.shape[2]
    tokens = keys.shape[1]
    for i in range(count):
        pairs += [(q_hbm.at[i], q.at[i]), (c_hbm.at[i], c.at[i])]
    pairs += [(k_hbm, k_out), (v_hbm, v_out)]
    copies = [pltpu.make_async_copy(a, b, sems.at[i]) for i, (a, b) in enumerate(pairs)]
    for copy in copies:
        copy.start()
    part = DH // n
    block = H * part
    me = lax.axis_index("prompt")
    targets = [lax.rem(me + k, n) for k in range(n)]

    def spread(at):
        for k in range(n):
            of = pl.ds(pl.multiple_of(targets[k] * part, part), part)
            msgs[k][at * part + (16 if at >= H else 0) : (at + 1) * part + (16 if at >= H else 0), :] = matrices[
                at, of, :
            ].astype(BF16)

    for copy in copies[:3]:
        copy.wait()
    piece = jnp.concatenate([pgates[0], jnp.zeros((H, slots - tokens), F32)], axis=1)
    gate_rows = [gates[i] for i in range(count)] + [piece, jnp.zeros((16 - H * (count + 1), slots), F32)]
    cum = lane_cumsum(jnp.concatenate(gate_rows, axis=0))
    carried = jnp.exp(cum)
    place = lax.broadcasted_iota(jnp.int32, (1, slots), 1)
    rows = []
    factors = []
    for i in range(count):
        weight = adv_ref[i].astype(F32) / 1024.0
        opened = jnp.where(place < lens_ref[0, i], 1.0, 0.0)
        live = mask[i : i + 1, :].astype(F32) * opened * weight
        rows += [cum[H * i : H * i + H], carried[H * i : H * i + H], live, opened, jnp.zeros((2, slots), F32)]
        factors.append(carried[H * i : H * i + H] * live)
    rows_ref[...] = jnp.concatenate(rows, axis=0).reshape(count, 8, slots)
    piece = cum[H * count : H * count + H]
    total = piece[:, -1:]
    suffix = total - piece
    rows += [suffix, jnp.zeros((128 - 8 * count - H, slots), F32)]
    cols_ref[...] = jnp.concatenate(rows, axis=0).T

    for copy in copies[3:5]:
        copy.wait()
    turned = keys[0].T
    later = jnp.exp(suffix[:, :tokens])
    for h in range(H):
        lanes = slice(h * DH, (h + 1) * DH)
        scaled = turned[lanes].astype(F32) * later[h : h + 1]
        high = scaled.astype(BF16)
        low = (scaled - high.astype(F32)).astype(BF16)
        both = mm(jnp.concatenate([high, low], axis=0), values[0, :, lanes])
        matrices[h] = both[:DH] + both[DH:]
        spread(h)
    notes = [jnp.broadcast_to(x[h : h + 1].astype(F32), (1, DH)) for x in three_terms(total) for h in range(H)]
    notes += [jnp.full((1, DH), ids_ref[i].astype(F32)) for i in range(count)]
    notes.append(jnp.zeros((16 - len(notes), DH), F32))
    notes = jnp.concatenate(notes, axis=0).astype(BF16)
    for k in range(n):
        msgs[k][block : block + 16, :] = notes

    for i in range(count):
        copies[5 + 2 * i].wait()
        turned = q[i].T
        copies[6 + 2 * i].wait()
        for h in range(H):
            lanes = slice(h * DH, (h + 1) * DH)
            scaled = (turned[lanes].astype(F32) * factors[i][h : h + 1]).astype(BF16)
            matrices[H * (1 + i) + h] = mm(scaled, c[i, :, lanes])
            spread(H * (1 + i) + h)
    for copy in copies[5 + 2 * count :]:
        copy.wait()


def noted_prompt(notes, i):
    return jnp.max(notes[3 * H + i : 3 * H + i + 1]).astype(jnp.int32)


def second_kernel(n, chips, cores, *refs):
    row, z_at = lax.axis_index("prompt"), lax.axis_index("z")
    got, msgs, later_ref, sums = refs[:n], refs[n + 1 : n + 1 + chips], refs[-2], refs[-1]
    part = DH // n
    block = H * part
    responses = (got[0].shape[0] - block - 16) // block
    place = [lax.rem(row + n - k, n) for k in range(n)]
    notes = [got[k][block : block + 16, :].astype(F32) for k in range(n)]
    logs = [x[0:H] + x[H : 2 * H] + x[2 * H : 3 * H] for x in notes]
    final = jnp.zeros((block, DH), F32)
    for k in range(n):
        later = jnp.zeros_like(logs[0])
        for other in range(n):
            if other != k:
                later = later + jnp.where(place[other] > place[k], logs[other], 0.0)
        if k == 0:
            later_ref[...] = jnp.concatenate([later, jnp.zeros((8 - H, DH), F32)], axis=0)
        decay = jnp.exp(later)
        decay = [jnp.broadcast_to(decay[h : h + 1], (part, DH)) for h in range(H)]
        final = final + jnp.concatenate(decay, axis=0) * got[k][0:block, :].astype(F32)
    sums[...] = jnp.zeros_like(sums)
    for k in range(n):
        for i in range(responses):
            at = block * (1 + i) + 16
            sums[noted_prompt(notes[k], i)] += got[k][at : at + block, :].astype(F32)
    final = final.astype(BF16)
    for k in range(chips):
        z = lax.rem(z_at + k, chips)
        msgs[k][0:block, :] = final
        for c in range(cores):
            msgs[k][(1 + c) * block : (2 + c) * block, :] = sums[z * cores + c].astype(BF16)


def swap_kernel(chips, *refs):
    got, sent_ref, kept_ref = refs[:chips], refs[chips + 1], refs[chips + 2]
    block = got[0].shape[0] // 3
    totals = []
    for c in range(2):
        total = got[0][(1 + c) * block : (2 + c) * block, :].astype(F32)
        for k in range(1, chips):
            total = total + got[k][(1 + c) * block : (2 + c) * block, :].astype(F32)
        totals.append(total)
    for k in range(chips):
        final = got[k][0:block, :]
        sent_ref[k * block : (k + 1) * block, :] = final
        kept_ref[k * block : (k + 1) * block, :] = final
    low = lax.axis_index("core") == 0
    sent_ref[chips * block :, :] = jnp.where(low, totals[1], totals[0]).astype(BF16)
    kept_ref[chips * block :, :] = jnp.where(low, totals[0], totals[1]).astype(BF16)


def third_kernel(n, chips, *refs):
    z_at, core = lax.axis_index("z"), lax.axis_index("core")
    noted, kept_ref, got_ref, msgs = refs[:n], refs[n], refs[n + 1], refs[n + 3 :]
    block = H * DH // n
    responses = (noted[0].shape[0] - block - 16) // block
    total = kept_ref[chips * block :, :].astype(F32) + got_ref[chips * block :, :].astype(F32)
    total = total.astype(BF16)
    for k in range(n):
        notes = noted[(n - k) % n][block : block + 16, :].astype(F32)
        for i in range(responses):
            p = noted_prompt(notes, i)
            slot = lax.rem(z_at + chips - lax.div(p, 2), chips)
            at = pl.ds(pl.multiple_of(slot * block, block), block)
            same = lax.rem(p, 2) == core
            state = jnp.where(same, kept_ref[at, :].astype(F32), got_ref[at, :].astype(F32))
            msgs[k][i * block : (i + 1) * block, :] = state.astype(BF16)
        msgs[k][responses * block :, :] = total


def sweep_kernel(r, cols_ref, rows_ref, q_ref, k_ref, v_ref, c_ref, *refs):
    out_ref, dq_ref, dk_hbm, dv_hbm, token_ref, dk_buf, dv_buf, sems = refs[-8:]
    token_ref[...] = jnp.zeros_like(token_ref)
    live = cols_ref[:, 8 * r + 4 : 8 * r + 5]
    causal = lax.broadcasted_iota(jnp.int32, (HALF, HALF), 0) >= lax.broadcasted_iota(
        jnp.int32, (HALF, HALF), 1
    )
    blocks = q_ref.shape[1] // HALF
    copies = []
    for h in range(H):
        lanes = slice(h * DH, (h + 1) * DH)
        cum = cols_ref[:, 8 * r + h : 8 * r + h + 1]
        dk = [None] * blocks
        dv = [None] * blocks
        for t in range(blocks):
            at = slice(t * HALF, (t + 1) * HALF)
            query = q_ref[r, at, lanes]
            grad_out = (c_ref[r, at, lanes].astype(F32) * live[at]).astype(BF16)
            out = None
            dq = None
            for s in range(t + 1):
                of = slice(s * HALF, (s + 1) * HALF)
                key = k_ref[r, of, lanes]
                value = v_ref[r, of, lanes]
                diff = cum[at] - rows_ref[r, h : h + 1, of]
                if s == t:
                    diff = jnp.where(causal, diff, NEVER)
                decay = jnp.exp(diff)
                mixing = (mm_nt(query, key) * decay).astype(BF16)
                scores = (mm_nt(grad_out, value) * decay).astype(BF16)
                o_new = mm(mixing, value)
                q_new = mm(scores, key)
                k_new = mm_tn(scores, query)
                v_new = mm_tn(mixing, grad_out)
                out = o_new if out is None else out + o_new
                dq = q_new if dq is None else dq + q_new
                dk[s] = k_new if dk[s] is None else dk[s] + k_new
                dv[s] = v_new if dv[s] is None else dv[s] + v_new
            out_ref[r, at, lanes] = out
            dq_ref[r, at, lanes] = dq
        for s in range(blocks):
            of = slice(s * HALF, (s + 1) * HALF)
            dk_buf[of, lanes] = dk[s].astype(BF16)
            dv_buf[of, lanes] = dv[s].astype(BF16)
        copies += [
            pltpu.make_async_copy(dk_buf.at[:, lanes], dk_hbm.at[r, :, lanes], sems.at[2 * h]),
            pltpu.make_async_copy(dv_buf.at[:, lanes], dv_hbm.at[r, :, lanes], sems.at[2 * h + 1]),
        ]
        copies[-2].start()
        copies[-1].start()
    for copy in copies:
        copy.wait()


def last_kernel(n, count, cols_ref, q_ref, c_ref, po_ref, pdq_ref, keys_ref, values_ref, later_ref, *refs):
    got, (out_hbm, dq_hbm, dk_ref, dv_ref, start, out_buf, dq_buf, sems) = refs[:n], refs[n + 1 :]
    part = DH // n
    block = H * part
    row = lax.axis_index("prompt")
    for r in range(count + 1):
        for k in range(n):
            of = pl.ds(pl.multiple_of(lax.rem(row + n - k, n) * part, part), part)
            for h in range(H):
                start[r, h, of, :] = got[k][r * block + h * part : r * block + (h + 1) * part, :]
    copies = []
    for r in range(count):
        live = cols_ref[:, 8 * r + 4 : 8 * r + 5]
        opened = cols_ref[:, 8 * r + 5 : 8 * r + 6]
        for h in range(H):
            lanes = slice(h * DH, (h + 1) * DH)
            carried = cols_ref[:, 8 * r + 2 + h : 8 * r + 3 + h]
            grad_out = (c_ref[r, :, lanes].astype(F32) * live).astype(BF16)
            out = po_ref[r, :, lanes] + carried * mm(q_ref[r, :, lanes], start[r, h])
            out_buf[r, :, lanes] = (opened * out).astype(BF16)
            dq = pdq_ref[r, :, lanes] + carried * mm_nt(grad_out, start[r, h])
            dq_buf[r, :, lanes] = dq.astype(BF16)
        copies += [
            pltpu.make_async_copy(out_buf.at[r], out_hbm.at[r], sems.at[2 * r]),
            pltpu.make_async_copy(dq_buf.at[r], dq_hbm.at[r], sems.at[2 * r + 1]),
        ]
        copies[-2].start()
        copies[-1].start()
    tokens = keys_ref.shape[1]
    for h in range(H):
        lanes = slice(h * DH, (h + 1) * DH)
        suffix = cols_ref[:tokens, 8 * count + h : 8 * count + h + 1]
        factor = jnp.exp(suffix + later_ref[h : h + 1, 0:1])
        dk_ref[0, :, lanes] = (factor * mm_nt(values_ref[0, :, lanes], start[count, h])).astype(BF16)
        dv_ref[0, :, lanes] = (factor * mm(keys_ref[0, :, lanes], start[count, h])).astype(BF16)
    for copy in copies:
        copy.wait()


def exchange(xs, axis):
    n = lax.axis_size(axis)
    moved = [lax.ppermute(xs[k], axis, [(s, (s + k) % n) for s in range(n)]) for k in range(1, n)]
    return [xs[0]] + moved


def shards(
    keys,
    values,
    prompt_gates,
    queries,
    resp_keys,
    resp_values,
    resp_gates,
    cotangent,
    group_ids,
    resp_lengths,
    loss_mask,
    advantages,
):
    n = lax.axis_size("prompt")
    chips = lax.axis_size("z")
    cores = lax.axis_size("core")
    responses, slots, width = queries.shape
    block = H * DH // n
    shape = jax.ShapeDtypeStruct

    outs = pl.pallas_call(
        lambda *refs: first_kernel(n, *refs),
        out_shape=[shape((block * (1 + responses) + 16, DH), BF16)] * n
        + [shape((slots, 128), F32), shape((responses, 8, slots), F32)]
        + [shape(queries.shape, BF16)] * 4,
        in_specs=[SMEM] * 3 + [ANY] * 9,
        out_specs=[VMEM] * (n + 6),
        scratch_shapes=[
            pltpu.VMEM(keys.shape, BF16),
            pltpu.VMEM(values.shape, BF16),
            pltpu.VMEM(prompt_gates.shape, F32),
            pltpu.VMEM(resp_gates.shape, F32),
            pltpu.VMEM(loss_mask.shape, jnp.int32),
            pltpu.VMEM((H * (1 + responses), DH, DH), F32),
            pltpu.SemaphoreType.DMA((7 + 2 * responses,)),
        ],
        compiler_params=params(32),
        name="first",
    )(
        *[in_hbm(x) for x in (group_ids, resp_lengths, advantages, keys, values, prompt_gates, resp_gates)],
        *[in_hbm(x) for x in (loss_mask, queries, cotangent, resp_keys, resp_values)],
    )
    msgs, (cols, rows, queries, cotangent, resp_keys, resp_values) = outs[:n], outs[n:]

    like = shape(queries.shape, F32)
    like_out = shape(queries.shape, BF16)

    def sweep(r, before, token):
        outs = pl.pallas_call(
            lambda *refs: sweep_kernel(r, *refs),
            out_shape=[like, like, like_out, like_out, shape((8, 128), F32)],
            in_specs=[VMEM] * 6 + [ANY] * (1 + len(before)),
            out_specs=[VMEM, VMEM, ANY, ANY, VMEM],
            scratch_shapes=[
                pltpu.VMEM((slots, width), BF16),
                pltpu.VMEM((slots, width), BF16),
                pltpu.SemaphoreType.DMA((2 * H,)),
            ],
            input_output_aliases={7 + k: k for k in range(len(before))},
            compiler_params=params(),
            name="sweep",
        )(cols, rows, queries, resp_keys, resp_values, cotangent, token, *before)
        return outs[:4], outs[4]

    got1 = exchange(msgs, "prompt")
    held, token = sweep(0, [], cols)
    outs = pl.pallas_call(
        lambda *refs: second_kernel(n, chips, cores, *refs),
        out_shape=[shape(((1 + cores) * block, DH), BF16)] * chips + [shape((8, DH), F32)],
        in_specs=[VMEM] * n + [ANY],
        out_specs=[VMEM] * (chips + 1),
        scratch_shapes=[pltpu.VMEM((chips * cores, block, DH), F32)],
        compiler_params=params(),
        name="second",
    )(*got1, token)
    msgs, later = outs[:chips], outs[chips]
    got2 = exchange(msgs, "z")
    held, token = sweep(1, held, later)
    sent, kept = pl.pallas_call(
        lambda *refs: swap_kernel(chips, *refs),
        out_shape=[shape(((chips + 1) * block, DH), BF16)] * 2,
        in_specs=[VMEM] * chips + [ANY],
        out_specs=[VMEM, VMEM],
        compiler_params=params(),
        name="swap",
    )(*got2, token)
    swapped = exchange([kept, sent], "core")[1]
    held, token = sweep(2, held, kept)
    msgs = pl.pallas_call(
        lambda *refs: third_kernel(n, chips, *refs),
        out_shape=[shape(((responses + 1) * block, DH), BF16)] * n,
        in_specs=[VMEM] * (n + 2) + [ANY],
        out_specs=[VMEM] * n,
        compiler_params=params(),
        name="third",
    )(*got1, kept, swapped, token)
    got3 = exchange(msgs, "prompt")
    held, token = sweep(3, held, msgs[0])
    partial_out, partial_dq, resp_dk, resp_dv = held

    resp_out, resp_dq, prompt_dk, prompt_dv = pl.pallas_call(
        lambda *refs: last_kernel(n, responses, *refs),
        out_shape=[like_out, like_out, shape(keys.shape, BF16), shape(keys.shape, BF16)],
        in_specs=[VMEM] * (8 + n) + [ANY],
        out_specs=[ANY, ANY, VMEM, VMEM],
        scratch_shapes=[
            pltpu.VMEM((responses + 1, H, DH, DH), BF16),
            pltpu.VMEM(queries.shape, BF16),
            pltpu.VMEM(queries.shape, BF16),
            pltpu.SemaphoreType.DMA((2 * responses,)),
        ],
        compiler_params=params(),
        name="last",
    )(cols, queries, cotangent, partial_out, partial_dq, keys, values, later, *got3, token)
    return (resp_out, resp_dq, resp_dk, resp_dv, prompt_dk, prompt_dv)


def solution(mesh):
    n, count = mesh.shape["prompt"], mesh.shape["resp"]
    mesh = jax.sharding.Mesh(mesh.devices.reshape(n, count // 2, 2), ("prompt", "z", "core"))
    spread = P(("prompt", "z", "core"))
    three = P(("prompt", "z", "core"), None, None)
    two = P(("prompt", "z", "core"), None)
    prompt = P(("z", "core"), "prompt", None)
    return jax.shard_map(
        shards,
        mesh=mesh,
        in_specs=(
            prompt,
            prompt,
            P(("z", "core"), None, "prompt"),
            three,
            three,
            three,
            three,
            three,
            spread,
            two,
            two,
            spread,
        ),
        out_specs=(three, three, three, three, prompt, prompt),
        check_vma=False,
    )
```

profile of v0, /device:TPU:0, one launch (start us, length us, event | category | flops | bytes accessed | tf_op | source)
XLA Modules:
  0.0 36.2 jit_solution(9619974411645170075)
XLA Ops:
  0.6 3.8 %first.1 = (bf16[336,128]{1,0:T(8,128)(2,1)S(1)}, bf16[336,128]{1,0:T(8,128)(2,1)S(1)}, bf16[336,128]{1,0:T(8,128)(2,1)S(1)}, bf16[336,128]{1,0:T(8,128)(2,1)S(1...) custom-call(s32[4]{0:T(128)} %refs_0_.1, ...), custom_call_target="tpu_custom_call" | custom-call | tf_op jit(solution)/shard_map/first/pallas_call | solution.py:339
  4.5 3.0 %collective-permute-start = (bf16[336,128]{1,0:T(8,128)(2,1)S(1)}, bf16[336,128]{1,0:T(8,128)(2,1)S(1)}, u32[]{:S(2)}, u32[]{:S(2)}) collective-permute-start(bf16[336,128]{1,0:T(8,128)(2,1)S(1)} %get-tuple-element.58), channel_id=1, source_target_pairs={{0,8},{8,16},{16,24},{24,0},{1,9},{9,17},{17,25},{25,1},{2,10},{10... | collective-permute-start | bytes 258056 | tf_op jit(solution)/shard_map/ppermute | solution.py:314
  7.5 1.5 %collective-permute-start.1 = (bf16[336,128]{1,0:T(8,128)(2,1)S(1)}, bf16[336,128]{1,0:T(8,128)(2,1)S(1)}, u32[]{:S(2)}, u32[]{:S(2)}) collective-permute-start(bf16[336,128]{1,0:T(8,128)(2,1)S(1)} %get-tuple-element.59), channel_id=1, source_target_pairs={{0,16},{8,24},{16,0},{24,8},{1,17},{9,25},{17,1},{25,9},{2,18},{10... | collective-permute-start | bytes 258056 | tf_op jit(solution)/shard_map/ppermute | solution.py:314
  9.0 1.4 %collective-permute-start.2 = (bf16[336,128]{1,0:T(8,128)(2,1)S(1)}, bf16[336,128]{1,0:T(8,128)(2,1)S(1)}, u32[]{:S(2)}, u32[]{:S(2)}) collective-permute-start(bf16[336,128]{1,0:T(8,128)(2,1)S(1)} %get-tuple-element.60), channel_id=1, source_target_pairs={{0,24},{8,0},{16,8},{24,16},{1,25},{9,1},{17,9},{25,17},{2,26},{10... | collective-permute-start | bytes 258056 | tf_op jit(solution)/shard_map/ppermute | solution.py:314
  10.4 2.8 %sweep.4 = (f32[4,512,256]{2,1,0:T(8,128)S(1)}, f32[4,512,256]{2,1,0:T(8,128)S(1)}, bf16[4,512,256]{2,1,0:T(8,128)(2,1)}, bf16[4,512,256]{2,1,0:T(8,128)(2,1)}, f32[8,128]{1,0:T(8,128)S(1)}) custom-call(f32[512,128]{1,0:T(8,128)S(1)} %get-tuple-element.51.refs_0_.refs_6_, f32[4,8,512]{2,1,0:T(8,128)S(1)} %get-tuple-element.54.refs_1_, ...), custom_call_target="tpu_custom_call" | custom-call | tf_op jit(solution)/shard_map/sweep/pallas_call | solution.py:367
  13.2 0.0 collective-permute-done.refs_1_
  13.3 0.0 collective-permute-done.1.refs_2_
  13.3 0.2 collective-permute-done.2.refs_3_
  13.5 0.2 second.1
  13.7 1.6 %collective-permute-start.3 = (bf16[192,128]{1,0:T(8,128)(2,1)S(1)}, bf16[192,128]{1,0:T(8,128)(2,1)S(1)}, u32[]{:S(2)}, u32[]{:S(2)}) collective-permute-start(bf16[192,128]{1,0:T(8,128)(2,1)S(1)} %get-tuple-element.63), channel_id=1, source_target_pairs={{0,2},{2,4},{4,6},{6,0},{1,3},{3,5},{5,7},{7,1},{8,10},{10,12},{12... | collective-permute-start | bytes 147464 | tf_op jit(solution)/shard_map/ppermute | solution.py:314
  15.4 2.6 %collective-permute-start.4 = (bf16[192,128]{1,0:T(8,128)(2,1)S(1)}, bf16[192,128]{1,0:T(8,128)(2,1)S(1)}, u32[]{:S(2)}, u32[]{:S(2)}) collective-permute-start(bf16[192,128]{1,0:T(8,128)(2,1)S(1)} %get-tuple-element.64), channel_id=1, source_target_pairs={{0,4},{2,6},{4,0},{6,2},{1,5},{3,7},{5,1},{7,3},{8,12},{10,14},{12... | collective-permute-start | bytes 147464 | tf_op jit(solution)/shard_map/ppermute | solution.py:314
  17.9 1.3 %collective-permute-start.5 = (bf16[192,128]{1,0:T(8,128)(2,1)S(1)}, bf16[192,128]{1,0:T(8,128)(2,1)S(1)}, u32[]{:S(2)}, u32[]{:S(2)}) collective-permute-start(bf16[192,128]{1,0:T(8,128)(2,1)S(1)} %get-tuple-element.65), channel_id=1, source_target_pairs={{0,6},{2,0},{4,2},{6,4},{1,7},{3,1},{5,3},{7,5},{8,14},{10,8},{12,... | collective-permute-start | bytes 147464 | tf_op jit(solution)/shard_map/ppermute | solution.py:314
  19.3 2.8 %sweep.5 = (f32[4,512,256]{2,1,0:T(8,128)S(1)}, f32[4,512,256]{2,1,0:T(8,128)S(1)}, bf16[4,512,256]{2,1,0:T(8,128)(2,1)}, bf16[4,512,256]{2,1,0:T(8,128)(2,1)}, f32[8,128]{1,0:T(8,128)S(1)}) custom-call(f32[512,128]{1,0:T(8,128)S(1)} %get-tuple-element.51.refs_0_.refs_6_, ...), custom_call_target="tpu_custom_call", output_to_operand_aliasing={{0}: (7, {}), {1}: (8, {}), {2}: (9, {}), {3}: (10, {})} | custom-call | tf_op jit(solution)/shard_map/sweep/pallas_call | solution.py:367
  22.1 0.0 collective-permute-done.3.refs_1_
  22.1 0.0 collective-permute-done.4.refs_2_
  22.1 0.0 collective-permute-done.5.refs_3_
  22.2 0.1 collective-permute-start.6
  22.3 2.8 %sweep.6 = (f32[4,512,256]{2,1,0:T(8,128)S(1)}, f32[4,512,256]{2,1,0:T(8,128)S(1)}, bf16[4,512,256]{2,1,0:T(8,128)(2,1)}, bf16[4,512,256]{2,1,0:T(8,128)(2,1)}, f32[8,128]{1,0:T(8,128)S(1)}) custom-call(f32[512,128]{1,0:T(8,128)S(1)} %get-tuple-element.51.refs_0_.refs_6_, ...), custom_call_target="tpu_custom_call", output_to_operand_aliasing={{0}: (7, {}), {1}: (8, {}), {2}: (9, {}), {3}: (10, {})} | custom-call | tf_op jit(solution)/shard_map/sweep/pallas_call | solution.py:367
  25.1 0.0 collective-permute-done.6.refs_5_
  25.1 0.3 third.1
  25.4 1.7 %collective-permute-start.7 = (bf16[320,128]{1,0:T(8,128)(2,1)S(1)}, bf16[320,128]{1,0:T(8,128)(2,1)S(1)}, u32[]{:S(2)}, u32[]{:S(2)}) collective-permute-start(bf16[320,128]{1,0:T(8,128)(2,1)S(1)} %get-tuple-element.86), channel_id=1, source_target_pairs={{0,8},{8,16},{16,24},{24,0},{1,9},{9,17},{17,25},{25,1},{2,10},{10... | collective-permute-start | bytes 245768 | tf_op jit(solution)/shard_map/ppermute | solution.py:314
  27.1 1.2 %collective-permute-start.8 = (bf16[320,128]{1,0:T(8,128)(2,1)S(1)}, bf16[320,128]{1,0:T(8,128)(2,1)S(1)}, u32[]{:S(2)}, u32[]{:S(2)}) collective-permute-start(bf16[320,128]{1,0:T(8,128)(2,1)S(1)} %get-tuple-element.87), channel_id=1, source_target_pairs={{0,16},{8,24},{16,0},{24,8},{1,17},{9,25},{17,1},{25,9},{2,18},{10... | collective-permute-start | bytes 245768 | tf_op jit(solution)/shard_map/ppermute | solution.py:314
  28.3 1.1 %collective-permute-start.9 = (bf16[320,128]{1,0:T(8,128)(2,1)S(1)}, bf16[320,128]{1,0:T(8,128)(2,1)S(1)}, u32[]{:S(2)}, u32[]{:S(2)}) collective-permute-start(bf16[320,128]{1,0:T(8,128)(2,1)S(1)} %get-tuple-element.88), channel_id=1, source_target_pairs={{0,24},{8,0},{16,8},{24,16},{1,25},{9,1},{17,9},{25,17},{2,26},{10... | collective-permute-start | bytes 245768 | tf_op jit(solution)/shard_map/ppermute | solution.py:314
  29.4 0.0 copy-start
  29.4 0.0 copy-start.1
  29.4 2.8 %sweep.7 = (f32[4,512,256]{2,1,0:T(8,128)S(1)}, f32[4,512,256]{2,1,0:T(8,128)S(1)}, bf16[4,512,256]{2,1,0:T(8,128)(2,1)}, bf16[4,512,256]{2,1,0:T(8,128)(2,1)}, f32[8,128]{1,0:T(8,128)S(1)}) custom-call(f32[512,128]{1,0:T(8,128)S(1)} %get-tuple-element.51.refs_0_.refs_6_, ...), custom_call_target="tpu_custom_call", output_to_operand_aliasing={{0}: (7, {}), {1}: (8, {}), {2}: (9, {}), {3}: (10, {})} | custom-call | tf_op jit(solution)/shard_map/sweep/pallas_call | solution.py:367
  32.3 0.0 collective-permute-done.7.refs_9_
  32.3 0.7 %collective-permute-done.8.refs_10_ = bf16[320,128]{1,0:T(8,128)(2,1)S(1)} collective-permute-done((bf16[320,128]{1,0:T(8,128)(2,1)S(1)}, bf16[320,128]{1,0:T(8,128)(2,1)S(1)}, u32[]{:S(2)}, u32[]{:S(2)}) %collective-permute-start.8) | collective-permute-done | bytes 81952 | tf_op jit(solution)/shard_map/ppermute | solution.py:314
  32.9 0.0 collective-permute-done.9.refs_11_
  32.9 0.0 copy-done
  32.9 0.0 copy-done.1
  33.0 3.1 %last.1 = (bf16[4,512,256]{2,1,0:T(8,128)(2,1)}, bf16[4,512,256]{2,1,0:T(8,128)(2,1)}, bf16[1,256,256]{2,1,0:T(8,128)(2,1)}, bf16[1,256,256]{2,1,0:T(8,128)(2,1)}) custom-call(f32[512,128]{1,0:T(8,128)S(1)} %get-tuple-element.51.refs_0_.refs_6_, bf16[4,512,256]{2,1,0:T(8,128)(2,1)S(1)} %get-tuple-element.52.refs_2_.refs_1_, ...), custom_call_target="tpu_custom_call" | custom-call | tf_op jit(solution)/shard_map/last/pallas_call | solution.py:419
  (1 shorter events, 0.0 us)
Async XLA Ops:
  4.5 8.8 %collective-permute-start = (bf16[336,128]{1,0:T(8,128)(2,1)S(1)}, bf16[336,128]{1,0:T(8,128)(2,1)S(1)}, u32[]{:S(2)}, u32[]{:S(2)}) collective-permute-start(bf16[336,128]{1,0:T(8,128)(2,1)S(1)} %get-tuple-element.58), channel_id=1, source_target_pairs={{0,8},{8,16},{16,24},{24,0},{1,9},{9,17},{17,25},{25,1},{2,10},{10... | collective-permute-start | bytes 258056 | tf_op jit(solution)/shard_map/ppermute | solution.py:314
  7.5 5.8 %collective-permute-start.1 = (bf16[336,128]{1,0:T(8,128)(2,1)S(1)}, bf16[336,128]{1,0:T(8,128)(2,1)S(1)}, u32[]{:S(2)}, u32[]{:S(2)}) collective-permute-start(bf16[336,128]{1,0:T(8,128)(2,1)S(1)} %get-tuple-element.59), channel_id=1, source_target_pairs={{0,16},{8,24},{16,0},{24,8},{1,17},{9,25},{17,1},{25,9},{2,18},{10... | collective-permute-start | bytes 258056 | tf_op jit(solution)/shard_map/ppermute | solution.py:314
  9.0 4.5 %collective-permute-start.2 = (bf16[336,128]{1,0:T(8,128)(2,1)S(1)}, bf16[336,128]{1,0:T(8,128)(2,1)S(1)}, u32[]{:S(2)}, u32[]{:S(2)}) collective-permute-start(bf16[336,128]{1,0:T(8,128)(2,1)S(1)} %get-tuple-element.60), channel_id=1, source_target_pairs={{0,24},{8,0},{16,8},{24,16},{1,25},{9,1},{17,9},{25,17},{2,26},{10... | collective-permute-start | bytes 258056 | tf_op jit(solution)/shard_map/ppermute | solution.py:314
  13.7 8.4 %collective-permute-start.3 = (bf16[192,128]{1,0:T(8,128)(2,1)S(1)}, bf16[192,128]{1,0:T(8,128)(2,1)S(1)}, u32[]{:S(2)}, u32[]{:S(2)}) collective-permute-start(bf16[192,128]{1,0:T(8,128)(2,1)S(1)} %get-tuple-element.63), channel_id=1, source_target_pairs={{0,2},{2,4},{4,6},{6,0},{1,3},{3,5},{5,7},{7,1},{8,10},{10,12},{12... | collective-permute-start | bytes 147464 | tf_op jit(solution)/shard_map/ppermute | solution.py:314
  15.4 6.8 %collective-permute-start.4 = (bf16[192,128]{1,0:T(8,128)(2,1)S(1)}, bf16[192,128]{1,0:T(8,128)(2,1)S(1)}, u32[]{:S(2)}, u32[]{:S(2)}) collective-permute-start(bf16[192,128]{1,0:T(8,128)(2,1)S(1)} %get-tuple-element.64), channel_id=1, source_target_pairs={{0,4},{2,6},{4,0},{6,2},{1,5},{3,7},{5,1},{7,3},{8,12},{10,14},{12... | collective-permute-start | bytes 147464 | tf_op jit(solution)/shard_map/ppermute | solution.py:314
  17.9 4.2 %collective-permute-start.5 = (bf16[192,128]{1,0:T(8,128)(2,1)S(1)}, bf16[192,128]{1,0:T(8,128)(2,1)S(1)}, u32[]{:S(2)}, u32[]{:S(2)}) collective-permute-start(bf16[192,128]{1,0:T(8,128)(2,1)S(1)} %get-tuple-element.65), channel_id=1, source_target_pairs={{0,6},{2,0},{4,2},{6,4},{1,7},{3,1},{5,3},{7,5},{8,14},{10,8},{12,... | collective-permute-start | bytes 147464 | tf_op jit(solution)/shard_map/ppermute | solution.py:314
  22.2 2.9 %collective-permute-start.6 = (bf16[320,128]{1,0:T(8,128)(2,1)S(1)}, bf16[320,128]{1,0:T(8,128)(2,1)S(1)}, u32[]{:S(2)}, u32[]{:S(2)}) collective-permute-start(bf16[320,128]{1,0:T(8,128)(2,1)S(1)} %get-tuple-element.73), channel_id=1, source_target_pairs={{0,1},{1,0},{2,3},{3,2},{4,5},{5,4},{6,7},{7,6},{8,9},{9,8},{10,11... | collective-permute-start | bytes 245768 | tf_op jit(solution)/shard_map/ppermute | solution.py:314
  25.4 6.9 %collective-permute-start.7 = (bf16[320,128]{1,0:T(8,128)(2,1)S(1)}, bf16[320,128]{1,0:T(8,128)(2,1)S(1)}, u32[]{:S(2)}, u32[]{:S(2)}) collective-permute-start(bf16[320,128]{1,0:T(8,128)(2,1)S(1)} %get-tuple-element.86), channel_id=1, source_target_pairs={{0,8},{8,16},{16,24},{24,0},{1,9},{9,17},{17,25},{25,1},{2,10},{10... | collective-permute-start | bytes 245768 | tf_op jit(solution)/shard_map/ppermute | solution.py:314
  27.1 5.8 %collective-permute-start.8 = (bf16[320,128]{1,0:T(8,128)(2,1)S(1)}, bf16[320,128]{1,0:T(8,128)(2,1)S(1)}, u32[]{:S(2)}, u32[]{:S(2)}) collective-permute-start(bf16[320,128]{1,0:T(8,128)(2,1)S(1)} %get-tuple-element.87), channel_id=1, source_target_pairs={{0,16},{8,24},{16,0},{24,8},{1,17},{9,25},{17,1},{25,9},{2,18},{10... | collective-permute-start | bytes 245768 | tf_op jit(solution)/shard_map/ppermute | solution.py:314
  28.3 4.6 %collective-permute-start.9 = (bf16[320,128]{1,0:T(8,128)(2,1)S(1)}, bf16[320,128]{1,0:T(8,128)(2,1)S(1)}, u32[]{:S(2)}, u32[]{:S(2)}) collective-permute-start(bf16[320,128]{1,0:T(8,128)(2,1)S(1)} %get-tuple-element.88), channel_id=1, source_target_pairs={{0,24},{8,0},{16,8},{24,16},{1,25},{9,1},{17,9},{25,17},{2,26},{10... | collective-permute-start | bytes 245768 | tf_op jit(solution)/shard_map/ppermute | solution.py:314
  29.4 3.5 %copy-start = (bf16[1,256,256]{2,1,0:T(8,128)(2,1)S(1)}, bf16[1,256,256]{2,1,0:T(8,128)(2,1)}, u32[]{:S(2)}) copy-start(bf16[1,256,256]{2,1,0:T(8,128)(2,1)} %refs_5_.3) | copy-start | bytes 393220
  29.4 3.5 %copy-start.1 = (bf16[1,256,256]{2,1,0:T(8,128)(2,1)S(1)}, bf16[1,256,256]{2,1,0:T(8,128)(2,1)}, u32[]{:S(2)}) copy-start(bf16[1,256,256]{2,1,0:T(8,128)(2,1)} %refs_6_.3) | copy-start | bytes 393220
where the time goes:
time: 36.4 us; the launch traced here: 36.2 us
  Pallas kernels  18.7 us (51%)
  starting transfers between devices  15.6 us (43%)
  between operations  0.93 us (3%)
  waiting for transfers between devices  0.9 us (2%)
    ppermute x10, starting transfers between devices, exchange(): lax.ppermute(xs[k], axis, [(s, (s + k) % n) for s in range(n)])  15.6 us
    pallas_call x4, Pallas kernels, sweep(): pl.pallas_call(lambda *refs: sweep_kernel(r, *refs), out_shape=[like, lik...  11.3 us
    pallas_call x1, Pallas kernels, shards(): pl.pallas_call(lambda *refs: first_kernel(n, *refs), out_shape=[shape((bl...  3.82 us
    pallas_call x1, Pallas kernels, shards(): pl.pallas_call(lambda *refs: last_kernel(n, responses, *refs), out_shape=...  3.05 us
    ppermute x10, waiting for transfers between devices, exchange(): lax.ppermute(xs[k], axis, [(s, (s + k) % n) for s in range(n)])  0.9 us
  transfers between devices with their start and end apart: 10, of which 2 were waited for; matrix products, arithmetic and copies ran while one was open for 0% of the time, Pallas kernels for 31%

commit v1 on v0

--- a/solution.py
+++ b/solution.py
@@ -8,6 +8,7 @@
 H = 2
 DH = 128
 HALF = 256
+LOG2E = 1.4426950408889634
 F32 = jnp.float32
 BF16 = jnp.bfloat16
 NEVER = -1e30
@@ -79,7 +80,7 @@
     part = DH // n
     block = H * part
     me = lax.axis_index("prompt")
-    targets = [lax.rem(me + k, n) for k in range(n)]
+    targets = [lax.bitwise_xor(me, k) for k in range(n)]
 
     def spread(at):
         for k in range(n):
@@ -152,7 +153,7 @@
     part = DH // n
     block = H * part
     responses = (got[0].shape[0] - block - 16) // block
-    place = [lax.rem(row + n - k, n) for k in range(n)]
+    place = [lax.bitwise_xor(row, k) for k in range(n)]
     notes = [got[k][block : block + 16, :].astype(F32) for k in range(n)]
     logs = [x[0:H] + x[H : 2 * H] + x[2 * H : 3 * H] for x in notes]
     final = jnp.zeros((block, DH), F32)
@@ -173,7 +174,7 @@
             sums[noted_prompt(notes[k], i)] += got[k][at : at + block, :].astype(F32)
     final = final.astype(BF16)
     for k in range(chips):
-        z = lax.rem(z_at + k, chips)
+        z = lax.bitwise_xor(z_at, k)
         msgs[k][0:block, :] = final
         for c in range(cores):
             msgs[k][(1 + c) * block : (2 + c) * block, :] = sums[z * cores + c].astype(BF16)
@@ -205,10 +206,10 @@
     total = kept_ref[chips * block :, :].astype(F32) + got_ref[chips * block :, :].astype(F32)
     total = total.astype(BF16)
     for k in range(n):
-        notes = noted[(n - k) % n][block : block + 16, :].astype(F32)
+        notes = noted[k][block : block + 16, :].astype(F32)
         for i in range(responses):
             p = noted_prompt(notes, i)
-            slot = lax.rem(z_at + chips - lax.div(p, 2), chips)
+            slot = lax.bitwise_xor(z_at, lax.div(p, 2))
             at = pl.ds(pl.multiple_of(slot * block, block), block)
             same = lax.rem(p, 2) == core
             state = jnp.where(same, kept_ref[at, :].astype(F32), got_ref[at, :].astype(F32))
@@ -219,37 +220,56 @@
 def sweep_kernel(r, cols_ref, rows_ref, q_ref, k_ref, v_ref, c_ref, *refs):
     out_ref, dq_ref, dk_hbm, dv_hbm, token_ref, dk_buf, dv_buf, sems = refs[-8:]
     token_ref[...] = jnp.zeros_like(token_ref)
+    slots = q_ref.shape[1]
     live = cols_ref[:, 8 * r + 4 : 8 * r + 5]
-    causal = lax.broadcasted_iota(jnp.int32, (HALF, HALF), 0) >= lax.broadcasted_iota(
-        jnp.int32, (HALF, HALF), 1
+    quarter = HALF // 2
+    causal = lax.broadcasted_iota(jnp.int32, (quarter, quarter), 0) >= lax.broadcasted_iota(
+        jnp.int32, (quarter, quarter), 1
     )
-    blocks = q_ref.shape[1] // HALF
+    blank = jnp.zeros((quarter, quarter), BF16)
+    grad_all = (c_ref[r].astype(F32) * live).astype(BF16)
+    query_turned = q_ref[r].T
+    grad_turned = grad_all.T
+    blocks = slots // HALF
     copies = []
+
+    def decayed(products, cum, row, diagonal):
+        if not diagonal:
+            decay = jnp.exp2(cum - row)
+            return [(x * decay).astype(BF16) for x in products]
+        first = jnp.exp2(jnp.where(causal, cum[:quarter] - row[:, :quarter], NEVER))
+        left = jnp.exp2(cum[quarter:] - row[:, :quarter])
+        right = jnp.exp2(jnp.where(causal, cum[quarter:] - row[:, quarter:], NEVER))
+        results = []
+        for x in products:
+            upper = jnp.concatenate([(x[:quarter, :quarter] * first).astype(BF16), blank], axis=1)
+            lower = [(x[quarter:, :quarter] * left).astype(BF16), (x[quarter:, quarter:] * right).astype(BF16)]
+            results.append(jnp.concatenate([upper, jnp.concatenate(lower, axis=1)], axis=0))
+        return results
+
     for h in range(H):
         lanes = slice(h * DH, (h + 1) * DH)
-        cum = cols_ref[:, 8 * r + h : 8 * r + h + 1]
+        cum = cols_ref[:, 8 * r + h : 8 * r + h + 1] * LOG2E
+        row = rows_ref[r, h : h + 1, :] * LOG2E
         dk = [None] * blocks
         dv = [None] * blocks
         for t in range(blocks):
             at = slice(t * HALF, (t + 1) * HALF)
             query = q_ref[r, at, lanes]
-            grad_out = (c_ref[r, at, lanes].astype(F32) * live[at]).astype(BF16)
+            grad_out = grad_all[at, lanes]
             out = None
             dq = None
             for s in range(t + 1):
                 of = slice(s * HALF, (s + 1) * HALF)
                 key = k_ref[r, of, lanes]
                 value = v_ref[r, of, lanes]
-                diff = cum[at] - rows_ref[r, h : h + 1, of]
-                if s == t:
-                    diff = jnp.where(causal, diff, NEVER)
-                decay = jnp.exp(diff)
-                mixing = (mm_nt(query, key) * decay).astype(BF16)
-                scores = (mm_nt(grad_out, value) * decay).astype(BF16)
+                mixing, scores = decayed(
+                    [mm_nt(query, key), mm_nt(grad_out, value)], cum[at], row[:, of], s == t
+                )
                 o_new = mm(mixing, value)
                 q_new = mm(scores, key)
-                k_new = mm_tn(scores, query)
-                v_new = mm_tn(mixing, grad_out)
+                k_new = mm(query_turned[lanes, at], scores)
+                v_new = mm(grad_turned[lanes, at], mixing)
                 out = o_new if out is None else out + o_new
                 dq = q_new if dq is None else dq + q_new
                 dk[s] = k_new if dk[s] is None else dk[s] + k_new
@@ -258,8 +278,8 @@
             dq_ref[r, at, lanes] = dq
         for s in range(blocks):
             of = slice(s * HALF, (s + 1) * HALF)
-            dk_buf[of, lanes] = dk[s].astype(BF16)
-            dv_buf[of, lanes] = dv[s].astype(BF16)
+            dk_buf[of, lanes] = dk[s].astype(BF16).T
+            dv_buf[of, lanes] = dv[s].astype(BF16).T
         copies += [
             pltpu.make_async_copy(dk_buf.at[:, lanes], dk_hbm.at[r, :, lanes], sems.at[2 * h]),
             pltpu.make_async_copy(dv_buf.at[:, lanes], dv_hbm.at[r, :, lanes], sems.at[2 * h + 1]),
@@ -271,47 +291,57 @@
 
 
 def last_kernel(n, count, cols_ref, q_ref, c_ref, po_ref, pdq_ref, keys_ref, values_ref, later_ref, *refs):
-    got, (out_hbm, dq_hbm, dk_ref, dv_ref, start, out_buf, dq_buf, sems) = refs[:n], refs[n + 1 :]
+    got, refs = refs[:n], refs[n + 1 :]
+    out_hbm, dq_hbm, dk_hbm, dv_hbm, start, out_buf, dq_buf, dk_buf, dv_buf, sems = refs
     part = DH // n
     block = H * part
     row = lax.axis_index("prompt")
+    slots = q_ref.shape[1]
+    tokens = keys_ref.shape[1]
+    copies = []
+
+    def send(a, b):
+        copies.append(pltpu.make_async_copy(a, b, sems.at[len(copies)]))
+        copies[-1].start()
+
+    start[...] = jnp.zeros_like(start)
     for r in range(count + 1):
         for k in range(n):
-            of = pl.ds(pl.multiple_of(lax.rem(row + n - k, n) * part, part), part)
             for h in range(H):
-                start[r, h, of, :] = got[k][r * block + h * part : r * block + (h + 1) * part, :]
-    copies = []
-    for r in range(count):
-        live = cols_ref[:, 8 * r + 4 : 8 * r + 5]
-        opened = cols_ref[:, 8 * r + 5 : 8 * r + 6]
+                of = pl.ds(pl.multiple_of(h * DH + lax.bitwise_xor(row, k) * part, part), part)
+                rows = got[k][r * block + h * part : r * block + (h + 1) * part, :]
+                start[r, of, h * DH : (h + 1) * DH] = rows
+    factor = [
+        jnp.exp(cols_ref[:tokens, 8 * count + h : 8 * count + h + 1] + later_ref[h : h + 1, 0:1]) for h in range(H)
+    ]
+    for buf, x in ((dk_buf, mm_nt(values_ref[0], start[count])), (dv_buf, mm(keys_ref[0], start[count]))):
         for h in range(H):
             lanes = slice(h * DH, (h + 1) * DH)
-            carried = cols_ref[:, 8 * r + 2 + h : 8 * r + 3 + h]
-            grad_out = (c_ref[r, :, lanes].astype(F32) * live).astype(BF16)
-            out = po_ref[r, :, lanes] + carried * mm(q_ref[r, :, lanes], start[r, h])
-            out_buf[r, :, lanes] = (opened * out).astype(BF16)
-            dq = pdq_ref[r, :, lanes] + carried * mm_nt(grad_out, start[r, h])
-            dq_buf[r, :, lanes] = dq.astype(BF16)
-        copies += [
-            pltpu.make_async_copy(out_buf.at[r], out_hbm.at[r], sems.at[2 * r]),
-            pltpu.make_async_copy(dq_buf.at[r], dq_hbm.at[r], sems.at[2 * r + 1]),
-        ]
-        copies[-2].start()
-        copies[-1].start()
-    tokens = keys_ref.shape[1]
-    for h in range(H):
-        lanes = slice(h * DH, (h + 1) * DH)
-        suffix = cols_ref[:tokens, 8 * count + h : 8 * count + h + 1]
-        factor = jnp.exp(suffix + later_ref[h : h + 1, 0:1])
-        dk_ref[0, :, lanes] = (factor * mm_nt(values_ref[0, :, lanes], start[count, h])).astype(BF16)
-        dv_ref[0, :, lanes] = (factor * mm(keys_ref[0, :, lanes], start[count, h])).astype(BF16)
+            buf[:, lanes] = (factor[h] * x[:, lanes]).astype(BF16)
+    send(dk_buf, dk_hbm.at[0])
+    send(dv_buf, dv_hbm.at[0])
+    for r in range(count):
+        for t in range(0, slots, HALF):
+            at = slice(t, t + HALF)
+            live = cols_ref[at, 8 * r + 4 : 8 * r + 5]
+            opened = cols_ref[at, 8 * r + 5 : 8 * r + 6]
+            grad_out = (c_ref[r, at, :].astype(F32) * live).astype(BF16)
+            x = mm(q_ref[r, at, :], start[r])
+            y = mm_nt(grad_out, start[r])
+            for h in range(H):
+                lanes = slice(h * DH, (h + 1) * DH)
+                carried = cols_ref[at, 8 * r + 2 + h : 8 * r + 3 + h]
+                out_buf[r, at, lanes] = (opened * (po_ref[r, at, lanes] + carried * x[:, lanes])).astype(BF16)
+                dq_buf[r, at, lanes] = (pdq_ref[r, at, lanes] + carried * y[:, lanes]).astype(BF16)
+            send(out_buf.at[r, at], out_hbm.at[r, at])
+            send(dq_buf.at[r, at], dq_hbm.at[r, at])
     for copy in copies:
         copy.wait()
 
 
 def exchange(xs, axis):
     n = lax.axis_size(axis)
-    moved = [lax.ppermute(xs[k], axis, [(s, (s + k) % n) for s in range(n)]) for k in range(1, n)]
+    moved = [lax.ppermute(xs[k], axis, [(s, s ^ k) for s in range(n)]) for k in range(1, n)]
     return [xs[0]] + moved
 
 
@@ -420,12 +450,14 @@
         lambda *refs: last_kernel(n, responses, *refs),
         out_shape=[like_out, like_out, shape(keys.shape, BF16), shape(keys.shape, BF16)],
         in_specs=[VMEM] * (8 + n) + [ANY],
-        out_specs=[ANY, ANY, VMEM, VMEM],
+        out_specs=[ANY] * 4,
         scratch_shapes=[
-            pltpu.VMEM((responses + 1, H, DH, DH), BF16),
+            pltpu.VMEM((responses + 1, width, width), BF16),
             pltpu.VMEM(queries.shape, BF16),
             pltpu.VMEM(queries.shape, BF16),
-            pltpu.SemaphoreType.DMA((2 * responses,)),
+            pltpu.VMEM(keys.shape[1:], BF16),
+            pltpu.VMEM(keys.shape[1:], BF16),
+            pltpu.SemaphoreType.DMA((2 + 2 * responses * (slots // HALF),)),
         ],
         compiler_params=params(),
         name="last",

time: 36.4 us -> 37.2 us (1.022)
  waiting for transfers between devices: 0.9 us -> 6.95 us
  starting transfers between devices: 15.6 us -> 12.6 us
  Pallas kernels: 18.7 us -> 16.7 us
    ppermute x10, waiting for transfers between devices: 0.9 us -> 6.95 us  [exchange(): lax.ppermute(xs[k], axis, [(s, s ^ k) for s in range(n)])]
    ppermute x10, starting transfers between devices: 15.6 us -> 12.6 us  [exchange(): lax.ppermute(xs[k], axis, [(s, s ^ k) for s in range(n)])]
    pallas_call x4, Pallas kernels: 11.3 us -> 9.88 us  [sweep(): pl.pallas_call(lambda *refs: sweep_kernel(r, *refs), out_shape=[like, lik...]
    pallas_call x1, Pallas kernels: 3.05 us -> 2.48 us  [shards(): pl.pallas_call(lambda *refs: last_kernel(n, responses, *refs), out_shape=...]
  transfers between devices with their start and end apart: 10 -> 10, of which waited for: 2 -> 5; matrix products, arithmetic and copies ran while one was open for 0% -> 0% of each run, Pallas kernels for 31% -> 27%
where the time goes in v1:
time: 37.2 us; the launch traced here: 37 us
  Pallas kernels  16.7 us (45%)
  starting transfers between devices  12.6 us (34%)
  waiting for transfers between devices  6.95 us (19%)
  between operations  0.74 us (2%)
    ppermute x10, starting transfers between devices, exchange(): lax.ppermute(xs[k], axis, [(s, s ^ k) for s in range(n)])  12.6 us
    pallas_call x4, Pallas kernels, sweep(): pl.pallas_call(lambda *refs: sweep_kernel(r, *refs), out_shape=[like, lik...  9.88 us
    ppermute x10, waiting for transfers between devices, exchange(): lax.ppermute(xs[k], axis, [(s, s ^ k) for s in range(n)])  6.95 us
    pallas_call x1, Pallas kernels, shards(): pl.pallas_call(lambda *refs: first_kernel(n, *refs), out_shape=[shape((bl...  3.81 us
    pallas_call x1, Pallas kernels, shards(): pl.pallas_call(lambda *refs: last_kernel(n, responses, *refs), out_shape=...  2.48 us
  transfers between devices with their start and end apart: 10, of which 5 were waited for; matrix products, arithmetic and copies ran while one was open for 0% of the time, Pallas kernels for 27%

profile of v1, /device:TPU:0, one launch (start us, length us, event | category | flops | bytes accessed | tf_op | source)
XLA Modules:
  0.0 37.0 jit_solution(5878654607465483255)
XLA Ops:
  0.6 3.8 %first.1 = (bf16[336,128]{1,0:T(8,128)(2,1)S(1)}, bf16[336,128]{1,0:T(8,128)(2,1)S(1)}, bf16[336,128]{1,0:T(8,128)(2,1)S(1)}, bf16[336,128]{1,0:T(8,128)(2,1)S(1...) custom-call(s32[4]{0:T(128)} %refs_0_.1, ...), custom_call_target="tpu_custom_call" | custom-call | tf_op jit(solution)/shard_map/first/pallas_call | solution.py:369
  4.4 3.0 %collective-permute-start = (bf16[336,128]{1,0:T(8,128)(2,1)S(1)}, bf16[336,128]{1,0:T(8,128)(2,1)S(1)}, u32[]{:S(2)}, u32[]{:S(2)}) collective-permute-start(bf16[336,128]{1,0:T(8,128)(2,1)S(1)} %get-tuple-element.58), channel_id=1, source_target_pairs={{0,8},{8,0},{16,24},{24,16},{1,9},{9,1},{17,25},{25,17},{2,10},{10... | collective-permute-start | bytes 258056 | tf_op jit(solution)/shard_map/ppermute | solution.py:344
  7.5 1.5 %collective-permute-start.1 = (bf16[336,128]{1,0:T(8,128)(2,1)S(1)}, bf16[336,128]{1,0:T(8,128)(2,1)S(1)}, u32[]{:S(2)}, u32[]{:S(2)}) collective-permute-start(bf16[336,128]{1,0:T(8,128)(2,1)S(1)} %get-tuple-element.59), channel_id=1, source_target_pairs={{0,16},{8,24},{16,0},{24,8},{1,17},{9,25},{17,1},{25,9},{2,18},{10... | collective-permute-start | bytes 258056 | tf_op jit(solution)/shard_map/ppermute | solution.py:344
  9.0 0.0 collective-permute-start.2
  9.0 2.5 %sweep.4 = (f32[4,512,256]{2,1,0:T(8,128)S(1)}, f32[4,512,256]{2,1,0:T(8,128)S(1)}, bf16[4,512,256]{2,1,0:T(8,128)(2,1)}, bf16[4,512,256]{2,1,0:T(8,128)(2,1)}, f32[8,128]{1,0:T(8,128)S(1)}) custom-call(f32[512,128]{1,0:T(8,128)S(1)} %get-tuple-element.51.refs_0_.refs_6_, f32[4,8,512]{2,1,0:T(8,128)S(1)} %get-tuple-element.54.refs_1_, ...), custom_call_target="tpu_custom_call" | custom-call | tf_op jit(solution)/shard_map/sweep/pallas_call | solution.py:397
  11.5 0.0 collective-permute-done.refs_1_
  11.5 1.4 %collective-permute-done.1.refs_2_ = bf16[336,128]{1,0:T(8,128)(2,1)S(1)} collective-permute-done((bf16[336,128]{1,0:T(8,128)(2,1)S(1)}, bf16[336,128]{1,0:T(8,128)(2,1)S(1)}, u32[]{:S(2)}, u32[]{:S(2)}) %collective-permute-start.1) | collective-permute-done | bytes 86048 | tf_op jit(solution)/shard_map/ppermute | solution.py:344
  12.9 1.5 %collective-permute-done.2.refs_3_ = bf16[336,128]{1,0:T(8,128)(2,1)S(1)} collective-permute-done((bf16[336,128]{1,0:T(8,128)(2,1)S(1)}, bf16[336,128]{1,0:T(8,128)(2,1)S(1)}, u32[]{:S(2)}, u32[]{:S(2)}) %collective-permute-start.2) | collective-permute-done | bytes 86048 | tf_op jit(solution)/shard_map/ppermute | solution.py:344
  14.4 0.2 second.1
  14.6 1.6 %collective-permute-start.3 = (bf16[192,128]{1,0:T(8,128)(2,1)S(1)}, bf16[192,128]{1,0:T(8,128)(2,1)S(1)}, u32[]{:S(2)}, u32[]{:S(2)}) collective-permute-start(bf16[192,128]{1,0:T(8,128)(2,1)S(1)} %get-tuple-element.63), channel_id=1, source_target_pairs={{0,2},{2,0},{4,6},{6,4},{1,3},{3,1},{5,7},{7,5},{8,10},{10,8},{12,... | collective-permute-start | bytes 147464 | tf_op jit(solution)/shard_map/ppermute | solution.py:344
  16.3 2.6 %collective-permute-start.4 = (bf16[192,128]{1,0:T(8,128)(2,1)S(1)}, bf16[192,128]{1,0:T(8,128)(2,1)S(1)}, u32[]{:S(2)}, u32[]{:S(2)}) collective-permute-start(bf16[192,128]{1,0:T(8,128)(2,1)S(1)} %get-tuple-element.64), channel_id=1, source_target_pairs={{0,4},{2,6},{4,0},{6,2},{1,5},{3,7},{5,1},{7,3},{8,12},{10,14},{12... | collective-permute-start | bytes 147464 | tf_op jit(solution)/shard_map/ppermute | solution.py:344
  18.9 0.2 collective-permute-start.5
  19.1 2.5 %sweep.5 = (f32[4,512,256]{2,1,0:T(8,128)S(1)}, f32[4,512,256]{2,1,0:T(8,128)S(1)}, bf16[4,512,256]{2,1,0:T(8,128)(2,1)}, bf16[4,512,256]{2,1,0:T(8,128)(2,1)}, f32[8,128]{1,0:T(8,128)S(1)}) custom-call(f32[512,128]{1,0:T(8,128)S(1)} %get-tuple-element.51.refs_0_.refs_6_, ...), custom_call_target="tpu_custom_call", output_to_operand_aliasing={{0}: (7, {}), {1}: (8, {}), {2}: (9, {}), {3}: (10, {})} | custom-call | tf_op jit(solution)/shard_map/sweep/pallas_call | solution.py:397
  21.5 0.0 collective-permute-done.3.refs_1_
  21.6 0.7 %collective-permute-done.4.refs_2_ = bf16[192,128]{1,0:T(8,128)(2,1)S(1)} collective-permute-done((bf16[192,128]{1,0:T(8,128)(2,1)S(1)}, bf16[192,128]{1,0:T(8,128)(2,1)S(1)}, u32[]{:S(2)}, u32[]{:S(2)}) %collective-permute-start.4) | collective-permute-done | bytes 49184 | tf_op jit(solution)/shard_map/ppermute | solution.py:344
  22.3 2.4 %collective-permute-done.5.refs_3_ = bf16[192,128]{1,0:T(8,128)(2,1)S(1)} collective-permute-done((bf16[192,128]{1,0:T(8,128)(2,1)S(1)}, bf16[192,128]{1,0:T(8,128)(2,1)S(1)}, u32[]{:S(2)}, u32[]{:S(2)}) %collective-permute-start.5) | collective-permute-done | bytes 49184 | tf_op jit(solution)/shard_map/ppermute | solution.py:344
  24.8 0.1 collective-permute-start.6
  24.9 2.5 %sweep.6 = (f32[4,512,256]{2,1,0:T(8,128)S(1)}, f32[4,512,256]{2,1,0:T(8,128)S(1)}, bf16[4,512,256]{2,1,0:T(8,128)(2,1)}, bf16[4,512,256]{2,1,0:T(8,128)(2,1)}, f32[8,128]{1,0:T(8,128)S(1)}) custom-call(f32[512,128]{1,0:T(8,128)S(1)} %get-tuple-element.51.refs_0_.refs_6_, ...), custom_call_target="tpu_custom_call", output_to_operand_aliasing={{0}: (7, {}), {1}: (8, {}), {2}: (9, {}), {3}: (10, {})} | custom-call | tf_op jit(solution)/shard_map/sweep/pallas_call | solution.py:397
  27.3 0.0 collective-permute-done.6.refs_5_
  27.4 0.2 third.1
  27.6 0.6 %collective-permute-start.7 = (bf16[320,128]{1,0:T(8,128)(2,1)S(1)}, bf16[320,128]{1,0:T(8,128)(2,1)S(1)}, u32[]{:S(2)}, u32[]{:S(2)}) collective-permute-start(bf16[320,128]{1,0:T(8,128)(2,1)S(1)} %get-tuple-element.86), channel_id=1, source_target_pairs={{0,8},{8,0},{16,24},{24,16},{1,9},{9,1},{17,25},{25,17},{2,10},{10... | collective-permute-start | bytes 245768 | tf_op jit(solution)/shard_map/ppermute | solution.py:344
  28.2 0.8 %collective-permute-start.8 = (bf16[320,128]{1,0:T(8,128)(2,1)S(1)}, bf16[320,128]{1,0:T(8,128)(2,1)S(1)}, u32[]{:S(2)}, u32[]{:S(2)}) collective-permute-start(bf16[320,128]{1,0:T(8,128)(2,1)S(1)} %get-tuple-element.87), channel_id=1, source_target_pairs={{0,16},{8,24},{16,0},{24,8},{1,17},{9,25},{17,1},{25,9},{2,18},{10... | collective-permute-start | bytes 245768 | tf_op jit(solution)/shard_map/ppermute | solution.py:344
  29.0 2.2 %collective-permute-start.9 = (bf16[320,128]{1,0:T(8,128)(2,1)S(1)}, bf16[320,128]{1,0:T(8,128)(2,1)S(1)}, u32[]{:S(2)}, u32[]{:S(2)}) collective-permute-start(bf16[320,128]{1,0:T(8,128)(2,1)S(1)} %get-tuple-element.88), channel_id=1, source_target_pairs={{0,24},{8,16},{16,8},{24,0},{1,25},{9,17},{17,9},{25,1},{2,26},{10... | collective-permute-start | bytes 245768 | tf_op jit(solution)/shard_map/ppermute | solution.py:344
  31.1 0.0 copy-start
  31.1 0.0 copy-start.1
  31.1 2.5 %sweep.7 = (f32[4,512,256]{2,1,0:T(8,128)S(1)}, f32[4,512,256]{2,1,0:T(8,128)S(1)}, bf16[4,512,256]{2,1,0:T(8,128)(2,1)}, bf16[4,512,256]{2,1,0:T(8,128)(2,1)}, f32[8,128]{1,0:T(8,128)S(1)}) custom-call(f32[512,128]{1,0:T(8,128)S(1)} %get-tuple-element.51.refs_0_.refs_6_, ...), custom_call_target="tpu_custom_call", output_to_operand_aliasing={{0}: (7, {}), {1}: (8, {}), {2}: (9, {}), {3}: (10, {})} | custom-call | tf_op jit(solution)/shard_map/sweep/pallas_call | solution.py:397
  33.6 0.0 collective-permute-done.7.refs_9_
  33.6 0.9 %collective-permute-done.8.refs_10_ = bf16[320,128]{1,0:T(8,128)(2,1)S(1)} collective-permute-done((bf16[320,128]{1,0:T(8,128)(2,1)S(1)}, bf16[320,128]{1,0:T(8,128)(2,1)S(1)}, u32[]{:S(2)}, u32[]{:S(2)}) %collective-permute-start.8) | collective-permute-done | bytes 81952 | tf_op jit(solution)/shard_map/ppermute | solution.py:344
  34.5 0.0 collective-permute-done.9.refs_11_
  34.5 0.0 copy-done
  34.5 0.0 copy-done.1
  34.5 2.5 %last.1 = (bf16[4,512,256]{2,1,0:T(8,128)(2,1)}, bf16[4,512,256]{2,1,0:T(8,128)(2,1)}, bf16[1,256,256]{2,1,0:T(8,128)(2,1)}, bf16[1,256,256]{2,1,0:T(8,128)(2,1)}) custom-call(f32[512,128]{1,0:T(8,128)S(1)} %get-tuple-element.51.refs_0_.refs_6_, bf16[4,512,256]{2,1,0:T(8,128)(2,1)S(1)} %get-tuple-element.52.refs_2_.refs_1_, ...), custom_call_target="tpu_custom_call" | custom-call | tf_op jit(solution)/shard_map/last/pallas_call | solution.py:449
  (1 shorter events, 0.0 us)
Async XLA Ops:
  4.4 7.0 %collective-permute-start = (bf16[336,128]{1,0:T(8,128)(2,1)S(1)}, bf16[336,128]{1,0:T(8,128)(2,1)S(1)}, u32[]{:S(2)}, u32[]{:S(2)}) collective-permute-start(bf16[336,128]{1,0:T(8,128)(2,1)S(1)} %get-tuple-element.58), channel_id=1, source_target_pairs={{0,8},{8,0},{16,24},{24,16},{1,9},{9,1},{17,25},{25,17},{2,10},{10... | collective-permute-start | bytes 258056 | tf_op jit(solution)/shard_map/ppermute | solution.py:344
  7.5 5.4 %collective-permute-start.1 = (bf16[336,128]{1,0:T(8,128)(2,1)S(1)}, bf16[336,128]{1,0:T(8,128)(2,1)S(1)}, u32[]{:S(2)}, u32[]{:S(2)}) collective-permute-start(bf16[336,128]{1,0:T(8,128)(2,1)S(1)} %get-tuple-element.59), channel_id=1, source_target_pairs={{0,16},{8,24},{16,0},{24,8},{1,17},{9,25},{17,1},{25,9},{2,18},{10... | collective-permute-start | bytes 258056 | tf_op jit(solution)/shard_map/ppermute | solution.py:344
  9.0 5.4 %collective-permute-start.2 = (bf16[336,128]{1,0:T(8,128)(2,1)S(1)}, bf16[336,128]{1,0:T(8,128)(2,1)S(1)}, u32[]{:S(2)}, u32[]{:S(2)}) collective-permute-start(bf16[336,128]{1,0:T(8,128)(2,1)S(1)} %get-tuple-element.60), channel_id=1, source_target_pairs={{0,24},{8,16},{16,8},{24,0},{1,25},{9,17},{17,9},{25,1},{2,26},{10... | collective-permute-start | bytes 258056 | tf_op jit(solution)/shard_map/ppermute | solution.py:344
  14.6 6.9 %collective-permute-start.3 = (bf16[192,128]{1,0:T(8,128)(2,1)S(1)}, bf16[192,128]{1,0:T(8,128)(2,1)S(1)}, u32[]{:S(2)}, u32[]{:S(2)}) collective-permute-start(bf16[192,128]{1,0:T(8,128)(2,1)S(1)} %get-tuple-element.63), channel_id=1, source_target_pairs={{0,2},{2,0},{4,6},{6,4},{1,3},{3,1},{5,7},{7,5},{8,10},{10,8},{12,... | collective-permute-start | bytes 147464 | tf_op jit(solution)/shard_map/ppermute | solution.py:344
  16.3 6.0 %collective-permute-start.4 = (bf16[192,128]{1,0:T(8,128)(2,1)S(1)}, bf16[192,128]{1,0:T(8,128)(2,1)S(1)}, u32[]{:S(2)}, u32[]{:S(2)}) collective-permute-start(bf16[192,128]{1,0:T(8,128)(2,1)S(1)} %get-tuple-element.64), channel_id=1, source_target_pairs={{0,4},{2,6},{4,0},{6,2},{1,5},{3,7},{5,1},{7,3},{8,12},{10,14},{12... | collective-permute-start | bytes 147464 | tf_op jit(solution)/shard_map/ppermute | solution.py:344
  18.9 5.9 %collective-permute-start.5 = (bf16[192,128]{1,0:T(8,128)(2,1)S(1)}, bf16[192,128]{1,0:T(8,128)(2,1)S(1)}, u32[]{:S(2)}, u32[]{:S(2)}) collective-permute-start(bf16[192,128]{1,0:T(8,128)(2,1)S(1)} %get-tuple-element.65), channel_id=1, source_target_pairs={{0,6},{2,4},{4,2},{6,0},{1,7},{3,5},{5,3},{7,1},{8,14},{10,12},{12... | collective-permute-start | bytes 147464 | tf_op jit(solution)/shard_map/ppermute | solution.py:344
  24.8 2.6 %collective-permute-start.6 = (bf16[320,128]{1,0:T(8,128)(2,1)S(1)}, bf16[320,128]{1,0:T(8,128)(2,1)S(1)}, u32[]{:S(2)}, u32[]{:S(2)}) collective-permute-start(bf16[320,128]{1,0:T(8,128)(2,1)S(1)} %get-tuple-element.73), channel_id=1, source_target_pairs={{0,1},{1,0},{2,3},{3,2},{4,5},{5,4},{6,7},{7,6},{8,9},{9,8},{10,11... | collective-permute-start | bytes 245768 | tf_op jit(solution)/shard_map/ppermute | solution.py:344
  27.6 6.0 %collective-permute-start.7 = (bf16[320,128]{1,0:T(8,128)(2,1)S(1)}, bf16[320,128]{1,0:T(8,128)(2,1)S(1)}, u32[]{:S(2)}, u32[]{:S(2)}) collective-permute-start(bf16[320,128]{1,0:T(8,128)(2,1)S(1)} %get-tuple-element.86), channel_id=1, source_target_pairs={{0,8},{8,0},{16,24},{24,16},{1,9},{9,1},{17,25},{25,17},{2,10},{10... | collective-permute-start | bytes 245768 | tf_op jit(solution)/shard_map/ppermute | solution.py:344
  28.2 6.3 %collective-permute-start.8 = (bf16[320,128]{1,0:T(8,128)(2,1)S(1)}, bf16[320,128]{1,0:T(8,128)(2,1)S(1)}, u32[]{:S(2)}, u32[]{:S(2)}) collective-permute-start(bf16[320,128]{1,0:T(8,128)(2,1)S(1)} %get-tuple-element.87), channel_id=1, source_target_pairs={{0,16},{8,24},{16,0},{24,8},{1,17},{9,25},{17,1},{25,9},{2,18},{10... | collective-permute-start | bytes 245768 | tf_op jit(solution)/shard_map/ppermute | solution.py:344
  29.0 5.5 %collective-permute-start.9 = (bf16[320,128]{1,0:T(8,128)(2,1)S(1)}, bf16[320,128]{1,0:T(8,128)(2,1)S(1)}, u32[]{:S(2)}, u32[]{:S(2)}) collective-permute-start(bf16[320,128]{1,0:T(8,128)(2,1)S(1)} %get-tuple-element.88), channel_id=1, source_target_pairs={{0,24},{8,16},{16,8},{24,0},{1,25},{9,17},{17,9},{25,1},{2,26},{10... | collective-permute-start | bytes 245768 | tf_op jit(solution)/shard_map/ppermute | solution.py:344
  31.1 3.4 %copy-start = (bf16[1,256,256]{2,1,0:T(8,128)(2,1)S(1)}, bf16[1,256,256]{2,1,0:T(8,128)(2,1)}, u32[]{:S(2)}) copy-start(bf16[1,256,256]{2,1,0:T(8,128)(2,1)} %refs_5_.3) | copy-start | bytes 393220
  31.1 3.4 %copy-start.1 = (bf16[1,256,256]{2,1,0:T(8,128)(2,1)S(1)}, bf16[1,256,256]{2,1,0:T(8,128)(2,1)}, u32[]{:S(2)}) copy-start(bf16[1,256,256]{2,1,0:T(8,128)(2,1)} %refs_6_.3) | copy-start | bytes 393220

commit v2 on v1

--- a/solution.py
+++ b/solution.py
@@ -62,12 +62,13 @@
 
 
 def first_kernel(
-    n, ids_ref, lens_ref, adv_ref, keys_hbm, values_hbm, pgates_hbm, gates_hbm, mask_hbm, q_hbm, c_hbm, k_hbm, v_hbm,
+    n, ids_hbm, lens_hbm, adv_hbm, keys_hbm, values_hbm, pgates_hbm, gates_hbm, mask_hbm, q_hbm, c_hbm, k_hbm, v_hbm,
     *refs,
 ):
     msgs, (cols_ref, rows_ref, q, c, k_out, v_out) = refs[:n], refs[n : n + 6]
-    keys, values, pgates, gates, mask, matrices, sems = refs[n + 6 :]
-    pairs = [(pgates_hbm, pgates), (gates_hbm, gates), (mask_hbm, mask), (keys_hbm, keys), (values_hbm, values)]
+    keys, values, pgates, gates, mask, ids_ref, lens_ref, adv_ref, matrices, sems = refs[n + 6 :]
+    pairs = [(pgates_hbm, pgates), (gates_hbm, gates), (mask_hbm, mask)]
+    pairs += [(ids_hbm, ids_ref), (lens_hbm, lens_ref), (adv_hbm, adv_ref), (keys_hbm, keys), (values_hbm, values)]
     count = gates.shape[0]
     slots = gates.shape[2]
     tokens = keys.shape[1]
@@ -89,7 +90,7 @@
                 at, of, :
             ].astype(BF16)
 
-    for copy in copies[:3]:
+    for copy in copies[:6]:
         copy.wait()
     piece = jnp.concatenate([pgates[0], jnp.zeros((H, slots - tokens), F32)], axis=1)
     gate_rows = [gates[i] for i in range(count)] + [piece, jnp.zeros((16 - H * (count + 1), slots), F32)]
@@ -102,7 +103,7 @@
         weight = adv_ref[i].astype(F32) / 1024.0
         opened = jnp.where(place < lens_ref[0, i], 1.0, 0.0)
         live = mask[i : i + 1, :].astype(F32) * opened * weight
-        rows += [cum[H * i : H * i + H], carried[H * i : H * i + H], live, opened, jnp.zeros((2, slots), F32)]
+        rows += [cum[H * i : H * i + H], carried[H * i : H * i + H] * opened, live, opened, jnp.zeros((2, slots), F32)]
         factors.append(carried[H * i : H * i + H] * live)
     rows_ref[...] = jnp.concatenate(rows, axis=0).reshape(count, 8, slots)
     piece = cum[H * count : H * count + H]
@@ -111,7 +112,7 @@
     rows += [suffix, jnp.zeros((128 - 8 * count - H, slots), F32)]
     cols_ref[...] = jnp.concatenate(rows, axis=0).T
 
-    for copy in copies[3:5]:
+    for copy in copies[6:8]:
         copy.wait()
     turned = keys[0].T
     later = jnp.exp(suffix[:, :tokens])
@@ -131,15 +132,15 @@
         msgs[k][block : block + 16, :] = notes
 
     for i in range(count):
-        copies[5 + 2 * i].wait()
+        copies[8 + 2 * i].wait()
         turned = q[i].T
-        copies[6 + 2 * i].wait()
+        copies[9 + 2 * i].wait()
         for h in range(H):
             lanes = slice(h * DH, (h + 1) * DH)
             scaled = (turned[lanes].astype(F32) * factors[i][h : h + 1]).astype(BF16)
             matrices[H * (1 + i) + h] = mm(scaled, c[i, :, lanes])
             spread(H * (1 + i) + h)
-    for copy in copies[5 + 2 * count :]:
+    for copy in copies[8 + 2 * count :]:
         copy.wait()
 
 
@@ -200,7 +201,7 @@
 
 def third_kernel(n, chips, *refs):
     z_at, core = lax.axis_index("z"), lax.axis_index("core")
-    noted, kept_ref, got_ref, msgs = refs[:n], refs[n], refs[n + 1], refs[n + 3 :]
+    noted, kept_ref, got_ref, msgs = refs[:n], refs[n], refs[n + 1], refs[n + 2 :]
     block = H * DH // n
     responses = (noted[0].shape[0] - block - 16) // block
     total = kept_ref[chips * block :, :].astype(F32) + got_ref[chips * block :, :].astype(F32)
@@ -217,20 +218,15 @@
         msgs[k][responses * block :, :] = total
 
 
-def sweep_kernel(r, cols_ref, rows_ref, q_ref, k_ref, v_ref, c_ref, *refs):
-    out_ref, dq_ref, dk_hbm, dv_hbm, token_ref, dk_buf, dv_buf, sems = refs[-8:]
+def sweep_kernel(units, cols_ref, rows_ref, q_ref, k_ref, v_ref, c_ref, *refs):
+    out_ref, dq_ref, grad_ref, dk_hbm, dv_hbm, token_ref, dk_buf, dv_buf, sems = refs[-9:]
     token_ref[...] = jnp.zeros_like(token_ref)
-    slots = q_ref.shape[1]
-    live = cols_ref[:, 8 * r + 4 : 8 * r + 5]
     quarter = HALF // 2
     causal = lax.broadcasted_iota(jnp.int32, (quarter, quarter), 0) >= lax.broadcasted_iota(
         jnp.int32, (quarter, quarter), 1
     )
     blank = jnp.zeros((quarter, quarter), BF16)
-    grad_all = (c_ref[r].astype(F32) * live).astype(BF16)
-    query_turned = q_ref[r].T
-    grad_turned = grad_all.T
-    blocks = slots // HALF
+    blocks = q_ref.shape[1] // HALF
     copies = []
 
     def decayed(products, cum, row, diagonal):
@@ -247,16 +243,22 @@
             results.append(jnp.concatenate([upper, jnp.concatenate(lower, axis=1)], axis=0))
         return results
 
-    for h in range(H):
+    for u, (r, h) in enumerate(units):
         lanes = slice(h * DH, (h + 1) * DH)
         cum = cols_ref[:, 8 * r + h : 8 * r + h + 1] * LOG2E
         row = rows_ref[r, h : h + 1, :] * LOG2E
+        live = cols_ref[:, 8 * r + 4 : 8 * r + 5]
+        opened = cols_ref[:, 8 * r + 5 : 8 * r + 6]
+        grad_all = (c_ref[r, :, lanes].astype(F32) * live).astype(BF16)
+        grad_ref[r, :, lanes] = grad_all
+        query_turned = q_ref[r, :, lanes].T
+        grad_turned = grad_all.T
         dk = [None] * blocks
         dv = [None] * blocks
         for t in range(blocks):
             at = slice(t * HALF, (t + 1) * HALF)
             query = q_ref[r, at, lanes]
-            grad_out = grad_all[at, lanes]
+            grad_out = grad_all[at]
             out = None
             dq = None
             for s in range(t + 1):
@@ -268,21 +270,21 @@
                 )
                 o_new = mm(mixing, value)
                 q_new = mm(scores, key)
-                k_new = mm(query_turned[lanes, at], scores)
-                v_new = mm(grad_turned[lanes, at], mixing)
+                k_new = mm(query_turned[:, at], scores)
+                v_new = mm(grad_turned[:, at], mixing)
                 out = o_new if out is None else out + o_new
                 dq = q_new if dq is None else dq + q_new
                 dk[s] = k_new if dk[s] is None else dk[s] + k_new
                 dv[s] = v_new if dv[s] is None else dv[s] + v_new
-            out_ref[r, at, lanes] = out
+            out_ref[r, at, lanes] = out * opened[at]
             dq_ref[r, at, lanes] = dq
         for s in range(blocks):
             of = slice(s * HALF, (s + 1) * HALF)
-            dk_buf[of, lanes] = dk[s].astype(BF16).T
-            dv_buf[of, lanes] = dv[s].astype(BF16).T
+            dk_buf[u, of, :] = dk[s].astype(BF16).T
+            dv_buf[u, of, :] = dv[s].astype(BF16).T
         copies += [
-            pltpu.make_async_copy(dk_buf.at[:, lanes], dk_hbm.at[r, :, lanes], sems.at[2 * h]),
-            pltpu.make_async_copy(dv_buf.at[:, lanes], dv_hbm.at[r, :, lanes], sems.at[2 * h + 1]),
+            pltpu.make_async_copy(dk_buf.at[u], dk_hbm.at[r, :, lanes], sems.at[2 * u]),
+            pltpu.make_async_copy(dv_buf.at[u], dv_hbm.at[r, :, lanes], sems.at[2 * u + 1]),
         ]
         copies[-2].start()
         copies[-1].start()
@@ -290,7 +292,7 @@
         copy.wait()
 
 
-def last_kernel(n, count, cols_ref, q_ref, c_ref, po_ref, pdq_ref, keys_ref, values_ref, later_ref, *refs):
+def last_kernel(n, count, cols_ref, q_ref, grad_ref, po_ref, pdq_ref, keys_ref, values_ref, later_ref, *refs):
     got, refs = refs[:n], refs[n + 1 :]
     out_hbm, dq_hbm, dk_hbm, dv_hbm, start, out_buf, dq_buf, dk_buf, dv_buf, sems = refs
     part = DH // n
@@ -323,15 +325,12 @@
     for r in range(count):
         for t in range(0, slots, HALF):
             at = slice(t, t + HALF)
-            live = cols_ref[at, 8 * r + 4 : 8 * r + 5]
-            opened = cols_ref[at, 8 * r + 5 : 8 * r + 6]
-            grad_out = (c_ref[r, at, :].astype(F32) * live).astype(BF16)
             x = mm(q_ref[r, at, :], start[r])
-            y = mm_nt(grad_out, start[r])
+            y = mm_nt(grad_ref[r, at, :], start[r])
             for h in range(H):
                 lanes = slice(h * DH, (h + 1) * DH)
                 carried = cols_ref[at, 8 * r + 2 + h : 8 * r + 3 + h]
-                out_buf[r, at, lanes] = (opened * (po_ref[r, at, lanes] + carried * x[:, lanes])).astype(BF16)
+                out_buf[r, at, lanes] = (po_ref[r, at, lanes] + carried * x[:, lanes]).astype(BF16)
                 dq_buf[r, at, lanes] = (pdq_ref[r, at, lanes] + carried * y[:, lanes]).astype(BF16)
             send(out_buf.at[r, at], out_hbm.at[r, at])
             send(dq_buf.at[r, at], dq_hbm.at[r, at])
@@ -341,8 +340,10 @@
 
 def exchange(xs, axis):
     n = lax.axis_size(axis)
-    moved = [lax.ppermute(xs[k], axis, [(s, s ^ k) for s in range(n)]) for k in range(1, n)]
-    return [xs[0]] + moved
+    got = [xs[0]] + [None] * (n - 1)
+    for k in sorted(range(1, n), key=lambda k: -k.bit_count()):
+        got[k] = lax.ppermute(xs[k], axis, [(s, s ^ k) for s in range(n)])
+    return got
 
 
 def shards(
@@ -371,7 +372,7 @@
         out_shape=[shape((block * (1 + responses) + 16, DH), BF16)] * n
         + [shape((slots, 128), F32), shape((responses, 8, slots), F32)]
         + [shape(queries.shape, BF16)] * 4,
-        in_specs=[SMEM] * 3 + [ANY] * 9,
+        in_specs=[ANY] * 12,
         out_specs=[VMEM] * (n + 6),
         scratch_shapes=[
             pltpu.VMEM(keys.shape, BF16),
@@ -379,8 +380,11 @@
             pltpu.VMEM(prompt_gates.shape, F32),
             pltpu.VMEM(resp_gates.shape, F32),
             pltpu.VMEM(loss_mask.shape, jnp.int32),
+            pltpu.SMEM(group_ids.shape, jnp.int32),
+            pltpu.SMEM(resp_lengths.shape, jnp.int32),
+            pltpu.SMEM(advantages.shape, jnp.int32),
             pltpu.VMEM((H * (1 + responses), DH, DH), F32),
-            pltpu.SemaphoreType.DMA((7 + 2 * responses,)),
+            pltpu.SemaphoreType.DMA((10 + 2 * responses,)),
         ],
         compiler_params=params(32),
         name="first",
@@ -393,25 +397,26 @@
     like = shape(queries.shape, F32)
     like_out = shape(queries.shape, BF16)
 
-    def sweep(r, before, token):
+    def sweep(units, before, token):
         outs = pl.pallas_call(
-            lambda *refs: sweep_kernel(r, *refs),
-            out_shape=[like, like, like_out, like_out, shape((8, 128), F32)],
+            lambda *refs: sweep_kernel(units, *refs),
+            out_shape=[like, like, like_out, like_out, like_out, shape((8, 128), F32)],
             in_specs=[VMEM] * 6 + [ANY] * (1 + len(before)),
-            out_specs=[VMEM, VMEM, ANY, ANY, VMEM],
+            out_specs=[VMEM, VMEM, VMEM, ANY, ANY, VMEM],
             scratch_shapes=[
-                pltpu.VMEM((slots, width), BF16),
-                pltpu.VMEM((slots, width), BF16),
-                pltpu.SemaphoreType.DMA((2 * H,)),
+                pltpu.VMEM((len(units), slots, DH), BF16),
+                pltpu.VMEM((len(units), slots, DH), BF16),
+                pltpu.SemaphoreType.DMA((2 * len(units),)),
             ],
             input_output_aliases={7 + k: k for k in range(len(before))},
             compiler_params=params(),
             name="sweep",
         )(cols, rows, queries, resp_keys, resp_values, cotangent, token, *before)
-        return outs[:4], outs[4]
-
+        return outs[:5], outs[5]
+
+    units = [(r, h) for r in range(responses) for h in range(H)]
     got1 = exchange(msgs, "prompt")
-    held, token = sweep(0, [], cols)
+    held, token = sweep(units[:3], [], cols)
     outs = pl.pallas_call(
         lambda *refs: second_kernel(n, chips, cores, *refs),
         out_shape=[shape(((1 + cores) * block, DH), BF16)] * chips + [shape((8, DH), F32)],
@@ -423,7 +428,7 @@
     )(*got1, token)
     msgs, later = outs[:chips], outs[chips]
     got2 = exchange(msgs, "z")
-    held, token = sweep(1, held, later)
+    held, token = sweep(units[3:6], held, later)
     sent, kept = pl.pallas_call(
         lambda *refs: swap_kernel(chips, *refs),
         out_shape=[shape(((chips + 1) * block, DH), BF16)] * 2,
@@ -433,18 +438,17 @@
         name="swap",
     )(*got2, token)
     swapped = exchange([kept, sent], "core")[1]
-    held, token = sweep(2, held, kept)
     msgs = pl.pallas_call(
         lambda *refs: third_kernel(n, chips, *refs),
         out_shape=[shape(((responses + 1) * block, DH), BF16)] * n,
-        in_specs=[VMEM] * (n + 2) + [ANY],
+        in_specs=[VMEM] * (n + 2),
         out_specs=[VMEM] * n,
         compiler_params=params(),
         name="third",
-    )(*got1, kept, swapped, token)
+    )(*got1, kept, swapped)
     got3 = exchange(msgs, "prompt")
-    held, token = sweep(3, held, msgs[0])
-    partial_out, partial_dq, resp_dk, resp_dv = held
+    held, token = sweep(units[6:], held, msgs[0])
+    partial_out, partial_dq, grad_out, resp_dk, resp_dv = held
 
     resp_out, resp_dq, prompt_dk, prompt_dv = pl.pallas_call(
         lambda *refs: last_kernel(n, responses, *refs),
@@ -461,7 +465,7 @@
         ],
         compiler_params=params(),
         name="last",
-    )(cols, queries, cotangent, partial_out, partial_dq, keys, values, later, *got3, token)
+    )(cols, queries, grad_out, partial_out, partial_dq, keys, values, later, *got3, token)
     return (resp_out, resp_dq, resp_dk, resp_dv, prompt_dk, prompt_dv)
 
 

time: 37.2 us -> 34.8 us (0.935)
  Pallas kernels: 16.7 us -> 14.8 us
  waiting for transfers between devices: 6.95 us -> 6.47 us
    pallas_call x4 -> x3, Pallas kernels: 9.88 us -> 9.07 us  [sweep(): pl.pallas_call(lambda *refs: sweep_kernel(units, *refs), out_shape=[like,...]
    pallas_call x1, Pallas kernels: 3.81 us -> 3.22 us  [shards(): pl.pallas_call(lambda *refs: first_kernel(n, *refs), out_shape=[shape((bl...]
    ppermute x10, waiting for transfers between devices: 6.95 us -> 6.47 us  [exchange(): got[k] = lax.ppermute(xs[k], axis, [(s, s ^ k) for s in range(n)])]
    pallas_call x1, Pallas kernels: 2.48 us -> 2 us  [shards(): pl.pallas_call(lambda *refs: last_kernel(n, responses, *refs), out_shape=...]
  transfers between devices with their start and end apart: 10 -> 10, of which waited for: 5 -> 5; matrix products, arithmetic and copies ran while one was open for 0% -> 0% of each run, Pallas kernels for 27% -> 26%
where the time goes in v2:
time: 34.8 us; the launch traced here: 34.6 us
  Pallas kernels  14.8 us (43%)
  starting transfers between devices  12.6 us (36%)
  waiting for transfers between devices  6.47 us (19%)
  between operations  0.74 us (2%)
    ppermute x10, starting transfers between devices, exchange(): got[k] = lax.ppermute(xs[k], axis, [(s, s ^ k) for s in range(n)])  12.6 us
    pallas_call x3, Pallas kernels, sweep(): pl.pallas_call(lambda *refs: sweep_kernel(units, *refs), out_shape=[like,...  9.07 us
    ppermute x10, waiting for transfers between devices, exchange(): got[k] = lax.ppermute(xs[k], axis, [(s, s ^ k) for s in range(n)])  6.47 us
    pallas_call x1, Pallas kernels, shards(): pl.pallas_call(lambda *refs: first_kernel(n, *refs), out_shape=[shape((bl...  3.22 us
    pallas_call x1, Pallas kernels, shards(): pl.pallas_call(lambda *refs: last_kernel(n, responses, *refs), out_shape=...  2 us
  transfers between devices with their start and end apart: 10, of which 5 were waited for; matrix products, arithmetic and copies ran while one was open for 0% of the time, Pallas kernels for 26%

profile of v2, /device:TPU:0, one launch (start us, length us, event | category | flops | bytes accessed | tf_op | source)
XLA Modules:
  0.0 34.6 jit_solution(17439128053916965608)
XLA Ops:
  0.6 3.2 %first.1 = (bf16[336,128]{1,0:T(8,128)(2,1)S(1)}, bf16[336,128]{1,0:T(8,128)(2,1)S(1)}, bf16[336,128]{1,0:T(8,128)(2,1)S(1)}, bf16[336,128]{1,0:T(8,128)(2,1)S(1...) custom-call(s32[4]{0:T(128)} %refs_0_.1, ...), custom_call_target="tpu_custom_call" | custom-call | tf_op jit(solution)/shard_map/first/pallas_call | solution.py:370
  3.9 3.0 %collective-permute-start = (bf16[336,128]{1,0:T(8,128)(2,1)S(1)}, bf16[336,128]{1,0:T(8,128)(2,1)S(1)}, u32[]{:S(2)}, u32[]{:S(2)}) collective-permute-start(bf16[336,128]{1,0:T(8,128)(2,1)S(1)} %get-tuple-element.56), channel_id=1, source_target_pairs={{0,8},{8,0},{16,24},{24,16},{1,9},{9,1},{17,25},{25,17},{2,10},{10... | collective-permute-start | bytes 258056 | tf_op jit(solution)/shard_map/ppermute | solution.py:345
  6.9 1.5 %collective-permute-start.1 = (bf16[336,128]{1,0:T(8,128)(2,1)S(1)}, bf16[336,128]{1,0:T(8,128)(2,1)S(1)}, u32[]{:S(2)}, u32[]{:S(2)}) collective-permute-start(bf16[336,128]{1,0:T(8,128)(2,1)S(1)} %get-tuple-element.57), channel_id=1, source_target_pairs={{0,16},{8,24},{16,0},{24,8},{1,17},{9,25},{17,1},{25,9},{2,18},{10... | collective-permute-start | bytes 258056 | tf_op jit(solution)/shard_map/ppermute | solution.py:345
  8.4 0.0 collective-permute-start.2
  8.4 3.3 %sweep.3 = (f32[4,512,256]{2,1,0:T(8,128)S(1)}, f32[4,512,256]{2,1,0:T(8,128)S(1)}, bf16[4,512,256]{2,1,0:T(8,128)(2,1)S(1)}, bf16[4,512,256]{2,1,0:T(8,128)(2,1...) custom-call(f32[512,128]{1,0:T(8,128)S(1)} %get-tuple-element.49.refs_0_.refs_6_, ...), custom_call_target="tpu_custom_call" | custom-call | tf_op jit(solution)/shard_map/sweep/pallas_call | solution.py:401
  11.7 0.0 collective-permute-done.refs_1_
  11.7 0.6 %collective-permute-done.1.refs_2_ = bf16[336,128]{1,0:T(8,128)(2,1)S(1)} collective-permute-done((bf16[336,128]{1,0:T(8,128)(2,1)S(1)}, bf16[336,128]{1,0:T(8,128)(2,1)S(1)}, u32[]{:S(2)}, u32[]{:S(2)}) %collective-permute-start.1) | collective-permute-done | bytes 86048 | tf_op jit(solution)/shard_map/ppermute | solution.py:345
  12.3 1.5 %collective-permute-done.2.refs_3_ = bf16[336,128]{1,0:T(8,128)(2,1)S(1)} collective-permute-done((bf16[336,128]{1,0:T(8,128)(2,1)S(1)}, bf16[336,128]{1,0:T(8,128)(2,1)S(1)}, u32[]{:S(2)}, u32[]{:S(2)}) %collective-permute-start.2) | collective-permute-done | bytes 86048 | tf_op jit(solution)/shard_map/ppermute | solution.py:345
  13.8 0.2 second.1
  14.0 1.6 %collective-permute-start.3 = (bf16[192,128]{1,0:T(8,128)(2,1)S(1)}, bf16[192,128]{1,0:T(8,128)(2,1)S(1)}, u32[]{:S(2)}, u32[]{:S(2)}) collective-permute-start(bf16[192,128]{1,0:T(8,128)(2,1)S(1)} %get-tuple-element.61), channel_id=1, source_target_pairs={{0,2},{2,0},{4,6},{6,4},{1,3},{3,1},{5,7},{7,5},{8,10},{10,8},{12,... | collective-permute-start | bytes 147464 | tf_op jit(solution)/shard_map/ppermute | solution.py:345
  15.7 2.6 %collective-permute-start.4 = (bf16[192,128]{1,0:T(8,128)(2,1)S(1)}, bf16[192,128]{1,0:T(8,128)(2,1)S(1)}, u32[]{:S(2)}, u32[]{:S(2)}) collective-permute-start(bf16[192,128]{1,0:T(8,128)(2,1)S(1)} %get-tuple-element.62), channel_id=1, source_target_pairs={{0,4},{2,6},{4,0},{6,2},{1,5},{3,7},{5,1},{7,3},{8,12},{10,14},{12... | collective-permute-start | bytes 147464 | tf_op jit(solution)/shard_map/ppermute | solution.py:345
  18.3 0.2 collective-permute-start.5
  18.5 3.3 %sweep.4 = (f32[4,512,256]{2,1,0:T(8,128)S(1)}, f32[4,512,256]{2,1,0:T(8,128)S(1)}, bf16[4,512,256]{2,1,0:T(8,128)(2,1)S(1)}, bf16[4,512,256]{2,1,0:T(8,128)(2,1...) custom-call(f32[512,128]{1,0:T(8,128)S(1)} %get-tuple-element.49.ref, ...), custom_call_target="tpu_custom_call", output_to_operand_aliasing={{0}: (7, {}), {1}: (8, {}), {2}: (9, {}), {3}: (10, {}), {4... | custom-call | tf_op jit(solution)/shard_map/sweep/pallas_call | solution.py:401
  21.8 0.0 collective-permute-done.3.refs_1_
  21.8 0.0 collective-permute-done.4.refs_2_
  21.8 2.3 %collective-permute-done.5.refs_3_ = bf16[192,128]{1,0:T(8,128)(2,1)S(1)} collective-permute-done((bf16[192,128]{1,0:T(8,128)(2,1)S(1)}, bf16[192,128]{1,0:T(8,128)(2,1)S(1)}, u32[]{:S(2)}, u32[]{:S(2)}) %collective-permute-start.5) | collective-permute-done | bytes 49184 | tf_op jit(solution)/shard_map/ppermute | solution.py:345
  24.2 0.1 collective-permute-start.6
  24.3 1.3 %collective-permute-done.6.refs_5_ = bf16[320,128]{1,0:T(8,128)(2,1)S(1)} collective-permute-done((bf16[320,128]{1,0:T(8,128)(2,1)S(1)}, bf16[320,128]{1,0:T(8,128)(2,1)S(1)}, u32[]{:S(2)}, u32[]{:S(2)}) %collective-permute-start.6) | collective-permute-done | bytes 81952 | tf_op jit(solution)/shard_map/ppermute | solution.py:345
  25.5 0.2 third.1
  25.8 0.6 %collective-permute-start.7 = (bf16[320,128]{1,0:T(8,128)(2,1)S(1)}, bf16[320,128]{1,0:T(8,128)(2,1)S(1)}, u32[]{:S(2)}, u32[]{:S(2)}) collective-permute-start(bf16[320,128]{1,0:T(8,128)(2,1)S(1)} %get-tuple-element.82), channel_id=1, source_target_pairs={{0,8},{8,0},{16,24},{24,16},{1,9},{9,1},{17,25},{25,17},{2,10},{10... | collective-permute-start | bytes 245768 | tf_op jit(solution)/shard_map/ppermute | solution.py:345
  26.4 0.9 %collective-permute-start.8 = (bf16[320,128]{1,0:T(8,128)(2,1)S(1)}, bf16[320,128]{1,0:T(8,128)(2,1)S(1)}, u32[]{:S(2)}, u32[]{:S(2)}) collective-permute-start(bf16[320,128]{1,0:T(8,128)(2,1)S(1)} %get-tuple-element.83), channel_id=1, source_target_pairs={{0,16},{8,24},{16,0},{24,8},{1,17},{9,25},{17,1},{25,9},{2,18},{10... | collective-permute-start | bytes 245768 | tf_op jit(solution)/shard_map/ppermute | solution.py:345
  27.3 2.0 %collective-permute-start.9 = (bf16[320,128]{1,0:T(8,128)(2,1)S(1)}, bf16[320,128]{1,0:T(8,128)(2,1)S(1)}, u32[]{:S(2)}, u32[]{:S(2)}) collective-permute-start(bf16[320,128]{1,0:T(8,128)(2,1)S(1)} %get-tuple-element.84), channel_id=1, source_target_pairs={{0,24},{8,16},{16,8},{24,0},{1,25},{9,17},{17,9},{25,1},{2,26},{10... | collective-permute-start | bytes 245768 | tf_op jit(solution)/shard_map/ppermute | solution.py:345
  29.3 0.0 copy-start
  29.3 0.0 copy-start.1
  29.3 2.5 %sweep.5 = (f32[4,512,256]{2,1,0:T(8,128)S(1)}, f32[4,512,256]{2,1,0:T(8,128)S(1)}, bf16[4,512,256]{2,1,0:T(8,128)(2,1)S(1)}, bf16[4,512,256]{2,1,0:T(8,128)(2,1...) custom-call(f32[512,128]{1,0:T(8,128)S(1)} %get-tuple-element.49.ref, ...), custom_call_target="tpu_custom_call", output_to_operand_aliasing={{0}: (7, {}), {1}: (8, {}), {2}: (9, {}), {3}: (10, {}), {4... | custom-call | tf_op jit(solution)/shard_map/sweep/pallas_call | solution.py:401
  31.8 0.0 collective-permute-done.7.refs_9_
  31.8 0.0 collective-permute-done.8.refs_10_
  31.8 0.8 %collective-permute-done.9.refs_11_ = bf16[320,128]{1,0:T(8,128)(2,1)S(1)} collective-permute-done((bf16[320,128]{1,0:T(8,128)(2,1)S(1)}, bf16[320,128]{1,0:T(8,128)(2,1)S(1)}, u32[]{:S(2)}, u32[]{:S(2)}) %collective-permute-start.9) | collective-permute-done | bytes 81952 | tf_op jit(solution)/shard_map/ppermute | solution.py:345
  32.6 0.0 copy-done
  32.6 0.0 copy-done.1
  32.6 2.0 %last.1 = (bf16[4,512,256]{2,1,0:T(8,128)(2,1)}, bf16[4,512,256]{2,1,0:T(8,128)(2,1)}, bf16[1,256,256]{2,1,0:T(8,128)(2,1)}, bf16[1,256,256]{2,1,0:T(8,128)(2,1)}) custom-call(f32[512,128]{1,0:T(8,128)S(1)} %get-tuple-element.49.refs_0_.refs_6_, bf16[4,512,256]{2,1,0:T(8,128)(2,1)S(1)} %get-tuple-element.50.refs_2_.refs_1_, ...), custom_call_target="tpu_custom_call" | custom-call | tf_op jit(solution)/shard_map/last/pallas_call | solution.py:453
  (1 shorter events, 0.0 us)
Async XLA Ops:
  3.9 7.9 %collective-permute-start = (bf16[336,128]{1,0:T(8,128)(2,1)S(1)}, bf16[336,128]{1,0:T(8,128)(2,1)S(1)}, u32[]{:S(2)}, u32[]{:S(2)}) collective-permute-start(bf16[336,128]{1,0:T(8,128)(2,1)S(1)} %get-tuple-element.56), channel_id=1, source_target_pairs={{0,8},{8,0},{16,24},{24,16},{1,9},{9,1},{17,25},{25,17},{2,10},{10... | collective-permute-start | bytes 258056 | tf_op jit(solution)/shard_map/ppermute | solution.py:345
  6.9 5.4 %collective-permute-start.1 = (bf16[336,128]{1,0:T(8,128)(2,1)S(1)}, bf16[336,128]{1,0:T(8,128)(2,1)S(1)}, u32[]{:S(2)}, u32[]{:S(2)}) collective-permute-start(bf16[336,128]{1,0:T(8,128)(2,1)S(1)} %get-tuple-element.57), channel_id=1, source_target_pairs={{0,16},{8,24},{16,0},{24,8},{1,17},{9,25},{17,1},{25,9},{2,18},{10... | collective-permute-start | bytes 258056 | tf_op jit(solution)/shard_map/ppermute | solution.py:345
  8.4 5.4 %collective-permute-start.2 = (bf16[336,128]{1,0:T(8,128)(2,1)S(1)}, bf16[336,128]{1,0:T(8,128)(2,1)S(1)}, u32[]{:S(2)}, u32[]{:S(2)}) collective-permute-start(bf16[336,128]{1,0:T(8,128)(2,1)S(1)} %get-tuple-element.58), channel_id=1, source_target_pairs={{0,24},{8,16},{16,8},{24,0},{1,25},{9,17},{17,9},{25,1},{2,26},{10... | collective-permute-start | bytes 258056 | tf_op jit(solution)/shard_map/ppermute | solution.py:345
  14.0 7.8 %collective-permute-start.3 = (bf16[192,128]{1,0:T(8,128)(2,1)S(1)}, bf16[192,128]{1,0:T(8,128)(2,1)S(1)}, u32[]{:S(2)}, u32[]{:S(2)}) collective-permute-start(bf16[192,128]{1,0:T(8,128)(2,1)S(1)} %get-tuple-element.61), channel_id=1, source_target_pairs={{0,2},{2,0},{4,6},{6,4},{1,3},{3,1},{5,7},{7,5},{8,10},{10,8},{12,... | collective-permute-start | bytes 147464 | tf_op jit(solution)/shard_map/ppermute | solution.py:345
  15.7 6.1 %collective-permute-start.4 = (bf16[192,128]{1,0:T(8,128)(2,1)S(1)}, bf16[192,128]{1,0:T(8,128)(2,1)S(1)}, u32[]{:S(2)}, u32[]{:S(2)}) collective-permute-start(bf16[192,128]{1,0:T(8,128)(2,1)S(1)} %get-tuple-element.62), channel_id=1, source_target_pairs={{0,4},{2,6},{4,0},{6,2},{1,5},{3,7},{5,1},{7,3},{8,12},{10,14},{12... | collective-permute-start | bytes 147464 | tf_op jit(solution)/shard_map/ppermute | solution.py:345
  18.3 5.9 %collective-permute-start.5 = (bf16[192,128]{1,0:T(8,128)(2,1)S(1)}, bf16[192,128]{1,0:T(8,128)(2,1)S(1)}, u32[]{:S(2)}, u32[]{:S(2)}) collective-permute-start(bf16[192,128]{1,0:T(8,128)(2,1)S(1)} %get-tuple-element.63), channel_id=1, source_target_pairs={{0,6},{2,4},{4,2},{6,0},{1,7},{3,5},{5,3},{7,1},{8,14},{10,12},{12... | collective-permute-start | bytes 147464 | tf_op jit(solution)/shard_map/ppermute | solution.py:345
  24.2 1.3 %collective-permute-start.6 = (bf16[320,128]{1,0:T(8,128)(2,1)S(1)}, bf16[320,128]{1,0:T(8,128)(2,1)S(1)}, u32[]{:S(2)}, u32[]{:S(2)}) collective-permute-start(bf16[320,128]{1,0:T(8,128)(2,1)S(1)} %get-tuple-element.72), channel_id=1, source_target_pairs={{0,1},{1,0},{2,3},{3,2},{4,5},{5,4},{6,7},{7,6},{8,9},{9,8},{10,11... | collective-permute-start | bytes 245768 | tf_op jit(solution)/shard_map/ppermute | solution.py:345
  25.8 6.0 %collective-permute-start.7 = (bf16[320,128]{1,0:T(8,128)(2,1)S(1)}, bf16[320,128]{1,0:T(8,128)(2,1)S(1)}, u32[]{:S(2)}, u32[]{:S(2)}) collective-permute-start(bf16[320,128]{1,0:T(8,128)(2,1)S(1)} %get-tuple-element.82), channel_id=1, source_target_pairs={{0,8},{8,0},{16,24},{24,16},{1,9},{9,1},{17,25},{25,17},{2,10},{10... | collective-permute-start | bytes 245768 | tf_op jit(solution)/shard_map/ppermute | solution.py:345
  26.4 5.5 %collective-permute-start.8 = (bf16[320,128]{1,0:T(8,128)(2,1)S(1)}, bf16[320,128]{1,0:T(8,128)(2,1)S(1)}, u32[]{:S(2)}, u32[]{:S(2)}) collective-permute-start(bf16[320,128]{1,0:T(8,128)(2,1)S(1)} %get-tuple-element.83), channel_id=1, source_target_pairs={{0,16},{8,24},{16,0},{24,8},{1,17},{9,25},{17,1},{25,9},{2,18},{10... | collective-permute-start | bytes 245768 | tf_op jit(solution)/shard_map/ppermute | solution.py:345
  27.3 5.3 %collective-permute-start.9 = (bf16[320,128]{1,0:T(8,128)(2,1)S(1)}, bf16[320,128]{1,0:T(8,128)(2,1)S(1)}, u32[]{:S(2)}, u32[]{:S(2)}) collective-permute-start(bf16[320,128]{1,0:T(8,128)(2,1)S(1)} %get-tuple-element.84), channel_id=1, source_target_pairs={{0,24},{8,16},{16,8},{24,0},{1,25},{9,17},{17,9},{25,1},{2,26},{10... | collective-permute-start | bytes 245768 | tf_op jit(solution)/shard_map/ppermute | solution.py:345
  29.3 3.3 %copy-start = (bf16[1,256,256]{2,1,0:T(8,128)(2,1)S(1)}, bf16[1,256,256]{2,1,0:T(8,128)(2,1)}, u32[]{:S(2)}) copy-start(bf16[1,256,256]{2,1,0:T(8,128)(2,1)} %refs_5_.3) | copy-start | bytes 393220
  29.3 3.3 %copy-start.1 = (bf16[1,256,256]{2,1,0:T(8,128)(2,1)S(1)}, bf16[1,256,256]{2,1,0:T(8,128)(2,1)}, u32[]{:S(2)}) copy-start(bf16[1,256,256]{2,1,0:T(8,128)(2,1)} %refs_6_.3) | copy-start | bytes 393220

commit v3 on v2

--- a/solution.py
+++ b/solution.py
@@ -150,7 +150,7 @@
 
 def second_kernel(n, chips, cores, *refs):
     row, z_at = lax.axis_index("prompt"), lax.axis_index("z")
-    got, msgs, later_ref, sums = refs[:n], refs[n + 1 : n + 1 + chips], refs[-2], refs[-1]
+    got, msgs, later_ref, sums = by_partner(refs[:n]), refs[n + 1 : n + 1 + chips], refs[-2], refs[-1]
     part = DH // n
     block = H * part
     responses = (got[0].shape[0] - block - 16) // block
@@ -182,7 +182,7 @@
 
 
 def swap_kernel(chips, *refs):
-    got, sent_ref, kept_ref = refs[:chips], refs[chips + 1], refs[chips + 2]
+    got, sent_ref, kept_ref = by_partner(refs[:chips]), refs[chips + 1], refs[chips + 2]
     block = got[0].shape[0] // 3
     totals = []
     for c in range(2):
@@ -201,7 +201,7 @@
 
 def third_kernel(n, chips, *refs):
     z_at, core = lax.axis_index("z"), lax.axis_index("core")
-    noted, kept_ref, got_ref, msgs = refs[:n], refs[n], refs[n + 1], refs[n + 2 :]
+    noted, kept_ref, got_ref, msgs = by_partner(refs[:n]), refs[n], refs[n + 1], refs[n + 3 :]
     block = H * DH // n
     responses = (noted[0].shape[0] - block - 16) // block
     total = kept_ref[chips * block :, :].astype(F32) + got_ref[chips * block :, :].astype(F32)
@@ -293,7 +293,7 @@
 
 
 def last_kernel(n, count, cols_ref, q_ref, grad_ref, po_ref, pdq_ref, keys_ref, values_ref, later_ref, *refs):
-    got, refs = refs[:n], refs[n + 1 :]
+    got, refs = by_partner(refs[:n]), refs[n + 1 :]
     out_hbm, dq_hbm, dk_hbm, dv_hbm, start, out_buf, dq_buf, dk_buf, dv_buf, sems = refs
     part = DH // n
     block = H * part
@@ -340,10 +340,11 @@
 
 def exchange(xs, axis):
     n = lax.axis_size(axis)
-    got = [xs[0]] + [None] * (n - 1)
-    for k in sorted(range(1, n), key=lambda k: -k.bit_count()):
-        got[k] = lax.ppermute(xs[k], axis, [(s, s ^ k) for s in range(n)])
-    return got
+    return [xs[0]] + [lax.ppermute(xs[k], axis, [(s, s ^ k) for s in range(n)]) for k in range(n - 1, 0, -1)]
+
+
+def by_partner(refs):
+    return [refs[0], *refs[:0:-1]]
 
 
 def shards(
@@ -416,7 +417,7 @@
 
     units = [(r, h) for r in range(responses) for h in range(H)]
     got1 = exchange(msgs, "prompt")
-    held, token = sweep(units[:3], [], cols)
+    held, token = sweep(units[:2], [], cols)
     outs = pl.pallas_call(
         lambda *refs: second_kernel(n, chips, cores, *refs),
         out_shape=[shape(((1 + cores) * block, DH), BF16)] * chips + [shape((8, DH), F32)],
@@ -428,7 +429,7 @@
     )(*got1, token)
     msgs, later = outs[:chips], outs[chips]
     got2 = exchange(msgs, "z")
-    held, token = sweep(units[3:6], held, later)
+    held, token = sweep(units[2:4], held, later)
     sent, kept = pl.pallas_call(
         lambda *refs: swap_kernel(chips, *refs),
         out_shape=[shape(((chips + 1) * block, DH), BF16)] * 2,
@@ -438,16 +439,17 @@
         name="swap",
     )(*got2, token)
     swapped = exchange([kept, sent], "core")[1]
+    held, token = sweep(units[4:5], held, kept)
     msgs = pl.pallas_call(
         lambda *refs: third_kernel(n, chips, *refs),
         out_shape=[shape(((responses + 1) * block, DH), BF16)] * n,
-        in_specs=[VMEM] * (n + 2),
+        in_specs=[VMEM] * (n + 2) + [ANY],
         out_specs=[VMEM] * n,
         compiler_params=params(),
         name="third",
-    )(*got1, kept, swapped)
+    )(*got1, kept, swapped, token)
     got3 = exchange(msgs, "prompt")
-    held, token = sweep(units[6:], held, msgs[0])
+    held, token = sweep(units[5:], held, msgs[0])
     partial_out, partial_dq, grad_out, resp_dk, resp_dv = held
 
     resp_out, resp_dq, prompt_dk, prompt_dv = pl.pallas_call(

time: 34.8 us -> 33.6 us (0.966)
  waiting for transfers between devices: 6.47 us -> 4.38 us
  Pallas kernels: 14.8 us -> 15.6 us
    ppermute x10, waiting for transfers between devices: 6.47 us -> 4.38 us  [exchange(): lax.ppermute(xs[k], axis, [(s, s ^ k) for s in range(n)])]
    pallas_call x3 -> x4, Pallas kernels: 9.07 us -> 9.89 us  [sweep(): pl.pallas_call(lambda *refs: sweep_kernel(units, *refs), out_shape=[like,...]
  transfers between devices with their start and end apart: 10 -> 10, of which waited for: 5 -> 5; matrix products, arithmetic and copies ran while one was open for 0% -> 0% of each run, Pallas kernels for 26% -> 30%
where the time goes in v3:
time: 33.6 us; the launch traced here: 33.4 us
  Pallas kernels  15.6 us (46%)
  starting transfers between devices  12.7 us (38%)
  waiting for transfers between devices  4.38 us (13%)
  between operations  0.74 us (2%)
    ppermute x10, starting transfers between devices, exchange(): lax.ppermute(xs[k], axis, [(s, s ^ k) for s in range(n)])  12.7 us
    pallas_call x4, Pallas kernels, sweep(): pl.pallas_call(lambda *refs: sweep_kernel(units, *refs), out_shape=[like,...  9.89 us
    ppermute x10, waiting for transfers between devices, exchange(): lax.ppermute(xs[k], axis, [(s, s ^ k) for s in range(n)])  4.38 us
    pallas_call x1, Pallas kernels, shards(): pl.pallas_call(lambda *refs: first_kernel(n, *refs), out_shape=[shape((bl...  3.22 us
    pallas_call x1, Pallas kernels, shards(): pl.pallas_call(lambda *refs: last_kernel(n, responses, *refs), out_shape=...  2 us
  transfers between devices with their start and end apart: 10, of which 5 were waited for; matrix products, arithmetic and copies ran while one was open for 0% of the time, Pallas kernels for 30%

profile of v3, /device:TPU:0, one launch (start us, length us, event | category | flops | bytes accessed | tf_op | source)
XLA Modules:
  0.0 33.4 jit_solution(8101263120230606555)
XLA Ops:
  0.6 3.2 %first.1 = (bf16[336,128]{1,0:T(8,128)(2,1)S(1)}, bf16[336,128]{1,0:T(8,128)(2,1)S(1)}, bf16[336,128]{1,0:T(8,128)(2,1)S(1)}, bf16[336,128]{1,0:T(8,128)(2,1)S(1...) custom-call(s32[4]{0:T(128)} %refs_0_.1, ...), custom_call_target="tpu_custom_call" | custom-call | tf_op jit(solution)/shard_map/first/pallas_call | solution.py:371
  3.9 4.0 %collective-permute-start = (bf16[336,128]{1,0:T(8,128)(2,1)S(1)}, bf16[336,128]{1,0:T(8,128)(2,1)S(1)}, u32[]{:S(2)}, u32[]{:S(2)}) collective-permute-start(bf16[336,128]{1,0:T(8,128)(2,1)S(1)} %get-tuple-element.62), channel_id=1, source_target_pairs={{0,24},{8,16},{16,8},{24,0},{1,25},{9,17},{17,9},{25,1},{2,26},{10... | collective-permute-start | bytes 258056 | tf_op jit(solution)/shard_map/ppermute | solution.py:343
  7.8 0.5 %collective-permute-start.1 = (bf16[336,128]{1,0:T(8,128)(2,1)S(1)}, bf16[336,128]{1,0:T(8,128)(2,1)S(1)}, u32[]{:S(2)}, u32[]{:S(2)}) collective-permute-start(bf16[336,128]{1,0:T(8,128)(2,1)S(1)} %get-tuple-element.63), channel_id=1, source_target_pairs={{0,16},{8,24},{16,0},{24,8},{1,17},{9,25},{17,1},{25,9},{2,18},{10... | collective-permute-start | bytes 258056 | tf_op jit(solution)/shard_map/ppermute | solution.py:343
  8.3 0.1 collective-permute-start.2
  8.5 2.5 %sweep.4 = (f32[4,512,256]{2,1,0:T(8,128)S(1)}, f32[4,512,256]{2,1,0:T(8,128)S(1)}, bf16[4,512,256]{2,1,0:T(8,128)(2,1)S(1)}, bf16[4,512,256]{2,1,0:T(8,128)(2,1...) custom-call(f32[512,128]{1,0:T(8,128)S(1)} %get-tuple-element.55.refs_0_.refs_6_, ...), custom_call_target="tpu_custom_call" | custom-call | tf_op jit(solution)/shard_map/sweep/pallas_call | solution.py:402
  11.0 0.0 collective-permute-done.refs_1_
  11.0 1.4 %collective-permute-done.1.refs_2_ = bf16[336,128]{1,0:T(8,128)(2,1)S(1)} collective-permute-done((bf16[336,128]{1,0:T(8,128)(2,1)S(1)}, bf16[336,128]{1,0:T(8,128)(2,1)S(1)}, u32[]{:S(2)}, u32[]{:S(2)}) %collective-permute-start.1) | collective-permute-done | bytes 86048 | tf_op jit(solution)/shard_map/ppermute | solution.py:343
  12.3 0.5 %collective-permute-done.2.refs_3_ = bf16[336,128]{1,0:T(8,128)(2,1)S(1)} collective-permute-done((bf16[336,128]{1,0:T(8,128)(2,1)S(1)}, bf16[336,128]{1,0:T(8,128)(2,1)S(1)}, u32[]{:S(2)}, u32[]{:S(2)}) %collective-permute-start.2) | collective-permute-done | bytes 86048 | tf_op jit(solution)/shard_map/ppermute | solution.py:343
  12.8 0.2 second.1
  13.1 3.7 %collective-permute-start.3 = (bf16[192,128]{1,0:T(8,128)(2,1)S(1)}, bf16[192,128]{1,0:T(8,128)(2,1)S(1)}, u32[]{:S(2)}, u32[]{:S(2)}) collective-permute-start(bf16[192,128]{1,0:T(8,128)(2,1)S(1)} %get-tuple-element.67), channel_id=1, source_target_pairs={{0,6},{2,4},{4,2},{6,0},{1,7},{3,5},{5,3},{7,1},{8,14},{10,12},{12... | collective-permute-start | bytes 147464 | tf_op jit(solution)/shard_map/ppermute | solution.py:343
  16.7 0.0 collective-permute-start.4
  16.7 0.8 %collective-permute-start.5 = (bf16[192,128]{1,0:T(8,128)(2,1)S(1)}, bf16[192,128]{1,0:T(8,128)(2,1)S(1)}, u32[]{:S(2)}, u32[]{:S(2)}) collective-permute-start(bf16[192,128]{1,0:T(8,128)(2,1)S(1)} %get-tuple-element.69), channel_id=1, source_target_pairs={{0,2},{2,0},{4,6},{6,4},{1,3},{3,1},{5,7},{7,5},{8,10},{10,8},{12,... | collective-permute-start | bytes 147464 | tf_op jit(solution)/shard_map/ppermute | solution.py:343
  17.5 2.5 %sweep.5 = (f32[4,512,256]{2,1,0:T(8,128)S(1)}, f32[4,512,256]{2,1,0:T(8,128)S(1)}, bf16[4,512,256]{2,1,0:T(8,128)(2,1)S(1)}, bf16[4,512,256]{2,1,0:T(8,128)(2,1...) custom-call(f32[512,128]{1,0:T(8,128)S(1)} %get-tuple-element.55.ref, ...), custom_call_target="tpu_custom_call", output_to_operand_aliasing={{0}: (7, {}), {1}: (8, {}), {2}: (9, {}), {3}: (10, {}), {4... | custom-call | tf_op jit(solution)/shard_map/sweep/pallas_call | solution.py:402
  20.0 0.0 collective-permute-done.3.refs_1_
  20.0 1.7 %collective-permute-done.4.refs_2_ = bf16[192,128]{1,0:T(8,128)(2,1)S(1)} collective-permute-done((bf16[192,128]{1,0:T(8,128)(2,1)S(1)}, bf16[192,128]{1,0:T(8,128)(2,1)S(1)}, u32[]{:S(2)}, u32[]{:S(2)}) %collective-permute-start.4) | collective-permute-done | bytes 49184 | tf_op jit(solution)/shard_map/ppermute | solution.py:343
  21.7 0.0 collective-permute-done.5.refs_3_
  21.8 0.1 collective-permute-start.6
  21.9 1.7 %sweep.6 = (f32[4,512,256]{2,1,0:T(8,128)S(1)}, f32[4,512,256]{2,1,0:T(8,128)S(1)}, bf16[4,512,256]{2,1,0:T(8,128)(2,1)S(1)}, bf16[4,512,256]{2,1,0:T(8,128)(2,1...) custom-call(f32[512,128]{1,0:T(8,128)S(1)} %get-tuple-element.55.ref, ...), custom_call_target="tpu_custom_call", output_to_operand_aliasing={{0}: (7, {}), {1}: (8, {}), {2}: (9, {}), {3}: (10, {}), {4... | custom-call | tf_op jit(solution)/shard_map/sweep/pallas_call | solution.py:402
  23.5 0.0 collective-permute-done.6.refs_5_
  23.5 0.2 third.1
  23.8 1.6 %collective-permute-start.7 = (bf16[320,128]{1,0:T(8,128)(2,1)S(1)}, bf16[320,128]{1,0:T(8,128)(2,1)S(1)}, u32[]{:S(2)}, u32[]{:S(2)}) collective-permute-start(bf16[320,128]{1,0:T(8,128)(2,1)S(1)} %get-tuple-element.94), channel_id=1, source_target_pairs={{0,24},{8,16},{16,8},{24,0},{1,25},{9,17},{17,9},{25,1},{2,26},{10... | collective-permute-start | bytes 245768 | tf_op jit(solution)/shard_map/ppermute | solution.py:343
  25.3 1.1 %collective-permute-start.8 = (bf16[320,128]{1,0:T(8,128)(2,1)S(1)}, bf16[320,128]{1,0:T(8,128)(2,1)S(1)}, u32[]{:S(2)}, u32[]{:S(2)}) collective-permute-start(bf16[320,128]{1,0:T(8,128)(2,1)S(1)} %get-tuple-element.95), channel_id=1, source_target_pairs={{0,16},{8,24},{16,0},{24,8},{1,17},{9,25},{17,1},{25,9},{2,18},{10... | collective-permute-start | bytes 245768 | tf_op jit(solution)/shard_map/ppermute | solution.py:343
  26.4 0.9 %collective-permute-start.9 = (bf16[320,128]{1,0:T(8,128)(2,1)S(1)}, bf16[320,128]{1,0:T(8,128)(2,1)S(1)}, u32[]{:S(2)}, u32[]{:S(2)}) collective-permute-start(bf16[320,128]{1,0:T(8,128)(2,1)S(1)} %get-tuple-element.96), channel_id=1, source_target_pairs={{0,8},{8,0},{16,24},{24,16},{1,9},{9,1},{17,25},{25,17},{2,10},{10... | collective-permute-start | bytes 245768 | tf_op jit(solution)/shard_map/ppermute | solution.py:343
  27.3 0.0 copy-start
  27.3 0.0 copy-start.1
  27.3 3.3 %sweep.7 = (f32[4,512,256]{2,1,0:T(8,128)S(1)}, f32[4,512,256]{2,1,0:T(8,128)S(1)}, bf16[4,512,256]{2,1,0:T(8,128)(2,1)S(1)}, bf16[4,512,256]{2,1,0:T(8,128)(2,1...) custom-call(f32[512,128]{1,0:T(8,128)S(1)} %get-tuple-element.55.ref, ...), custom_call_target="tpu_custom_call", output_to_operand_aliasing={{0}: (7, {}), {1}: (8, {}), {2}: (9, {}), {3}: (10, {}), {4... | custom-call | tf_op jit(solution)/shard_map/sweep/pallas_call | solution.py:402
  30.6 0.0 collective-permute-done.7.refs_9_
  30.6 0.7 %collective-permute-done.8.refs_10_ = bf16[320,128]{1,0:T(8,128)(2,1)S(1)} collective-permute-done((bf16[320,128]{1,0:T(8,128)(2,1)S(1)}, bf16[320,128]{1,0:T(8,128)(2,1)S(1)}, u32[]{:S(2)}, u32[]{:S(2)}) %collective-permute-start.8) | collective-permute-done | bytes 81952 | tf_op jit(solution)/shard_map/ppermute | solution.py:343
  31.3 0.1 collective-permute-done.9.refs_11_
  31.4 0.0 copy-done
  31.4 0.0 copy-done.1
  31.4 2.0 %last.1 = (bf16[4,512,256]{2,1,0:T(8,128)(2,1)}, bf16[4,512,256]{2,1,0:T(8,128)(2,1)}, bf16[1,256,256]{2,1,0:T(8,128)(2,1)}, bf16[1,256,256]{2,1,0:T(8,128)(2,1)}) custom-call(f32[512,128]{1,0:T(8,128)S(1)} %get-tuple-element.55.refs_0_.refs_6_, bf16[4,512,256]{2,1,0:T(8,128)(2,1)S(1)} %get-tuple-element.56.refs_2_.refs_1_, ...), custom_call_target="tpu_custom_call" | custom-call | tf_op jit(solution)/shard_map/last/pallas_call | solution.py:455
  (1 shorter events, 0.0 us)
Async XLA Ops:
  3.9 7.1 %collective-permute-start = (bf16[336,128]{1,0:T(8,128)(2,1)S(1)}, bf16[336,128]{1,0:T(8,128)(2,1)S(1)}, u32[]{:S(2)}, u32[]{:S(2)}) collective-permute-start(bf16[336,128]{1,0:T(8,128)(2,1)S(1)} %get-tuple-element.62), channel_id=1, source_target_pairs={{0,24},{8,16},{16,8},{24,0},{1,25},{9,17},{17,9},{25,1},{2,26},{10... | collective-permute-start | bytes 258056 | tf_op jit(solution)/shard_map/ppermute | solution.py:343
  7.8 4.5 %collective-permute-start.1 = (bf16[336,128]{1,0:T(8,128)(2,1)S(1)}, bf16[336,128]{1,0:T(8,128)(2,1)S(1)}, u32[]{:S(2)}, u32[]{:S(2)}) collective-permute-start(bf16[336,128]{1,0:T(8,128)(2,1)S(1)} %get-tuple-element.63), channel_id=1, source_target_pairs={{0,16},{8,24},{16,0},{24,8},{1,17},{9,25},{17,1},{25,9},{2,18},{10... | collective-permute-start | bytes 258056 | tf_op jit(solution)/shard_map/ppermute | solution.py:343
  8.3 4.5 %collective-permute-start.2 = (bf16[336,128]{1,0:T(8,128)(2,1)S(1)}, bf16[336,128]{1,0:T(8,128)(2,1)S(1)}, u32[]{:S(2)}, u32[]{:S(2)}) collective-permute-start(bf16[336,128]{1,0:T(8,128)(2,1)S(1)} %get-tuple-element.64), channel_id=1, source_target_pairs={{0,8},{8,0},{16,24},{24,16},{1,9},{9,1},{17,25},{25,17},{2,10},{10... | collective-permute-start | bytes 258056 | tf_op jit(solution)/shard_map/ppermute | solution.py:343
  13.1 6.9 %collective-permute-start.3 = (bf16[192,128]{1,0:T(8,128)(2,1)S(1)}, bf16[192,128]{1,0:T(8,128)(2,1)S(1)}, u32[]{:S(2)}, u32[]{:S(2)}) collective-permute-start(bf16[192,128]{1,0:T(8,128)(2,1)S(1)} %get-tuple-element.67), channel_id=1, source_target_pairs={{0,6},{2,4},{4,2},{6,0},{1,7},{3,5},{5,3},{7,1},{8,14},{10,12},{12... | collective-permute-start | bytes 147464 | tf_op jit(solution)/shard_map/ppermute | solution.py:343
  16.7 5.0 %collective-permute-start.4 = (bf16[192,128]{1,0:T(8,128)(2,1)S(1)}, bf16[192,128]{1,0:T(8,128)(2,1)S(1)}, u32[]{:S(2)}, u32[]{:S(2)}) collective-permute-start(bf16[192,128]{1,0:T(8,128)(2,1)S(1)} %get-tuple-element.68), channel_id=1, source_target_pairs={{0,4},{2,6},{4,0},{6,2},{1,5},{3,7},{5,1},{7,3},{8,12},{10,14},{12... | collective-permute-start | bytes 147464 | tf_op jit(solution)/shard_map/ppermute | solution.py:343
  16.7 5.0 %collective-permute-start.5 = (bf16[192,128]{1,0:T(8,128)(2,1)S(1)}, bf16[192,128]{1,0:T(8,128)(2,1)S(1)}, u32[]{:S(2)}, u32[]{:S(2)}) collective-permute-start(bf16[192,128]{1,0:T(8,128)(2,1)S(1)} %get-tuple-element.69), channel_id=1, source_target_pairs={{0,2},{2,0},{4,6},{6,4},{1,3},{3,1},{5,7},{7,5},{8,10},{10,8},{12,... | collective-permute-start | bytes 147464 | tf_op jit(solution)/shard_map/ppermute | solution.py:343
  21.8 1.7 %collective-permute-start.6 = (bf16[320,128]{1,0:T(8,128)(2,1)S(1)}, bf16[320,128]{1,0:T(8,128)(2,1)S(1)}, u32[]{:S(2)}, u32[]{:S(2)}) collective-permute-start(bf16[320,128]{1,0:T(8,128)(2,1)S(1)} %get-tuple-element.78), channel_id=1, source_target_pairs={{0,1},{1,0},{2,3},{3,2},{4,5},{5,4},{6,7},{7,6},{8,9},{9,8},{10,11... | collective-permute-start | bytes 245768 | tf_op jit(solution)/shard_map/ppermute | solution.py:343
  23.8 6.9 %collective-permute-start.7 = (bf16[320,128]{1,0:T(8,128)(2,1)S(1)}, bf16[320,128]{1,0:T(8,128)(2,1)S(1)}, u32[]{:S(2)}, u32[]{:S(2)}) collective-permute-start(bf16[320,128]{1,0:T(8,128)(2,1)S(1)} %get-tuple-element.94), channel_id=1, source_target_pairs={{0,24},{8,16},{16,8},{24,0},{1,25},{9,17},{17,9},{25,1},{2,26},{10... | collective-permute-start | bytes 245768 | tf_op jit(solution)/shard_map/ppermute | solution.py:343
  25.3 6.0 %collective-permute-start.8 = (bf16[320,128]{1,0:T(8,128)(2,1)S(1)}, bf16[320,128]{1,0:T(8,128)(2,1)S(1)}, u32[]{:S(2)}, u32[]{:S(2)}) collective-permute-start(bf16[320,128]{1,0:T(8,128)(2,1)S(1)} %get-tuple-element.95), channel_id=1, source_target_pairs={{0,16},{8,24},{16,0},{24,8},{1,17},{9,25},{17,1},{25,9},{2,18},{10... | collective-permute-start | bytes 245768 | tf_op jit(solution)/shard_map/ppermute | solution.py:343
  26.4 5.0 %collective-permute-start.9 = (bf16[320,128]{1,0:T(8,128)(2,1)S(1)}, bf16[320,128]{1,0:T(8,128)(2,1)S(1)}, u32[]{:S(2)}, u32[]{:S(2)}) collective-permute-start(bf16[320,128]{1,0:T(8,128)(2,1)S(1)} %get-tuple-element.96), channel_id=1, source_target_pairs={{0,8},{8,0},{16,24},{24,16},{1,9},{9,1},{17,25},{25,17},{2,10},{10... | collective-permute-start | bytes 245768 | tf_op jit(solution)/shard_map/ppermute | solution.py:343
  27.3 4.1 %copy-start = (bf16[1,256,256]{2,1,0:T(8,128)(2,1)S(1)}, bf16[1,256,256]{2,1,0:T(8,128)(2,1)}, u32[]{:S(2)}) copy-start(bf16[1,256,256]{2,1,0:T(8,128)(2,1)} %refs_5_.3) | copy-start | bytes 393220
  27.3 4.1 %copy-start.1 = (bf16[1,256,256]{2,1,0:T(8,128)(2,1)S(1)}, bf16[1,256,256]{2,1,0:T(8,128)(2,1)}, u32[]{:S(2)}) copy-start(bf16[1,256,256]{2,1,0:T(8,128)(2,1)} %refs_6_.3) | copy-start | bytes 393220

commit v4 on v3

--- a/solution.py
+++ b/solution.py
@@ -80,8 +80,7 @@
         copy.start()
     part = DH // n
     block = H * part
-    me = lax.axis_index("prompt")
-    targets = [lax.bitwise_xor(me, k) for k in range(n)]
+    targets = partners(n)
 
     def spread(at):
         for k in range(n):
@@ -149,12 +148,12 @@
 
 
 def second_kernel(n, chips, cores, *refs):
-    row, z_at = lax.axis_index("prompt"), lax.axis_index("z")
-    got, msgs, later_ref, sums = by_partner(refs[:n]), refs[n + 1 : n + 1 + chips], refs[-2], refs[-1]
+    z_at = lax.axis_index("z")
+    got, msgs, later_ref, sums = refs[:n], refs[n + 1 : n + 1 + chips], refs[-2], refs[-1]
     part = DH // n
     block = H * part
     responses = (got[0].shape[0] - block - 16) // block
-    place = [lax.bitwise_xor(row, k) for k in range(n)]
+    place = partners(n)
     notes = [got[k][block : block + 16, :].astype(F32) for k in range(n)]
     logs = [x[0:H] + x[H : 2 * H] + x[2 * H : 3 * H] for x in notes]
     final = jnp.zeros((block, DH), F32)
@@ -201,7 +200,7 @@
 
 def third_kernel(n, chips, *refs):
     z_at, core = lax.axis_index("z"), lax.axis_index("core")
-    noted, kept_ref, got_ref, msgs = by_partner(refs[:n]), refs[n], refs[n + 1], refs[n + 3 :]
+    noted, kept_ref, got_ref, msgs = refs[:n], refs[n], refs[n + 1], refs[n + 3 :]
     block = H * DH // n
     responses = (noted[0].shape[0] - block - 16) // block
     total = kept_ref[chips * block :, :].astype(F32) + got_ref[chips * block :, :].astype(F32)
@@ -219,7 +218,7 @@
 
 
 def sweep_kernel(units, cols_ref, rows_ref, q_ref, k_ref, v_ref, c_ref, *refs):
-    out_ref, dq_ref, grad_ref, dk_hbm, dv_hbm, token_ref, dk_buf, dv_buf, sems = refs[-9:]
+    out_ref, dq_ref, grad_ref, dk_ref, dv_ref, token_ref = refs[-6:]
     token_ref[...] = jnp.zeros_like(token_ref)
     quarter = HALF // 2
     causal = lax.broadcasted_iota(jnp.int32, (quarter, quarter), 0) >= lax.broadcasted_iota(
@@ -227,7 +226,6 @@
     )
     blank = jnp.zeros((quarter, quarter), BF16)
     blocks = q_ref.shape[1] // HALF
-    copies = []
 
     def decayed(products, cum, row, diagonal):
         if not diagonal:
@@ -243,7 +241,7 @@
             results.append(jnp.concatenate([upper, jnp.concatenate(lower, axis=1)], axis=0))
         return results
 
-    for u, (r, h) in enumerate(units):
+    for r, h in units:
         lanes = slice(h * DH, (h + 1) * DH)
         cum = cols_ref[:, 8 * r + h : 8 * r + h + 1] * LOG2E
         row = rows_ref[r, h : h + 1, :] * LOG2E
@@ -280,24 +278,18 @@
             dq_ref[r, at, lanes] = dq
         for s in range(blocks):
             of = slice(s * HALF, (s + 1) * HALF)
-            dk_buf[u, of, :] = dk[s].astype(BF16).T
-            dv_buf[u, of, :] = dv[s].astype(BF16).T
-        copies += [
-            pltpu.make_async_copy(dk_buf.at[u], dk_hbm.at[r, :, lanes], sems.at[2 * u]),
-            pltpu.make_async_copy(dv_buf.at[u], dv_hbm.at[r, :, lanes], sems.at[2 * u + 1]),
-        ]
-        copies[-2].start()
-        copies[-1].start()
-    for copy in copies:
-        copy.wait()
-
-
-def last_kernel(n, count, cols_ref, q_ref, grad_ref, po_ref, pdq_ref, keys_ref, values_ref, later_ref, *refs):
-    got, refs = by_partner(refs[:n]), refs[n + 1 :]
-    out_hbm, dq_hbm, dk_hbm, dv_hbm, start, out_buf, dq_buf, dk_buf, dv_buf, sems = refs
+            dk_ref[r, of, lanes] = dk[s].astype(BF16).T
+            dv_ref[r, of, lanes] = dv[s].astype(BF16).T
+
+
+def last_kernel(
+    n, count, cols_ref, q_ref, grad_ref, po_ref, pdq_ref, rdk_ref, rdv_ref, keys_ref, values_ref, later_ref, *refs
+):
+    got, refs = refs[:n], refs[n + 1 :]
+    out_hbm, dq_hbm, rdk_hbm, rdv_hbm, dk_hbm, dv_hbm, start, out_buf, dq_buf, dk_buf, dv_buf, sems = refs
     part = DH // n
     block = H * part
-    row = lax.axis_index("prompt")
+    place = partners(n)
     slots = q_ref.shape[1]
     tokens = keys_ref.shape[1]
     copies = []
@@ -306,11 +298,13 @@
         copies.append(pltpu.make_async_copy(a, b, sems.at[len(copies)]))
         copies[-1].start()
 
+    send(rdk_ref, rdk_hbm)
+    send(rdv_ref, rdv_hbm)
     start[...] = jnp.zeros_like(start)
     for r in range(count + 1):
         for k in range(n):
             for h in range(H):
-                of = pl.ds(pl.multiple_of(h * DH + lax.bitwise_xor(row, k) * part, part), part)
+                of = pl.ds(pl.multiple_of(h * DH + place[k] * part, part), part)
                 rows = got[k][r * block + h * part : r * block + (h + 1) * part, :]
                 start[r, of, h * DH : (h + 1) * DH] = rows
     factor = [
@@ -336,6 +330,26 @@
             send(dq_buf.at[r, at], dq_hbm.at[r, at])
     for copy in copies:
         copy.wait()
+
+
+def steps(n):
+    first = list(range(n - 1, 0, -1))
+    return [0, *first], [0, *first[-1:], *first[:-1]]
+
+
+def partners(n):
+    me = lax.axis_index("prompt")
+    low = lax.axis_index("core") == 0
+    return [lax.bitwise_xor(me, jnp.where(low, a, b)) for a, b in zip(*steps(n))]
+
+
+def exchange_prompt(xs):
+    n = lax.axis_size("prompt")
+    got = [xs[0]]
+    for x, ks in zip(xs[1:], list(zip(*steps(n)))[1:]):
+        pairs = [(2 * s + c, 2 * (s ^ ks[c]) + c) for s in range(n) for c in range(2)]
+        got.append(lax.ppermute(x, ("prompt", "core"), pairs))
+    return got
 
 
 def exchange(xs, axis):
@@ -403,12 +417,7 @@
             lambda *refs: sweep_kernel(units, *refs),
             out_shape=[like, like, like_out, like_out, like_out, shape((8, 128), F32)],
             in_specs=[VMEM] * 6 + [ANY] * (1 + len(before)),
-            out_specs=[VMEM, VMEM, VMEM, ANY, ANY, VMEM],
-            scratch_shapes=[
-                pltpu.VMEM((len(units), slots, DH), BF16),
-                pltpu.VMEM((len(units), slots, DH), BF16),
-                pltpu.SemaphoreType.DMA((2 * len(units),)),
-            ],
+            out_specs=[VMEM] * 6,
             input_output_aliases={7 + k: k for k in range(len(before))},
             compiler_params=params(),
             name="sweep",
@@ -416,7 +425,7 @@
         return outs[:5], outs[5]
 
     units = [(r, h) for r in range(responses) for h in range(H)]
-    got1 = exchange(msgs, "prompt")
+    got1 = exchange_prompt(msgs)
     held, token = sweep(units[:2], [], cols)
     outs = pl.pallas_call(
         lambda *refs: second_kernel(n, chips, cores, *refs),
@@ -448,26 +457,26 @@
         compiler_params=params(),
         name="third",
     )(*got1, kept, swapped, token)
-    got3 = exchange(msgs, "prompt")
+    got3 = exchange_prompt(msgs)
     held, token = sweep(units[5:], held, msgs[0])
     partial_out, partial_dq, grad_out, resp_dk, resp_dv = held
 
-    resp_out, resp_dq, prompt_dk, prompt_dv = pl.pallas_call(
+    resp_out, resp_dq, resp_dk, resp_dv, prompt_dk, prompt_dv = pl.pallas_call(
         lambda *refs: last_kernel(n, responses, *refs),
-        out_shape=[like_out, like_out, shape(keys.shape, BF16), shape(keys.shape, BF16)],
-        in_specs=[VMEM] * (8 + n) + [ANY],
-        out_specs=[ANY] * 4,
+        out_shape=[like_out] * 4 + [shape(keys.shape, BF16)] * 2,
+        in_specs=[VMEM] * (10 + n) + [ANY],
+        out_specs=[ANY] * 6,
         scratch_shapes=[
             pltpu.VMEM((responses + 1, width, width), BF16),
             pltpu.VMEM(queries.shape, BF16),
             pltpu.VMEM(queries.shape, BF16),
             pltpu.VMEM(keys.shape[1:], BF16),
             pltpu.VMEM(keys.shape[1:], BF16),
-            pltpu.SemaphoreType.DMA((2 + 2 * responses * (slots // HALF),)),
+            pltpu.SemaphoreType.DMA((4 + 2 * responses * (slots // HALF),)),
         ],
         compiler_params=params(),
         name="last",
-    )(cols, queries, grad_out, partial_out, partial_dq, keys, values, later, *got3, token)
+    )(cols, queries, grad_out, partial_out, partial_dq, resp_dk, resp_dv, keys, values, later, *got3, token)
     return (resp_out, resp_dq, resp_dk, resp_dv, prompt_dk, prompt_dv)
 
 

time: 33.6 us -> 34.6 us (1.030)
  waiting for transfers between devices: 4.38 us -> 7.93 us
  Pallas kernels: 15.6 us -> 13 us
    ppermute x0 -> x6, starting transfers between devices: none -> 8.16 us  [exchange_prompt(): got.append(lax.ppermute(x, ('prompt', 'core'), pairs))]
    ppermute x10 -> x4, starting transfers between devices: 12.7 us -> 4.54 us  [exchange(): lax.ppermute(xs[k], axis, [(s, s ^ k) for s in range(n)])]
    ppermute x0 -> x6, waiting for transfers between devices: none -> 5.05 us  [exchange_prompt(): got.append(lax.ppermute(x, ('prompt', 'core'), pairs))]
    pallas_call x4, Pallas kernels: 9.89 us -> 7.02 us  [sweep(): pl.pallas_call(lambda *refs: sweep_kernel(units, *refs), out_shape=[like,...]
    ppermute x10 -> x4, waiting for transfers between devices: 4.38 us -> 2.88 us  [exchange(): lax.ppermute(xs[k], axis, [(s, s ^ k) for s in range(n)])]
  transfers between devices with their start and end apart: 10 -> 10, of which waited for: 5 -> 5; matrix products, arithmetic and copies ran while one was open for 0% -> 0% of each run, Pallas kernels for 30% -> 20%
where the time goes in v4:
time: 34.6 us; the launch traced here: 34.4 us
  Pallas kernels  13 us (38%)
  starting transfers between devices  12.7 us (37%)
  waiting for transfers between devices  7.93 us (23%)
  between operations  0.73 us (2%)
    ppermute x6, starting transfers between devices, exchange_prompt(): got.append(lax.ppermute(x, ('prompt', 'core'), pairs))  8.16 us
    pallas_call x4, Pallas kernels, sweep(): pl.pallas_call(lambda *refs: sweep_kernel(units, *refs), out_shape=[like,...  7.02 us
    ppermute x6, waiting for transfers between devices, exchange_prompt(): got.append(lax.ppermute(x, ('prompt', 'core'), pairs))  5.05 us
    ppermute x4, starting transfers between devices, exchange(): lax.ppermute(xs[k], axis, [(s, s ^ k) for s in range(n)])  4.54 us
    pallas_call x1, Pallas kernels, shards(): pl.pallas_call(lambda *refs: first_kernel(n, *refs), out_shape=[shape((bl...  3.23 us
    ppermute x4, waiting for transfers between devices, exchange(): lax.ppermute(xs[k], axis, [(s, s ^ k) for s in range(n)])  2.88 us
    pallas_call x1, Pallas kernels, shards(): pl.pallas_call(lambda *refs: last_kernel(n, responses, *refs), out_shape=...  2.28 us
  transfers between devices with their start and end apart: 10, of which 5 were waited for; matrix products, arithmetic and copies ran while one was open for 0% of the time, Pallas kernels for 20%

profile of v4, /device:TPU:0, one launch (start us, length us, event | category | flops | bytes accessed | tf_op | source)
XLA Modules:
  0.0 34.4 jit_solution(15974957465121185132)
XLA Ops:
  0.6 3.2 %first.1 = (bf16[336,128]{1,0:T(8,128)(2,1)S(1)}, bf16[336,128]{1,0:T(8,128)(2,1)S(1)}, bf16[336,128]{1,0:T(8,128)(2,1)S(1)}, bf16[336,128]{1,0:T(8,128)(2,1)S(1...) custom-call(s32[4]{0:T(128)} %refs_0_.1, ...), custom_call_target="tpu_custom_call" | custom-call | tf_op jit(solution)/shard_map/first/pallas_call | solution.py:385
  3.9 4.0 %collective-permute-start = (bf16[336,128]{1,0:T(8,128)(2,1)S(1)}, bf16[336,128]{1,0:T(8,128)(2,1)S(1)}, u32[]{:S(2)}, u32[]{:S(2)}) collective-permute-start(bf16[336,128]{1,0:T(8,128)(2,1)S(1)} %get-tuple-element.58), channel_id=1, source_target_pairs={{0,24},{1,9},{8,16},{9,1},{16,8},{17,25},{24,0},{25,17},{2,26},{3,... | collective-permute-start | bytes 258056 | tf_op jit(solution)/shard_map/ppermute | solution.py:351
  7.8 0.5 %collective-permute-start.1 = (bf16[336,128]{1,0:T(8,128)(2,1)S(1)}, bf16[336,128]{1,0:T(8,128)(2,1)S(1)}, u32[]{:S(2)}, u32[]{:S(2)}) collective-permute-start(bf16[336,128]{1,0:T(8,128)(2,1)S(1)} %get-tuple-element.59), channel_id=1, source_target_pairs={{0,16},{1,25},{8,24},{9,17},{16,0},{17,9},{24,8},{25,1},{2,18},{3,... | collective-permute-start | bytes 258056 | tf_op jit(solution)/shard_map/ppermute | solution.py:351
  8.3 0.1 collective-permute-start.2
  8.5 1.7 %sweep.4 = (f32[4,512,256]{2,1,0:T(8,128)S(1)}, f32[4,512,256]{2,1,0:T(8,128)S(1)}, bf16[4,512,256]{2,1,0:T(8,128)(2,1)S(1)}, bf16[4,512,256]{2,1,0:T(8,128)(2,1...) custom-call(f32[512,128]{1,0:T(8,128)S(1)} %get-tuple-element.51.refs_0_.refs_6_, ...), custom_call_target="tpu_custom_call" | custom-call | tf_op jit(solution)/shard_map/sweep/pallas_call | solution.py:416
  10.2 1.0 %collective-permute-done.refs_1_ = bf16[336,128]{1,0:T(8,128)(2,1)S(1)} collective-permute-done((bf16[336,128]{1,0:T(8,128)(2,1)S(1)}, bf16[336,128]{1,0:T(8,128)(2,1)S(1)}, u32[]{:S(2)}, u32[]{:S(2)}) %collective-permute-start) | collective-permute-done | bytes 86048 | tf_op jit(solution)/shard_map/ppermute | solution.py:351
  11.3 2.1 %collective-permute-done.1.refs_2_ = bf16[336,128]{1,0:T(8,128)(2,1)S(1)} collective-permute-done((bf16[336,128]{1,0:T(8,128)(2,1)S(1)}, bf16[336,128]{1,0:T(8,128)(2,1)S(1)}, u32[]{:S(2)}, u32[]{:S(2)}) %collective-permute-start.1) | collective-permute-done | bytes 86048 | tf_op jit(solution)/shard_map/ppermute | solution.py:351
  13.4 0.0 collective-permute-done.2.refs_3_
  13.4 0.2 second.1
  13.6 3.8 %collective-permute-start.3 = (bf16[192,128]{1,0:T(8,128)(2,1)S(1)}, bf16[192,128]{1,0:T(8,128)(2,1)S(1)}, u32[]{:S(2)}, u32[]{:S(2)}) collective-permute-start(bf16[192,128]{1,0:T(8,128)(2,1)S(1)} %get-tuple-element.63), channel_id=1, source_target_pairs={{0,6},{2,4},{4,2},{6,0},{1,7},{3,5},{5,3},{7,1},{8,14},{10,12},{12... | collective-permute-start | bytes 147464 | tf_op jit(solution)/shard_map/ppermute | solution.py:357
  17.5 0.0 collective-permute-start.4
  17.5 0.6 %collective-permute-start.5 = (bf16[192,128]{1,0:T(8,128)(2,1)S(1)}, bf16[192,128]{1,0:T(8,128)(2,1)S(1)}, u32[]{:S(2)}, u32[]{:S(2)}) collective-permute-start(bf16[192,128]{1,0:T(8,128)(2,1)S(1)} %get-tuple-element.65), channel_id=1, source_target_pairs={{0,2},{2,0},{4,6},{6,4},{1,3},{3,1},{5,7},{7,5},{8,10},{10,8},{12,... | collective-permute-start | bytes 147464 | tf_op jit(solution)/shard_map/ppermute | solution.py:357
  18.1 1.8 %sweep.5 = (f32[4,512,256]{2,1,0:T(8,128)S(1)}, f32[4,512,256]{2,1,0:T(8,128)S(1)}, bf16[4,512,256]{2,1,0:T(8,128)(2,1)S(1)}, bf16[4,512,256]{2,1,0:T(8,128)(2,1...) custom-call(f32[512,128]{1,0:T(8,128)S(1)} %get-tuple-element.51.ref, ...), custom_call_target="tpu_custom_call", output_to_operand_aliasing={{0}: (7, {}), {1}: (8, {}), {2}: (9, {}), {3}: (10, {}), {4... | custom-call | tf_op jit(solution)/shard_map/sweep/pallas_call | solution.py:416
  19.9 0.0 collective-permute-done.3.refs_1_
  19.9 2.6 %collective-permute-done.4.refs_2_ = bf16[192,128]{1,0:T(8,128)(2,1)S(1)} collective-permute-done((bf16[192,128]{1,0:T(8,128)(2,1)S(1)}, bf16[192,128]{1,0:T(8,128)(2,1)S(1)}, u32[]{:S(2)}, u32[]{:S(2)}) %collective-permute-start.4) | collective-permute-done | bytes 49184 | tf_op jit(solution)/shard_map/ppermute | solution.py:357
  22.4 0.0 collective-permute-done.5.refs_3_
  22.5 0.1 collective-permute-start.6
  22.6 1.0 %sweep.6 = (f32[4,512,256]{2,1,0:T(8,128)S(1)}, f32[4,512,256]{2,1,0:T(8,128)S(1)}, bf16[4,512,256]{2,1,0:T(8,128)(2,1)S(1)}, bf16[4,512,256]{2,1,0:T(8,128)(2,1...) custom-call(f32[512,128]{1,0:T(8,128)S(1)} %get-tuple-element.51.ref, ...), custom_call_target="tpu_custom_call", output_to_operand_aliasing={{0}: (7, {}), {1}: (8, {}), {2}: (9, {}), {3}: (10, {}), {4... | custom-call | tf_op jit(solution)/shard_map/sweep/pallas_call | solution.py:416
  23.5 0.3 collective-permute-done.6.refs_5_
  23.8 0.2 third.1
  24.1 1.6 %collective-permute-start.7 = (bf16[320,128]{1,0:T(8,128)(2,1)S(1)}, bf16[320,128]{1,0:T(8,128)(2,1)S(1)}, u32[]{:S(2)}, u32[]{:S(2)}) collective-permute-start(bf16[320,128]{1,0:T(8,128)(2,1)S(1)} %get-tuple-element.92), channel_id=1, source_target_pairs={{0,24},{1,9},{8,16},{9,1},{16,8},{17,25},{24,0},{25,17},{2,26},{3,... | collective-permute-start | bytes 245768 | tf_op jit(solution)/shard_map/ppermute | solution.py:351
  25.7 1.2 %collective-permute-start.8 = (bf16[320,128]{1,0:T(8,128)(2,1)S(1)}, bf16[320,128]{1,0:T(8,128)(2,1)S(1)}, u32[]{:S(2)}, u32[]{:S(2)}) collective-permute-start(bf16[320,128]{1,0:T(8,128)(2,1)S(1)} %get-tuple-element.93), channel_id=1, source_target_pairs={{0,16},{1,25},{8,24},{9,17},{16,0},{17,9},{24,8},{25,1},{2,18},{3,... | collective-permute-start | bytes 245768 | tf_op jit(solution)/shard_map/ppermute | solution.py:351
  26.9 0.7 %collective-permute-start.9 = (bf16[320,128]{1,0:T(8,128)(2,1)S(1)}, bf16[320,128]{1,0:T(8,128)(2,1)S(1)}, u32[]{:S(2)}, u32[]{:S(2)}) collective-permute-start(bf16[320,128]{1,0:T(8,128)(2,1)S(1)} %get-tuple-element.94), channel_id=1, source_target_pairs={{0,8},{1,17},{8,0},{9,25},{16,24},{17,1},{24,16},{25,9},{2,10},{3,... | collective-permute-start | bytes 245768 | tf_op jit(solution)/shard_map/ppermute | solution.py:351
  27.6 0.0 copy-start
  27.6 0.0 copy-start.1
  27.6 2.6 %sweep.7 = (f32[4,512,256]{2,1,0:T(8,128)S(1)}, f32[4,512,256]{2,1,0:T(8,128)S(1)}, bf16[4,512,256]{2,1,0:T(8,128)(2,1)S(1)}, bf16[4,512,256]{2,1,0:T(8,128)(2,1...) custom-call(f32[512,128]{1,0:T(8,128)S(1)} %get-tuple-element.51.ref, ...), custom_call_target="tpu_custom_call", output_to_operand_aliasing={{0}: (7, {}), {1}: (8, {}), {2}: (9, {}), {3}: (10, {}), {4... | custom-call | tf_op jit(solution)/shard_map/sweep/pallas_call | solution.py:416
  30.2 0.0 collective-permute-done.7.refs_11_
  30.2 1.9 %collective-permute-done.8.refs_12_ = bf16[320,128]{1,0:T(8,128)(2,1)S(1)} collective-permute-done((bf16[320,128]{1,0:T(8,128)(2,1)S(1)}, bf16[320,128]{1,0:T(8,128)(2,1)S(1)}, u32[]{:S(2)}, u32[]{:S(2)}) %collective-permute-start.8) | collective-permute-done | bytes 81952 | tf_op jit(solution)/shard_map/ppermute | solution.py:351
  32.1 0.0 collective-permute-done.9.refs_13_
  32.1 0.0 copy-done
  32.1 0.0 copy-done.1
  32.1 2.3 %last.1 = (bf16[4,512,256]{2,1,0:T(8,128)(2,1)}, bf16[4,512,256]{2,1,0:T(8,128)(2,1)}, bf16[4,512,256]{2,1,0:T(8,128)(2,1)}, bf16[4,512,256]{2,1,0:T(8,128)(2,1)...) custom-call(f32[512,128]{1,0:T(8,128)S(1)} %get-tuple-element.51.refs_0_.refs_6_, ...), custom_call_target="tpu_custom_call" | custom-call | tf_op jit(solution)/shard_map/last/pallas_call | solution.py:464
  (1 shorter events, 0.0 us)
Async XLA Ops:
  3.9 7.4 %collective-permute-start = (bf16[336,128]{1,0:T(8,128)(2,1)S(1)}, bf16[336,128]{1,0:T(8,128)(2,1)S(1)}, u32[]{:S(2)}, u32[]{:S(2)}) collective-permute-start(bf16[336,128]{1,0:T(8,128)(2,1)S(1)} %get-tuple-element.58), channel_id=1, source_target_pairs={{0,24},{1,9},{8,16},{9,1},{16,8},{17,25},{24,0},{25,17},{2,26},{3,... | collective-permute-start | bytes 258056 | tf_op jit(solution)/shard_map/ppermute | solution.py:351
  7.8 5.5 %collective-permute-start.1 = (bf16[336,128]{1,0:T(8,128)(2,1)S(1)}, bf16[336,128]{1,0:T(8,128)(2,1)S(1)}, u32[]{:S(2)}, u32[]{:S(2)}) collective-permute-start(bf16[336,128]{1,0:T(8,128)(2,1)S(1)} %get-tuple-element.59), channel_id=1, source_target_pairs={{0,16},{1,25},{8,24},{9,17},{16,0},{17,9},{24,8},{25,1},{2,18},{3,... | collective-permute-start | bytes 258056 | tf_op jit(solution)/shard_map/ppermute | solution.py:351
  8.3 5.0 %collective-permute-start.2 = (bf16[336,128]{1,0:T(8,128)(2,1)S(1)}, bf16[336,128]{1,0:T(8,128)(2,1)S(1)}, u32[]{:S(2)}, u32[]{:S(2)}) collective-permute-start(bf16[336,128]{1,0:T(8,128)(2,1)S(1)} %get-tuple-element.60), channel_id=1, source_target_pairs={{0,8},{1,17},{8,0},{9,25},{16,24},{17,1},{24,16},{25,9},{2,10},{3,... | collective-permute-start | bytes 258056 | tf_op jit(solution)/shard_map/ppermute | solution.py:351
  13.6 6.2 %collective-permute-start.3 = (bf16[192,128]{1,0:T(8,128)(2,1)S(1)}, bf16[192,128]{1,0:T(8,128)(2,1)S(1)}, u32[]{:S(2)}, u32[]{:S(2)}) collective-permute-start(bf16[192,128]{1,0:T(8,128)(2,1)S(1)} %get-tuple-element.63), channel_id=1, source_target_pairs={{0,6},{2,4},{4,2},{6,0},{1,7},{3,5},{5,3},{7,1},{8,14},{10,12},{12... | collective-permute-start | bytes 147464 | tf_op jit(solution)/shard_map/ppermute | solution.py:357
  17.5 5.0 %collective-permute-start.4 = (bf16[192,128]{1,0:T(8,128)(2,1)S(1)}, bf16[192,128]{1,0:T(8,128)(2,1)S(1)}, u32[]{:S(2)}, u32[]{:S(2)}) collective-permute-start(bf16[192,128]{1,0:T(8,128)(2,1)S(1)} %get-tuple-element.64), channel_id=1, source_target_pairs={{0,4},{2,6},{4,0},{6,2},{1,5},{3,7},{5,1},{7,3},{8,12},{10,14},{12... | collective-permute-start | bytes 147464 | tf_op jit(solution)/shard_map/ppermute | solution.py:357
  17.5 5.0 %collective-permute-start.5 = (bf16[192,128]{1,0:T(8,128)(2,1)S(1)}, bf16[192,128]{1,0:T(8,128)(2,1)S(1)}, u32[]{:S(2)}, u32[]{:S(2)}) collective-permute-start(bf16[192,128]{1,0:T(8,128)(2,1)S(1)} %get-tuple-element.65), channel_id=1, source_target_pairs={{0,2},{2,0},{4,6},{6,4},{1,3},{3,1},{5,7},{7,5},{8,10},{10,8},{12,... | collective-permute-start | bytes 147464 | tf_op jit(solution)/shard_map/ppermute | solution.py:357
  22.5 1.3 %collective-permute-start.6 = (bf16[320,128]{1,0:T(8,128)(2,1)S(1)}, bf16[320,128]{1,0:T(8,128)(2,1)S(1)}, u32[]{:S(2)}, u32[]{:S(2)}) collective-permute-start(bf16[320,128]{1,0:T(8,128)(2,1)S(1)} %get-tuple-element.74), channel_id=1, source_target_pairs={{0,1},{1,0},{2,3},{3,2},{4,5},{5,4},{6,7},{7,6},{8,9},{9,8},{10,11... | collective-permute-start | bytes 245768 | tf_op jit(solution)/shard_map/ppermute | solution.py:357
  24.1 6.1 %collective-permute-start.7 = (bf16[320,128]{1,0:T(8,128)(2,1)S(1)}, bf16[320,128]{1,0:T(8,128)(2,1)S(1)}, u32[]{:S(2)}, u32[]{:S(2)}) collective-permute-start(bf16[320,128]{1,0:T(8,128)(2,1)S(1)} %get-tuple-element.92), channel_id=1, source_target_pairs={{0,24},{1,9},{8,16},{9,1},{16,8},{17,25},{24,0},{25,17},{2,26},{3,... | collective-permute-start | bytes 245768 | tf_op jit(solution)/shard_map/ppermute | solution.py:351
  25.7 6.4 %collective-permute-start.8 = (bf16[320,128]{1,0:T(8,128)(2,1)S(1)}, bf16[320,128]{1,0:T(8,128)(2,1)S(1)}, u32[]{:S(2)}, u32[]{:S(2)}) collective-permute-start(bf16[320,128]{1,0:T(8,128)(2,1)S(1)} %get-tuple-element.93), channel_id=1, source_target_pairs={{0,16},{1,25},{8,24},{9,17},{16,0},{17,9},{24,8},{25,1},{2,18},{3,... | collective-permute-start | bytes 245768 | tf_op jit(solution)/shard_map/ppermute | solution.py:351
  26.9 5.2 %collective-permute-start.9 = (bf16[320,128]{1,0:T(8,128)(2,1)S(1)}, bf16[320,128]{1,0:T(8,128)(2,1)S(1)}, u32[]{:S(2)}, u32[]{:S(2)}) collective-permute-start(bf16[320,128]{1,0:T(8,128)(2,1)S(1)} %get-tuple-element.94), channel_id=1, source_target_pairs={{0,8},{1,17},{8,0},{9,25},{16,24},{17,1},{24,16},{25,9},{2,10},{3,... | collective-permute-start | bytes 245768 | tf_op jit(solution)/shard_map/ppermute | solution.py:351
  27.6 4.5 %copy-start = (bf16[1,256,256]{2,1,0:T(8,128)(2,1)S(1)}, bf16[1,256,256]{2,1,0:T(8,128)(2,1)}, u32[]{:S(2)}) copy-start(bf16[1,256,256]{2,1,0:T(8,128)(2,1)} %refs_7_.3) | copy-start | bytes 393220
  27.6 4.5 %copy-start.1 = (bf16[1,256,256]{2,1,0:T(8,128)(2,1)S(1)}, bf16[1,256,256]{2,1,0:T(8,128)(2,1)}, u32[]{:S(2)}) copy-start(bf16[1,256,256]{2,1,0:T(8,128)(2,1)} %refs_8_.3) | copy-start | bytes 393220

commit v5 on v4

--- a/solution.py
+++ b/solution.py
@@ -181,7 +181,7 @@
 
 
 def swap_kernel(chips, *refs):
-    got, sent_ref, kept_ref = by_partner(refs[:chips]), refs[chips + 1], refs[chips + 2]
+    got, sent_ref, kept_ref = refs[:chips], refs[chips + 1], refs[chips + 2]
     block = got[0].shape[0] // 3
     totals = []
     for c in range(2):
@@ -217,8 +217,20 @@
         msgs[k][responses * block :, :] = total
 
 
-def sweep_kernel(units, cols_ref, rows_ref, q_ref, k_ref, v_ref, c_ref, *refs):
-    out_ref, dq_ref, grad_ref, dk_ref, dv_ref, token_ref = refs[-6:]
+def sweep_kernel(units, done, cols_ref, rows_ref, q_ref, k_ref, v_ref, c_ref, *refs):
+    writes = len(done) > 0
+    if writes:
+        *refs, dk_hbm, dv_hbm, sems = refs
+    out_ref, dq_ref, query_ref, grad_ref, dk_ref, dv_ref, token_ref = refs[-7:]
+    copies = []
+
+    def send(r):
+        for a, b in ((dk_ref, dk_hbm), (dv_ref, dv_hbm)):
+            copies.append(pltpu.make_async_copy(a.at[r], b.at[r], sems.at[len(copies)]))
+            copies[-1].start()
+
+    for r in done:
+        send(r)
     token_ref[...] = jnp.zeros_like(token_ref)
     quarter = HALF // 2
     causal = lax.broadcasted_iota(jnp.int32, (quarter, quarter), 0) >= lax.broadcasted_iota(
@@ -248,7 +260,9 @@
         live = cols_ref[:, 8 * r + 4 : 8 * r + 5]
         opened = cols_ref[:, 8 * r + 5 : 8 * r + 6]
         grad_all = (c_ref[r, :, lanes].astype(F32) * live).astype(BF16)
-        grad_ref[r, :, lanes] = grad_all
+        carried = cols_ref[:, 8 * r + 2 + h : 8 * r + 3 + h]
+        query_ref[r, :, lanes] = (q_ref[r, :, lanes].astype(F32) * carried).astype(BF16)
+        grad_ref[r, :, lanes] = (grad_all.astype(F32) * carried).astype(BF16)
         query_turned = q_ref[r, :, lanes].T
         grad_turned = grad_all.T
         dk = [None] * blocks
@@ -280,13 +294,17 @@
             of = slice(s * HALF, (s + 1) * HALF)
             dk_ref[r, of, lanes] = dk[s].astype(BF16).T
             dv_ref[r, of, lanes] = dv[s].astype(BF16).T
+        if writes and h == H - 1:
+            send(r)
+    for copy in copies:
+        copy.wait()
 
 
 def last_kernel(
-    n, count, cols_ref, q_ref, grad_ref, po_ref, pdq_ref, rdk_ref, rdv_ref, keys_ref, values_ref, later_ref, *refs
+    n, count, cols_ref, q_ref, grad_ref, po_ref, pdq_ref, keys_ref, values_ref, later_ref, *refs
 ):
     got, refs = refs[:n], refs[n + 1 :]
-    out_hbm, dq_hbm, rdk_hbm, rdv_hbm, dk_hbm, dv_hbm, start, out_buf, dq_buf, dk_buf, dv_buf, sems = refs
+    out_hbm, dq_hbm, dk_hbm, dv_hbm, start, out_buf, dq_buf, dk_buf, dv_buf, sems = refs
     part = DH // n
     block = H * part
     place = partners(n)
@@ -298,8 +316,6 @@
         copies.append(pltpu.make_async_copy(a, b, sems.at[len(copies)]))
         copies[-1].start()
 
-    send(rdk_ref, rdk_hbm)
-    send(rdv_ref, rdv_hbm)
     start[...] = jnp.zeros_like(start)
     for r in range(count + 1):
         for k in range(n):
@@ -319,46 +335,22 @@
     for r in range(count):
         for t in range(0, slots, HALF):
             at = slice(t, t + HALF)
-            x = mm(q_ref[r, at, :], start[r])
-            y = mm_nt(grad_ref[r, at, :], start[r])
-            for h in range(H):
-                lanes = slice(h * DH, (h + 1) * DH)
-                carried = cols_ref[at, 8 * r + 2 + h : 8 * r + 3 + h]
-                out_buf[r, at, lanes] = (po_ref[r, at, lanes] + carried * x[:, lanes]).astype(BF16)
-                dq_buf[r, at, lanes] = (pdq_ref[r, at, lanes] + carried * y[:, lanes]).astype(BF16)
+            out_buf[r, at, :] = (po_ref[r, at, :] + mm(q_ref[r, at, :], start[r])).astype(BF16)
+            dq_buf[r, at, :] = (pdq_ref[r, at, :] + mm_nt(grad_ref[r, at, :], start[r])).astype(BF16)
             send(out_buf.at[r, at], out_hbm.at[r, at])
             send(dq_buf.at[r, at], dq_hbm.at[r, at])
     for copy in copies:
         copy.wait()
 
 
-def steps(n):
-    first = list(range(n - 1, 0, -1))
-    return [0, *first], [0, *first[-1:], *first[:-1]]
+def exchange(xs, axis):
+    n = lax.axis_size(axis)
+    return [xs[0]] + [lax.ppermute(xs[k], axis, [(s, s ^ k) for s in range(n)]) for k in range(1, n)]
 
 
 def partners(n):
     me = lax.axis_index("prompt")
-    low = lax.axis_index("core") == 0
-    return [lax.bitwise_xor(me, jnp.where(low, a, b)) for a, b in zip(*steps(n))]
-
-
-def exchange_prompt(xs):
-    n = lax.axis_size("prompt")
-    got = [xs[0]]
-    for x, ks in zip(xs[1:], list(zip(*steps(n)))[1:]):
-        pairs = [(2 * s + c, 2 * (s ^ ks[c]) + c) for s in range(n) for c in range(2)]
-        got.append(lax.ppermute(x, ("prompt", "core"), pairs))
-    return got
-
-
-def exchange(xs, axis):
-    n = lax.axis_size(axis)
-    return [xs[0]] + [lax.ppermute(xs[k], axis, [(s, s ^ k) for s in range(n)]) for k in range(n - 1, 0, -1)]
-
-
-def by_partner(refs):
-    return [refs[0], *refs[:0:-1]]
+    return [lax.bitwise_xor(me, k) for k in range(n)]
 
 
 def shards(
@@ -412,21 +404,23 @@
     like = shape(queries.shape, F32)
     like_out = shape(queries.shape, BF16)
 
-    def sweep(units, before, token):
+    def sweep(units, before, token, done=()):
+        writes = len(done) > 0
         outs = pl.pallas_call(
-            lambda *refs: sweep_kernel(units, *refs),
-            out_shape=[like, like, like_out, like_out, like_out, shape((8, 128), F32)],
+            lambda *refs: sweep_kernel(units, done, *refs),
+            out_shape=[like, like] + [like_out] * 4 + [shape((8, 128), F32)] + [like_out] * (2 * writes),
             in_specs=[VMEM] * 6 + [ANY] * (1 + len(before)),
-            out_specs=[VMEM] * 6,
+            out_specs=[VMEM] * 7 + [ANY] * (2 * writes),
+            scratch_shapes=[pltpu.SemaphoreType.DMA((2 * responses,))] * writes,
             input_output_aliases={7 + k: k for k in range(len(before))},
             compiler_params=params(),
             name="sweep",
         )(cols, rows, queries, resp_keys, resp_values, cotangent, token, *before)
-        return outs[:5], outs[5]
+        return (outs[:4] + outs[7:] if writes else outs[:6]), outs[6]
 
     units = [(r, h) for r in range(responses) for h in range(H)]
-    got1 = exchange_prompt(msgs)
-    held, token = sweep(units[:2], [], cols)
+    got1 = exchange(msgs, "prompt")
+    held, token = sweep(units[:3], [], cols)
     outs = pl.pallas_call(
         lambda *refs: second_kernel(n, chips, cores, *refs),
         out_shape=[shape(((1 + cores) * block, DH), BF16)] * chips + [shape((8, DH), F32)],
@@ -438,7 +432,7 @@
     )(*got1, token)
     msgs, later = outs[:chips], outs[chips]
     got2 = exchange(msgs, "z")
-    held, token = sweep(units[2:4], held, later)
+    held, token = sweep(units[3:5], held, later)
     sent, kept = pl.pallas_call(
         lambda *refs: swap_kernel(chips, *refs),
         out_shape=[shape(((chips + 1) * block, DH), BF16)] * 2,
@@ -448,7 +442,7 @@
         name="swap",
     )(*got2, token)
     swapped = exchange([kept, sent], "core")[1]
-    held, token = sweep(units[4:5], held, kept)
+    held, token = sweep(units[5:6], held, kept)
     msgs = pl.pallas_call(
         lambda *refs: third_kernel(n, chips, *refs),
         out_shape=[shape(((responses + 1) * block, DH), BF16)] * n,
@@ -457,26 +451,26 @@
         compiler_params=params(),
         name="third",
     )(*got1, kept, swapped, token)
-    got3 = exchange_prompt(msgs)
-    held, token = sweep(units[5:], held, msgs[0])
-    partial_out, partial_dq, grad_out, resp_dk, resp_dv = held
-
-    resp_out, resp_dq, resp_dk, resp_dv, prompt_dk, prompt_dv = pl.pallas_call(
+    got3 = exchange(msgs, "prompt")
+    held, token = sweep(units[6:], held, msgs[0], range(responses - 1))
+    partial_out, partial_dq, query, grad_out, resp_dk, resp_dv = held
+
+    resp_out, resp_dq, prompt_dk, prompt_dv = pl.pallas_call(
         lambda *refs: last_kernel(n, responses, *refs),
-        out_shape=[like_out] * 4 + [shape(keys.shape, BF16)] * 2,
-        in_specs=[VMEM] * (10 + n) + [ANY],
-        out_specs=[ANY] * 6,
+        out_shape=[like_out] * 2 + [shape(keys.shape, BF16)] * 2,
+        in_specs=[VMEM] * (8 + n) + [ANY],
+        out_specs=[ANY] * 4,
         scratch_shapes=[
             pltpu.VMEM((responses + 1, width, width), BF16),
             pltpu.VMEM(queries.shape, BF16),
             pltpu.VMEM(queries.shape, BF16),
             pltpu.VMEM(keys.shape[1:], BF16),
             pltpu.VMEM(keys.shape[1:], BF16),
-            pltpu.SemaphoreType.DMA((4 + 2 * responses * (slots // HALF),)),
+            pltpu.SemaphoreType.DMA((2 + 2 * responses * (slots // HALF),)),
         ],
         compiler_params=params(),
         name="last",
-    )(cols, queries, grad_out, partial_out, partial_dq, resp_dk, resp_dv, keys, values, later, *got3, token)
+    )(cols, query, grad_out, partial_out, partial_dq, keys, values, later, *got3, token)
     return (resp_out, resp_dq, resp_dk, resp_dv, prompt_dk, prompt_dv)
 
 

time: 34.6 us -> 34.7 us (level)
  Pallas kernels: 13 us -> 13.5 us
    ppermute x6 -> x0, starting transfers between devices: 8.16 us -> none  [exchange_prompt(): got.append(lax.ppermute(x, ('prompt', 'core'), pairs))]
    ppermute x4 -> x10, starting transfers between devices: 4.54 us -> 12.6 us  [exchange(): lax.ppermute(xs[k], axis, [(s, s ^ k) for s in range(n)])]
    ppermute x6 -> x0, waiting for transfers between devices: 5.05 us -> none  [exchange_prompt(): got.append(lax.ppermute(x, ('prompt', 'core'), pairs))]
    ppermute x4 -> x10, waiting for transfers between devices: 2.88 us -> 7.6 us  [exchange(): lax.ppermute(xs[k], axis, [(s, s ^ k) for s in range(n)])]
    pallas_call x4, Pallas kernels: 7.02 us -> 7.88 us  [sweep(): pl.pallas_call(lambda *refs: sweep_kernel(units, done, *refs), out_shape=...]
    pallas_call x1, Pallas kernels: 2.28 us -> 1.92 us  [shards(): pl.pallas_call(lambda *refs: last_kernel(n, responses, *refs), out_shape=...]
  transfers between devices with their start and end apart: 10 -> 10, of which waited for: 5 -> 6; matrix products, arithmetic and copies ran while one was open for 0% -> 0% of each run, Pallas kernels for 20% -> 23%
where the time goes in v5:
time: 34.7 us; the launch traced here: 34.5 us
  Pallas kernels  13.5 us (39%)
  starting transfers between devices  12.6 us (36%)
  waiting for transfers between devices  7.6 us (22%)
  between operations  0.73 us (2%)
    ppermute x10, starting transfers between devices, exchange(): lax.ppermute(xs[k], axis, [(s, s ^ k) for s in range(n)])  12.6 us
    pallas_call x4, Pallas kernels, sweep(): pl.pallas_call(lambda *refs: sweep_kernel(units, done, *refs), out_shape=...  7.88 us
    ppermute x10, waiting for transfers between devices, exchange(): lax.ppermute(xs[k], axis, [(s, s ^ k) for s in range(n)])  7.6 us
    pallas_call x1, Pallas kernels, shards(): pl.pallas_call(lambda *refs: first_kernel(n, *refs), out_shape=[shape((bl...  3.22 us
    pallas_call x1, Pallas kernels, shards(): pl.pallas_call(lambda *refs: last_kernel(n, responses, *refs), out_shape=...  1.92 us
  transfers between devices with their start and end apart: 10, of which 6 were waited for; matrix products, arithmetic and copies ran while one was open for 0% of the time, Pallas kernels for 23%

profile of v5, /device:TPU:0, one launch (start us, length us, event | category | flops | bytes accessed | tf_op | source)
XLA Modules:
  0.0 34.5 jit_solution(14170747618499641634)
XLA Ops:
  0.6 3.2 %first.1 = (bf16[336,128]{1,0:T(8,128)(2,1)S(1)}, bf16[336,128]{1,0:T(8,128)(2,1)S(1)}, bf16[336,128]{1,0:T(8,128)(2,1)S(1)}, bf16[336,128]{1,0:T(8,128)(2,1)S(1...) custom-call(s32[4]{0:T(128)} %refs_0_.1, ...), custom_call_target="tpu_custom_call" | custom-call | tf_op jit(solution)/shard_map/first/pallas_call | solution.py:377
  3.9 3.0 %collective-permute-start = (bf16[336,128]{1,0:T(8,128)(2,1)S(1)}, bf16[336,128]{1,0:T(8,128)(2,1)S(1)}, u32[]{:S(2)}, u32[]{:S(2)}) collective-permute-start(bf16[336,128]{1,0:T(8,128)(2,1)S(1)} %get-tuple-element.66), channel_id=1, source_target_pairs={{0,8},{8,0},{16,24},{24,16},{1,9},{9,1},{17,25},{25,17},{2,10},{10... | collective-permute-start | bytes 258056 | tf_op jit(solution)/shard_map/ppermute | solution.py:348
  6.9 1.5 %collective-permute-start.1 = (bf16[336,128]{1,0:T(8,128)(2,1)S(1)}, bf16[336,128]{1,0:T(8,128)(2,1)S(1)}, u32[]{:S(2)}, u32[]{:S(2)}) collective-permute-start(bf16[336,128]{1,0:T(8,128)(2,1)S(1)} %get-tuple-element.67), channel_id=1, source_target_pairs={{0,16},{8,24},{16,0},{24,8},{1,17},{9,25},{17,1},{25,9},{2,18},{10... | collective-permute-start | bytes 258056 | tf_op jit(solution)/shard_map/ppermute | solution.py:348
  8.4 0.0 collective-permute-start.2
  8.4 2.6 %sweep.4 = (f32[4,512,256]{2,1,0:T(8,128)S(1)}, f32[4,512,256]{2,1,0:T(8,128)S(1)}, bf16[4,512,256]{2,1,0:T(8,128)(2,1)S(1)}, bf16[4,512,256]{2,1,0:T(8,128)(2,1...) custom-call(f32[512,128]{1,0:T(8,128)S(1)} %get-tuple-element.59.refs_0_.refs_6_, ...), custom_call_target="tpu_custom_call" | custom-call | tf_op jit(solution)/shard_map/sweep/pallas_call | solution.py:409
  11.0 0.0 collective-permute-done.refs_1_
  11.0 1.3 %collective-permute-done.1.refs_2_ = bf16[336,128]{1,0:T(8,128)(2,1)S(1)} collective-permute-done((bf16[336,128]{1,0:T(8,128)(2,1)S(1)}, bf16[336,128]{1,0:T(8,128)(2,1)S(1)}, u32[]{:S(2)}, u32[]{:S(2)}) %collective-permute-start.1) | collective-permute-done | bytes 86048 | tf_op jit(solution)/shard_map/ppermute | solution.py:348
  12.3 1.5 %collective-permute-done.2.refs_3_ = bf16[336,128]{1,0:T(8,128)(2,1)S(1)} collective-permute-done((bf16[336,128]{1,0:T(8,128)(2,1)S(1)}, bf16[336,128]{1,0:T(8,128)(2,1)S(1)}, u32[]{:S(2)}, u32[]{:S(2)}) %collective-permute-start.2) | collective-permute-done | bytes 86048 | tf_op jit(solution)/shard_map/ppermute | solution.py:348
  13.8 0.2 second.1
  14.0 1.6 %collective-permute-start.3 = (bf16[192,128]{1,0:T(8,128)(2,1)S(1)}, bf16[192,128]{1,0:T(8,128)(2,1)S(1)}, u32[]{:S(2)}, u32[]{:S(2)}) collective-permute-start(bf16[192,128]{1,0:T(8,128)(2,1)S(1)} %get-tuple-element.71), channel_id=1, source_target_pairs={{0,2},{2,0},{4,6},{6,4},{1,3},{3,1},{5,7},{7,5},{8,10},{10,8},{12,... | collective-permute-start | bytes 147464 | tf_op jit(solution)/shard_map/ppermute | solution.py:348
  15.7 2.6 %collective-permute-start.4 = (bf16[192,128]{1,0:T(8,128)(2,1)S(1)}, bf16[192,128]{1,0:T(8,128)(2,1)S(1)}, u32[]{:S(2)}, u32[]{:S(2)}) collective-permute-start(bf16[192,128]{1,0:T(8,128)(2,1)S(1)} %get-tuple-element.72), channel_id=1, source_target_pairs={{0,4},{2,6},{4,0},{6,2},{1,5},{3,7},{5,1},{7,3},{8,12},{10,14},{12... | collective-permute-start | bytes 147464 | tf_op jit(solution)/shard_map/ppermute | solution.py:348
  18.3 0.2 collective-permute-start.5
  18.5 1.8 %sweep.5 = (f32[4,512,256]{2,1,0:T(8,128)S(1)}, f32[4,512,256]{2,1,0:T(8,128)S(1)}, bf16[4,512,256]{2,1,0:T(8,128)(2,1)S(1)}, bf16[4,512,256]{2,1,0:T(8,128)(2,1...) custom-call(f32[512,128]{1,0:T(8,128)S(1)} %get-tuple-element.59.ref, ...), custom_call_target="tpu_custom_call", output_to_operand_aliasing={{0}: (7, {}), {1}: (8, {}), {2}: (9, {}), {3}: (10, {}), {4... | custom-call | tf_op jit(solution)/shard_map/sweep/pallas_call | solution.py:409
  20.3 0.0 collective-permute-done.3.refs_1_
  20.3 1.5 %collective-permute-done.4.refs_2_ = bf16[192,128]{1,0:T(8,128)(2,1)S(1)} collective-permute-done((bf16[192,128]{1,0:T(8,128)(2,1)S(1)}, bf16[192,128]{1,0:T(8,128)(2,1)S(1)}, u32[]{:S(2)}, u32[]{:S(2)}) %collective-permute-start.4) | collective-permute-done | bytes 49184 | tf_op jit(solution)/shard_map/ppermute | solution.py:348
  21.7 2.4 %collective-permute-done.5.refs_3_ = bf16[192,128]{1,0:T(8,128)(2,1)S(1)} collective-permute-done((bf16[192,128]{1,0:T(8,128)(2,1)S(1)}, bf16[192,128]{1,0:T(8,128)(2,1)S(1)}, u32[]{:S(2)}, u32[]{:S(2)}) %collective-permute-start.5) | collective-permute-done | bytes 49184 | tf_op jit(solution)/shard_map/ppermute | solution.py:348
  24.2 0.1 collective-permute-start.6
  24.3 1.0 %sweep.6 = (f32[4,512,256]{2,1,0:T(8,128)S(1)}, f32[4,512,256]{2,1,0:T(8,128)S(1)}, bf16[4,512,256]{2,1,0:T(8,128)(2,1)S(1)}, bf16[4,512,256]{2,1,0:T(8,128)(2,1...) custom-call(f32[512,128]{1,0:T(8,128)S(1)} %get-tuple-element.59.ref, ...), custom_call_target="tpu_custom_call", output_to_operand_aliasing={{0}: (7, {}), {1}: (8, {}), {2}: (9, {}), {3}: (10, {}), {4... | custom-call | tf_op jit(solution)/shard_map/sweep/pallas_call | solution.py:409
  25.2 0.3 collective-permute-done.6.refs_5_
  25.5 0.2 third.1
  25.8 0.6 %collective-permute-start.7 = (bf16[320,128]{1,0:T(8,128)(2,1)S(1)}, bf16[320,128]{1,0:T(8,128)(2,1)S(1)}, u32[]{:S(2)}, u32[]{:S(2)}) collective-permute-start(bf16[320,128]{1,0:T(8,128)(2,1)S(1)} %get-tuple-element.102), channel_id=1, source_target_pairs={{0,8},{8,0},{16,24},{24,16},{1,9},{9,1},{17,25},{25,17},{2,10},{10... | collective-permute-start | bytes 245768 | tf_op jit(solution)/shard_map/ppermute | solution.py:348
  26.4 0.8 %collective-permute-start.8 = (bf16[320,128]{1,0:T(8,128)(2,1)S(1)}, bf16[320,128]{1,0:T(8,128)(2,1)S(1)}, u32[]{:S(2)}, u32[]{:S(2)}) collective-permute-start(bf16[320,128]{1,0:T(8,128)(2,1)S(1)} %get-tuple-element.103), channel_id=1, source_target_pairs={{0,16},{8,24},{16,0},{24,8},{1,17},{9,25},{17,1},{25,9},{2,18},{10... | collective-permute-start | bytes 245768 | tf_op jit(solution)/shard_map/ppermute | solution.py:348
  27.2 2.2 %collective-permute-start.9 = (bf16[320,128]{1,0:T(8,128)(2,1)S(1)}, bf16[320,128]{1,0:T(8,128)(2,1)S(1)}, u32[]{:S(2)}, u32[]{:S(2)}) collective-permute-start(bf16[320,128]{1,0:T(8,128)(2,1)S(1)} %get-tuple-element.104), channel_id=1, source_target_pairs={{0,24},{8,16},{16,8},{24,0},{1,25},{9,17},{17,9},{25,1},{2,26},{10... | collective-permute-start | bytes 245768 | tf_op jit(solution)/shard_map/ppermute | solution.py:348
  29.3 0.0 copy-start
  29.3 0.0 copy-start.1
  29.3 2.6 %sweep.7 = (f32[4,512,256]{2,1,0:T(8,128)S(1)}, f32[4,512,256]{2,1,0:T(8,128)S(1)}, bf16[4,512,256]{2,1,0:T(8,128)(2,1)S(1)}, bf16[4,512,256]{2,1,0:T(8,128)(2,1...) custom-call(f32[512,128]{1,0:T(8,128)S(1)} %get-tuple-element.59.ref, ...), custom_call_target="tpu_custom_call", output_to_operand_aliasing={{0}: (7, {}), {1}: (8, {}), {2}: (9, {}), {3}: (10, {}), {4... | custom-call | tf_op jit(solution)/shard_map/sweep/pallas_call | solution.py:409
  32.0 0.0 collective-permute-done.7.refs_9_
  32.0 0.6 %collective-permute-done.8.refs_10_ = bf16[320,128]{1,0:T(8,128)(2,1)S(1)} collective-permute-done((bf16[320,128]{1,0:T(8,128)(2,1)S(1)}, bf16[320,128]{1,0:T(8,128)(2,1)S(1)}, u32[]{:S(2)}, u32[]{:S(2)}) %collective-permute-start.8) | collective-permute-done | bytes 81952 | tf_op jit(solution)/shard_map/ppermute | solution.py:348
  32.6 0.0 collective-permute-done.9.refs_11_
  32.6 0.0 copy-done
  32.6 0.0 copy-done.1
  32.6 1.9 %last.1 = (bf16[4,512,256]{2,1,0:T(8,128)(2,1)}, bf16[4,512,256]{2,1,0:T(8,128)(2,1)}, bf16[1,256,256]{2,1,0:T(8,128)(2,1)}, bf16[1,256,256]{2,1,0:T(8,128)(2,1)}) custom-call(f32[512,128]{1,0:T(8,128)S(1)} %get-tuple-element.59.refs_0_.refs_6_, bf16[4,512,256]{2,1,0:T(8,128)(2,1)S(1)} %get-tuple-element.98.refs_1_, ...), custom_call_target="tpu_custom_call" | custom-call | tf_op jit(solution)/shard_map/last/pallas_call | solution.py:458
  (1 shorter events, 0.0 us)
Async XLA Ops:
  3.9 7.1 %collective-permute-start = (bf16[336,128]{1,0:T(8,128)(2,1)S(1)}, bf16[336,128]{1,0:T(8,128)(2,1)S(1)}, u32[]{:S(2)}, u32[]{:S(2)}) collective-permute-start(bf16[336,128]{1,0:T(8,128)(2,1)S(1)} %get-tuple-element.66), channel_id=1, source_target_pairs={{0,8},{8,0},{16,24},{24,16},{1,9},{9,1},{17,25},{25,17},{2,10},{10... | collective-permute-start | bytes 258056 | tf_op jit(solution)/shard_map/ppermute | solution.py:348
  6.9 5.4 %collective-permute-start.1 = (bf16[336,128]{1,0:T(8,128)(2,1)S(1)}, bf16[336,128]{1,0:T(8,128)(2,1)S(1)}, u32[]{:S(2)}, u32[]{:S(2)}) collective-permute-start(bf16[336,128]{1,0:T(8,128)(2,1)S(1)} %get-tuple-element.67), channel_id=1, source_target_pairs={{0,16},{8,24},{16,0},{24,8},{1,17},{9,25},{17,1},{25,9},{2,18},{10... | collective-permute-start | bytes 258056 | tf_op jit(solution)/shard_map/ppermute | solution.py:348
  8.4 5.4 %collective-permute-start.2 = (bf16[336,128]{1,0:T(8,128)(2,1)S(1)}, bf16[336,128]{1,0:T(8,128)(2,1)S(1)}, u32[]{:S(2)}, u32[]{:S(2)}) collective-permute-start(bf16[336,128]{1,0:T(8,128)(2,1)S(1)} %get-tuple-element.68), channel_id=1, source_target_pairs={{0,24},{8,16},{16,8},{24,0},{1,25},{9,17},{17,9},{25,1},{2,26},{10... | collective-permute-start | bytes 258056 | tf_op jit(solution)/shard_map/ppermute | solution.py:348
  14.0 6.2 %collective-permute-start.3 = (bf16[192,128]{1,0:T(8,128)(2,1)S(1)}, bf16[192,128]{1,0:T(8,128)(2,1)S(1)}, u32[]{:S(2)}, u32[]{:S(2)}) collective-permute-start(bf16[192,128]{1,0:T(8,128)(2,1)S(1)} %get-tuple-element.71), channel_id=1, source_target_pairs={{0,2},{2,0},{4,6},{6,4},{1,3},{3,1},{5,7},{7,5},{8,10},{10,8},{12,... | collective-permute-start | bytes 147464 | tf_op jit(solution)/shard_map/ppermute | solution.py:348
  15.7 6.0 %collective-permute-start.4 = (bf16[192,128]{1,0:T(8,128)(2,1)S(1)}, bf16[192,128]{1,0:T(8,128)(2,1)S(1)}, u32[]{:S(2)}, u32[]{:S(2)}) collective-permute-start(bf16[192,128]{1,0:T(8,128)(2,1)S(1)} %get-tuple-element.72), channel_id=1, source_target_pairs={{0,4},{2,6},{4,0},{6,2},{1,5},{3,7},{5,1},{7,3},{8,12},{10,14},{12... | collective-permute-start | bytes 147464 | tf_op jit(solution)/shard_map/ppermute | solution.py:348
  18.3 5.9 %collective-permute-start.5 = (bf16[192,128]{1,0:T(8,128)(2,1)S(1)}, bf16[192,128]{1,0:T(8,128)(2,1)S(1)}, u32[]{:S(2)}, u32[]{:S(2)}) collective-permute-start(bf16[192,128]{1,0:T(8,128)(2,1)S(1)} %get-tuple-element.73), channel_id=1, source_target_pairs={{0,6},{2,4},{4,2},{6,0},{1,7},{3,5},{5,3},{7,1},{8,14},{10,12},{12... | collective-permute-start | bytes 147464 | tf_op jit(solution)/shard_map/ppermute | solution.py:348
  24.2 1.3 %collective-permute-start.6 = (bf16[320,128]{1,0:T(8,128)(2,1)S(1)}, bf16[320,128]{1,0:T(8,128)(2,1)S(1)}, u32[]{:S(2)}, u32[]{:S(2)}) collective-permute-start(bf16[320,128]{1,0:T(8,128)(2,1)S(1)} %get-tuple-element.83), channel_id=1, source_target_pairs={{0,1},{1,0},{2,3},{3,2},{4,5},{5,4},{6,7},{7,6},{8,9},{9,8},{10,11... | collective-permute-start | bytes 245768 | tf_op jit(solution)/shard_map/ppermute | solution.py:348
  25.8 6.2 %collective-permute-start.7 = (bf16[320,128]{1,0:T(8,128)(2,1)S(1)}, bf16[320,128]{1,0:T(8,128)(2,1)S(1)}, u32[]{:S(2)}, u32[]{:S(2)}) collective-permute-start(bf16[320,128]{1,0:T(8,128)(2,1)S(1)} %get-tuple-element.102), channel_id=1, source_target_pairs={{0,8},{8,0},{16,24},{24,16},{1,9},{9,1},{17,25},{25,17},{2,10},{10... | collective-permute-start | bytes 245768 | tf_op jit(solution)/shard_map/ppermute | solution.py:348
  26.4 6.2 %collective-permute-start.8 = (bf16[320,128]{1,0:T(8,128)(2,1)S(1)}, bf16[320,128]{1,0:T(8,128)(2,1)S(1)}, u32[]{:S(2)}, u32[]{:S(2)}) collective-permute-start(bf16[320,128]{1,0:T(8,128)(2,1)S(1)} %get-tuple-element.103), channel_id=1, source_target_pairs={{0,16},{8,24},{16,0},{24,8},{1,17},{9,25},{17,1},{25,9},{2,18},{10... | collective-permute-start | bytes 245768 | tf_op jit(solution)/shard_map/ppermute | solution.py:348
  27.2 5.4 %collective-permute-start.9 = (bf16[320,128]{1,0:T(8,128)(2,1)S(1)}, bf16[320,128]{1,0:T(8,128)(2,1)S(1)}, u32[]{:S(2)}, u32[]{:S(2)}) collective-permute-start(bf16[320,128]{1,0:T(8,128)(2,1)S(1)} %get-tuple-element.104), channel_id=1, source_target_pairs={{0,24},{8,16},{16,8},{24,0},{1,25},{9,17},{17,9},{25,1},{2,26},{10... | collective-permute-start | bytes 245768 | tf_op jit(solution)/shard_map/ppermute | solution.py:348
  29.3 3.2 %copy-start = (bf16[1,256,256]{2,1,0:T(8,128)(2,1)S(1)}, bf16[1,256,256]{2,1,0:T(8,128)(2,1)}, u32[]{:S(2)}) copy-start(bf16[1,256,256]{2,1,0:T(8,128)(2,1)} %refs_5_.3) | copy-start | bytes 393220
  29.3 3.2 %copy-start.1 = (bf16[1,256,256]{2,1,0:T(8,128)(2,1)S(1)}, bf16[1,256,256]{2,1,0:T(8,128)(2,1)}, u32[]{:S(2)}) copy-start(bf16[1,256,256]{2,1,0:T(8,128)(2,1)} %refs_6_.3) | copy-start | bytes 393220

commit v6 on v5

--- a/solution.py
+++ b/solution.py
@@ -31,6 +31,10 @@
 
 def mm_tn(a, b):
     return lax.dot_general(a, b, (((0,), (0,)), ((), ())), preferred_element_type=F32)
+
+
+def to_columns(rows):
+    return jnp.concatenate([rows, jnp.zeros((128 - rows.shape[0], rows.shape[1]), F32)], axis=0).T
 
 
 def in_hbm(x):
@@ -65,8 +69,8 @@
     n, ids_hbm, lens_hbm, adv_hbm, keys_hbm, values_hbm, pgates_hbm, gates_hbm, mask_hbm, q_hbm, c_hbm, k_hbm, v_hbm,
     *refs,
 ):
-    msgs, (cols_ref, rows_ref, q, c, k_out, v_out) = refs[:n], refs[n : n + 6]
-    keys, values, pgates, gates, mask, ids_ref, lens_ref, adv_ref, matrices, sems = refs[n + 6 :]
+    msgs, (rows_ref, q, c, k_out, v_out) = refs[:n], refs[n : n + 5]
+    keys, values, pgates, gates, mask, ids_ref, lens_ref, adv_ref, matrices, sems = refs[n + 5 :]
     pairs = [(pgates_hbm, pgates), (gates_hbm, gates), (mask_hbm, mask)]
     pairs += [(ids_hbm, ids_ref), (lens_hbm, lens_ref), (adv_hbm, adv_ref), (keys_hbm, keys), (values_hbm, values)]
     count = gates.shape[0]
@@ -104,12 +108,11 @@
         live = mask[i : i + 1, :].astype(F32) * opened * weight
         rows += [cum[H * i : H * i + H], carried[H * i : H * i + H] * opened, live, opened, jnp.zeros((2, slots), F32)]
         factors.append(carried[H * i : H * i + H] * live)
-    rows_ref[...] = jnp.concatenate(rows, axis=0).reshape(count, 8, slots)
     piece = cum[H * count : H * count + H]
     total = piece[:, -1:]
     suffix = total - piece
-    rows += [suffix, jnp.zeros((128 - 8 * count - H, slots), F32)]
-    cols_ref[...] = jnp.concatenate(rows, axis=0).T
+    rows += [suffix, jnp.zeros((8 - H, slots), F32)]
+    rows_ref[...] = jnp.concatenate(rows, axis=0)
 
     for copy in copies[6:8]:
         copy.wait()
@@ -149,7 +152,7 @@
 
 def second_kernel(n, chips, cores, *refs):
     z_at = lax.axis_index("z")
-    got, msgs, later_ref, sums = refs[:n], refs[n + 1 : n + 1 + chips], refs[-2], refs[-1]
+    got, msgs, later_ref, sums = far_first(refs[:n]), refs[n + 1 : n + 1 + chips], refs[-2], refs[-1]
     part = DH // n
     block = H * part
     responses = (got[0].shape[0] - block - 16) // block
@@ -181,7 +184,7 @@
 
 
 def swap_kernel(chips, *refs):
-    got, sent_ref, kept_ref = refs[:chips], refs[chips + 1], refs[chips + 2]
+    got, sent_ref, kept_ref = far_first(refs[:chips]), refs[chips + 1], refs[chips + 2]
     block = got[0].shape[0] // 3
     totals = []
     for c in range(2):
@@ -200,7 +203,7 @@
 
 def third_kernel(n, chips, *refs):
     z_at, core = lax.axis_index("z"), lax.axis_index("core")
-    noted, kept_ref, got_ref, msgs = refs[:n], refs[n], refs[n + 1], refs[n + 3 :]
+    noted, kept_ref, got_ref, msgs = far_first(refs[:n]), refs[n], refs[n + 1], refs[n + 3 :]
     block = H * DH // n
     responses = (noted[0].shape[0] - block - 16) // block
     total = kept_ref[chips * block :, :].astype(F32) + got_ref[chips * block :, :].astype(F32)
@@ -217,11 +220,14 @@
         msgs[k][responses * block :, :] = total
 
 
-def sweep_kernel(units, done, cols_ref, rows_ref, q_ref, k_ref, v_ref, c_ref, *refs):
+def sweep_kernel(units, done, rows_ref, q_ref, k_ref, v_ref, c_ref, cols_ref, *refs):
     writes = len(done) > 0
     if writes:
         *refs, dk_hbm, dv_hbm, sems = refs
     out_ref, dq_ref, query_ref, grad_ref, dk_ref, dv_ref, token_ref = refs[-7:]
+    if cols_ref is None:
+        cols_ref = refs[0]
+        cols_ref[...] = to_columns(rows_ref[...])
     copies = []
 
     def send(r):
@@ -256,7 +262,7 @@
     for r, h in units:
         lanes = slice(h * DH, (h + 1) * DH)
         cum = cols_ref[:, 8 * r + h : 8 * r + h + 1] * LOG2E
-        row = rows_ref[r, h : h + 1, :] * LOG2E
+        row = rows_ref[8 * r + h : 8 * r + h + 1, :] * LOG2E
         live = cols_ref[:, 8 * r + 4 : 8 * r + 5]
         opened = cols_ref[:, 8 * r + 5 : 8 * r + 6]
         grad_all = (c_ref[r, :, lanes].astype(F32) * live).astype(BF16)
@@ -348,6 +354,10 @@
     return [xs[0]] + [lax.ppermute(xs[k], axis, [(s, s ^ k) for s in range(n)]) for k in range(1, n)]
 
 
+def far_first(refs):
+    return [refs[0], *refs[:0:-1]]
+
+
 def partners(n):
     me = lax.axis_index("prompt")
     return [lax.bitwise_xor(me, k) for k in range(n)]
@@ -377,10 +387,10 @@
     outs = pl.pallas_call(
         lambda *refs: first_kernel(n, *refs),
         out_shape=[shape((block * (1 + responses) + 16, DH), BF16)] * n
-        + [shape((slots, 128), F32), shape((responses, 8, slots), F32)]
+        + [shape((8 * (responses + 1), slots), F32)]
         + [shape(queries.shape, BF16)] * 4,
         in_specs=[ANY] * 12,
-        out_specs=[VMEM] * (n + 6),
+        out_specs=[VMEM] * (n + 5),
         scratch_shapes=[
             pltpu.VMEM(keys.shape, BF16),
             pltpu.VMEM(values.shape, BF16),
@@ -399,28 +409,41 @@
         *[in_hbm(x) for x in (group_ids, resp_lengths, advantages, keys, values, prompt_gates, resp_gates)],
         *[in_hbm(x) for x in (loss_mask, queries, cotangent, resp_keys, resp_values)],
     )
-    msgs, (cols, rows, queries, cotangent, resp_keys, resp_values) = outs[:n], outs[n:]
+    msgs, (rows, queries, cotangent, resp_keys, resp_values) = outs[:n], outs[n:]
 
     like = shape(queries.shape, F32)
     like_out = shape(queries.shape, BF16)
+
+    held_shapes = [like, like] + [like_out] * 4 + [shape((8, 128), F32)]
+
+    def first_sweep(units):
+        outs = pl.pallas_call(
+            lambda *refs: sweep_kernel(units, (), *refs[:5], None, *refs[5:]),
+            out_shape=[shape((slots, 128), F32)] + held_shapes,
+            in_specs=[VMEM] * 5,
+            out_specs=[VMEM] * 8,
+            compiler_params=params(),
+            name="sweep",
+        )(rows, queries, resp_keys, resp_values, cotangent)
+        return outs[0], outs[1:7], outs[7]
 
     def sweep(units, before, token, done=()):
         writes = len(done) > 0
         outs = pl.pallas_call(
             lambda *refs: sweep_kernel(units, done, *refs),
-            out_shape=[like, like] + [like_out] * 4 + [shape((8, 128), F32)] + [like_out] * (2 * writes),
-            in_specs=[VMEM] * 6 + [ANY] * (1 + len(before)),
+            out_shape=held_shapes + [like_out] * (2 * writes),
+            in_specs=[VMEM] * 6 + [ANY] * 7,
             out_specs=[VMEM] * 7 + [ANY] * (2 * writes),
             scratch_shapes=[pltpu.SemaphoreType.DMA((2 * responses,))] * writes,
-            input_output_aliases={7 + k: k for k in range(len(before))},
+            input_output_aliases={7 + k: k for k in range(6)},
             compiler_params=params(),
             name="sweep",
-        )(cols, rows, queries, resp_keys, resp_values, cotangent, token, *before)
+        )(rows, queries, resp_keys, resp_values, cotangent, cols, token, *before)
         return (outs[:4] + outs[7:] if writes else outs[:6]), outs[6]
 
     units = [(r, h) for r in range(responses) for h in range(H)]
-    got1 = exchange(msgs, "prompt")
-    held, token = sweep(units[:3], [], cols)
+    got1 = far_first(exchange(msgs, "prompt"))
+    cols, held, token = first_sweep(units[:3])
     outs = pl.pallas_call(
         lambda *refs: second_kernel(n, chips, cores, *refs),
         out_shape=[shape(((1 + cores) * block, DH), BF16)] * chips + [shape((8, DH), F32)],
@@ -431,7 +454,7 @@
         name="second",
     )(*got1, token)
     msgs, later = outs[:chips], outs[chips]
-    got2 = exchange(msgs, "z")
+    got2 = far_first(exchange(msgs, "z"))
     held, token = sweep(units[3:5], held, later)
     sent, kept = pl.pallas_call(
         lambda *refs: swap_kernel(chips, *refs),

time: 34.7 us -> 32.8 us (0.945)
  waiting for transfers between devices: 7.6 us -> 5.4 us
    pallas_call x0 -> x1, Pallas kernels: none -> 2.86 us  [first_sweep(): pl.pallas_call(lambda *refs: sweep_kernel(units, (), *refs[:5], None, *re...]
    pallas_call x4 -> x3, Pallas kernels: 7.88 us -> 5.4 us  [sweep(): pl.pallas_call(lambda *refs: sweep_kernel(units, done, *refs), out_shape=...]
    ppermute x10, waiting for transfers between devices: 7.6 us -> 5.4 us  [exchange(): lax.ppermute(xs[k], axis, [(s, s ^ k) for s in range(n)])]
  transfers between devices with their start and end apart: 10 -> 10, of which waited for: 6 -> 6; matrix products, arithmetic and copies ran while one was open for 0% -> 0% of each run, Pallas kernels for 23% -> 25%
where the time goes in v6:
time: 32.8 us; the launch traced here: 32.6 us
  Pallas kernels  13.8 us (42%)
  starting transfers between devices  12.7 us (39%)
  waiting for transfers between devices  5.4 us (16%)
  between operations  0.73 us (2%)
    ppermute x10, starting transfers between devices, exchange(): lax.ppermute(xs[k], axis, [(s, s ^ k) for s in range(n)])  12.7 us
    ppermute x10, waiting for transfers between devices, exchange(): lax.ppermute(xs[k], axis, [(s, s ^ k) for s in range(n)])  5.4 us
    pallas_call x3, Pallas kernels, sweep(): pl.pallas_call(lambda *refs: sweep_kernel(units, done, *refs), out_shape=...  5.4 us
    pallas_call x1, Pallas kernels, shards(): pl.pallas_call(lambda *refs: first_kernel(n, *refs), out_shape=[shape((bl...  3.1 us
    pallas_call x1, Pallas kernels, first_sweep(): pl.pallas_call(lambda *refs: sweep_kernel(units, (), *refs[:5], None, *re...  2.86 us
    pallas_call x1, Pallas kernels, shards(): pl.pallas_call(lambda *refs: last_kernel(n, responses, *refs), out_shape=...  1.93 us
  transfers between devices with their start and end apart: 10, of which 6 were waited for; matrix products, arithmetic and copies ran while one was open for 0% of the time, Pallas kernels for 25%

profile of v6, /device:TPU:0, one launch (start us, length us, event | category | flops | bytes accessed | tf_op | source)
XLA Modules:
  0.0 32.6 jit_solution(1612562974465343817)
XLA Ops:
  0.6 3.1 %first.1 = (bf16[336,128]{1,0:T(8,128)(2,1)S(1)}, bf16[336,128]{1,0:T(8,128)(2,1)S(1)}, bf16[336,128]{1,0:T(8,128)(2,1)S(1)}, bf16[336,128]{1,0:T(8,128)(2,1)S(1...) custom-call(s32[4]{0:T(128)} %refs_0_.1, ...), custom_call_target="tpu_custom_call" | custom-call | tf_op jit(solution)/shard_map/first/pallas_call | solution.py:387
  3.7 4.0 %collective-permute-start = (bf16[336,128]{1,0:T(8,128)(2,1)S(1)}, bf16[336,128]{1,0:T(8,128)(2,1)S(1)}, u32[]{:S(2)}, u32[]{:S(2)}) collective-permute-start(bf16[336,128]{1,0:T(8,128)(2,1)S(1)} %get-tuple-element.66), channel_id=1, source_target_pairs={{0,24},{8,16},{16,8},{24,0},{1,25},{9,17},{17,9},{25,1},{2,26},{10... | collective-permute-start | bytes 258056 | tf_op jit(solution)/shard_map/ppermute | solution.py:354
  7.7 0.5 %collective-permute-start.1 = (bf16[336,128]{1,0:T(8,128)(2,1)S(1)}, bf16[336,128]{1,0:T(8,128)(2,1)S(1)}, u32[]{:S(2)}, u32[]{:S(2)}) collective-permute-start(bf16[336,128]{1,0:T(8,128)(2,1)S(1)} %get-tuple-element.67), channel_id=1, source_target_pairs={{0,16},{8,24},{16,0},{24,8},{1,17},{9,25},{17,1},{25,9},{2,18},{10... | collective-permute-start | bytes 258056 | tf_op jit(solution)/shard_map/ppermute | solution.py:354
  8.2 0.1 collective-permute-start.2
  8.4 2.9 %sweep.4 = (f32[512,128]{1,0:T(8,128)S(1)}, f32[4,512,256]{2,1,0:T(8,128)S(1)}, f32[4,512,256]{2,1,0:T(8,128)S(1)}, bf16[4,512,256]{2,1,0:T(8,128)(2,1)S(1)}, bf...) custom-call(f32[40,512]{1,0:T(8,128)S(1)} %get-tuple-element.59.refs, ...), custom_call_target="tpu_custom_call" | custom-call | tf_op jit(solution)/shard_map/sweep/pallas_call | solution.py:420
  11.2 0.0 collective-permute-done.refs_1_
  11.2 1.0 %collective-permute-done.1.refs_2_ = bf16[336,128]{1,0:T(8,128)(2,1)S(1)} collective-permute-done((bf16[336,128]{1,0:T(8,128)(2,1)S(1)}, bf16[336,128]{1,0:T(8,128)(2,1)S(1)}, u32[]{:S(2)}, u32[]{:S(2)}) %collective-permute-start.1) | collective-permute-done | bytes 86048 | tf_op jit(solution)/shard_map/ppermute | solution.py:354
  12.2 0.5 %collective-permute-done.2.refs_3_ = bf16[336,128]{1,0:T(8,128)(2,1)S(1)} collective-permute-done((bf16[336,128]{1,0:T(8,128)(2,1)S(1)}, bf16[336,128]{1,0:T(8,128)(2,1)S(1)}, u32[]{:S(2)}, u32[]{:S(2)}) %collective-permute-start.2) | collective-permute-done | bytes 86048 | tf_op jit(solution)/shard_map/ppermute | solution.py:354
  12.7 0.2 second.1
  12.9 3.7 %collective-permute-start.3 = (bf16[192,128]{1,0:T(8,128)(2,1)S(1)}, bf16[192,128]{1,0:T(8,128)(2,1)S(1)}, u32[]{:S(2)}, u32[]{:S(2)}) collective-permute-start(bf16[192,128]{1,0:T(8,128)(2,1)S(1)} %get-tuple-element.71), channel_id=1, source_target_pairs={{0,6},{2,4},{4,2},{6,0},{1,7},{3,5},{5,3},{7,1},{8,14},{10,12},{12... | collective-permute-start | bytes 147464 | tf_op jit(solution)/shard_map/ppermute | solution.py:354
  16.6 0.0 collective-permute-start.4
  16.6 0.8 %collective-permute-start.5 = (bf16[192,128]{1,0:T(8,128)(2,1)S(1)}, bf16[192,128]{1,0:T(8,128)(2,1)S(1)}, u32[]{:S(2)}, u32[]{:S(2)}) collective-permute-start(bf16[192,128]{1,0:T(8,128)(2,1)S(1)} %get-tuple-element.73), channel_id=1, source_target_pairs={{0,2},{2,0},{4,6},{6,4},{1,3},{3,1},{5,7},{7,5},{8,10},{10,8},{12,... | collective-permute-start | bytes 147464 | tf_op jit(solution)/shard_map/ppermute | solution.py:354
  17.4 1.8 %sweep.5 = (f32[4,512,256]{2,1,0:T(8,128)S(1)}, f32[4,512,256]{2,1,0:T(8,128)S(1)}, bf16[4,512,256]{2,1,0:T(8,128)(2,1)S(1)}, bf16[4,512,256]{2,1,0:T(8,128)(2,1...) custom-call(f32[40,512]{1,0:T(8,128)S(1)} %get-tuple-element.59.refs, ...), custom_call_target="tpu_custom_call", output_to_operand_aliasing={{0}: (7, {}), {1}: (8, {}), {2}: (9, {}), {3}: (10, {}), {4... | custom-call | tf_op jit(solution)/shard_map/sweep/pallas_call | solution.py:432
  19.2 0.0 collective-permute-done.3.refs_1_
  19.2 2.4 %collective-permute-done.4.refs_2_ = bf16[192,128]{1,0:T(8,128)(2,1)S(1)} collective-permute-done((bf16[192,128]{1,0:T(8,128)(2,1)S(1)}, bf16[192,128]{1,0:T(8,128)(2,1)S(1)}, u32[]{:S(2)}, u32[]{:S(2)}) %collective-permute-start.4) | collective-permute-done | bytes 49184 | tf_op jit(solution)/shard_map/ppermute | solution.py:354
  21.6 0.0 collective-permute-done.5.refs_3_
  21.7 0.1 collective-permute-start.6
  21.7 1.0 %sweep.6 = (f32[4,512,256]{2,1,0:T(8,128)S(1)}, f32[4,512,256]{2,1,0:T(8,128)S(1)}, bf16[4,512,256]{2,1,0:T(8,128)(2,1)S(1)}, bf16[4,512,256]{2,1,0:T(8,128)(2,1...) custom-call(f32[40,512]{1,0:T(8,128)S(1)} %get-tuple-element.59.refs, ...), custom_call_target="tpu_custom_call", output_to_operand_aliasing={{0}: (7, {}), {1}: (8, {}), {2}: (9, {}), {3}: (10, {}), {4... | custom-call | tf_op jit(solution)/shard_map/sweep/pallas_call | solution.py:432
  22.7 0.3 collective-permute-done.6.refs_5_
  23.0 0.2 third.1
  23.2 1.2 %collective-permute-start.7 = (bf16[320,128]{1,0:T(8,128)(2,1)S(1)}, bf16[320,128]{1,0:T(8,128)(2,1)S(1)}, u32[]{:S(2)}, u32[]{:S(2)}) collective-permute-start(bf16[320,128]{1,0:T(8,128)(2,1)S(1)} %get-tuple-element.102), channel_id=1, source_target_pairs={{0,8},{8,0},{16,24},{24,16},{1,9},{9,1},{17,25},{25,17},{2,10},{10... | collective-permute-start | bytes 245768 | tf_op jit(solution)/shard_map/ppermute | solution.py:354
  24.4 0.9 %collective-permute-start.8 = (bf16[320,128]{1,0:T(8,128)(2,1)S(1)}, bf16[320,128]{1,0:T(8,128)(2,1)S(1)}, u32[]{:S(2)}, u32[]{:S(2)}) collective-permute-start(bf16[320,128]{1,0:T(8,128)(2,1)S(1)} %get-tuple-element.103), channel_id=1, source_target_pairs={{0,16},{8,24},{16,0},{24,8},{1,17},{9,25},{17,1},{25,9},{2,18},{10... | collective-permute-start | bytes 245768 | tf_op jit(solution)/shard_map/ppermute | solution.py:354
  25.3 1.4 %collective-permute-start.9 = (bf16[320,128]{1,0:T(8,128)(2,1)S(1)}, bf16[320,128]{1,0:T(8,128)(2,1)S(1)}, u32[]{:S(2)}, u32[]{:S(2)}) collective-permute-start(bf16[320,128]{1,0:T(8,128)(2,1)S(1)} %get-tuple-element.104), channel_id=1, source_target_pairs={{0,24},{8,16},{16,8},{24,0},{1,25},{9,17},{17,9},{25,1},{2,26},{10... | collective-permute-start | bytes 245768 | tf_op jit(solution)/shard_map/ppermute | solution.py:354
  26.8 0.0 copy-start
  26.8 0.0 copy-start.1
  26.8 2.6 %sweep.7 = (f32[4,512,256]{2,1,0:T(8,128)S(1)}, f32[4,512,256]{2,1,0:T(8,128)S(1)}, bf16[4,512,256]{2,1,0:T(8,128)(2,1)S(1)}, bf16[4,512,256]{2,1,0:T(8,128)(2,1...) custom-call(f32[40,512]{1,0:T(8,128)S(1)} %get-tuple-element.59.refs, ...), custom_call_target="tpu_custom_call", output_to_operand_aliasing={{0}: (7, {}), {1}: (8, {}), {2}: (9, {}), {3}: (10, {}), {4... | custom-call | tf_op jit(solution)/shard_map/sweep/pallas_call | solution.py:432
  29.4 0.0 collective-permute-done.7.refs_9_
  29.4 0.2 collective-permute-done.8.refs_10_
  29.7 1.0 %collective-permute-done.9.refs_11_ = bf16[320,128]{1,0:T(8,128)(2,1)S(1)} collective-permute-done((bf16[320,128]{1,0:T(8,128)(2,1)S(1)}, bf16[320,128]{1,0:T(8,128)(2,1)S(1)}, u32[]{:S(2)}, u32[]{:S(2)}) %collective-permute-start.9) | collective-permute-done | bytes 81952 | tf_op jit(solution)/shard_map/ppermute | solution.py:354
  30.7 0.0 copy-done
  30.7 0.0 copy-done.1
  30.7 1.9 %last.1 = (bf16[4,512,256]{2,1,0:T(8,128)(2,1)}, bf16[4,512,256]{2,1,0:T(8,128)(2,1)}, bf16[1,256,256]{2,1,0:T(8,128)(2,1)}, bf16[1,256,256]{2,1,0:T(8,128)(2,1)}) custom-call(f32[512,128]{1,0:T(8,128)S(1)} %get-tuple-element.64.refs_5_.refs_0_, bf16[4,512,256]{2,1,0:T(8,128)(2,1)S(1)} %get-tuple-element.98.refs_1_, ...), custom_call_target="tpu_custom_call" | custom-call | tf_op jit(solution)/shard_map/last/pallas_call | solution.py:481
  (1 shorter events, 0.0 us)
Async XLA Ops:
  3.7 7.5 %collective-permute-start = (bf16[336,128]{1,0:T(8,128)(2,1)S(1)}, bf16[336,128]{1,0:T(8,128)(2,1)S(1)}, u32[]{:S(2)}, u32[]{:S(2)}) collective-permute-start(bf16[336,128]{1,0:T(8,128)(2,1)S(1)} %get-tuple-element.66), channel_id=1, source_target_pairs={{0,24},{8,16},{16,8},{24,0},{1,25},{9,17},{17,9},{25,1},{2,26},{10... | collective-permute-start | bytes 258056 | tf_op jit(solution)/shard_map/ppermute | solution.py:354
  7.7 4.5 %collective-permute-start.1 = (bf16[336,128]{1,0:T(8,128)(2,1)S(1)}, bf16[336,128]{1,0:T(8,128)(2,1)S(1)}, u32[]{:S(2)}, u32[]{:S(2)}) collective-permute-start(bf16[336,128]{1,0:T(8,128)(2,1)S(1)} %get-tuple-element.67), channel_id=1, source_target_pairs={{0,16},{8,24},{16,0},{24,8},{1,17},{9,25},{17,1},{25,9},{2,18},{10... | collective-permute-start | bytes 258056 | tf_op jit(solution)/shard_map/ppermute | solution.py:354
  8.2 4.5 %collective-permute-start.2 = (bf16[336,128]{1,0:T(8,128)(2,1)S(1)}, bf16[336,128]{1,0:T(8,128)(2,1)S(1)}, u32[]{:S(2)}, u32[]{:S(2)}) collective-permute-start(bf16[336,128]{1,0:T(8,128)(2,1)S(1)} %get-tuple-element.68), channel_id=1, source_target_pairs={{0,8},{8,0},{16,24},{24,16},{1,9},{9,1},{17,25},{25,17},{2,10},{10... | collective-permute-start | bytes 258056 | tf_op jit(solution)/shard_map/ppermute | solution.py:354
  12.9 6.3 %collective-permute-start.3 = (bf16[192,128]{1,0:T(8,128)(2,1)S(1)}, bf16[192,128]{1,0:T(8,128)(2,1)S(1)}, u32[]{:S(2)}, u32[]{:S(2)}) collective-permute-start(bf16[192,128]{1,0:T(8,128)(2,1)S(1)} %get-tuple-element.71), channel_id=1, source_target_pairs={{0,6},{2,4},{4,2},{6,0},{1,7},{3,5},{5,3},{7,1},{8,14},{10,12},{12... | collective-permute-start | bytes 147464 | tf_op jit(solution)/shard_map/ppermute | solution.py:354
  16.6 5.0 %collective-permute-start.4 = (bf16[192,128]{1,0:T(8,128)(2,1)S(1)}, bf16[192,128]{1,0:T(8,128)(2,1)S(1)}, u32[]{:S(2)}, u32[]{:S(2)}) collective-permute-start(bf16[192,128]{1,0:T(8,128)(2,1)S(1)} %get-tuple-element.72), channel_id=1, source_target_pairs={{0,4},{2,6},{4,0},{6,2},{1,5},{3,7},{5,1},{7,3},{8,12},{10,14},{12... | collective-permute-start | bytes 147464 | tf_op jit(solution)/shard_map/ppermute | solution.py:354
  16.6 5.0 %collective-permute-start.5 = (bf16[192,128]{1,0:T(8,128)(2,1)S(1)}, bf16[192,128]{1,0:T(8,128)(2,1)S(1)}, u32[]{:S(2)}, u32[]{:S(2)}) collective-permute-start(bf16[192,128]{1,0:T(8,128)(2,1)S(1)} %get-tuple-element.73), channel_id=1, source_target_pairs={{0,2},{2,0},{4,6},{6,4},{1,3},{3,1},{5,7},{7,5},{8,10},{10,8},{12,... | collective-permute-start | bytes 147464 | tf_op jit(solution)/shard_map/ppermute | solution.py:354
  21.7 1.3 %collective-permute-start.6 = (bf16[320,128]{1,0:T(8,128)(2,1)S(1)}, bf16[320,128]{1,0:T(8,128)(2,1)S(1)}, u32[]{:S(2)}, u32[]{:S(2)}) collective-permute-start(bf16[320,128]{1,0:T(8,128)(2,1)S(1)} %get-tuple-element.83), channel_id=1, source_target_pairs={{0,1},{1,0},{2,3},{3,2},{4,5},{5,4},{6,7},{7,6},{8,9},{9,8},{10,11... | collective-permute-start | bytes 245768 | tf_op jit(solution)/shard_map/ppermute | solution.py:354
  23.2 6.2 %collective-permute-start.7 = (bf16[320,128]{1,0:T(8,128)(2,1)S(1)}, bf16[320,128]{1,0:T(8,128)(2,1)S(1)}, u32[]{:S(2)}, u32[]{:S(2)}) collective-permute-start(bf16[320,128]{1,0:T(8,128)(2,1)S(1)} %get-tuple-element.102), channel_id=1, source_target_pairs={{0,8},{8,0},{16,24},{24,16},{1,9},{9,1},{17,25},{25,17},{2,10},{10... | collective-permute-start | bytes 245768 | tf_op jit(solution)/shard_map/ppermute | solution.py:354
  24.4 5.3 %collective-permute-start.8 = (bf16[320,128]{1,0:T(8,128)(2,1)S(1)}, bf16[320,128]{1,0:T(8,128)(2,1)S(1)}, u32[]{:S(2)}, u32[]{:S(2)}) collective-permute-start(bf16[320,128]{1,0:T(8,128)(2,1)S(1)} %get-tuple-element.103), channel_id=1, source_target_pairs={{0,16},{8,24},{16,0},{24,8},{1,17},{9,25},{17,1},{25,9},{2,18},{10... | collective-permute-start | bytes 245768 | tf_op jit(solution)/shard_map/ppermute | solution.py:354
  25.3 5.3 %collective-permute-start.9 = (bf16[320,128]{1,0:T(8,128)(2,1)S(1)}, bf16[320,128]{1,0:T(8,128)(2,1)S(1)}, u32[]{:S(2)}, u32[]{:S(2)}) collective-permute-start(bf16[320,128]{1,0:T(8,128)(2,1)S(1)} %get-tuple-element.104), channel_id=1, source_target_pairs={{0,24},{8,16},{16,8},{24,0},{1,25},{9,17},{17,9},{25,1},{2,26},{10... | collective-permute-start | bytes 245768 | tf_op jit(solution)/shard_map/ppermute | solution.py:354
  26.8 3.9 %copy-start = (bf16[1,256,256]{2,1,0:T(8,128)(2,1)S(1)}, bf16[1,256,256]{2,1,0:T(8,128)(2,1)}, u32[]{:S(2)}) copy-start(bf16[1,256,256]{2,1,0:T(8,128)(2,1)} %refs_5_.3) | copy-start | bytes 393220
  26.8 3.9 %copy-start.1 = (bf16[1,256,256]{2,1,0:T(8,128)(2,1)S(1)}, bf16[1,256,256]{2,1,0:T(8,128)(2,1)}, u32[]{:S(2)}) copy-start(bf16[1,256,256]{2,1,0:T(8,128)(2,1)} %refs_6_.3) | copy-start | bytes 393220

commit v7 on v6

--- a/solution.py
+++ b/solution.py
@@ -72,13 +72,12 @@
     msgs, (rows_ref, q, c, k_out, v_out) = refs[:n], refs[n : n + 5]
     keys, values, pgates, gates, mask, ids_ref, lens_ref, adv_ref, matrices, sems = refs[n + 5 :]
     pairs = [(pgates_hbm, pgates), (gates_hbm, gates), (mask_hbm, mask)]
-    pairs += [(ids_hbm, ids_ref), (lens_hbm, lens_ref), (adv_hbm, adv_ref), (keys_hbm, keys), (values_hbm, values)]
+    pairs += [(ids_hbm, ids_ref), (lens_hbm, lens_ref), (adv_hbm, adv_ref), (keys_hbm, keys), (q_hbm, q)]
+    pairs += [(values_hbm, values)]
     count = gates.shape[0]
     slots = gates.shape[2]
     tokens = keys.shape[1]
-    for i in range(count):
-        pairs += [(q_hbm.at[i], q.at[i]), (c_hbm.at[i], c.at[i])]
-    pairs += [(k_hbm, k_out), (v_hbm, v_out)]
+    pairs += [(c_hbm.at[i], c.at[i]) for i in range(count)] + [(k_hbm, k_out), (v_hbm, v_out)]
     copies = [pltpu.make_async_copy(a, b, sems.at[i]) for i, (a, b) in enumerate(pairs)]
     for copy in copies:
         copy.start()
@@ -93,8 +92,10 @@
                 at, of, :
             ].astype(BF16)
 
-    for copy in copies[:6]:
+    for copy in copies[:8]:
         copy.wait()
+    turned_keys = keys[0].T
+    turned = [q[i].T for i in range(count)]
     piece = jnp.concatenate([pgates[0], jnp.zeros((H, slots - tokens), F32)], axis=1)
     gate_rows = [gates[i] for i in range(count)] + [piece, jnp.zeros((16 - H * (count + 1), slots), F32)]
     cum = lane_cumsum(jnp.concatenate(gate_rows, axis=0))
@@ -114,13 +115,11 @@
     rows += [suffix, jnp.zeros((8 - H, slots), F32)]
     rows_ref[...] = jnp.concatenate(rows, axis=0)
 
-    for copy in copies[6:8]:
-        copy.wait()
-    turned = keys[0].T
+    copies[8].wait()
     later = jnp.exp(suffix[:, :tokens])
     for h in range(H):
         lanes = slice(h * DH, (h + 1) * DH)
-        scaled = turned[lanes].astype(F32) * later[h : h + 1]
+        scaled = turned_keys[lanes].astype(F32) * later[h : h + 1]
         high = scaled.astype(BF16)
         low = (scaled - high.astype(F32)).astype(BF16)
         both = mm(jnp.concatenate([high, low], axis=0), values[0, :, lanes])
@@ -134,15 +133,13 @@
         msgs[k][block : block + 16, :] = notes
 
     for i in range(count):
-        copies[8 + 2 * i].wait()
-        turned = q[i].T
-        copies[9 + 2 * i].wait()
+        copies[9 + i].wait()
         for h in range(H):
             lanes = slice(h * DH, (h + 1) * DH)
-            scaled = (turned[lanes].astype(F32) * factors[i][h : h + 1]).astype(BF16)
+            scaled = (turned[i][lanes].astype(F32) * factors[i][h : h + 1]).astype(BF16)
             matrices[H * (1 + i) + h] = mm(scaled, c[i, :, lanes])
             spread(H * (1 + i) + h)
-    for copy in copies[8 + 2 * count :]:
+    for copy in copies[9 + count :]:
         copy.wait()
 
 
@@ -177,14 +174,14 @@
             sums[noted_prompt(notes[k], i)] += got[k][at : at + block, :].astype(F32)
     final = final.astype(BF16)
     for k in range(chips):
-        z = lax.bitwise_xor(z_at, k)
+        z = lax.rem(z_at + k, chips)
         msgs[k][0:block, :] = final
         for c in range(cores):
             msgs[k][(1 + c) * block : (2 + c) * block, :] = sums[z * cores + c].astype(BF16)
 
 
 def swap_kernel(chips, *refs):
-    got, sent_ref, kept_ref = far_first(refs[:chips]), refs[chips + 1], refs[chips + 2]
+    got, sent_ref, kept_ref = refs[:chips], refs[chips + 1], refs[chips + 2]
     block = got[0].shape[0] // 3
     totals = []
     for c in range(2):
@@ -212,7 +209,7 @@
         notes = noted[k][block : block + 16, :].astype(F32)
         for i in range(responses):
             p = noted_prompt(notes, i)
-            slot = lax.bitwise_xor(z_at, lax.div(p, 2))
+            slot = lax.rem(z_at + chips - lax.div(p, 2), chips)
             at = pl.ds(pl.multiple_of(slot * block, block), block)
             same = lax.rem(p, 2) == core
             state = jnp.where(same, kept_ref[at, :].astype(F32), got_ref[at, :].astype(F32))
@@ -354,6 +351,11 @@
     return [xs[0]] + [lax.ppermute(xs[k], axis, [(s, s ^ k) for s in range(n)]) for k in range(1, n)]
 
 
+def exchange_ring(xs, axis):
+    n = lax.axis_size(axis)
+    return [xs[0]] + [lax.ppermute(xs[k], axis, [(s, (s + k) % n) for s in range(n)]) for k in range(1, n)]
+
+
 def far_first(refs):
     return [refs[0], *refs[:0:-1]]
 
@@ -401,7 +403,7 @@
             pltpu.SMEM(resp_lengths.shape, jnp.int32),
             pltpu.SMEM(advantages.shape, jnp.int32),
             pltpu.VMEM((H * (1 + responses), DH, DH), F32),
-            pltpu.SemaphoreType.DMA((10 + 2 * responses,)),
+            pltpu.SemaphoreType.DMA((11 + responses,)),
         ],
         compiler_params=params(32),
         name="first",
@@ -454,7 +456,7 @@
         name="second",
     )(*got1, token)
     msgs, later = outs[:chips], outs[chips]
-    got2 = far_first(exchange(msgs, "z"))
+    got2 = exchange_ring(msgs, "z")
     held, token = sweep(units[3:5], held, later)
     sent, kept = pl.pallas_call(
         lambda *refs: swap_kernel(chips, *refs),

time: 32.8 us -> 32.7 us (level)
  waiting for transfers between devices: 5.4 us -> 4.02 us
  starting transfers between devices: 12.7 us -> 13.8 us
    ppermute x0 -> x3, starting transfers between devices: none -> 5.56 us  [exchange_ring(): lax.ppermute(xs[k], axis, [(s, (s + k) % n) for s in range(n)])]
    ppermute x10 -> x7, starting transfers between devices: 12.7 us -> 8.25 us  [exchange(): lax.ppermute(xs[k], axis, [(s, s ^ k) for s in range(n)])]
    ppermute x10 -> x7, waiting for transfers between devices: 5.4 us -> 3.09 us  [exchange(): lax.ppermute(xs[k], axis, [(s, s ^ k) for s in range(n)])]
    ppermute x0 -> x3, waiting for transfers between devices: none -> 0.93 us  [exchange_ring(): lax.ppermute(xs[k], axis, [(s, (s + k) % n) for s in range(n)])]
  transfers between devices with their start and end apart: 10 -> 10, of which waited for: 6 -> 5; matrix products, arithmetic and copies ran while one was open for 0% -> 0% of each run, Pallas kernels for 25% -> 25%
where the time goes in v7:
time: 32.7 us; the launch traced here: 32.6 us
  Pallas kernels  14 us (43%)
  starting transfers between devices  13.8 us (42%)
  waiting for transfers between devices  4.02 us (12%)
  between operations  0.74 us (2%)
    ppermute x7, starting transfers between devices, exchange(): lax.ppermute(xs[k], axis, [(s, s ^ k) for s in range(n)])  8.25 us
    ppermute x3, starting transfers between devices, exchange_ring(): lax.ppermute(xs[k], axis, [(s, (s + k) % n) for s in range(n)])  5.56 us
    pallas_call x3, Pallas kernels, sweep(): pl.pallas_call(lambda *refs: sweep_kernel(units, done, *refs), out_shape=...  5.4 us
    pallas_call x1, Pallas kernels, shards(): pl.pallas_call(lambda *refs: first_kernel(n, *refs), out_shape=[shape((bl...  3.29 us
    ppermute x7, waiting for transfers between devices, exchange(): lax.ppermute(xs[k], axis, [(s, s ^ k) for s in range(n)])  3.09 us
    pallas_call x1, Pallas kernels, first_sweep(): pl.pallas_call(lambda *refs: sweep_kernel(units, (), *refs[:5], None, *re...  2.86 us
    pallas_call x1, Pallas kernels, shards(): pl.pallas_call(lambda *refs: last_kernel(n, responses, *refs), out_shape=...  1.92 us
    ppermute x3, waiting for transfers between devices, exchange_ring(): lax.ppermute(xs[k], axis, [(s, (s + k) % n) for s in range(n)])  0.93 us
  transfers between devices with their start and end apart: 10, of which 5 were waited for; matrix products, arithmetic and copies ran while one was open for 0% of the time, Pallas kernels for 25%

profile of v7, /device:TPU:0, one launch (start us, length us, event | category | flops | bytes accessed | tf_op | source)
XLA Modules:
  0.0 32.6 jit_solution(4657967890029421154)
XLA Ops:
  0.6 3.3 %first.1 = (bf16[336,128]{1,0:T(8,128)(2,1)S(1)}, bf16[336,128]{1,0:T(8,128)(2,1)S(1)}, bf16[336,128]{1,0:T(8,128)(2,1)S(1)}, bf16[336,128]{1,0:T(8,128)(2,1)S(1...) custom-call(s32[4]{0:T(128)} %refs_0_.1, ...), custom_call_target="tpu_custom_call" | custom-call | tf_op jit(solution)/shard_map/first/pallas_call | solution.py:389
  3.9 4.0 %collective-permute-start = (bf16[336,128]{1,0:T(8,128)(2,1)S(1)}, bf16[336,128]{1,0:T(8,128)(2,1)S(1)}, u32[]{:S(2)}, u32[]{:S(2)}) collective-permute-start(bf16[336,128]{1,0:T(8,128)(2,1)S(1)} %get-tuple-element.66), channel_id=1, source_target_pairs={{0,24},{8,16},{16,8},{24,0},{1,25},{9,17},{17,9},{25,1},{2,26},{10... | collective-permute-start | bytes 258056 | tf_op jit(solution)/shard_map/ppermute | solution.py:351
  7.9 0.5 %collective-permute-start.1 = (bf16[336,128]{1,0:T(8,128)(2,1)S(1)}, bf16[336,128]{1,0:T(8,128)(2,1)S(1)}, u32[]{:S(2)}, u32[]{:S(2)}) collective-permute-start(bf16[336,128]{1,0:T(8,128)(2,1)S(1)} %get-tuple-element.67), channel_id=1, source_target_pairs={{0,16},{8,24},{16,0},{24,8},{1,17},{9,25},{17,1},{25,9},{2,18},{10... | collective-permute-start | bytes 258056 | tf_op jit(solution)/shard_map/ppermute | solution.py:351
  8.4 0.1 collective-permute-start.2
  8.6 2.9 %sweep.4 = (f32[512,128]{1,0:T(8,128)S(1)}, f32[4,512,256]{2,1,0:T(8,128)S(1)}, f32[4,512,256]{2,1,0:T(8,128)S(1)}, bf16[4,512,256]{2,1,0:T(8,128)(2,1)S(1)}, bf...) custom-call(f32[40,512]{1,0:T(8,128)S(1)} %get-tuple-element.59.refs, ...), custom_call_target="tpu_custom_call" | custom-call | tf_op jit(solution)/shard_map/sweep/pallas_call | solution.py:422
  11.4 0.0 collective-permute-done.refs_1_
  11.4 1.0 %collective-permute-done.1.refs_2_ = bf16[336,128]{1,0:T(8,128)(2,1)S(1)} collective-permute-done((bf16[336,128]{1,0:T(8,128)(2,1)S(1)}, bf16[336,128]{1,0:T(8,128)(2,1)S(1)}, u32[]{:S(2)}, u32[]{:S(2)}) %collective-permute-start.1) | collective-permute-done | bytes 86048 | tf_op jit(solution)/shard_map/ppermute | solution.py:351
  12.4 0.5 %collective-permute-done.2.refs_3_ = bf16[336,128]{1,0:T(8,128)(2,1)S(1)} collective-permute-done((bf16[336,128]{1,0:T(8,128)(2,1)S(1)}, bf16[336,128]{1,0:T(8,128)(2,1)S(1)}, u32[]{:S(2)}, u32[]{:S(2)}) %collective-permute-start.2) | collective-permute-done | bytes 86048 | tf_op jit(solution)/shard_map/ppermute | solution.py:351
  12.9 0.2 second.1
  13.1 1.6 %collective-permute-start.3 = (bf16[192,128]{1,0:T(8,128)(2,1)S(1)}, bf16[192,128]{1,0:T(8,128)(2,1)S(1)}, u32[]{:S(2)}, u32[]{:S(2)}) collective-permute-start(bf16[192,128]{1,0:T(8,128)(2,1)S(1)} %get-tuple-element.71), channel_id=1, source_target_pairs={{0,2},{2,4},{4,6},{6,0},{1,3},{3,5},{5,7},{7,1},{8,10},{10,12},{12... | collective-permute-start | bytes 147464 | tf_op jit(solution)/shard_map/ppermute | solution.py:356
  14.8 2.6 %collective-permute-start.4 = (bf16[192,128]{1,0:T(8,128)(2,1)S(1)}, bf16[192,128]{1,0:T(8,128)(2,1)S(1)}, u32[]{:S(2)}, u32[]{:S(2)}) collective-permute-start(bf16[192,128]{1,0:T(8,128)(2,1)S(1)} %get-tuple-element.72), channel_id=1, source_target_pairs={{0,4},{2,6},{4,0},{6,2},{1,5},{3,7},{5,1},{7,3},{8,12},{10,14},{12... | collective-permute-start | bytes 147464 | tf_op jit(solution)/shard_map/ppermute | solution.py:356
  17.4 1.3 %collective-permute-start.5 = (bf16[192,128]{1,0:T(8,128)(2,1)S(1)}, bf16[192,128]{1,0:T(8,128)(2,1)S(1)}, u32[]{:S(2)}, u32[]{:S(2)}) collective-permute-start(bf16[192,128]{1,0:T(8,128)(2,1)S(1)} %get-tuple-element.73), channel_id=1, source_target_pairs={{0,6},{2,0},{4,2},{6,4},{1,7},{3,1},{5,3},{7,5},{8,14},{10,8},{12,... | collective-permute-start | bytes 147464 | tf_op jit(solution)/shard_map/ppermute | solution.py:356
  18.7 1.8 %sweep.5 = (f32[4,512,256]{2,1,0:T(8,128)S(1)}, f32[4,512,256]{2,1,0:T(8,128)S(1)}, bf16[4,512,256]{2,1,0:T(8,128)(2,1)S(1)}, bf16[4,512,256]{2,1,0:T(8,128)(2,1...) custom-call(f32[40,512]{1,0:T(8,128)S(1)} %get-tuple-element.59.refs, ...), custom_call_target="tpu_custom_call", output_to_operand_aliasing={{0}: (7, {}), {1}: (8, {}), {2}: (9, {}), {3}: (10, {}), {4... | custom-call | tf_op jit(solution)/shard_map/sweep/pallas_call | solution.py:434
  20.5 0.0 collective-permute-done.3.refs_1_
  20.5 0.0 collective-permute-done.4.refs_2_
  20.5 0.9 %collective-permute-done.5.refs_3_ = bf16[192,128]{1,0:T(8,128)(2,1)S(1)} collective-permute-done((bf16[192,128]{1,0:T(8,128)(2,1)S(1)}, bf16[192,128]{1,0:T(8,128)(2,1)S(1)}, u32[]{:S(2)}, u32[]{:S(2)}) %collective-permute-start.5) | collective-permute-done | bytes 49184 | tf_op jit(solution)/shard_map/ppermute | solution.py:356
  21.5 0.1 collective-permute-start.6
  21.6 1.0 %sweep.6 = (f32[4,512,256]{2,1,0:T(8,128)S(1)}, f32[4,512,256]{2,1,0:T(8,128)S(1)}, bf16[4,512,256]{2,1,0:T(8,128)(2,1)S(1)}, bf16[4,512,256]{2,1,0:T(8,128)(2,1...) custom-call(f32[40,512]{1,0:T(8,128)S(1)} %get-tuple-element.59.refs, ...), custom_call_target="tpu_custom_call", output_to_operand_aliasing={{0}: (7, {}), {1}: (8, {}), {2}: (9, {}), {3}: (10, {}), {4... | custom-call | tf_op jit(solution)/shard_map/sweep/pallas_call | solution.py:434
  22.5 0.3 collective-permute-done.6.refs_5_
  22.8 0.3 third.1
  23.1 1.3 %collective-permute-start.7 = (bf16[320,128]{1,0:T(8,128)(2,1)S(1)}, bf16[320,128]{1,0:T(8,128)(2,1)S(1)}, u32[]{:S(2)}, u32[]{:S(2)}) collective-permute-start(bf16[320,128]{1,0:T(8,128)(2,1)S(1)} %get-tuple-element.102), channel_id=1, source_target_pairs={{0,8},{8,0},{16,24},{24,16},{1,9},{9,1},{17,25},{25,17},{2,10},{10... | collective-permute-start | bytes 245768 | tf_op jit(solution)/shard_map/ppermute | solution.py:351
  24.4 0.8 %collective-permute-start.8 = (bf16[320,128]{1,0:T(8,128)(2,1)S(1)}, bf16[320,128]{1,0:T(8,128)(2,1)S(1)}, u32[]{:S(2)}, u32[]{:S(2)}) collective-permute-start(bf16[320,128]{1,0:T(8,128)(2,1)S(1)} %get-tuple-element.103), channel_id=1, source_target_pairs={{0,16},{8,24},{16,0},{24,8},{1,17},{9,25},{17,1},{25,9},{2,18},{10... | collective-permute-start | bytes 245768 | tf_op jit(solution)/shard_map/ppermute | solution.py:351
  25.2 1.4 %collective-permute-start.9 = (bf16[320,128]{1,0:T(8,128)(2,1)S(1)}, bf16[320,128]{1,0:T(8,128)(2,1)S(1)}, u32[]{:S(2)}, u32[]{:S(2)}) collective-permute-start(bf16[320,128]{1,0:T(8,128)(2,1)S(1)} %get-tuple-element.104), channel_id=1, source_target_pairs={{0,24},{8,16},{16,8},{24,0},{1,25},{9,17},{17,9},{25,1},{2,26},{10... | collective-permute-start | bytes 245768 | tf_op jit(solution)/shard_map/ppermute | solution.py:351
  26.6 0.0 copy-start
  26.7 0.0 copy-start.1
  26.7 2.6 %sweep.7 = (f32[4,512,256]{2,1,0:T(8,128)S(1)}, f32[4,512,256]{2,1,0:T(8,128)S(1)}, bf16[4,512,256]{2,1,0:T(8,128)(2,1)S(1)}, bf16[4,512,256]{2,1,0:T(8,128)(2,1...) custom-call(f32[40,512]{1,0:T(8,128)S(1)} %get-tuple-element.59.refs, ...), custom_call_target="tpu_custom_call", output_to_operand_aliasing={{0}: (7, {}), {1}: (8, {}), {2}: (9, {}), {3}: (10, {}), {4... | custom-call | tf_op jit(solution)/shard_map/sweep/pallas_call | solution.py:434
  29.3 0.0 collective-permute-done.7.refs_9_
  29.3 1.3 %collective-permute-done.8.refs_10_ = bf16[320,128]{1,0:T(8,128)(2,1)S(1)} collective-permute-done((bf16[320,128]{1,0:T(8,128)(2,1)S(1)}, bf16[320,128]{1,0:T(8,128)(2,1)S(1)}, u32[]{:S(2)}, u32[]{:S(2)}) %collective-permute-start.8) | collective-permute-done | bytes 81952 | tf_op jit(solution)/shard_map/ppermute | solution.py:351
  30.6 0.0 collective-permute-done.9.refs_11_
  30.6 0.0 copy-done
  30.6 0.0 copy-done.1
  30.7 1.9 %last.1 = (bf16[4,512,256]{2,1,0:T(8,128)(2,1)}, bf16[4,512,256]{2,1,0:T(8,128)(2,1)}, bf16[1,256,256]{2,1,0:T(8,128)(2,1)}, bf16[1,256,256]{2,1,0:T(8,128)(2,1)}) custom-call(f32[512,128]{1,0:T(8,128)S(1)} %get-tuple-element.64.refs_5_.refs_0_, bf16[4,512,256]{2,1,0:T(8,128)(2,1)S(1)} %get-tuple-element.98.refs_1_, ...), custom_call_target="tpu_custom_call" | custom-call | tf_op jit(solution)/shard_map/last/pallas_call | solution.py:483
  (1 shorter events, 0.0 us)
Async XLA Ops:
  3.9 7.5 %collective-permute-start = (bf16[336,128]{1,0:T(8,128)(2,1)S(1)}, bf16[336,128]{1,0:T(8,128)(2,1)S(1)}, u32[]{:S(2)}, u32[]{:S(2)}) collective-permute-start(bf16[336,128]{1,0:T(8,128)(2,1)S(1)} %get-tuple-element.66), channel_id=1, source_target_pairs={{0,24},{8,16},{16,8},{24,0},{1,25},{9,17},{17,9},{25,1},{2,26},{10... | collective-permute-start | bytes 258056 | tf_op jit(solution)/shard_map/ppermute | solution.py:351
  7.9 4.5 %collective-permute-start.1 = (bf16[336,128]{1,0:T(8,128)(2,1)S(1)}, bf16[336,128]{1,0:T(8,128)(2,1)S(1)}, u32[]{:S(2)}, u32[]{:S(2)}) collective-permute-start(bf16[336,128]{1,0:T(8,128)(2,1)S(1)} %get-tuple-element.67), channel_id=1, source_target_pairs={{0,16},{8,24},{16,0},{24,8},{1,17},{9,25},{17,1},{25,9},{2,18},{10... | collective-permute-start | bytes 258056 | tf_op jit(solution)/shard_map/ppermute | solution.py:351
  8.4 4.5 %collective-permute-start.2 = (bf16[336,128]{1,0:T(8,128)(2,1)S(1)}, bf16[336,128]{1,0:T(8,128)(2,1)S(1)}, u32[]{:S(2)}, u32[]{:S(2)}) collective-permute-start(bf16[336,128]{1,0:T(8,128)(2,1)S(1)} %get-tuple-element.68), channel_id=1, source_target_pairs={{0,8},{8,0},{16,24},{24,16},{1,9},{9,1},{17,25},{25,17},{2,10},{10... | collective-permute-start | bytes 258056 | tf_op jit(solution)/shard_map/ppermute | solution.py:351
  13.1 7.4 %collective-permute-start.3 = (bf16[192,128]{1,0:T(8,128)(2,1)S(1)}, bf16[192,128]{1,0:T(8,128)(2,1)S(1)}, u32[]{:S(2)}, u32[]{:S(2)}) collective-permute-start(bf16[192,128]{1,0:T(8,128)(2,1)S(1)} %get-tuple-element.71), channel_id=1, source_target_pairs={{0,2},{2,4},{4,6},{6,0},{1,3},{3,5},{5,7},{7,1},{8,10},{10,12},{12... | collective-permute-start | bytes 147464 | tf_op jit(solution)/shard_map/ppermute | solution.py:356
  14.8 5.8 %collective-permute-start.4 = (bf16[192,128]{1,0:T(8,128)(2,1)S(1)}, bf16[192,128]{1,0:T(8,128)(2,1)S(1)}, u32[]{:S(2)}, u32[]{:S(2)}) collective-permute-start(bf16[192,128]{1,0:T(8,128)(2,1)S(1)} %get-tuple-element.72), channel_id=1, source_target_pairs={{0,4},{2,6},{4,0},{6,2},{1,5},{3,7},{5,1},{7,3},{8,12},{10,14},{12... | collective-permute-start | bytes 147464 | tf_op jit(solution)/shard_map/ppermute | solution.py:356
  17.4 4.1 %collective-permute-start.5 = (bf16[192,128]{1,0:T(8,128)(2,1)S(1)}, bf16[192,128]{1,0:T(8,128)(2,1)S(1)}, u32[]{:S(2)}, u32[]{:S(2)}) collective-permute-start(bf16[192,128]{1,0:T(8,128)(2,1)S(1)} %get-tuple-element.73), channel_id=1, source_target_pairs={{0,6},{2,0},{4,2},{6,4},{1,7},{3,1},{5,3},{7,5},{8,14},{10,8},{12,... | collective-permute-start | bytes 147464 | tf_op jit(solution)/shard_map/ppermute | solution.py:356
  21.5 1.3 %collective-permute-start.6 = (bf16[320,128]{1,0:T(8,128)(2,1)S(1)}, bf16[320,128]{1,0:T(8,128)(2,1)S(1)}, u32[]{:S(2)}, u32[]{:S(2)}) collective-permute-start(bf16[320,128]{1,0:T(8,128)(2,1)S(1)} %get-tuple-element.83), channel_id=1, source_target_pairs={{0,1},{1,0},{2,3},{3,2},{4,5},{5,4},{6,7},{7,6},{8,9},{9,8},{10,11... | collective-permute-start | bytes 245768 | tf_op jit(solution)/shard_map/ppermute | solution.py:351
  23.1 6.2 %collective-permute-start.7 = (bf16[320,128]{1,0:T(8,128)(2,1)S(1)}, bf16[320,128]{1,0:T(8,128)(2,1)S(1)}, u32[]{:S(2)}, u32[]{:S(2)}) collective-permute-start(bf16[320,128]{1,0:T(8,128)(2,1)S(1)} %get-tuple-element.102), channel_id=1, source_target_pairs={{0,8},{8,0},{16,24},{24,16},{1,9},{9,1},{17,25},{25,17},{2,10},{10... | collective-permute-start | bytes 245768 | tf_op jit(solution)/shard_map/ppermute | solution.py:351
  24.4 6.2 %collective-permute-start.8 = (bf16[320,128]{1,0:T(8,128)(2,1)S(1)}, bf16[320,128]{1,0:T(8,128)(2,1)S(1)}, u32[]{:S(2)}, u32[]{:S(2)}) collective-permute-start(bf16[320,128]{1,0:T(8,128)(2,1)S(1)} %get-tuple-element.103), channel_id=1, source_target_pairs={{0,16},{8,24},{16,0},{24,8},{1,17},{9,25},{17,1},{25,9},{2,18},{10... | collective-permute-start | bytes 245768 | tf_op jit(solution)/shard_map/ppermute | solution.py:351
  25.2 5.4 %collective-permute-start.9 = (bf16[320,128]{1,0:T(8,128)(2,1)S(1)}, bf16[320,128]{1,0:T(8,128)(2,1)S(1)}, u32[]{:S(2)}, u32[]{:S(2)}) collective-permute-start(bf16[320,128]{1,0:T(8,128)(2,1)S(1)} %get-tuple-element.104), channel_id=1, source_target_pairs={{0,24},{8,16},{16,8},{24,0},{1,25},{9,17},{17,9},{25,1},{2,26},{10... | collective-permute-start | bytes 245768 | tf_op jit(solution)/shard_map/ppermute | solution.py:351
  26.6 4.0 %copy-start = (bf16[1,256,256]{2,1,0:T(8,128)(2,1)S(1)}, bf16[1,256,256]{2,1,0:T(8,128)(2,1)}, u32[]{:S(2)}) copy-start(bf16[1,256,256]{2,1,0:T(8,128)(2,1)} %refs_5_.3) | copy-start | bytes 393220
  26.7 4.0 %copy-start.1 = (bf16[1,256,256]{2,1,0:T(8,128)(2,1)S(1)}, bf16[1,256,256]{2,1,0:T(8,128)(2,1)}, u32[]{:S(2)}) copy-start(bf16[1,256,256]{2,1,0:T(8,128)(2,1)} %refs_6_.3) | copy-start | bytes 393220

commit v8 on v6

--- a/solution.py
+++ b/solution.py
@@ -39,6 +39,12 @@
 
 def in_hbm(x):
     return pltpu.with_memory_space_constraint(x, pltpu.HBM)
+
+
+def turn(x):
+    size = x.shape[1]
+    same = lax.broadcasted_iota(jnp.int32, (size, size), 0) == lax.broadcasted_iota(jnp.int32, (size, size), 1)
+    return mm_nt(same.astype(F32).astype(BF16), x)
 
 
 def three_terms(x):
@@ -116,11 +122,11 @@
 
     for copy in copies[6:8]:
         copy.wait()
-    turned = keys[0].T
+    turned = turn(keys[0])
     later = jnp.exp(suffix[:, :tokens])
     for h in range(H):
         lanes = slice(h * DH, (h + 1) * DH)
-        scaled = turned[lanes].astype(F32) * later[h : h + 1]
+        scaled = turned[lanes] * later[h : h + 1]
         high = scaled.astype(BF16)
         low = (scaled - high.astype(F32)).astype(BF16)
         both = mm(jnp.concatenate([high, low], axis=0), values[0, :, lanes])
@@ -135,11 +141,11 @@
 
     for i in range(count):
         copies[8 + 2 * i].wait()
-        turned = q[i].T
+        turned = turn(q[i])
         copies[9 + 2 * i].wait()
         for h in range(H):
             lanes = slice(h * DH, (h + 1) * DH)
-            scaled = (turned[lanes].astype(F32) * factors[i][h : h + 1]).astype(BF16)
+            scaled = (turned[lanes] * factors[i][h : h + 1]).astype(BF16)
             matrices[H * (1 + i) + h] = mm(scaled, c[i, :, lanes])
             spread(H * (1 + i) + h)
     for copy in copies[8 + 2 * count :]:
@@ -177,14 +183,14 @@
             sums[noted_prompt(notes[k], i)] += got[k][at : at + block, :].astype(F32)
     final = final.astype(BF16)
     for k in range(chips):
-        z = lax.bitwise_xor(z_at, k)
+        z = lax.rem(z_at + k, chips)
         msgs[k][0:block, :] = final
         for c in range(cores):
             msgs[k][(1 + c) * block : (2 + c) * block, :] = sums[z * cores + c].astype(BF16)
 
 
 def swap_kernel(chips, *refs):
-    got, sent_ref, kept_ref = far_first(refs[:chips]), refs[chips + 1], refs[chips + 2]
+    got, sent_ref, kept_ref = refs[:chips], refs[chips + 1], refs[chips + 2]
     block = got[0].shape[0] // 3
     totals = []
     for c in range(2):
@@ -212,7 +218,7 @@
         notes = noted[k][block : block + 16, :].astype(F32)
         for i in range(responses):
             p = noted_prompt(notes, i)
-            slot = lax.bitwise_xor(z_at, lax.div(p, 2))
+            slot = lax.rem(z_at + chips - lax.div(p, 2), chips)
             at = pl.ds(pl.multiple_of(slot * block, block), block)
             same = lax.rem(p, 2) == core
             state = jnp.where(same, kept_ref[at, :].astype(F32), got_ref[at, :].astype(F32))
@@ -354,6 +360,11 @@
     return [xs[0]] + [lax.ppermute(xs[k], axis, [(s, s ^ k) for s in range(n)]) for k in range(1, n)]
 
 
+def exchange_ring(xs, axis):
+    n = lax.axis_size(axis)
+    return [xs[0]] + [lax.ppermute(xs[k], axis, [(s, (s + k) % n) for s in range(n)]) for k in range(1, n)]
+
+
 def far_first(refs):
     return [refs[0], *refs[:0:-1]]
 
@@ -454,7 +465,7 @@
         name="second",
     )(*got1, token)
     msgs, later = outs[:chips], outs[chips]
-    got2 = far_first(exchange(msgs, "z"))
+    got2 = exchange_ring(msgs, "z")
     held, token = sweep(units[3:5], held, later)
     sent, kept = pl.pallas_call(
         lambda *refs: swap_kernel(chips, *refs),

time: 32.8 us -> 33.3 us (1.015)
  waiting for transfers between devices: 5.4 us -> 3.99 us
  starting transfers between devices: 12.7 us -> 13.8 us
  Pallas kernels: 13.8 us -> 14.6 us
    ppermute x0 -> x3, starting transfers between devices: none -> 5.57 us  [exchange_ring(): lax.ppermute(xs[k], axis, [(s, (s + k) % n) for s in range(n)])]
    ppermute x10 -> x7, starting transfers between devices: 12.7 us -> 8.24 us  [exchange(): lax.ppermute(xs[k], axis, [(s, s ^ k) for s in range(n)])]
    ppermute x10 -> x7, waiting for transfers between devices: 5.4 us -> 3.07 us  [exchange(): lax.ppermute(xs[k], axis, [(s, s ^ k) for s in range(n)])]
    ppermute x0 -> x3, waiting for transfers between devices: none -> 0.92 us  [exchange_ring(): lax.ppermute(xs[k], axis, [(s, (s + k) % n) for s in range(n)])]
    pallas_call x1, Pallas kernels: 3.1 us -> 3.86 us  [shards(): pl.pallas_call(lambda *refs: first_kernel(n, *refs), out_shape=[shape((bl...]
  transfers between devices with their start and end apart: 10 -> 10, of which waited for: 6 -> 5; matrix products, arithmetic and copies ran while one was open for 0% -> 0% of each run, Pallas kernels for 25% -> 25%
where the time goes in v8:
time: 33.3 us; the launch traced here: 33.1 us
  Pallas kernels  14.6 us (44%)
  starting transfers between devices  13.8 us (41%)
  waiting for transfers between devices  3.99 us (12%)
  between operations  0.74 us (2%)
    ppermute x7, starting transfers between devices, exchange(): lax.ppermute(xs[k], axis, [(s, s ^ k) for s in range(n)])  8.24 us
    ppermute x3, starting transfers between devices, exchange_ring(): lax.ppermute(xs[k], axis, [(s, (s + k) % n) for s in range(n)])  5.57 us
    pallas_call x3, Pallas kernels, sweep(): pl.pallas_call(lambda *refs: sweep_kernel(units, done, *refs), out_shape=...  5.41 us
    pallas_call x1, Pallas kernels, shards(): pl.pallas_call(lambda *refs: first_kernel(n, *refs), out_shape=[shape((bl...  3.86 us
    ppermute x7, waiting for transfers between devices, exchange(): lax.ppermute(xs[k], axis, [(s, s ^ k) for s in range(n)])  3.07 us
    pallas_call x1, Pallas kernels, first_sweep(): pl.pallas_call(lambda *refs: sweep_kernel(units, (), *refs[:5], None, *re...  2.86 us
    pallas_call x1, Pallas kernels, shards(): pl.pallas_call(lambda *refs: last_kernel(n, responses, *refs), out_shape=...  1.93 us
    ppermute x3, waiting for transfers between devices, exchange_ring(): lax.ppermute(xs[k], axis, [(s, (s + k) % n) for s in range(n)])  0.92 us
  transfers between devices with their start and end apart: 10, of which 5 were waited for; matrix products, arithmetic and copies ran while one was open for 0% of the time, Pallas kernels for 25%

profile of v8, /device:TPU:0, one launch (start us, length us, event | category | flops | bytes accessed | tf_op | source)
XLA Modules:
  0.0 33.1 jit_solution(13222270834518349168)
XLA Ops:
  0.6 3.9 %first.1 = (bf16[336,128]{1,0:T(8,128)(2,1)S(1)}, bf16[336,128]{1,0:T(8,128)(2,1)S(1)}, bf16[336,128]{1,0:T(8,128)(2,1)S(1)}, bf16[336,128]{1,0:T(8,128)(2,1)S(1...) custom-call(s32[4]{0:T(128)} %refs_0_.1, ...), custom_call_target="tpu_custom_call" | custom-call | tf_op jit(solution)/shard_map/first/pallas_call | solution.py:398
  4.5 4.0 %collective-permute-start = (bf16[336,128]{1,0:T(8,128)(2,1)S(1)}, bf16[336,128]{1,0:T(8,128)(2,1)S(1)}, u32[]{:S(2)}, u32[]{:S(2)}) collective-permute-start(bf16[336,128]{1,0:T(8,128)(2,1)S(1)} %get-tuple-element.66), channel_id=1, source_target_pairs={{0,24},{8,16},{16,8},{24,0},{1,25},{9,17},{17,9},{25,1},{2,26},{10... | collective-permute-start | bytes 258056 | tf_op jit(solution)/shard_map/ppermute | solution.py:360
  8.5 0.5 %collective-permute-start.1 = (bf16[336,128]{1,0:T(8,128)(2,1)S(1)}, bf16[336,128]{1,0:T(8,128)(2,1)S(1)}, u32[]{:S(2)}, u32[]{:S(2)}) collective-permute-start(bf16[336,128]{1,0:T(8,128)(2,1)S(1)} %get-tuple-element.67), channel_id=1, source_target_pairs={{0,16},{8,24},{16,0},{24,8},{1,17},{9,25},{17,1},{25,9},{2,18},{10... | collective-permute-start | bytes 258056 | tf_op jit(solution)/shard_map/ppermute | solution.py:360
  9.0 0.1 collective-permute-start.2
  9.1 2.9 %sweep.4 = (f32[512,128]{1,0:T(8,128)S(1)}, f32[4,512,256]{2,1,0:T(8,128)S(1)}, f32[4,512,256]{2,1,0:T(8,128)S(1)}, bf16[4,512,256]{2,1,0:T(8,128)(2,1)S(1)}, bf...) custom-call(f32[40,512]{1,0:T(8,128)S(1)} %get-tuple-element.59.refs, ...), custom_call_target="tpu_custom_call" | custom-call | tf_op jit(solution)/shard_map/sweep/pallas_call | solution.py:431
  12.0 0.0 collective-permute-done.refs_1_
  12.0 1.0 %collective-permute-done.1.refs_2_ = bf16[336,128]{1,0:T(8,128)(2,1)S(1)} collective-permute-done((bf16[336,128]{1,0:T(8,128)(2,1)S(1)}, bf16[336,128]{1,0:T(8,128)(2,1)S(1)}, u32[]{:S(2)}, u32[]{:S(2)}) %collective-permute-start.1) | collective-permute-done | bytes 86048 | tf_op jit(solution)/shard_map/ppermute | solution.py:360
  13.0 0.5 %collective-permute-done.2.refs_3_ = bf16[336,128]{1,0:T(8,128)(2,1)S(1)} collective-permute-done((bf16[336,128]{1,0:T(8,128)(2,1)S(1)}, bf16[336,128]{1,0:T(8,128)(2,1)S(1)}, u32[]{:S(2)}, u32[]{:S(2)}) %collective-permute-start.2) | collective-permute-done | bytes 86048 | tf_op jit(solution)/shard_map/ppermute | solution.py:360
  13.5 0.2 second.1
  13.7 1.6 %collective-permute-start.3 = (bf16[192,128]{1,0:T(8,128)(2,1)S(1)}, bf16[192,128]{1,0:T(8,128)(2,1)S(1)}, u32[]{:S(2)}, u32[]{:S(2)}) collective-permute-start(bf16[192,128]{1,0:T(8,128)(2,1)S(1)} %get-tuple-element.71), channel_id=1, source_target_pairs={{0,2},{2,4},{4,6},{6,0},{1,3},{3,5},{5,7},{7,1},{8,10},{10,12},{12... | collective-permute-start | bytes 147464 | tf_op jit(solution)/shard_map/ppermute | solution.py:365
  15.3 2.6 %collective-permute-start.4 = (bf16[192,128]{1,0:T(8,128)(2,1)S(1)}, bf16[192,128]{1,0:T(8,128)(2,1)S(1)}, u32[]{:S(2)}, u32[]{:S(2)}) collective-permute-start(bf16[192,128]{1,0:T(8,128)(2,1)S(1)} %get-tuple-element.72), channel_id=1, source_target_pairs={{0,4},{2,6},{4,0},{6,2},{1,5},{3,7},{5,1},{7,3},{8,12},{10,14},{12... | collective-permute-start | bytes 147464 | tf_op jit(solution)/shard_map/ppermute | solution.py:365
  17.9 1.3 %collective-permute-start.5 = (bf16[192,128]{1,0:T(8,128)(2,1)S(1)}, bf16[192,128]{1,0:T(8,128)(2,1)S(1)}, u32[]{:S(2)}, u32[]{:S(2)}) collective-permute-start(bf16[192,128]{1,0:T(8,128)(2,1)S(1)} %get-tuple-element.73), channel_id=1, source_target_pairs={{0,6},{2,0},{4,2},{6,4},{1,7},{3,1},{5,3},{7,5},{8,14},{10,8},{12,... | collective-permute-start | bytes 147464 | tf_op jit(solution)/shard_map/ppermute | solution.py:365
  19.3 1.8 %sweep.5 = (f32[4,512,256]{2,1,0:T(8,128)S(1)}, f32[4,512,256]{2,1,0:T(8,128)S(1)}, bf16[4,512,256]{2,1,0:T(8,128)(2,1)S(1)}, bf16[4,512,256]{2,1,0:T(8,128)(2,1...) custom-call(f32[40,512]{1,0:T(8,128)S(1)} %get-tuple-element.59.refs, ...), custom_call_target="tpu_custom_call", output_to_operand_aliasing={{0}: (7, {}), {1}: (8, {}), {2}: (9, {}), {3}: (10, {}), {4... | custom-call | tf_op jit(solution)/shard_map/sweep/pallas_call | solution.py:443
  21.1 0.0 collective-permute-done.3.refs_1_
  21.1 0.0 collective-permute-done.4.refs_2_
  21.1 0.9 %collective-permute-done.5.refs_3_ = bf16[192,128]{1,0:T(8,128)(2,1)S(1)} collective-permute-done((bf16[192,128]{1,0:T(8,128)(2,1)S(1)}, bf16[192,128]{1,0:T(8,128)(2,1)S(1)}, u32[]{:S(2)}, u32[]{:S(2)}) %collective-permute-start.5) | collective-permute-done | bytes 49184 | tf_op jit(solution)/shard_map/ppermute | solution.py:365
  22.1 0.1 collective-permute-start.6
  22.1 1.0 %sweep.6 = (f32[4,512,256]{2,1,0:T(8,128)S(1)}, f32[4,512,256]{2,1,0:T(8,128)S(1)}, bf16[4,512,256]{2,1,0:T(8,128)(2,1)S(1)}, bf16[4,512,256]{2,1,0:T(8,128)(2,1...) custom-call(f32[40,512]{1,0:T(8,128)S(1)} %get-tuple-element.59.refs, ...), custom_call_target="tpu_custom_call", output_to_operand_aliasing={{0}: (7, {}), {1}: (8, {}), {2}: (9, {}), {3}: (10, {}), {4... | custom-call | tf_op jit(solution)/shard_map/sweep/pallas_call | solution.py:443
  23.1 0.3 collective-permute-done.6.refs_5_
  23.4 0.3 third.1
  23.7 1.3 %collective-permute-start.7 = (bf16[320,128]{1,0:T(8,128)(2,1)S(1)}, bf16[320,128]{1,0:T(8,128)(2,1)S(1)}, u32[]{:S(2)}, u32[]{:S(2)}) collective-permute-start(bf16[320,128]{1,0:T(8,128)(2,1)S(1)} %get-tuple-element.102), channel_id=1, source_target_pairs={{0,8},{8,0},{16,24},{24,16},{1,9},{9,1},{17,25},{25,17},{2,10},{10... | collective-permute-start | bytes 245768 | tf_op jit(solution)/shard_map/ppermute | solution.py:360
  25.0 0.8 %collective-permute-start.8 = (bf16[320,128]{1,0:T(8,128)(2,1)S(1)}, bf16[320,128]{1,0:T(8,128)(2,1)S(1)}, u32[]{:S(2)}, u32[]{:S(2)}) collective-permute-start(bf16[320,128]{1,0:T(8,128)(2,1)S(1)} %get-tuple-element.103), channel_id=1, source_target_pairs={{0,16},{8,24},{16,0},{24,8},{1,17},{9,25},{17,1},{25,9},{2,18},{10... | collective-permute-start | bytes 245768 | tf_op jit(solution)/shard_map/ppermute | solution.py:360
  25.8 1.4 %collective-permute-start.9 = (bf16[320,128]{1,0:T(8,128)(2,1)S(1)}, bf16[320,128]{1,0:T(8,128)(2,1)S(1)}, u32[]{:S(2)}, u32[]{:S(2)}) collective-permute-start(bf16[320,128]{1,0:T(8,128)(2,1)S(1)} %get-tuple-element.104), channel_id=1, source_target_pairs={{0,24},{8,16},{16,8},{24,0},{1,25},{9,17},{17,9},{25,1},{2,26},{10... | collective-permute-start | bytes 245768 | tf_op jit(solution)/shard_map/ppermute | solution.py:360
  27.2 0.0 copy-start
  27.2 0.0 copy-start.1
  27.2 2.6 %sweep.7 = (f32[4,512,256]{2,1,0:T(8,128)S(1)}, f32[4,512,256]{2,1,0:T(8,128)S(1)}, bf16[4,512,256]{2,1,0:T(8,128)(2,1)S(1)}, bf16[4,512,256]{2,1,0:T(8,128)(2,1...) custom-call(f32[40,512]{1,0:T(8,128)S(1)} %get-tuple-element.59.refs, ...), custom_call_target="tpu_custom_call", output_to_operand_aliasing={{0}: (7, {}), {1}: (8, {}), {2}: (9, {}), {3}: (10, {}), {4... | custom-call | tf_op jit(solution)/shard_map/sweep/pallas_call | solution.py:443
  29.9 0.0 collective-permute-done.7.refs_9_
  29.9 1.3 %collective-permute-done.8.refs_10_ = bf16[320,128]{1,0:T(8,128)(2,1)S(1)} collective-permute-done((bf16[320,128]{1,0:T(8,128)(2,1)S(1)}, bf16[320,128]{1,0:T(8,128)(2,1)S(1)}, u32[]{:S(2)}, u32[]{:S(2)}) %collective-permute-start.8) | collective-permute-done | bytes 81952 | tf_op jit(solution)/shard_map/ppermute | solution.py:360
  31.2 0.0 collective-permute-done.9.refs_11_
  31.2 0.0 copy-done
  31.2 0.0 copy-done.1
  31.2 1.9 %last.1 = (bf16[4,512,256]{2,1,0:T(8,128)(2,1)}, bf16[4,512,256]{2,1,0:T(8,128)(2,1)}, bf16[1,256,256]{2,1,0:T(8,128)(2,1)}, bf16[1,256,256]{2,1,0:T(8,128)(2,1)}) custom-call(f32[512,128]{1,0:T(8,128)S(1)} %get-tuple-element.64.refs_5_.refs_0_, bf16[4,512,256]{2,1,0:T(8,128)(2,1)S(1)} %get-tuple-element.98.refs_1_, ...), custom_call_target="tpu_custom_call" | custom-call | tf_op jit(solution)/shard_map/last/pallas_call | solution.py:492
  (1 shorter events, 0.0 us)
Async XLA Ops:
  4.5 7.5 %collective-permute-start = (bf16[336,128]{1,0:T(8,128)(2,1)S(1)}, bf16[336,128]{1,0:T(8,128)(2,1)S(1)}, u32[]{:S(2)}, u32[]{:S(2)}) collective-permute-start(bf16[336,128]{1,0:T(8,128)(2,1)S(1)} %get-tuple-element.66), channel_id=1, source_target_pairs={{0,24},{8,16},{16,8},{24,0},{1,25},{9,17},{17,9},{25,1},{2,26},{10... | collective-permute-start | bytes 258056 | tf_op jit(solution)/shard_map/ppermute | solution.py:360
  8.5 4.5 %collective-permute-start.1 = (bf16[336,128]{1,0:T(8,128)(2,1)S(1)}, bf16[336,128]{1,0:T(8,128)(2,1)S(1)}, u32[]{:S(2)}, u32[]{:S(2)}) collective-permute-start(bf16[336,128]{1,0:T(8,128)(2,1)S(1)} %get-tuple-element.67), channel_id=1, source_target_pairs={{0,16},{8,24},{16,0},{24,8},{1,17},{9,25},{17,1},{25,9},{2,18},{10... | collective-permute-start | bytes 258056 | tf_op jit(solution)/shard_map/ppermute | solution.py:360
  9.0 4.5 %collective-permute-start.2 = (bf16[336,128]{1,0:T(8,128)(2,1)S(1)}, bf16[336,128]{1,0:T(8,128)(2,1)S(1)}, u32[]{:S(2)}, u32[]{:S(2)}) collective-permute-start(bf16[336,128]{1,0:T(8,128)(2,1)S(1)} %get-tuple-element.68), channel_id=1, source_target_pairs={{0,8},{8,0},{16,24},{24,16},{1,9},{9,1},{17,25},{25,17},{2,10},{10... | collective-permute-start | bytes 258056 | tf_op jit(solution)/shard_map/ppermute | solution.py:360
  13.7 7.4 %collective-permute-start.3 = (bf16[192,128]{1,0:T(8,128)(2,1)S(1)}, bf16[192,128]{1,0:T(8,128)(2,1)S(1)}, u32[]{:S(2)}, u32[]{:S(2)}) collective-permute-start(bf16[192,128]{1,0:T(8,128)(2,1)S(1)} %get-tuple-element.71), channel_id=1, source_target_pairs={{0,2},{2,4},{4,6},{6,0},{1,3},{3,5},{5,7},{7,1},{8,10},{10,12},{12... | collective-permute-start | bytes 147464 | tf_op jit(solution)/shard_map/ppermute | solution.py:365
  15.3 5.8 %collective-permute-start.4 = (bf16[192,128]{1,0:T(8,128)(2,1)S(1)}, bf16[192,128]{1,0:T(8,128)(2,1)S(1)}, u32[]{:S(2)}, u32[]{:S(2)}) collective-permute-start(bf16[192,128]{1,0:T(8,128)(2,1)S(1)} %get-tuple-element.72), channel_id=1, source_target_pairs={{0,4},{2,6},{4,0},{6,2},{1,5},{3,7},{5,1},{7,3},{8,12},{10,14},{12... | collective-permute-start | bytes 147464 | tf_op jit(solution)/shard_map/ppermute | solution.py:365
  17.9 4.1 %collective-permute-start.5 = (bf16[192,128]{1,0:T(8,128)(2,1)S(1)}, bf16[192,128]{1,0:T(8,128)(2,1)S(1)}, u32[]{:S(2)}, u32[]{:S(2)}) collective-permute-start(bf16[192,128]{1,0:T(8,128)(2,1)S(1)} %get-tuple-element.73), channel_id=1, source_target_pairs={{0,6},{2,0},{4,2},{6,4},{1,7},{3,1},{5,3},{7,5},{8,14},{10,8},{12,... | collective-permute-start | bytes 147464 | tf_op jit(solution)/shard_map/ppermute | solution.py:365
  22.1 1.3 %collective-permute-start.6 = (bf16[320,128]{1,0:T(8,128)(2,1)S(1)}, bf16[320,128]{1,0:T(8,128)(2,1)S(1)}, u32[]{:S(2)}, u32[]{:S(2)}) collective-permute-start(bf16[320,128]{1,0:T(8,128)(2,1)S(1)} %get-tuple-element.83), channel_id=1, source_target_pairs={{0,1},{1,0},{2,3},{3,2},{4,5},{5,4},{6,7},{7,6},{8,9},{9,8},{10,11... | collective-permute-start | bytes 245768 | tf_op jit(solution)/shard_map/ppermute | solution.py:360
  23.7 6.2 %collective-permute-start.7 = (bf16[320,128]{1,0:T(8,128)(2,1)S(1)}, bf16[320,128]{1,0:T(8,128)(2,1)S(1)}, u32[]{:S(2)}, u32[]{:S(2)}) collective-permute-start(bf16[320,128]{1,0:T(8,128)(2,1)S(1)} %get-tuple-element.102), channel_id=1, source_target_pairs={{0,8},{8,0},{16,24},{24,16},{1,9},{9,1},{17,25},{25,17},{2,10},{10... | collective-permute-start | bytes 245768 | tf_op jit(solution)/shard_map/ppermute | solution.py:360
  25.0 6.2 %collective-permute-start.8 = (bf16[320,128]{1,0:T(8,128)(2,1)S(1)}, bf16[320,128]{1,0:T(8,128)(2,1)S(1)}, u32[]{:S(2)}, u32[]{:S(2)}) collective-permute-start(bf16[320,128]{1,0:T(8,128)(2,1)S(1)} %get-tuple-element.103), channel_id=1, source_target_pairs={{0,16},{8,24},{16,0},{24,8},{1,17},{9,25},{17,1},{25,9},{2,18},{10... | collective-permute-start | bytes 245768 | tf_op jit(solution)/shard_map/ppermute | solution.py:360
  25.8 5.4 %collective-permute-start.9 = (bf16[320,128]{1,0:T(8,128)(2,1)S(1)}, bf16[320,128]{1,0:T(8,128)(2,1)S(1)}, u32[]{:S(2)}, u32[]{:S(2)}) collective-permute-start(bf16[320,128]{1,0:T(8,128)(2,1)S(1)} %get-tuple-element.104), channel_id=1, source_target_pairs={{0,24},{8,16},{16,8},{24,0},{1,25},{9,17},{17,9},{25,1},{2,26},{10... | collective-permute-start | bytes 245768 | tf_op jit(solution)/shard_map/ppermute | solution.py:360
  27.2 4.0 %copy-start = (bf16[1,256,256]{2,1,0:T(8,128)(2,1)S(1)}, bf16[1,256,256]{2,1,0:T(8,128)(2,1)}, u32[]{:S(2)}) copy-start(bf16[1,256,256]{2,1,0:T(8,128)(2,1)} %refs_5_.3) | copy-start | bytes 393220
  27.2 4.0 %copy-start.1 = (bf16[1,256,256]{2,1,0:T(8,128)(2,1)S(1)}, bf16[1,256,256]{2,1,0:T(8,128)(2,1)}, u32[]{:S(2)}) copy-start(bf16[1,256,256]{2,1,0:T(8,128)(2,1)} %refs_6_.3) | copy-start | bytes 393220

commit v9 on v7

--- a/solution.py
+++ b/solution.py
@@ -72,15 +72,14 @@
     msgs, (rows_ref, q, c, k_out, v_out) = refs[:n], refs[n : n + 5]
     keys, values, pgates, gates, mask, ids_ref, lens_ref, adv_ref, matrices, sems = refs[n + 5 :]
     pairs = [(pgates_hbm, pgates), (gates_hbm, gates), (mask_hbm, mask)]
-    pairs += [(ids_hbm, ids_ref), (lens_hbm, lens_ref), (adv_hbm, adv_ref), (keys_hbm, keys), (q_hbm, q)]
-    pairs += [(values_hbm, values)]
+    pairs += [(ids_hbm, ids_ref), (lens_hbm, lens_ref), (adv_hbm, adv_ref), (keys_hbm, keys), (values_hbm, values)]
+    pairs += [(q_hbm, q), (c_hbm, c), (k_hbm, k_out), (v_hbm, v_out)]
+    copies = [pltpu.make_async_copy(a, b, sems.at[i]) for i, (a, b) in enumerate(pairs)]
+    for copy in copies[:10]:
+        copy.start()
     count = gates.shape[0]
     slots = gates.shape[2]
     tokens = keys.shape[1]
-    pairs += [(c_hbm.at[i], c.at[i]) for i in range(count)] + [(k_hbm, k_out), (v_hbm, v_out)]
-    copies = [pltpu.make_async_copy(a, b, sems.at[i]) for i, (a, b) in enumerate(pairs)]
-    for copy in copies:
-        copy.start()
     part = DH // n
     block = H * part
     targets = partners(n)
@@ -92,10 +91,10 @@
                 at, of, :
             ].astype(BF16)
 
-    for copy in copies[:8]:
+    for copy in copies[:6]:
         copy.wait()
-    turned_keys = keys[0].T
-    turned = [q[i].T for i in range(count)]
+    for copy in copies[10:]:
+        copy.start()
     piece = jnp.concatenate([pgates[0], jnp.zeros((H, slots - tokens), F32)], axis=1)
     gate_rows = [gates[i] for i in range(count)] + [piece, jnp.zeros((16 - H * (count + 1), slots), F32)]
     cum = lane_cumsum(jnp.concatenate(gate_rows, axis=0))
@@ -115,11 +114,13 @@
     rows += [suffix, jnp.zeros((8 - H, slots), F32)]
     rows_ref[...] = jnp.concatenate(rows, axis=0)
 
-    copies[8].wait()
+    copies[6].wait()
+    copies[7].wait()
+    turned = keys[0].T
     later = jnp.exp(suffix[:, :tokens])
     for h in range(H):
         lanes = slice(h * DH, (h + 1) * DH)
-        scaled = turned_keys[lanes].astype(F32) * later[h : h + 1]
+        scaled = turned[lanes].astype(F32) * later[h : h + 1]
         high = scaled.astype(BF16)
         low = (scaled - high.astype(F32)).astype(BF16)
         both = mm(jnp.concatenate([high, low], axis=0), values[0, :, lanes])
@@ -132,14 +133,16 @@
     for k in range(n):
         msgs[k][block : block + 16, :] = notes
 
+    copies[8].wait()
+    copies[9].wait()
     for i in range(count):
-        copies[9 + i].wait()
+        turned = q[i].T
         for h in range(H):
             lanes = slice(h * DH, (h + 1) * DH)
-            scaled = (turned[i][lanes].astype(F32) * factors[i][h : h + 1]).astype(BF16)
+            scaled = (turned[lanes].astype(F32) * factors[i][h : h + 1]).astype(BF16)
             matrices[H * (1 + i) + h] = mm(scaled, c[i, :, lanes])
             spread(H * (1 + i) + h)
-    for copy in copies[9 + count :]:
+    for copy in copies[10:]:
         copy.wait()
 
 
@@ -340,8 +343,8 @@
             at = slice(t, t + HALF)
             out_buf[r, at, :] = (po_ref[r, at, :] + mm(q_ref[r, at, :], start[r])).astype(BF16)
             dq_buf[r, at, :] = (pdq_ref[r, at, :] + mm_nt(grad_ref[r, at, :], start[r])).astype(BF16)
-            send(out_buf.at[r, at], out_hbm.at[r, at])
-            send(dq_buf.at[r, at], dq_hbm.at[r, at])
+        send(out_buf.at[r], out_hbm.at[r])
+        send(dq_buf.at[r], dq_hbm.at[r])
     for copy in copies:
         copy.wait()
 
@@ -403,7 +406,7 @@
             pltpu.SMEM(resp_lengths.shape, jnp.int32),
             pltpu.SMEM(advantages.shape, jnp.int32),
             pltpu.VMEM((H * (1 + responses), DH, DH), F32),
-            pltpu.SemaphoreType.DMA((11 + responses,)),
+            pltpu.SemaphoreType.DMA((12,)),
         ],
         compiler_params=params(32),
         name="first",
@@ -491,7 +494,7 @@
             pltpu.VMEM(queries.shape, BF16),
             pltpu.VMEM(keys.shape[1:], BF16),
             pltpu.VMEM(keys.shape[1:], BF16),
-            pltpu.SemaphoreType.DMA((2 + 2 * responses * (slots // HALF),)),
+            pltpu.SemaphoreType.DMA((2 + 2 * responses,)),
         ],
         compiler_params=params(),
         name="last",

time: 32.7 us -> 32.1 us (0.982)
  Pallas kernels: 14 us -> 13.4 us
    pallas_call x1, Pallas kernels: 3.29 us -> 2.67 us  [shards(): pl.pallas_call(lambda *refs: first_kernel(n, *refs), out_shape=[shape((bl...]
  transfers between devices with their start and end apart: 10 -> 10, of which waited for: 5 -> 5; matrix products, arithmetic and copies ran while one was open for 0% -> 0% of each run, Pallas kernels for 25% -> 26%
where the time goes in v9:
time: 32.1 us; the launch traced here: 31.9 us
  starting transfers between devices  13.8 us (43%)
  Pallas kernels  13.4 us (42%)
  waiting for transfers between devices  4.02 us (13%)
  between operations  0.74 us (2%)
    ppermute x7, starting transfers between devices, exchange(): lax.ppermute(xs[k], axis, [(s, s ^ k) for s in range(n)])  8.23 us
    ppermute x3, starting transfers between devices, exchange_ring(): lax.ppermute(xs[k], axis, [(s, (s + k) % n) for s in range(n)])  5.56 us
    pallas_call x3, Pallas kernels, sweep(): pl.pallas_call(lambda *refs: sweep_kernel(units, done, *refs), out_shape=...  5.4 us
    ppermute x7, waiting for transfers between devices, exchange(): lax.ppermute(xs[k], axis, [(s, s ^ k) for s in range(n)])  3.09 us
    pallas_call x1, Pallas kernels, first_sweep(): pl.pallas_call(lambda *refs: sweep_kernel(units, (), *refs[:5], None, *re...  2.86 us
    pallas_call x1, Pallas kernels, shards(): pl.pallas_call(lambda *refs: first_kernel(n, *refs), out_shape=[shape((bl...  2.67 us
    pallas_call x1, Pallas kernels, shards(): pl.pallas_call(lambda *refs: last_kernel(n, responses, *refs), out_shape=...  1.92 us
    ppermute x3, waiting for transfers between devices, exchange_ring(): lax.ppermute(xs[k], axis, [(s, (s + k) % n) for s in range(n)])  0.92 us
  transfers between devices with their start and end apart: 10, of which 5 were waited for; matrix products, arithmetic and copies ran while one was open for 0% of the time, Pallas kernels for 26%

profile of v9, /device:TPU:0, one launch (start us, length us, event | category | flops | bytes accessed | tf_op | source)
XLA Modules:
  0.0 31.9 jit_solution(11314595686978282682)
XLA Ops:
  0.6 2.7 %first.1 = (bf16[336,128]{1,0:T(8,128)(2,1)S(1)}, bf16[336,128]{1,0:T(8,128)(2,1)S(1)}, bf16[336,128]{1,0:T(8,128)(2,1)S(1)}, bf16[336,128]{1,0:T(8,128)(2,1)S(1...) custom-call(s32[4]{0:T(128)} %refs_0_.1, ...), custom_call_target="tpu_custom_call" | custom-call | tf_op jit(solution)/shard_map/first/pallas_call | solution.py:392
  3.3 4.0 %collective-permute-start = (bf16[336,128]{1,0:T(8,128)(2,1)S(1)}, bf16[336,128]{1,0:T(8,128)(2,1)S(1)}, u32[]{:S(2)}, u32[]{:S(2)}) collective-permute-start(bf16[336,128]{1,0:T(8,128)(2,1)S(1)} %get-tuple-element.66), channel_id=1, source_target_pairs={{0,24},{8,16},{16,8},{24,0},{1,25},{9,17},{17,9},{25,1},{2,26},{10... | collective-permute-start | bytes 258056 | tf_op jit(solution)/shard_map/ppermute | solution.py:354
  7.3 0.5 %collective-permute-start.1 = (bf16[336,128]{1,0:T(8,128)(2,1)S(1)}, bf16[336,128]{1,0:T(8,128)(2,1)S(1)}, u32[]{:S(2)}, u32[]{:S(2)}) collective-permute-start(bf16[336,128]{1,0:T(8,128)(2,1)S(1)} %get-tuple-element.67), channel_id=1, source_target_pairs={{0,16},{8,24},{16,0},{24,8},{1,17},{9,25},{17,1},{25,9},{2,18},{10... | collective-permute-start | bytes 258056 | tf_op jit(solution)/shard_map/ppermute | solution.py:354
  7.8 0.1 collective-permute-start.2
  7.9 2.9 %sweep.4 = (f32[512,128]{1,0:T(8,128)S(1)}, f32[4,512,256]{2,1,0:T(8,128)S(1)}, f32[4,512,256]{2,1,0:T(8,128)S(1)}, bf16[4,512,256]{2,1,0:T(8,128)(2,1)S(1)}, bf...) custom-call(f32[40,512]{1,0:T(8,128)S(1)} %get-tuple-element.59.refs, ...), custom_call_target="tpu_custom_call" | custom-call | tf_op jit(solution)/shard_map/sweep/pallas_call | solution.py:425
  10.8 0.0 collective-permute-done.refs_1_
  10.8 1.0 %collective-permute-done.1.refs_2_ = bf16[336,128]{1,0:T(8,128)(2,1)S(1)} collective-permute-done((bf16[336,128]{1,0:T(8,128)(2,1)S(1)}, bf16[336,128]{1,0:T(8,128)(2,1)S(1)}, u32[]{:S(2)}, u32[]{:S(2)}) %collective-permute-start.1) | collective-permute-done | bytes 86048 | tf_op jit(solution)/shard_map/ppermute | solution.py:354
  11.8 0.5 %collective-permute-done.2.refs_3_ = bf16[336,128]{1,0:T(8,128)(2,1)S(1)} collective-permute-done((bf16[336,128]{1,0:T(8,128)(2,1)S(1)}, bf16[336,128]{1,0:T(8,128)(2,1)S(1)}, u32[]{:S(2)}, u32[]{:S(2)}) %collective-permute-start.2) | collective-permute-done | bytes 86048 | tf_op jit(solution)/shard_map/ppermute | solution.py:354
  12.3 0.2 second.1
  12.5 1.6 %collective-permute-start.3 = (bf16[192,128]{1,0:T(8,128)(2,1)S(1)}, bf16[192,128]{1,0:T(8,128)(2,1)S(1)}, u32[]{:S(2)}, u32[]{:S(2)}) collective-permute-start(bf16[192,128]{1,0:T(8,128)(2,1)S(1)} %get-tuple-element.71), channel_id=1, source_target_pairs={{0,2},{2,4},{4,6},{6,0},{1,3},{3,5},{5,7},{7,1},{8,10},{10,12},{12... | collective-permute-start | bytes 147464 | tf_op jit(solution)/shard_map/ppermute | solution.py:359
  14.1 2.6 %collective-permute-start.4 = (bf16[192,128]{1,0:T(8,128)(2,1)S(1)}, bf16[192,128]{1,0:T(8,128)(2,1)S(1)}, u32[]{:S(2)}, u32[]{:S(2)}) collective-permute-start(bf16[192,128]{1,0:T(8,128)(2,1)S(1)} %get-tuple-element.72), channel_id=1, source_target_pairs={{0,4},{2,6},{4,0},{6,2},{1,5},{3,7},{5,1},{7,3},{8,12},{10,14},{12... | collective-permute-start | bytes 147464 | tf_op jit(solution)/shard_map/ppermute | solution.py:359
  16.7 1.3 %collective-permute-start.5 = (bf16[192,128]{1,0:T(8,128)(2,1)S(1)}, bf16[192,128]{1,0:T(8,128)(2,1)S(1)}, u32[]{:S(2)}, u32[]{:S(2)}) collective-permute-start(bf16[192,128]{1,0:T(8,128)(2,1)S(1)} %get-tuple-element.73), channel_id=1, source_target_pairs={{0,6},{2,0},{4,2},{6,4},{1,7},{3,1},{5,3},{7,5},{8,14},{10,8},{12,... | collective-permute-start | bytes 147464 | tf_op jit(solution)/shard_map/ppermute | solution.py:359
  18.1 1.8 %sweep.5 = (f32[4,512,256]{2,1,0:T(8,128)S(1)}, f32[4,512,256]{2,1,0:T(8,128)S(1)}, bf16[4,512,256]{2,1,0:T(8,128)(2,1)S(1)}, bf16[4,512,256]{2,1,0:T(8,128)(2,1...) custom-call(f32[40,512]{1,0:T(8,128)S(1)} %get-tuple-element.59.refs, ...), custom_call_target="tpu_custom_call", output_to_operand_aliasing={{0}: (7, {}), {1}: (8, {}), {2}: (9, {}), {3}: (10, {}), {4... | custom-call | tf_op jit(solution)/shard_map/sweep/pallas_call | solution.py:437
  19.9 0.0 collective-permute-done.3.refs_1_
  19.9 0.0 collective-permute-done.4.refs_2_
  19.9 0.9 %collective-permute-done.5.refs_3_ = bf16[192,128]{1,0:T(8,128)(2,1)S(1)} collective-permute-done((bf16[192,128]{1,0:T(8,128)(2,1)S(1)}, bf16[192,128]{1,0:T(8,128)(2,1)S(1)}, u32[]{:S(2)}, u32[]{:S(2)}) %collective-permute-start.5) | collective-permute-done | bytes 49184 | tf_op jit(solution)/shard_map/ppermute | solution.py:359
  20.9 0.1 collective-permute-start.6
  20.9 1.0 %sweep.6 = (f32[4,512,256]{2,1,0:T(8,128)S(1)}, f32[4,512,256]{2,1,0:T(8,128)S(1)}, bf16[4,512,256]{2,1,0:T(8,128)(2,1)S(1)}, bf16[4,512,256]{2,1,0:T(8,128)(2,1...) custom-call(f32[40,512]{1,0:T(8,128)S(1)} %get-tuple-element.59.refs, ...), custom_call_target="tpu_custom_call", output_to_operand_aliasing={{0}: (7, {}), {1}: (8, {}), {2}: (9, {}), {3}: (10, {}), {4... | custom-call | tf_op jit(solution)/shard_map/sweep/pallas_call | solution.py:437
  21.9 0.3 collective-permute-done.6.refs_5_
  22.2 0.3 third.1
  22.5 1.3 %collective-permute-start.7 = (bf16[320,128]{1,0:T(8,128)(2,1)S(1)}, bf16[320,128]{1,0:T(8,128)(2,1)S(1)}, u32[]{:S(2)}, u32[]{:S(2)}) collective-permute-start(bf16[320,128]{1,0:T(8,128)(2,1)S(1)} %get-tuple-element.102), channel_id=1, source_target_pairs={{0,8},{8,0},{16,24},{24,16},{1,9},{9,1},{17,25},{25,17},{2,10},{10... | collective-permute-start | bytes 245768 | tf_op jit(solution)/shard_map/ppermute | solution.py:354
  23.8 0.8 %collective-permute-start.8 = (bf16[320,128]{1,0:T(8,128)(2,1)S(1)}, bf16[320,128]{1,0:T(8,128)(2,1)S(1)}, u32[]{:S(2)}, u32[]{:S(2)}) collective-permute-start(bf16[320,128]{1,0:T(8,128)(2,1)S(1)} %get-tuple-element.103), channel_id=1, source_target_pairs={{0,16},{8,24},{16,0},{24,8},{1,17},{9,25},{17,1},{25,9},{2,18},{10... | collective-permute-start | bytes 245768 | tf_op jit(solution)/shard_map/ppermute | solution.py:354
  24.6 1.4 %collective-permute-start.9 = (bf16[320,128]{1,0:T(8,128)(2,1)S(1)}, bf16[320,128]{1,0:T(8,128)(2,1)S(1)}, u32[]{:S(2)}, u32[]{:S(2)}) collective-permute-start(bf16[320,128]{1,0:T(8,128)(2,1)S(1)} %get-tuple-element.104), channel_id=1, source_target_pairs={{0,24},{8,16},{16,8},{24,0},{1,25},{9,17},{17,9},{25,1},{2,26},{10... | collective-permute-start | bytes 245768 | tf_op jit(solution)/shard_map/ppermute | solution.py:354
  26.0 0.0 copy-start
  26.0 0.0 copy-start.1
  26.0 2.6 %sweep.7 = (f32[4,512,256]{2,1,0:T(8,128)S(1)}, f32[4,512,256]{2,1,0:T(8,128)S(1)}, bf16[4,512,256]{2,1,0:T(8,128)(2,1)S(1)}, bf16[4,512,256]{2,1,0:T(8,128)(2,1...) custom-call(f32[40,512]{1,0:T(8,128)S(1)} %get-tuple-element.59.refs, ...), custom_call_target="tpu_custom_call", output_to_operand_aliasing={{0}: (7, {}), {1}: (8, {}), {2}: (9, {}), {3}: (10, {}), {4... | custom-call | tf_op jit(solution)/shard_map/sweep/pallas_call | solution.py:437
  28.7 0.0 collective-permute-done.7.refs_9_
  28.7 1.3 %collective-permute-done.8.refs_10_ = bf16[320,128]{1,0:T(8,128)(2,1)S(1)} collective-permute-done((bf16[320,128]{1,0:T(8,128)(2,1)S(1)}, bf16[320,128]{1,0:T(8,128)(2,1)S(1)}, u32[]{:S(2)}, u32[]{:S(2)}) %collective-permute-start.8) | collective-permute-done | bytes 81952 | tf_op jit(solution)/shard_map/ppermute | solution.py:354
  30.0 0.0 collective-permute-done.9.refs_11_
  30.0 0.0 copy-done
  30.0 0.0 copy-done.1
  30.0 1.9 %last.1 = (bf16[4,512,256]{2,1,0:T(8,128)(2,1)}, bf16[4,512,256]{2,1,0:T(8,128)(2,1)}, bf16[1,256,256]{2,1,0:T(8,128)(2,1)}, bf16[1,256,256]{2,1,0:T(8,128)(2,1)}) custom-call(f32[512,128]{1,0:T(8,128)S(1)} %get-tuple-element.64.refs_5_.refs_0_, bf16[4,512,256]{2,1,0:T(8,128)(2,1)S(1)} %get-tuple-element.98.refs_1_, ...), custom_call_target="tpu_custom_call" | custom-call | tf_op jit(solution)/shard_map/last/pallas_call | solution.py:486
  (1 shorter events, 0.0 us)
Async XLA Ops:
  3.3 7.5 %collective-permute-start = (bf16[336,128]{1,0:T(8,128)(2,1)S(1)}, bf16[336,128]{1,0:T(8,128)(2,1)S(1)}, u32[]{:S(2)}, u32[]{:S(2)}) collective-permute-start(bf16[336,128]{1,0:T(8,128)(2,1)S(1)} %get-tuple-element.66), channel_id=1, source_target_pairs={{0,24},{8,16},{16,8},{24,0},{1,25},{9,17},{17,9},{25,1},{2,26},{10... | collective-permute-start | bytes 258056 | tf_op jit(solution)/shard_map/ppermute | solution.py:354
  7.3 4.5 %collective-permute-start.1 = (bf16[336,128]{1,0:T(8,128)(2,1)S(1)}, bf16[336,128]{1,0:T(8,128)(2,1)S(1)}, u32[]{:S(2)}, u32[]{:S(2)}) collective-permute-start(bf16[336,128]{1,0:T(8,128)(2,1)S(1)} %get-tuple-element.67), channel_id=1, source_target_pairs={{0,16},{8,24},{16,0},{24,8},{1,17},{9,25},{17,1},{25,9},{2,18},{10... | collective-permute-start | bytes 258056 | tf_op jit(solution)/shard_map/ppermute | solution.py:354
  7.8 4.5 %collective-permute-start.2 = (bf16[336,128]{1,0:T(8,128)(2,1)S(1)}, bf16[336,128]{1,0:T(8,128)(2,1)S(1)}, u32[]{:S(2)}, u32[]{:S(2)}) collective-permute-start(bf16[336,128]{1,0:T(8,128)(2,1)S(1)} %get-tuple-element.68), channel_id=1, source_target_pairs={{0,8},{8,0},{16,24},{24,16},{1,9},{9,1},{17,25},{25,17},{2,10},{10... | collective-permute-start | bytes 258056 | tf_op jit(solution)/shard_map/ppermute | solution.py:354
  12.5 7.4 %collective-permute-start.3 = (bf16[192,128]{1,0:T(8,128)(2,1)S(1)}, bf16[192,128]{1,0:T(8,128)(2,1)S(1)}, u32[]{:S(2)}, u32[]{:S(2)}) collective-permute-start(bf16[192,128]{1,0:T(8,128)(2,1)S(1)} %get-tuple-element.71), channel_id=1, source_target_pairs={{0,2},{2,4},{4,6},{6,0},{1,3},{3,5},{5,7},{7,1},{8,10},{10,12},{12... | collective-permute-start | bytes 147464 | tf_op jit(solution)/shard_map/ppermute | solution.py:359
  14.1 5.8 %collective-permute-start.4 = (bf16[192,128]{1,0:T(8,128)(2,1)S(1)}, bf16[192,128]{1,0:T(8,128)(2,1)S(1)}, u32[]{:S(2)}, u32[]{:S(2)}) collective-permute-start(bf16[192,128]{1,0:T(8,128)(2,1)S(1)} %get-tuple-element.72), channel_id=1, source_target_pairs={{0,4},{2,6},{4,0},{6,2},{1,5},{3,7},{5,1},{7,3},{8,12},{10,14},{12... | collective-permute-start | bytes 147464 | tf_op jit(solution)/shard_map/ppermute | solution.py:359
  16.7 4.1 %collective-permute-start.5 = (bf16[192,128]{1,0:T(8,128)(2,1)S(1)}, bf16[192,128]{1,0:T(8,128)(2,1)S(1)}, u32[]{:S(2)}, u32[]{:S(2)}) collective-permute-start(bf16[192,128]{1,0:T(8,128)(2,1)S(1)} %get-tuple-element.73), channel_id=1, source_target_pairs={{0,6},{2,0},{4,2},{6,4},{1,7},{3,1},{5,3},{7,5},{8,14},{10,8},{12,... | collective-permute-start | bytes 147464 | tf_op jit(solution)/shard_map/ppermute | solution.py:359
  20.9 1.3 %collective-permute-start.6 = (bf16[320,128]{1,0:T(8,128)(2,1)S(1)}, bf16[320,128]{1,0:T(8,128)(2,1)S(1)}, u32[]{:S(2)}, u32[]{:S(2)}) collective-permute-start(bf16[320,128]{1,0:T(8,128)(2,1)S(1)} %get-tuple-element.83), channel_id=1, source_target_pairs={{0,1},{1,0},{2,3},{3,2},{4,5},{5,4},{6,7},{7,6},{8,9},{9,8},{10,11... | collective-permute-start | bytes 245768 | tf_op jit(solution)/shard_map/ppermute | solution.py:354
  22.5 6.2 %collective-permute-start.7 = (bf16[320,128]{1,0:T(8,128)(2,1)S(1)}, bf16[320,128]{1,0:T(8,128)(2,1)S(1)}, u32[]{:S(2)}, u32[]{:S(2)}) collective-permute-start(bf16[320,128]{1,0:T(8,128)(2,1)S(1)} %get-tuple-element.102), channel_id=1, source_target_pairs={{0,8},{8,0},{16,24},{24,16},{1,9},{9,1},{17,25},{25,17},{2,10},{10... | collective-permute-start | bytes 245768 | tf_op jit(solution)/shard_map/ppermute | solution.py:354
  23.8 6.2 %collective-permute-start.8 = (bf16[320,128]{1,0:T(8,128)(2,1)S(1)}, bf16[320,128]{1,0:T(8,128)(2,1)S(1)}, u32[]{:S(2)}, u32[]{:S(2)}) collective-permute-start(bf16[320,128]{1,0:T(8,128)(2,1)S(1)} %get-tuple-element.103), channel_id=1, source_target_pairs={{0,16},{8,24},{16,0},{24,8},{1,17},{9,25},{17,1},{25,9},{2,18},{10... | collective-permute-start | bytes 245768 | tf_op jit(solution)/shard_map/ppermute | solution.py:354
  24.6 5.4 %collective-permute-start.9 = (bf16[320,128]{1,0:T(8,128)(2,1)S(1)}, bf16[320,128]{1,0:T(8,128)(2,1)S(1)}, u32[]{:S(2)}, u32[]{:S(2)}) collective-permute-start(bf16[320,128]{1,0:T(8,128)(2,1)S(1)} %get-tuple-element.104), channel_id=1, source_target_pairs={{0,24},{8,16},{16,8},{24,0},{1,25},{9,17},{17,9},{25,1},{2,26},{10... | collective-permute-start | bytes 245768 | tf_op jit(solution)/shard_map/ppermute | solution.py:354
  26.0 4.0 %copy-start = (bf16[1,256,256]{2,1,0:T(8,128)(2,1)S(1)}, bf16[1,256,256]{2,1,0:T(8,128)(2,1)}, u32[]{:S(2)}) copy-start(bf16[1,256,256]{2,1,0:T(8,128)(2,1)} %refs_5_.3) | copy-start | bytes 393220
  26.0 4.0 %copy-start.1 = (bf16[1,256,256]{2,1,0:T(8,128)(2,1)S(1)}, bf16[1,256,256]{2,1,0:T(8,128)(2,1)}, u32[]{:S(2)}) copy-start(bf16[1,256,256]{2,1,0:T(8,128)(2,1)} %refs_6_.3) | copy-start | bytes 393220

commit v10 on v9

--- a/solution.py
+++ b/solution.py
@@ -118,13 +118,13 @@
     copies[7].wait()
     turned = keys[0].T
     later = jnp.exp(suffix[:, :tokens])
+    scaled = [turned[h * DH : (h + 1) * DH].astype(F32) * later[h : h + 1] for h in range(H)]
+    high = [x.astype(BF16) for x in scaled]
+    low = [(x - y.astype(F32)).astype(BF16) for x, y in zip(scaled, high)]
+    both = mm(jnp.concatenate(high + low, axis=0), values[0])
     for h in range(H):
         lanes = slice(h * DH, (h + 1) * DH)
-        scaled = turned[lanes].astype(F32) * later[h : h + 1]
-        high = scaled.astype(BF16)
-        low = (scaled - high.astype(F32)).astype(BF16)
-        both = mm(jnp.concatenate([high, low], axis=0), values[0, :, lanes])
-        matrices[h] = both[:DH] + both[DH:]
+        matrices[h] = both[h * DH : (h + 1) * DH, lanes] + both[(H + h) * DH : (H + h + 1) * DH, lanes]
         spread(h)
     notes = [jnp.broadcast_to(x[h : h + 1].astype(F32), (1, DH)) for x in three_terms(total) for h in range(H)]
     notes += [jnp.full((1, DH), ids_ref[i].astype(F32)) for i in range(count)]
@@ -137,10 +137,11 @@
     copies[9].wait()
     for i in range(count):
         turned = q[i].T
+        scaled = [turned[h * DH : (h + 1) * DH].astype(F32) * factors[i][h : h + 1] for h in range(H)]
+        grads = mm(jnp.concatenate(scaled, axis=0).astype(BF16), c[i])
         for h in range(H):
             lanes = slice(h * DH, (h + 1) * DH)
-            scaled = (turned[lanes].astype(F32) * factors[i][h : h + 1]).astype(BF16)
-            matrices[H * (1 + i) + h] = mm(scaled, c[i, :, lanes])
+            matrices[H * (1 + i) + h] = grads[lanes, lanes]
             spread(H * (1 + i) + h)
     for copy in copies[10:]:
         copy.wait()
@@ -152,7 +153,7 @@
 
 def second_kernel(n, chips, cores, *refs):
     z_at = lax.axis_index("z")
-    got, msgs, later_ref, sums = far_first(refs[:n]), refs[n + 1 : n + 1 + chips], refs[-2], refs[-1]
+    got, msgs, later_ref, sums = by_partner(refs[:n]), refs[n + 1 : n + 1 + chips], refs[-2], refs[-1]
     part = DH // n
     block = H * part
     responses = (got[0].shape[0] - block - 16) // block
@@ -203,7 +204,7 @@
 
 def third_kernel(n, chips, *refs):
     z_at, core = lax.axis_index("z"), lax.axis_index("core")
-    noted, kept_ref, got_ref, msgs = far_first(refs[:n]), refs[n], refs[n + 1], refs[n + 3 :]
+    noted, kept_ref, got_ref, msgs = by_partner(refs[:n]), refs[n], refs[n + 1], refs[n + 3 :]
     block = H * DH // n
     responses = (noted[0].shape[0] - block - 16) // block
     total = kept_ref[chips * block :, :].astype(F32) + got_ref[chips * block :, :].astype(F32)
@@ -309,7 +310,7 @@
 def last_kernel(
     n, count, cols_ref, q_ref, grad_ref, po_ref, pdq_ref, keys_ref, values_ref, later_ref, *refs
 ):
-    got, refs = refs[:n], refs[n + 1 :]
+    got, refs = by_partner(refs[:n]), refs[n + 1 :]
     out_hbm, dq_hbm, dk_hbm, dv_hbm, start, out_buf, dq_buf, dk_buf, dv_buf, sems = refs
     part = DH // n
     block = H * part
@@ -359,8 +360,16 @@
     return [xs[0]] + [lax.ppermute(xs[k], axis, [(s, (s + k) % n) for s in range(n)]) for k in range(1, n)]
 
 
-def far_first(refs):
-    return [refs[0], *refs[:0:-1]]
+def order(n):
+    return [0, *sorted(range(1, n), key=lambda k: (k % 2, -k))]
+
+
+def taken(xs):
+    return [xs[k] for k in order(len(xs))]
+
+
+def by_partner(refs):
+    return [refs[order(len(refs)).index(k)] for k in range(len(refs))]
 
 
 def partners(n):
@@ -447,7 +456,7 @@
         return (outs[:4] + outs[7:] if writes else outs[:6]), outs[6]
 
     units = [(r, h) for r in range(responses) for h in range(H)]
-    got1 = far_first(exchange(msgs, "prompt"))
+    got1 = taken(exchange(msgs, "prompt"))
     cols, held, token = first_sweep(units[:3])
     outs = pl.pallas_call(
         lambda *refs: second_kernel(n, chips, cores, *refs),
@@ -479,7 +488,7 @@
         compiler_params=params(),
         name="third",
     )(*got1, kept, swapped, token)
-    got3 = exchange(msgs, "prompt")
+    got3 = taken(exchange(msgs, "prompt"))
     held, token = sweep(units[6:], held, msgs[0], range(responses - 1))
     partial_out, partial_dq, query, grad_out, resp_dk, resp_dv = held
 

time: 32.1 us -> 32.4 us (level)
  transfers between devices with their start and end apart: 10 -> 10, of which waited for: 5 -> 4; matrix products, arithmetic and copies ran while one was open for 0% -> 0% of each run, Pallas kernels for 26% -> 26%
where the time goes in v10:
time: 32.4 us; the launch traced here: 32.2 us
  starting transfers between devices  13.8 us (43%)
  Pallas kernels  13.4 us (41%)
  waiting for transfers between devices  4.34 us (13%)
  between operations  0.74 us (2%)
    ppermute x7, starting transfers between devices, exchange(): lax.ppermute(xs[k], axis, [(s, s ^ k) for s in range(n)])  8.2 us
    ppermute x3, starting transfers between devices, exchange_ring(): lax.ppermute(xs[k], axis, [(s, (s + k) % n) for s in range(n)])  5.56 us
    pallas_call x3, Pallas kernels, sweep(): pl.pallas_call(lambda *refs: sweep_kernel(units, done, *refs), out_shape=...  5.4 us
    ppermute x7, waiting for transfers between devices, exchange(): lax.ppermute(xs[k], axis, [(s, s ^ k) for s in range(n)])  3.41 us
    pallas_call x1, Pallas kernels, first_sweep(): pl.pallas_call(lambda *refs: sweep_kernel(units, (), *refs[:5], None, *re...  2.86 us
    pallas_call x1, Pallas kernels, shards(): pl.pallas_call(lambda *refs: first_kernel(n, *refs), out_shape=[shape((bl...  2.67 us
    pallas_call x1, Pallas kernels, shards(): pl.pallas_call(lambda *refs: last_kernel(n, responses, *refs), out_shape=...  1.92 us
    ppermute x3, waiting for transfers between devices, exchange_ring(): lax.ppermute(xs[k], axis, [(s, (s + k) % n) for s in range(n)])  0.92 us
  transfers between devices with their start and end apart: 10, of which 4 were waited for; matrix products, arithmetic and copies ran while one was open for 0% of the time, Pallas kernels for 26%

profile of v10, /device:TPU:0, one launch (start us, length us, event | category | flops | bytes accessed | tf_op | source)
XLA Modules:
  0.0 32.2 jit_solution(9785623246979014116)
XLA Ops:
  0.6 2.7 %first.1 = (bf16[336,128]{1,0:T(8,128)(2,1)S(1)}, bf16[336,128]{1,0:T(8,128)(2,1)S(1)}, bf16[336,128]{1,0:T(8,128)(2,1)S(1)}, bf16[336,128]{1,0:T(8,128)(2,1)S(1...) custom-call(s32[4]{0:T(128)} %refs_0_.1, ...), custom_call_target="tpu_custom_call" | custom-call | tf_op jit(solution)/shard_map/first/pallas_call | solution.py:401
  3.3 3.0 %collective-permute-start = (bf16[336,128]{1,0:T(8,128)(2,1)S(1)}, bf16[336,128]{1,0:T(8,128)(2,1)S(1)}, u32[]{:S(2)}, u32[]{:S(2)}) collective-permute-start(bf16[336,128]{1,0:T(8,128)(2,1)S(1)} %get-tuple-element.66), channel_id=1, source_target_pairs={{0,16},{8,24},{16,0},{24,8},{1,17},{9,25},{17,1},{25,9},{2,18},{10... | collective-permute-start | bytes 258056 | tf_op jit(solution)/shard_map/ppermute | solution.py:355
  6.3 1.4 %collective-permute-start.1 = (bf16[336,128]{1,0:T(8,128)(2,1)S(1)}, bf16[336,128]{1,0:T(8,128)(2,1)S(1)}, u32[]{:S(2)}, u32[]{:S(2)}) collective-permute-start(bf16[336,128]{1,0:T(8,128)(2,1)S(1)} %get-tuple-element.67), channel_id=1, source_target_pairs={{0,24},{8,16},{16,8},{24,0},{1,25},{9,17},{17,9},{25,1},{2,26},{10... | collective-permute-start | bytes 258056 | tf_op jit(solution)/shard_map/ppermute | solution.py:355
  7.8 0.1 collective-permute-start.2
  7.9 2.9 %sweep.4 = (f32[512,128]{1,0:T(8,128)S(1)}, f32[4,512,256]{2,1,0:T(8,128)S(1)}, f32[4,512,256]{2,1,0:T(8,128)S(1)}, bf16[4,512,256]{2,1,0:T(8,128)(2,1)S(1)}, bf...) custom-call(f32[40,512]{1,0:T(8,128)S(1)} %get-tuple-element.59.refs, ...), custom_call_target="tpu_custom_call" | custom-call | tf_op jit(solution)/shard_map/sweep/pallas_call | solution.py:434
  10.8 0.0 collective-permute-done.refs_1_
  10.8 1.7 %collective-permute-done.1.refs_2_ = bf16[336,128]{1,0:T(8,128)(2,1)S(1)} collective-permute-done((bf16[336,128]{1,0:T(8,128)(2,1)S(1)}, bf16[336,128]{1,0:T(8,128)(2,1)S(1)}, u32[]{:S(2)}, u32[]{:S(2)}) %collective-permute-start.1) | collective-permute-done | bytes 86048 | tf_op jit(solution)/shard_map/ppermute | solution.py:355
  12.4 0.0 collective-permute-done.2.refs_3_
  12.4 0.2 second.1
  12.7 1.6 %collective-permute-start.3 = (bf16[192,128]{1,0:T(8,128)(2,1)S(1)}, bf16[192,128]{1,0:T(8,128)(2,1)S(1)}, u32[]{:S(2)}, u32[]{:S(2)}) collective-permute-start(bf16[192,128]{1,0:T(8,128)(2,1)S(1)} %get-tuple-element.71), channel_id=1, source_target_pairs={{0,2},{2,4},{4,6},{6,0},{1,3},{3,5},{5,7},{7,1},{8,10},{10,12},{12... | collective-permute-start | bytes 147464 | tf_op jit(solution)/shard_map/ppermute | solution.py:360
  14.3 2.6 %collective-permute-start.4 = (bf16[192,128]{1,0:T(8,128)(2,1)S(1)}, bf16[192,128]{1,0:T(8,128)(2,1)S(1)}, u32[]{:S(2)}, u32[]{:S(2)}) collective-permute-start(bf16[192,128]{1,0:T(8,128)(2,1)S(1)} %get-tuple-element.72), channel_id=1, source_target_pairs={{0,4},{2,6},{4,0},{6,2},{1,5},{3,7},{5,1},{7,3},{8,12},{10,14},{12... | collective-permute-start | bytes 147464 | tf_op jit(solution)/shard_map/ppermute | solution.py:360
  16.9 1.3 %collective-permute-start.5 = (bf16[192,128]{1,0:T(8,128)(2,1)S(1)}, bf16[192,128]{1,0:T(8,128)(2,1)S(1)}, u32[]{:S(2)}, u32[]{:S(2)}) collective-permute-start(bf16[192,128]{1,0:T(8,128)(2,1)S(1)} %get-tuple-element.73), channel_id=1, source_target_pairs={{0,6},{2,0},{4,2},{6,4},{1,7},{3,1},{5,3},{7,5},{8,14},{10,8},{12,... | collective-permute-start | bytes 147464 | tf_op jit(solution)/shard_map/ppermute | solution.py:360
  18.3 1.8 %sweep.5 = (f32[4,512,256]{2,1,0:T(8,128)S(1)}, f32[4,512,256]{2,1,0:T(8,128)S(1)}, bf16[4,512,256]{2,1,0:T(8,128)(2,1)S(1)}, bf16[4,512,256]{2,1,0:T(8,128)(2,1...) custom-call(f32[40,512]{1,0:T(8,128)S(1)} %get-tuple-element.59.refs, ...), custom_call_target="tpu_custom_call", output_to_operand_aliasing={{0}: (7, {}), {1}: (8, {}), {2}: (9, {}), {3}: (10, {}), {4... | custom-call | tf_op jit(solution)/shard_map/sweep/pallas_call | solution.py:446
  20.1 0.0 collective-permute-done.3.refs_1_
  20.1 0.0 collective-permute-done.4.refs_2_
  20.1 0.9 %collective-permute-done.5.refs_3_ = bf16[192,128]{1,0:T(8,128)(2,1)S(1)} collective-permute-done((bf16[192,128]{1,0:T(8,128)(2,1)S(1)}, bf16[192,128]{1,0:T(8,128)(2,1)S(1)}, u32[]{:S(2)}, u32[]{:S(2)}) %collective-permute-start.5) | collective-permute-done | bytes 49184 | tf_op jit(solution)/shard_map/ppermute | solution.py:360
  21.0 0.1 collective-permute-start.6
  21.1 1.0 %sweep.6 = (f32[4,512,256]{2,1,0:T(8,128)S(1)}, f32[4,512,256]{2,1,0:T(8,128)S(1)}, bf16[4,512,256]{2,1,0:T(8,128)(2,1)S(1)}, bf16[4,512,256]{2,1,0:T(8,128)(2,1...) custom-call(f32[40,512]{1,0:T(8,128)S(1)} %get-tuple-element.59.refs, ...), custom_call_target="tpu_custom_call", output_to_operand_aliasing={{0}: (7, {}), {1}: (8, {}), {2}: (9, {}), {3}: (10, {}), {4... | custom-call | tf_op jit(solution)/shard_map/sweep/pallas_call | solution.py:446
  22.1 0.3 collective-permute-done.6.refs_5_
  22.4 0.3 third.1
  22.6 1.5 %collective-permute-start.7 = (bf16[320,128]{1,0:T(8,128)(2,1)S(1)}, bf16[320,128]{1,0:T(8,128)(2,1)S(1)}, u32[]{:S(2)}, u32[]{:S(2)}) collective-permute-start(bf16[320,128]{1,0:T(8,128)(2,1)S(1)} %get-tuple-element.102), channel_id=1, source_target_pairs={{0,16},{8,24},{16,0},{24,8},{1,17},{9,25},{17,1},{25,9},{2,18},{10... | collective-permute-start | bytes 245768 | tf_op jit(solution)/shard_map/ppermute | solution.py:355
  24.2 1.2 %collective-permute-start.8 = (bf16[320,128]{1,0:T(8,128)(2,1)S(1)}, bf16[320,128]{1,0:T(8,128)(2,1)S(1)}, u32[]{:S(2)}, u32[]{:S(2)}) collective-permute-start(bf16[320,128]{1,0:T(8,128)(2,1)S(1)} %get-tuple-element.103), channel_id=1, source_target_pairs={{0,24},{8,16},{16,8},{24,0},{1,25},{9,17},{17,9},{25,1},{2,26},{10... | collective-permute-start | bytes 245768 | tf_op jit(solution)/shard_map/ppermute | solution.py:355
  25.4 0.8 %collective-permute-start.9 = (bf16[320,128]{1,0:T(8,128)(2,1)S(1)}, bf16[320,128]{1,0:T(8,128)(2,1)S(1)}, u32[]{:S(2)}, u32[]{:S(2)}) collective-permute-start(bf16[320,128]{1,0:T(8,128)(2,1)S(1)} %get-tuple-element.104), channel_id=1, source_target_pairs={{0,8},{8,0},{16,24},{24,16},{1,9},{9,1},{17,25},{25,17},{2,10},{10... | collective-permute-start | bytes 245768 | tf_op jit(solution)/shard_map/ppermute | solution.py:355
  26.2 0.0 copy-start
  26.2 0.0 copy-start.1
  26.2 2.6 %sweep.7 = (f32[4,512,256]{2,1,0:T(8,128)S(1)}, f32[4,512,256]{2,1,0:T(8,128)S(1)}, bf16[4,512,256]{2,1,0:T(8,128)(2,1)S(1)}, bf16[4,512,256]{2,1,0:T(8,128)(2,1...) custom-call(f32[40,512]{1,0:T(8,128)S(1)} %get-tuple-element.59.refs, ...), custom_call_target="tpu_custom_call", output_to_operand_aliasing={{0}: (7, {}), {1}: (8, {}), {2}: (9, {}), {3}: (10, {}), {4... | custom-call | tf_op jit(solution)/shard_map/sweep/pallas_call | solution.py:446
  28.9 0.0 collective-permute-done.7.refs_9_
  28.9 1.4 %collective-permute-done.8.refs_10_ = bf16[320,128]{1,0:T(8,128)(2,1)S(1)} collective-permute-done((bf16[320,128]{1,0:T(8,128)(2,1)S(1)}, bf16[320,128]{1,0:T(8,128)(2,1)S(1)}, u32[]{:S(2)}, u32[]{:S(2)}) %collective-permute-start.8) | collective-permute-done | bytes 81952 | tf_op jit(solution)/shard_map/ppermute | solution.py:355
  30.3 0.0 collective-permute-done.9.refs_11_
  30.3 0.0 copy-done
  30.3 0.0 copy-done.1
  30.3 1.9 %last.1 = (bf16[4,512,256]{2,1,0:T(8,128)(2,1)}, bf16[4,512,256]{2,1,0:T(8,128)(2,1)}, bf16[1,256,256]{2,1,0:T(8,128)(2,1)}, bf16[1,256,256]{2,1,0:T(8,128)(2,1)}) custom-call(f32[512,128]{1,0:T(8,128)S(1)} %get-tuple-element.64.refs_5_.refs_0_, bf16[4,512,256]{2,1,0:T(8,128)(2,1)S(1)} %get-tuple-element.98.refs_1_, ...), custom_call_target="tpu_custom_call" | custom-call | tf_op jit(solution)/shard_map/last/pallas_call | solution.py:495
  (1 shorter events, 0.0 us)
Async XLA Ops:
  3.3 7.4 %collective-permute-start = (bf16[336,128]{1,0:T(8,128)(2,1)S(1)}, bf16[336,128]{1,0:T(8,128)(2,1)S(1)}, u32[]{:S(2)}, u32[]{:S(2)}) collective-permute-start(bf16[336,128]{1,0:T(8,128)(2,1)S(1)} %get-tuple-element.66), channel_id=1, source_target_pairs={{0,16},{8,24},{16,0},{24,8},{1,17},{9,25},{17,1},{25,9},{2,18},{10... | collective-permute-start | bytes 258056 | tf_op jit(solution)/shard_map/ppermute | solution.py:355
  6.3 6.1 %collective-permute-start.1 = (bf16[336,128]{1,0:T(8,128)(2,1)S(1)}, bf16[336,128]{1,0:T(8,128)(2,1)S(1)}, u32[]{:S(2)}, u32[]{:S(2)}) collective-permute-start(bf16[336,128]{1,0:T(8,128)(2,1)S(1)} %get-tuple-element.67), channel_id=1, source_target_pairs={{0,24},{8,16},{16,8},{24,0},{1,25},{9,17},{17,9},{25,1},{2,26},{10... | collective-permute-start | bytes 258056 | tf_op jit(solution)/shard_map/ppermute | solution.py:355
  7.8 4.7 %collective-permute-start.2 = (bf16[336,128]{1,0:T(8,128)(2,1)S(1)}, bf16[336,128]{1,0:T(8,128)(2,1)S(1)}, u32[]{:S(2)}, u32[]{:S(2)}) collective-permute-start(bf16[336,128]{1,0:T(8,128)(2,1)S(1)} %get-tuple-element.68), channel_id=1, source_target_pairs={{0,8},{8,0},{16,24},{24,16},{1,9},{9,1},{17,25},{25,17},{2,10},{10... | collective-permute-start | bytes 258056 | tf_op jit(solution)/shard_map/ppermute | solution.py:355
  12.7 7.4 %collective-permute-start.3 = (bf16[192,128]{1,0:T(8,128)(2,1)S(1)}, bf16[192,128]{1,0:T(8,128)(2,1)S(1)}, u32[]{:S(2)}, u32[]{:S(2)}) collective-permute-start(bf16[192,128]{1,0:T(8,128)(2,1)S(1)} %get-tuple-element.71), channel_id=1, source_target_pairs={{0,2},{2,4},{4,6},{6,0},{1,3},{3,5},{5,7},{7,1},{8,10},{10,12},{12... | collective-permute-start | bytes 147464 | tf_op jit(solution)/shard_map/ppermute | solution.py:360
  14.3 5.8 %collective-permute-start.4 = (bf16[192,128]{1,0:T(8,128)(2,1)S(1)}, bf16[192,128]{1,0:T(8,128)(2,1)S(1)}, u32[]{:S(2)}, u32[]{:S(2)}) collective-permute-start(bf16[192,128]{1,0:T(8,128)(2,1)S(1)} %get-tuple-element.72), channel_id=1, source_target_pairs={{0,4},{2,6},{4,0},{6,2},{1,5},{3,7},{5,1},{7,3},{8,12},{10,14},{12... | collective-permute-start | bytes 147464 | tf_op jit(solution)/shard_map/ppermute | solution.py:360
  16.9 4.1 %collective-permute-start.5 = (bf16[192,128]{1,0:T(8,128)(2,1)S(1)}, bf16[192,128]{1,0:T(8,128)(2,1)S(1)}, u32[]{:S(2)}, u32[]{:S(2)}) collective-permute-start(bf16[192,128]{1,0:T(8,128)(2,1)S(1)} %get-tuple-element.73), channel_id=1, source_target_pairs={{0,6},{2,0},{4,2},{6,4},{1,7},{3,1},{5,3},{7,5},{8,14},{10,8},{12,... | collective-permute-start | bytes 147464 | tf_op jit(solution)/shard_map/ppermute | solution.py:360
  21.0 1.3 %collective-permute-start.6 = (bf16[320,128]{1,0:T(8,128)(2,1)S(1)}, bf16[320,128]{1,0:T(8,128)(2,1)S(1)}, u32[]{:S(2)}, u32[]{:S(2)}) collective-permute-start(bf16[320,128]{1,0:T(8,128)(2,1)S(1)} %get-tuple-element.83), channel_id=1, source_target_pairs={{0,1},{1,0},{2,3},{3,2},{4,5},{5,4},{6,7},{7,6},{8,9},{9,8},{10,11... | collective-permute-start | bytes 245768 | tf_op jit(solution)/shard_map/ppermute | solution.py:355
  22.6 6.2 %collective-permute-start.7 = (bf16[320,128]{1,0:T(8,128)(2,1)S(1)}, bf16[320,128]{1,0:T(8,128)(2,1)S(1)}, u32[]{:S(2)}, u32[]{:S(2)}) collective-permute-start(bf16[320,128]{1,0:T(8,128)(2,1)S(1)} %get-tuple-element.102), channel_id=1, source_target_pairs={{0,16},{8,24},{16,0},{24,8},{1,17},{9,25},{17,1},{25,9},{2,18},{10... | collective-permute-start | bytes 245768 | tf_op jit(solution)/shard_map/ppermute | solution.py:355
  24.2 6.1 %collective-permute-start.8 = (bf16[320,128]{1,0:T(8,128)(2,1)S(1)}, bf16[320,128]{1,0:T(8,128)(2,1)S(1)}, u32[]{:S(2)}, u32[]{:S(2)}) collective-permute-start(bf16[320,128]{1,0:T(8,128)(2,1)S(1)} %get-tuple-element.103), channel_id=1, source_target_pairs={{0,24},{8,16},{16,8},{24,0},{1,25},{9,17},{17,9},{25,1},{2,26},{10... | collective-permute-start | bytes 245768 | tf_op jit(solution)/shard_map/ppermute | solution.py:355
  25.4 4.9 %collective-permute-start.9 = (bf16[320,128]{1,0:T(8,128)(2,1)S(1)}, bf16[320,128]{1,0:T(8,128)(2,1)S(1)}, u32[]{:S(2)}, u32[]{:S(2)}) collective-permute-start(bf16[320,128]{1,0:T(8,128)(2,1)S(1)} %get-tuple-element.104), channel_id=1, source_target_pairs={{0,8},{8,0},{16,24},{24,16},{1,9},{9,1},{17,25},{25,17},{2,10},{10... | collective-permute-start | bytes 245768 | tf_op jit(solution)/shard_map/ppermute | solution.py:355
  26.2 4.1 %copy-start = (bf16[1,256,256]{2,1,0:T(8,128)(2,1)S(1)}, bf16[1,256,256]{2,1,0:T(8,128)(2,1)}, u32[]{:S(2)}) copy-start(bf16[1,256,256]{2,1,0:T(8,128)(2,1)} %refs_5_.3) | copy-start | bytes 393220
  26.2 4.1 %copy-start.1 = (bf16[1,256,256]{2,1,0:T(8,128)(2,1)S(1)}, bf16[1,256,256]{2,1,0:T(8,128)(2,1)}, u32[]{:S(2)}) copy-start(bf16[1,256,256]{2,1,0:T(8,128)(2,1)} %refs_6_.3) | copy-start | bytes 393220

commit v11 on v9

--- a/solution.py
+++ b/solution.py
@@ -184,7 +184,7 @@
 
 
 def swap_kernel(chips, *refs):
-    got, sent_ref, kept_ref = refs[:chips], refs[chips + 1], refs[chips + 2]
+    got, sent_ref, kept_ref = [refs[middle_first(chips).index(k)] for k in range(chips)], refs[chips + 1], refs[chips + 2]
     block = got[0].shape[0] // 3
     totals = []
     for c in range(2):
@@ -314,7 +314,6 @@
     part = DH // n
     block = H * part
     place = partners(n)
-    slots = q_ref.shape[1]
     tokens = keys_ref.shape[1]
     copies = []
 
@@ -339,10 +338,8 @@
     send(dk_buf, dk_hbm.at[0])
     send(dv_buf, dv_hbm.at[0])
     for r in range(count):
-        for t in range(0, slots, HALF):
-            at = slice(t, t + HALF)
-            out_buf[r, at, :] = (po_ref[r, at, :] + mm(q_ref[r, at, :], start[r])).astype(BF16)
-            dq_buf[r, at, :] = (pdq_ref[r, at, :] + mm_nt(grad_ref[r, at, :], start[r])).astype(BF16)
+        out_buf[r] = (po_ref[r] + mm(q_ref[r], start[r])).astype(BF16)
+        dq_buf[r] = (pdq_ref[r] + mm_nt(grad_ref[r], start[r])).astype(BF16)
         send(out_buf.at[r], out_hbm.at[r])
         send(dq_buf.at[r], dq_hbm.at[r])
     for copy in copies:
@@ -357,6 +354,10 @@
 def exchange_ring(xs, axis):
     n = lax.axis_size(axis)
     return [xs[0]] + [lax.ppermute(xs[k], axis, [(s, (s + k) % n) for s in range(n)]) for k in range(1, n)]
+
+
+def middle_first(n):
+    return [0, *sorted(range(1, n), key=lambda k: (-min(k, n - k), k))]
 
 
 def far_first(refs):
@@ -460,6 +461,7 @@
     )(*got1, token)
     msgs, later = outs[:chips], outs[chips]
     got2 = exchange_ring(msgs, "z")
+    got2 = [got2[k] for k in middle_first(chips)]
     held, token = sweep(units[3:5], held, later)
     sent, kept = pl.pallas_call(
         lambda *refs: swap_kernel(chips, *refs),

time: 32.1 us -> 32.5 us (1.012)
  starting transfers between devices: 13.8 us -> 14.7 us
  waiting for transfers between devices: 4.02 us -> 3.57 us
    ppermute x3, starting transfers between devices: 5.56 us -> 6.48 us  [exchange_ring(): lax.ppermute(xs[k], axis, [(s, (s + k) % n) for s in range(n)])]
    ppermute x3, waiting for transfers between devices: 0.92 us -> 0.56 us  [exchange_ring(): lax.ppermute(xs[k], axis, [(s, (s + k) % n) for s in range(n)])]
  transfers between devices with their start and end apart: 10 -> 10, of which waited for: 5 -> 7; matrix products, arithmetic and copies ran while one was open for 0% -> 0% of each run, Pallas kernels for 26% -> 25%
where the time goes in v11:
time: 32.5 us; the launch traced here: 32.4 us
  starting transfers between devices  14.7 us (45%)
  Pallas kernels  13.3 us (41%)
  waiting for transfers between devices  3.57 us (11%)
  between operations  0.73 us (2%)
    ppermute x7, starting transfers between devices, exchange(): lax.ppermute(xs[k], axis, [(s, s ^ k) for s in range(n)])  8.23 us
    ppermute x3, starting transfers between devices, exchange_ring(): lax.ppermute(xs[k], axis, [(s, (s + k) % n) for s in range(n)])  6.48 us
    pallas_call x3, Pallas kernels, sweep(): pl.pallas_call(lambda *refs: sweep_kernel(units, done, *refs), out_shape=...  5.4 us
    ppermute x7, waiting for transfers between devices, exchange(): lax.ppermute(xs[k], axis, [(s, s ^ k) for s in range(n)])  3.01 us
    pallas_call x1, Pallas kernels, first_sweep(): pl.pallas_call(lambda *refs: sweep_kernel(units, (), *refs[:5], None, *re...  2.86 us
    pallas_call x1, Pallas kernels, shards(): pl.pallas_call(lambda *refs: first_kernel(n, *refs), out_shape=[shape((bl...  2.67 us
    pallas_call x1, Pallas kernels, shards(): pl.pallas_call(lambda *refs: last_kernel(n, responses, *refs), out_shape=...  1.89 us
  transfers between devices with their start and end apart: 10, of which 7 were waited for; matrix products, arithmetic and copies ran while one was open for 0% of the time, Pallas kernels for 25%

profile of v11, /device:TPU:0, one launch (start us, length us, event | category | flops | bytes accessed | tf_op | source)
XLA Modules:
  0.0 32.4 jit_solution(2454373494911890767)
XLA Ops:
  0.6 2.7 %first.1 = (bf16[336,128]{1,0:T(8,128)(2,1)S(1)}, bf16[336,128]{1,0:T(8,128)(2,1)S(1)}, bf16[336,128]{1,0:T(8,128)(2,1)S(1)}, bf16[336,128]{1,0:T(8,128)(2,1)S(1...) custom-call(s32[4]{0:T(128)} %refs_0_.1, ...), custom_call_target="tpu_custom_call" | custom-call | tf_op jit(solution)/shard_map/first/pallas_call | solution.py:393
  3.3 4.0 %collective-permute-start = (bf16[336,128]{1,0:T(8,128)(2,1)S(1)}, bf16[336,128]{1,0:T(8,128)(2,1)S(1)}, u32[]{:S(2)}, u32[]{:S(2)}) collective-permute-start(bf16[336,128]{1,0:T(8,128)(2,1)S(1)} %get-tuple-element.66), channel_id=1, source_target_pairs={{0,24},{8,16},{16,8},{24,0},{1,25},{9,17},{17,9},{25,1},{2,26},{10... | collective-permute-start | bytes 258056 | tf_op jit(solution)/shard_map/ppermute | solution.py:351
  7.3 0.5 %collective-permute-start.1 = (bf16[336,128]{1,0:T(8,128)(2,1)S(1)}, bf16[336,128]{1,0:T(8,128)(2,1)S(1)}, u32[]{:S(2)}, u32[]{:S(2)}) collective-permute-start(bf16[336,128]{1,0:T(8,128)(2,1)S(1)} %get-tuple-element.67), channel_id=1, source_target_pairs={{0,16},{8,24},{16,0},{24,8},{1,17},{9,25},{17,1},{25,9},{2,18},{10... | collective-permute-start | bytes 258056 | tf_op jit(solution)/shard_map/ppermute | solution.py:351
  7.8 0.1 collective-permute-start.2
  7.9 2.9 %sweep.4 = (f32[512,128]{1,0:T(8,128)S(1)}, f32[4,512,256]{2,1,0:T(8,128)S(1)}, f32[4,512,256]{2,1,0:T(8,128)S(1)}, bf16[4,512,256]{2,1,0:T(8,128)(2,1)S(1)}, bf...) custom-call(f32[40,512]{1,0:T(8,128)S(1)} %get-tuple-element.59.refs, ...), custom_call_target="tpu_custom_call" | custom-call | tf_op jit(solution)/shard_map/sweep/pallas_call | solution.py:426
  10.8 0.0 collective-permute-done.refs_1_
  10.8 1.0 %collective-permute-done.1.refs_2_ = bf16[336,128]{1,0:T(8,128)(2,1)S(1)} collective-permute-done((bf16[336,128]{1,0:T(8,128)(2,1)S(1)}, bf16[336,128]{1,0:T(8,128)(2,1)S(1)}, u32[]{:S(2)}, u32[]{:S(2)}) %collective-permute-start.1) | collective-permute-done | bytes 86048 | tf_op jit(solution)/shard_map/ppermute | solution.py:351
  11.8 0.5 %collective-permute-done.2.refs_3_ = bf16[336,128]{1,0:T(8,128)(2,1)S(1)} collective-permute-done((bf16[336,128]{1,0:T(8,128)(2,1)S(1)}, bf16[336,128]{1,0:T(8,128)(2,1)S(1)}, u32[]{:S(2)}, u32[]{:S(2)}) %collective-permute-start.2) | collective-permute-done | bytes 86048 | tf_op jit(solution)/shard_map/ppermute | solution.py:351
  12.3 0.2 second.1
  12.5 2.7 %collective-permute-start.3 = (bf16[192,128]{1,0:T(8,128)(2,1)S(1)}, bf16[192,128]{1,0:T(8,128)(2,1)S(1)}, u32[]{:S(2)}, u32[]{:S(2)}) collective-permute-start(bf16[192,128]{1,0:T(8,128)(2,1)S(1)} %get-tuple-element.71), channel_id=1, source_target_pairs={{0,4},{2,6},{4,0},{6,2},{1,5},{3,7},{5,1},{7,3},{8,12},{10,14},{12... | collective-permute-start | bytes 147464 | tf_op jit(solution)/shard_map/ppermute | solution.py:356
  15.2 1.6 %collective-permute-start.4 = (bf16[192,128]{1,0:T(8,128)(2,1)S(1)}, bf16[192,128]{1,0:T(8,128)(2,1)S(1)}, u32[]{:S(2)}, u32[]{:S(2)}) collective-permute-start(bf16[192,128]{1,0:T(8,128)(2,1)S(1)} %get-tuple-element.72), channel_id=1, source_target_pairs={{0,2},{2,4},{4,6},{6,0},{1,3},{3,5},{5,7},{7,1},{8,10},{10,12},{12... | collective-permute-start | bytes 147464 | tf_op jit(solution)/shard_map/ppermute | solution.py:356
  16.7 2.2 %collective-permute-start.5 = (bf16[192,128]{1,0:T(8,128)(2,1)S(1)}, bf16[192,128]{1,0:T(8,128)(2,1)S(1)}, u32[]{:S(2)}, u32[]{:S(2)}) collective-permute-start(bf16[192,128]{1,0:T(8,128)(2,1)S(1)} %get-tuple-element.73), channel_id=1, source_target_pairs={{0,6},{2,0},{4,2},{6,4},{1,7},{3,1},{5,3},{7,5},{8,14},{10,8},{12,... | collective-permute-start | bytes 147464 | tf_op jit(solution)/shard_map/ppermute | solution.py:356
  19.0 1.8 %sweep.5 = (f32[4,512,256]{2,1,0:T(8,128)S(1)}, f32[4,512,256]{2,1,0:T(8,128)S(1)}, bf16[4,512,256]{2,1,0:T(8,128)(2,1)S(1)}, bf16[4,512,256]{2,1,0:T(8,128)(2,1...) custom-call(f32[40,512]{1,0:T(8,128)S(1)} %get-tuple-element.59.refs, ...), custom_call_target="tpu_custom_call", output_to_operand_aliasing={{0}: (7, {}), {1}: (8, {}), {2}: (9, {}), {3}: (10, {}), {4... | custom-call | tf_op jit(solution)/shard_map/sweep/pallas_call | solution.py:438
  20.8 0.0 collective-permute-done.3.refs_1_
  20.8 0.4 %collective-permute-done.4.refs_2_ = bf16[192,128]{1,0:T(8,128)(2,1)S(1)} collective-permute-done((bf16[192,128]{1,0:T(8,128)(2,1)S(1)}, bf16[192,128]{1,0:T(8,128)(2,1)S(1)}, u32[]{:S(2)}, u32[]{:S(2)}) %collective-permute-start.4) | collective-permute-done | bytes 49184 | tf_op jit(solution)/shard_map/ppermute | solution.py:356
  21.1 0.2 collective-permute-done.5.refs_3_
  21.4 0.1 collective-permute-start.6
  21.5 1.0 %sweep.6 = (f32[4,512,256]{2,1,0:T(8,128)S(1)}, f32[4,512,256]{2,1,0:T(8,128)S(1)}, bf16[4,512,256]{2,1,0:T(8,128)(2,1)S(1)}, bf16[4,512,256]{2,1,0:T(8,128)(2,1...) custom-call(f32[40,512]{1,0:T(8,128)S(1)} %get-tuple-element.59.refs, ...), custom_call_target="tpu_custom_call", output_to_operand_aliasing={{0}: (7, {}), {1}: (8, {}), {2}: (9, {}), {3}: (10, {}), {4... | custom-call | tf_op jit(solution)/shard_map/sweep/pallas_call | solution.py:438
  22.4 0.3 collective-permute-done.6.refs_5_
  22.7 0.3 third.1
  23.0 1.2 %collective-permute-start.7 = (bf16[320,128]{1,0:T(8,128)(2,1)S(1)}, bf16[320,128]{1,0:T(8,128)(2,1)S(1)}, u32[]{:S(2)}, u32[]{:S(2)}) collective-permute-start(bf16[320,128]{1,0:T(8,128)(2,1)S(1)} %get-tuple-element.102), channel_id=1, source_target_pairs={{0,8},{8,0},{16,24},{24,16},{1,9},{9,1},{17,25},{25,17},{2,10},{10... | collective-permute-start | bytes 245768 | tf_op jit(solution)/shard_map/ppermute | solution.py:351
  24.2 0.9 %collective-permute-start.8 = (bf16[320,128]{1,0:T(8,128)(2,1)S(1)}, bf16[320,128]{1,0:T(8,128)(2,1)S(1)}, u32[]{:S(2)}, u32[]{:S(2)}) collective-permute-start(bf16[320,128]{1,0:T(8,128)(2,1)S(1)} %get-tuple-element.103), channel_id=1, source_target_pairs={{0,16},{8,24},{16,0},{24,8},{1,17},{9,25},{17,1},{25,9},{2,18},{10... | collective-permute-start | bytes 245768 | tf_op jit(solution)/shard_map/ppermute | solution.py:351
  25.1 1.4 %collective-permute-start.9 = (bf16[320,128]{1,0:T(8,128)(2,1)S(1)}, bf16[320,128]{1,0:T(8,128)(2,1)S(1)}, u32[]{:S(2)}, u32[]{:S(2)}) collective-permute-start(bf16[320,128]{1,0:T(8,128)(2,1)S(1)} %get-tuple-element.104), channel_id=1, source_target_pairs={{0,24},{8,16},{16,8},{24,0},{1,25},{9,17},{17,9},{25,1},{2,26},{10... | collective-permute-start | bytes 245768 | tf_op jit(solution)/shard_map/ppermute | solution.py:351
  26.6 0.0 copy-start
  26.6 0.0 copy-start.1
  26.6 2.6 %sweep.7 = (f32[4,512,256]{2,1,0:T(8,128)S(1)}, f32[4,512,256]{2,1,0:T(8,128)S(1)}, bf16[4,512,256]{2,1,0:T(8,128)(2,1)S(1)}, bf16[4,512,256]{2,1,0:T(8,128)(2,1...) custom-call(f32[40,512]{1,0:T(8,128)S(1)} %get-tuple-element.59.refs, ...), custom_call_target="tpu_custom_call", output_to_operand_aliasing={{0}: (7, {}), {1}: (8, {}), {2}: (9, {}), {3}: (10, {}), {4... | custom-call | tf_op jit(solution)/shard_map/sweep/pallas_call | solution.py:438
  29.2 0.0 collective-permute-done.7.refs_9_
  29.2 0.2 collective-permute-done.8.refs_10_
  29.4 1.1 %collective-permute-done.9.refs_11_ = bf16[320,128]{1,0:T(8,128)(2,1)S(1)} collective-permute-done((bf16[320,128]{1,0:T(8,128)(2,1)S(1)}, bf16[320,128]{1,0:T(8,128)(2,1)S(1)}, u32[]{:S(2)}, u32[]{:S(2)}) %collective-permute-start.9) | collective-permute-done | bytes 81952 | tf_op jit(solution)/shard_map/ppermute | solution.py:351
  30.5 0.0 copy-done
  30.5 0.0 copy-done.1
  30.5 1.9 %last.1 = (bf16[4,512,256]{2,1,0:T(8,128)(2,1)}, bf16[4,512,256]{2,1,0:T(8,128)(2,1)}, bf16[1,256,256]{2,1,0:T(8,128)(2,1)}, bf16[1,256,256]{2,1,0:T(8,128)(2,1)}) custom-call(f32[512,128]{1,0:T(8,128)S(1)} %get-tuple-element.64.refs_5_.refs_0_, bf16[4,512,256]{2,1,0:T(8,128)(2,1)S(1)} %get-tuple-element.98.refs_1_, ...), custom_call_target="tpu_custom_call" | custom-call | tf_op jit(solution)/shard_map/last/pallas_call | solution.py:488
  (1 shorter events, 0.0 us)
Async XLA Ops:
  3.3 7.5 %collective-permute-start = (bf16[336,128]{1,0:T(8,128)(2,1)S(1)}, bf16[336,128]{1,0:T(8,128)(2,1)S(1)}, u32[]{:S(2)}, u32[]{:S(2)}) collective-permute-start(bf16[336,128]{1,0:T(8,128)(2,1)S(1)} %get-tuple-element.66), channel_id=1, source_target_pairs={{0,24},{8,16},{16,8},{24,0},{1,25},{9,17},{17,9},{25,1},{2,26},{10... | collective-permute-start | bytes 258056 | tf_op jit(solution)/shard_map/ppermute | solution.py:351
  7.3 4.5 %collective-permute-start.1 = (bf16[336,128]{1,0:T(8,128)(2,1)S(1)}, bf16[336,128]{1,0:T(8,128)(2,1)S(1)}, u32[]{:S(2)}, u32[]{:S(2)}) collective-permute-start(bf16[336,128]{1,0:T(8,128)(2,1)S(1)} %get-tuple-element.67), channel_id=1, source_target_pairs={{0,16},{8,24},{16,0},{24,8},{1,17},{9,25},{17,1},{25,9},{2,18},{10... | collective-permute-start | bytes 258056 | tf_op jit(solution)/shard_map/ppermute | solution.py:351
  7.8 4.5 %collective-permute-start.2 = (bf16[336,128]{1,0:T(8,128)(2,1)S(1)}, bf16[336,128]{1,0:T(8,128)(2,1)S(1)}, u32[]{:S(2)}, u32[]{:S(2)}) collective-permute-start(bf16[336,128]{1,0:T(8,128)(2,1)S(1)} %get-tuple-element.68), channel_id=1, source_target_pairs={{0,8},{8,0},{16,24},{24,16},{1,9},{9,1},{17,25},{25,17},{2,10},{10... | collective-permute-start | bytes 258056 | tf_op jit(solution)/shard_map/ppermute | solution.py:351
  12.5 8.3 %collective-permute-start.3 = (bf16[192,128]{1,0:T(8,128)(2,1)S(1)}, bf16[192,128]{1,0:T(8,128)(2,1)S(1)}, u32[]{:S(2)}, u32[]{:S(2)}) collective-permute-start(bf16[192,128]{1,0:T(8,128)(2,1)S(1)} %get-tuple-element.71), channel_id=1, source_target_pairs={{0,4},{2,6},{4,0},{6,2},{1,5},{3,7},{5,1},{7,3},{8,12},{10,14},{12... | collective-permute-start | bytes 147464 | tf_op jit(solution)/shard_map/ppermute | solution.py:356
  15.2 6.0 %collective-permute-start.4 = (bf16[192,128]{1,0:T(8,128)(2,1)S(1)}, bf16[192,128]{1,0:T(8,128)(2,1)S(1)}, u32[]{:S(2)}, u32[]{:S(2)}) collective-permute-start(bf16[192,128]{1,0:T(8,128)(2,1)S(1)} %get-tuple-element.72), channel_id=1, source_target_pairs={{0,2},{2,4},{4,6},{6,0},{1,3},{3,5},{5,7},{7,1},{8,10},{10,12},{12... | collective-permute-start | bytes 147464 | tf_op jit(solution)/shard_map/ppermute | solution.py:356
  16.7 4.6 %collective-permute-start.5 = (bf16[192,128]{1,0:T(8,128)(2,1)S(1)}, bf16[192,128]{1,0:T(8,128)(2,1)S(1)}, u32[]{:S(2)}, u32[]{:S(2)}) collective-permute-start(bf16[192,128]{1,0:T(8,128)(2,1)S(1)} %get-tuple-element.73), channel_id=1, source_target_pairs={{0,6},{2,0},{4,2},{6,4},{1,7},{3,1},{5,3},{7,5},{8,14},{10,8},{12,... | collective-permute-start | bytes 147464 | tf_op jit(solution)/shard_map/ppermute | solution.py:356
  21.4 1.3 %collective-permute-start.6 = (bf16[320,128]{1,0:T(8,128)(2,1)S(1)}, bf16[320,128]{1,0:T(8,128)(2,1)S(1)}, u32[]{:S(2)}, u32[]{:S(2)}) collective-permute-start(bf16[320,128]{1,0:T(8,128)(2,1)S(1)} %get-tuple-element.83), channel_id=1, source_target_pairs={{0,1},{1,0},{2,3},{3,2},{4,5},{5,4},{6,7},{7,6},{8,9},{9,8},{10,11... | collective-permute-start | bytes 245768 | tf_op jit(solution)/shard_map/ppermute | solution.py:351
  23.0 6.2 %collective-permute-start.7 = (bf16[320,128]{1,0:T(8,128)(2,1)S(1)}, bf16[320,128]{1,0:T(8,128)(2,1)S(1)}, u32[]{:S(2)}, u32[]{:S(2)}) collective-permute-start(bf16[320,128]{1,0:T(8,128)(2,1)S(1)} %get-tuple-element.102), channel_id=1, source_target_pairs={{0,8},{8,0},{16,24},{24,16},{1,9},{9,1},{17,25},{25,17},{2,10},{10... | collective-permute-start | bytes 245768 | tf_op jit(solution)/shard_map/ppermute | solution.py:351
  24.2 5.2 %collective-permute-start.8 = (bf16[320,128]{1,0:T(8,128)(2,1)S(1)}, bf16[320,128]{1,0:T(8,128)(2,1)S(1)}, u32[]{:S(2)}, u32[]{:S(2)}) collective-permute-start(bf16[320,128]{1,0:T(8,128)(2,1)S(1)} %get-tuple-element.103), channel_id=1, source_target_pairs={{0,16},{8,24},{16,0},{24,8},{1,17},{9,25},{17,1},{25,9},{2,18},{10... | collective-permute-start | bytes 245768 | tf_op jit(solution)/shard_map/ppermute | solution.py:351
  25.1 5.3 %collective-permute-start.9 = (bf16[320,128]{1,0:T(8,128)(2,1)S(1)}, bf16[320,128]{1,0:T(8,128)(2,1)S(1)}, u32[]{:S(2)}, u32[]{:S(2)}) collective-permute-start(bf16[320,128]{1,0:T(8,128)(2,1)S(1)} %get-tuple-element.104), channel_id=1, source_target_pairs={{0,24},{8,16},{16,8},{24,0},{1,25},{9,17},{17,9},{25,1},{2,26},{10... | collective-permute-start | bytes 245768 | tf_op jit(solution)/shard_map/ppermute | solution.py:351
  26.6 3.9 %copy-start = (bf16[1,256,256]{2,1,0:T(8,128)(2,1)S(1)}, bf16[1,256,256]{2,1,0:T(8,128)(2,1)}, u32[]{:S(2)}) copy-start(bf16[1,256,256]{2,1,0:T(8,128)(2,1)} %refs_5_.3) | copy-start | bytes 393220
  26.6 3.9 %copy-start.1 = (bf16[1,256,256]{2,1,0:T(8,128)(2,1)S(1)}, bf16[1,256,256]{2,1,0:T(8,128)(2,1)}, u32[]{:S(2)}) copy-start(bf16[1,256,256]{2,1,0:T(8,128)(2,1)} %refs_6_.3) | copy-start | bytes 393220

commit v12 on v9

--- a/solution.py
+++ b/solution.py
@@ -71,9 +71,9 @@
 ):
     msgs, (rows_ref, q, c, k_out, v_out) = refs[:n], refs[n : n + 5]
     keys, values, pgates, gates, mask, ids_ref, lens_ref, adv_ref, matrices, sems = refs[n + 5 :]
-    pairs = [(pgates_hbm, pgates), (gates_hbm, gates), (mask_hbm, mask)]
-    pairs += [(ids_hbm, ids_ref), (lens_hbm, lens_ref), (adv_hbm, adv_ref), (keys_hbm, keys), (values_hbm, values)]
-    pairs += [(q_hbm, q), (c_hbm, c), (k_hbm, k_out), (v_hbm, v_out)]
+    pairs = [(pgates_hbm, pgates), (gates_hbm, gates), (lens_hbm, lens_ref), (adv_hbm, adv_ref), (mask_hbm, mask)]
+    pairs += [(keys_hbm, keys), (values_hbm, values), (q_hbm, q), (c_hbm, c), (ids_hbm, ids_ref)]
+    pairs += [(k_hbm, k_out), (v_hbm, v_out)]
     copies = [pltpu.make_async_copy(a, b, sems.at[i]) for i, (a, b) in enumerate(pairs)]
     for copy in copies[:10]:
         copy.start()
@@ -91,15 +91,17 @@
                 at, of, :
             ].astype(BF16)
 
-    for copy in copies[:6]:
-        copy.wait()
     for copy in copies[10:]:
         copy.start()
+    copies[0].wait()
+    copies[1].wait()
     piece = jnp.concatenate([pgates[0], jnp.zeros((H, slots - tokens), F32)], axis=1)
     gate_rows = [gates[i] for i in range(count)] + [piece, jnp.zeros((16 - H * (count + 1), slots), F32)]
     cum = lane_cumsum(jnp.concatenate(gate_rows, axis=0))
     carried = jnp.exp(cum)
     place = lax.broadcasted_iota(jnp.int32, (1, slots), 1)
+    for copy in copies[2:5]:
+        copy.wait()
     rows = []
     factors = []
     for i in range(count):
@@ -114,8 +116,8 @@
     rows += [suffix, jnp.zeros((8 - H, slots), F32)]
     rows_ref[...] = jnp.concatenate(rows, axis=0)
 
+    copies[5].wait()
     copies[6].wait()
-    copies[7].wait()
     turned = keys[0].T
     later = jnp.exp(suffix[:, :tokens])
     for h in range(H):
@@ -126,15 +128,8 @@
         both = mm(jnp.concatenate([high, low], axis=0), values[0, :, lanes])
         matrices[h] = both[:DH] + both[DH:]
         spread(h)
-    notes = [jnp.broadcast_to(x[h : h + 1].astype(F32), (1, DH)) for x in three_terms(total) for h in range(H)]
-    notes += [jnp.full((1, DH), ids_ref[i].astype(F32)) for i in range(count)]
-    notes.append(jnp.zeros((16 - len(notes), DH), F32))
-    notes = jnp.concatenate(notes, axis=0).astype(BF16)
-    for k in range(n):
-        msgs[k][block : block + 16, :] = notes
-
+    copies[7].wait()
     copies[8].wait()
-    copies[9].wait()
     for i in range(count):
         turned = q[i].T
         for h in range(H):
@@ -142,6 +137,13 @@
             scaled = (turned[lanes].astype(F32) * factors[i][h : h + 1]).astype(BF16)
             matrices[H * (1 + i) + h] = mm(scaled, c[i, :, lanes])
             spread(H * (1 + i) + h)
+    copies[9].wait()
+    notes = [jnp.broadcast_to(x[h : h + 1].astype(F32), (1, DH)) for x in three_terms(total) for h in range(H)]
+    notes += [jnp.full((1, DH), ids_ref[i].astype(F32)) for i in range(count)]
+    notes.append(jnp.zeros((16 - len(notes), DH), F32))
+    notes = jnp.concatenate(notes, axis=0).astype(BF16)
+    for k in range(n):
+        msgs[k][block : block + 16, :] = notes
     for copy in copies[10:]:
         copy.wait()
 
@@ -329,6 +331,13 @@
                 of = pl.ds(pl.multiple_of(h * DH + place[k] * part, part), part)
                 rows = got[k][r * block + h * part : r * block + (h + 1) * part, :]
                 start[r, of, h * DH : (h + 1) * DH] = rows
+    for r in range(count):
+        for t in range(0, slots, HALF):
+            at = slice(t, t + HALF)
+            out_buf[r, at, :] = (po_ref[r, at, :] + mm(q_ref[r, at, :], start[r])).astype(BF16)
+            dq_buf[r, at, :] = (pdq_ref[r, at, :] + mm_nt(grad_ref[r, at, :], start[r])).astype(BF16)
+        send(out_buf.at[r], out_hbm.at[r])
+        send(dq_buf.at[r], dq_hbm.at[r])
     factor = [
         jnp.exp(cols_ref[:tokens, 8 * count + h : 8 * count + h + 1] + later_ref[h : h + 1, 0:1]) for h in range(H)
     ]
@@ -338,13 +347,6 @@
             buf[:, lanes] = (factor[h] * x[:, lanes]).astype(BF16)
     send(dk_buf, dk_hbm.at[0])
     send(dv_buf, dv_hbm.at[0])
-    for r in range(count):
-        for t in range(0, slots, HALF):
-            at = slice(t, t + HALF)
-            out_buf[r, at, :] = (po_ref[r, at, :] + mm(q_ref[r, at, :], start[r])).astype(BF16)
-            dq_buf[r, at, :] = (pdq_ref[r, at, :] + mm_nt(grad_ref[r, at, :], start[r])).astype(BF16)
-        send(out_buf.at[r], out_hbm.at[r])
-        send(dq_buf.at[r], dq_hbm.at[r])
     for copy in copies:
         copy.wait()
 

time: 32.1 us -> 31.9 us (level)
  no operation moved by 1% of the time
where the time goes in v12:
time: 31.9 us; the launch traced here: 31.7 us
  starting transfers between devices  13.8 us (43%)
  Pallas kernels  13.1 us (41%)
  waiting for transfers between devices  4.02 us (13%)
  between operations  0.74 us (2%)
    ppermute x7, starting transfers between devices, exchange(): lax.ppermute(xs[k], axis, [(s, s ^ k) for s in range(n)])  8.23 us
    ppermute x3, starting transfers between devices, exchange_ring(): lax.ppermute(xs[k], axis, [(s, (s + k) % n) for s in range(n)])  5.56 us
    pallas_call x3, Pallas kernels, sweep(): pl.pallas_call(lambda *refs: sweep_kernel(units, done, *refs), out_shape=...  5.4 us
    ppermute x7, waiting for transfers between devices, exchange(): lax.ppermute(xs[k], axis, [(s, s ^ k) for s in range(n)])  3.09 us
    pallas_call x1, Pallas kernels, first_sweep(): pl.pallas_call(lambda *refs: sweep_kernel(units, (), *refs[:5], None, *re...  2.86 us
    pallas_call x1, Pallas kernels, shards(): pl.pallas_call(lambda *refs: first_kernel(n, *refs), out_shape=[shape((bl...  2.47 us
    pallas_call x1, Pallas kernels, shards(): pl.pallas_call(lambda *refs: last_kernel(n, responses, *refs), out_shape=...  1.89 us
    ppermute x3, waiting for transfers between devices, exchange_ring(): lax.ppermute(xs[k], axis, [(s, (s + k) % n) for s in range(n)])  0.93 us
  transfers between devices with their start and end apart: 10, of which 5 were waited for; matrix products, arithmetic and copies ran while one was open for 0% of the time, Pallas kernels for 26%

profile of v12, /device:TPU:0, one launch (start us, length us, event | category | flops | bytes accessed | tf_op | source)
XLA Modules:
  0.0 31.7 jit_solution(16610375707216230851)
XLA Ops:
  0.6 2.5 %first.1 = (bf16[336,128]{1,0:T(8,128)(2,1)S(1)}, bf16[336,128]{1,0:T(8,128)(2,1)S(1)}, bf16[336,128]{1,0:T(8,128)(2,1)S(1)}, bf16[336,128]{1,0:T(8,128)(2,1)S(1...) custom-call(s32[4]{0:T(128)} %refs_0_.1, ...), custom_call_target="tpu_custom_call" | custom-call | tf_op jit(solution)/shard_map/first/pallas_call | solution.py:394
  3.1 4.0 %collective-permute-start = (bf16[336,128]{1,0:T(8,128)(2,1)S(1)}, bf16[336,128]{1,0:T(8,128)(2,1)S(1)}, u32[]{:S(2)}, u32[]{:S(2)}) collective-permute-start(bf16[336,128]{1,0:T(8,128)(2,1)S(1)} %get-tuple-element.66), channel_id=1, source_target_pairs={{0,24},{8,16},{16,8},{24,0},{1,25},{9,17},{17,9},{25,1},{2,26},{10... | collective-permute-start | bytes 258056 | tf_op jit(solution)/shard_map/ppermute | solution.py:356
  7.1 0.5 %collective-permute-start.1 = (bf16[336,128]{1,0:T(8,128)(2,1)S(1)}, bf16[336,128]{1,0:T(8,128)(2,1)S(1)}, u32[]{:S(2)}, u32[]{:S(2)}) collective-permute-start(bf16[336,128]{1,0:T(8,128)(2,1)S(1)} %get-tuple-element.67), channel_id=1, source_target_pairs={{0,16},{8,24},{16,0},{24,8},{1,17},{9,25},{17,1},{25,9},{2,18},{10... | collective-permute-start | bytes 258056 | tf_op jit(solution)/shard_map/ppermute | solution.py:356
  7.6 0.1 collective-permute-start.2
  7.7 2.9 %sweep.4 = (f32[512,128]{1,0:T(8,128)S(1)}, f32[4,512,256]{2,1,0:T(8,128)S(1)}, f32[4,512,256]{2,1,0:T(8,128)S(1)}, bf16[4,512,256]{2,1,0:T(8,128)(2,1)S(1)}, bf...) custom-call(f32[40,512]{1,0:T(8,128)S(1)} %get-tuple-element.59.refs, ...), custom_call_target="tpu_custom_call" | custom-call | tf_op jit(solution)/shard_map/sweep/pallas_call | solution.py:427
  10.6 0.0 collective-permute-done.refs_1_
  10.6 1.0 %collective-permute-done.1.refs_2_ = bf16[336,128]{1,0:T(8,128)(2,1)S(1)} collective-permute-done((bf16[336,128]{1,0:T(8,128)(2,1)S(1)}, bf16[336,128]{1,0:T(8,128)(2,1)S(1)}, u32[]{:S(2)}, u32[]{:S(2)}) %collective-permute-start.1) | collective-permute-done | bytes 86048 | tf_op jit(solution)/shard_map/ppermute | solution.py:356
  11.6 0.5 %collective-permute-done.2.refs_3_ = bf16[336,128]{1,0:T(8,128)(2,1)S(1)} collective-permute-done((bf16[336,128]{1,0:T(8,128)(2,1)S(1)}, bf16[336,128]{1,0:T(8,128)(2,1)S(1)}, u32[]{:S(2)}, u32[]{:S(2)}) %collective-permute-start.2) | collective-permute-done | bytes 86048 | tf_op jit(solution)/shard_map/ppermute | solution.py:356
  12.1 0.2 second.1
  12.3 1.6 %collective-permute-start.3 = (bf16[192,128]{1,0:T(8,128)(2,1)S(1)}, bf16[192,128]{1,0:T(8,128)(2,1)S(1)}, u32[]{:S(2)}, u32[]{:S(2)}) collective-permute-start(bf16[192,128]{1,0:T(8,128)(2,1)S(1)} %get-tuple-element.71), channel_id=1, source_target_pairs={{0,2},{2,4},{4,6},{6,0},{1,3},{3,5},{5,7},{7,1},{8,10},{10,12},{12... | collective-permute-start | bytes 147464 | tf_op jit(solution)/shard_map/ppermute | solution.py:361
  13.9 2.6 %collective-permute-start.4 = (bf16[192,128]{1,0:T(8,128)(2,1)S(1)}, bf16[192,128]{1,0:T(8,128)(2,1)S(1)}, u32[]{:S(2)}, u32[]{:S(2)}) collective-permute-start(bf16[192,128]{1,0:T(8,128)(2,1)S(1)} %get-tuple-element.72), channel_id=1, source_target_pairs={{0,4},{2,6},{4,0},{6,2},{1,5},{3,7},{5,1},{7,3},{8,12},{10,14},{12... | collective-permute-start | bytes 147464 | tf_op jit(solution)/shard_map/ppermute | solution.py:361
  16.5 1.3 %collective-permute-start.5 = (bf16[192,128]{1,0:T(8,128)(2,1)S(1)}, bf16[192,128]{1,0:T(8,128)(2,1)S(1)}, u32[]{:S(2)}, u32[]{:S(2)}) collective-permute-start(bf16[192,128]{1,0:T(8,128)(2,1)S(1)} %get-tuple-element.73), channel_id=1, source_target_pairs={{0,6},{2,0},{4,2},{6,4},{1,7},{3,1},{5,3},{7,5},{8,14},{10,8},{12,... | collective-permute-start | bytes 147464 | tf_op jit(solution)/shard_map/ppermute | solution.py:361
  17.9 1.8 %sweep.5 = (f32[4,512,256]{2,1,0:T(8,128)S(1)}, f32[4,512,256]{2,1,0:T(8,128)S(1)}, bf16[4,512,256]{2,1,0:T(8,128)(2,1)S(1)}, bf16[4,512,256]{2,1,0:T(8,128)(2,1...) custom-call(f32[40,512]{1,0:T(8,128)S(1)} %get-tuple-element.59.refs, ...), custom_call_target="tpu_custom_call", output_to_operand_aliasing={{0}: (7, {}), {1}: (8, {}), {2}: (9, {}), {3}: (10, {}), {4... | custom-call | tf_op jit(solution)/shard_map/sweep/pallas_call | solution.py:439
  19.7 0.0 collective-permute-done.3.refs_1_
  19.7 0.0 collective-permute-done.4.refs_2_
  19.7 0.9 %collective-permute-done.5.refs_3_ = bf16[192,128]{1,0:T(8,128)(2,1)S(1)} collective-permute-done((bf16[192,128]{1,0:T(8,128)(2,1)S(1)}, bf16[192,128]{1,0:T(8,128)(2,1)S(1)}, u32[]{:S(2)}, u32[]{:S(2)}) %collective-permute-start.5) | collective-permute-done | bytes 49184 | tf_op jit(solution)/shard_map/ppermute | solution.py:361
  20.7 0.1 collective-permute-start.6
  20.7 1.0 %sweep.6 = (f32[4,512,256]{2,1,0:T(8,128)S(1)}, f32[4,512,256]{2,1,0:T(8,128)S(1)}, bf16[4,512,256]{2,1,0:T(8,128)(2,1)S(1)}, bf16[4,512,256]{2,1,0:T(8,128)(2,1...) custom-call(f32[40,512]{1,0:T(8,128)S(1)} %get-tuple-element.59.refs, ...), custom_call_target="tpu_custom_call", output_to_operand_aliasing={{0}: (7, {}), {1}: (8, {}), {2}: (9, {}), {3}: (10, {}), {4... | custom-call | tf_op jit(solution)/shard_map/sweep/pallas_call | solution.py:439
  21.7 0.3 collective-permute-done.6.refs_5_
  22.0 0.3 third.1
  22.3 1.3 %collective-permute-start.7 = (bf16[320,128]{1,0:T(8,128)(2,1)S(1)}, bf16[320,128]{1,0:T(8,128)(2,1)S(1)}, u32[]{:S(2)}, u32[]{:S(2)}) collective-permute-start(bf16[320,128]{1,0:T(8,128)(2,1)S(1)} %get-tuple-element.102), channel_id=1, source_target_pairs={{0,8},{8,0},{16,24},{24,16},{1,9},{9,1},{17,25},{25,17},{2,10},{10... | collective-permute-start | bytes 245768 | tf_op jit(solution)/shard_map/ppermute | solution.py:356
  23.6 0.8 %collective-permute-start.8 = (bf16[320,128]{1,0:T(8,128)(2,1)S(1)}, bf16[320,128]{1,0:T(8,128)(2,1)S(1)}, u32[]{:S(2)}, u32[]{:S(2)}) collective-permute-start(bf16[320,128]{1,0:T(8,128)(2,1)S(1)} %get-tuple-element.103), channel_id=1, source_target_pairs={{0,16},{8,24},{16,0},{24,8},{1,17},{9,25},{17,1},{25,9},{2,18},{10... | collective-permute-start | bytes 245768 | tf_op jit(solution)/shard_map/ppermute | solution.py:356
  24.4 1.4 %collective-permute-start.9 = (bf16[320,128]{1,0:T(8,128)(2,1)S(1)}, bf16[320,128]{1,0:T(8,128)(2,1)S(1)}, u32[]{:S(2)}, u32[]{:S(2)}) collective-permute-start(bf16[320,128]{1,0:T(8,128)(2,1)S(1)} %get-tuple-element.104), channel_id=1, source_target_pairs={{0,24},{8,16},{16,8},{24,0},{1,25},{9,17},{17,9},{25,1},{2,26},{10... | collective-permute-start | bytes 245768 | tf_op jit(solution)/shard_map/ppermute | solution.py:356
  25.8 0.0 copy-start
  25.8 0.0 copy-start.1
  25.8 2.6 %sweep.7 = (f32[4,512,256]{2,1,0:T(8,128)S(1)}, f32[4,512,256]{2,1,0:T(8,128)S(1)}, bf16[4,512,256]{2,1,0:T(8,128)(2,1)S(1)}, bf16[4,512,256]{2,1,0:T(8,128)(2,1...) custom-call(f32[40,512]{1,0:T(8,128)S(1)} %get-tuple-element.59.refs, ...), custom_call_target="tpu_custom_call", output_to_operand_aliasing={{0}: (7, {}), {1}: (8, {}), {2}: (9, {}), {3}: (10, {}), {4... | custom-call | tf_op jit(solution)/shard_map/sweep/pallas_call | solution.py:439
  28.5 0.0 collective-permute-done.7.refs_9_
  28.5 1.3 %collective-permute-done.8.refs_10_ = bf16[320,128]{1,0:T(8,128)(2,1)S(1)} collective-permute-done((bf16[320,128]{1,0:T(8,128)(2,1)S(1)}, bf16[320,128]{1,0:T(8,128)(2,1)S(1)}, u32[]{:S(2)}, u32[]{:S(2)}) %collective-permute-start.8) | collective-permute-done | bytes 81952 | tf_op jit(solution)/shard_map/ppermute | solution.py:356
  29.8 0.0 collective-permute-done.9.refs_11_
  29.8 0.0 copy-done
  29.8 0.0 copy-done.1
  29.8 1.9 %last.1 = (bf16[4,512,256]{2,1,0:T(8,128)(2,1)}, bf16[4,512,256]{2,1,0:T(8,128)(2,1)}, bf16[1,256,256]{2,1,0:T(8,128)(2,1)}, bf16[1,256,256]{2,1,0:T(8,128)(2,1)}) custom-call(f32[512,128]{1,0:T(8,128)S(1)} %get-tuple-element.64.refs_5_.refs_0_, bf16[4,512,256]{2,1,0:T(8,128)(2,1)S(1)} %get-tuple-element.98.refs_1_, ...), custom_call_target="tpu_custom_call" | custom-call | tf_op jit(solution)/shard_map/last/pallas_call | solution.py:488
  (1 shorter events, 0.0 us)
Async XLA Ops:
  3.1 7.5 %collective-permute-start = (bf16[336,128]{1,0:T(8,128)(2,1)S(1)}, bf16[336,128]{1,0:T(8,128)(2,1)S(1)}, u32[]{:S(2)}, u32[]{:S(2)}) collective-permute-start(bf16[336,128]{1,0:T(8,128)(2,1)S(1)} %get-tuple-element.66), channel_id=1, source_target_pairs={{0,24},{8,16},{16,8},{24,0},{1,25},{9,17},{17,9},{25,1},{2,26},{10... | collective-permute-start | bytes 258056 | tf_op jit(solution)/shard_map/ppermute | solution.py:356
  7.1 4.5 %collective-permute-start.1 = (bf16[336,128]{1,0:T(8,128)(2,1)S(1)}, bf16[336,128]{1,0:T(8,128)(2,1)S(1)}, u32[]{:S(2)}, u32[]{:S(2)}) collective-permute-start(bf16[336,128]{1,0:T(8,128)(2,1)S(1)} %get-tuple-element.67), channel_id=1, source_target_pairs={{0,16},{8,24},{16,0},{24,8},{1,17},{9,25},{17,1},{25,9},{2,18},{10... | collective-permute-start | bytes 258056 | tf_op jit(solution)/shard_map/ppermute | solution.py:356
  7.6 4.5 %collective-permute-start.2 = (bf16[336,128]{1,0:T(8,128)(2,1)S(1)}, bf16[336,128]{1,0:T(8,128)(2,1)S(1)}, u32[]{:S(2)}, u32[]{:S(2)}) collective-permute-start(bf16[336,128]{1,0:T(8,128)(2,1)S(1)} %get-tuple-element.68), channel_id=1, source_target_pairs={{0,8},{8,0},{16,24},{24,16},{1,9},{9,1},{17,25},{25,17},{2,10},{10... | collective-permute-start | bytes 258056 | tf_op jit(solution)/shard_map/ppermute | solution.py:356
  12.3 7.4 %collective-permute-start.3 = (bf16[192,128]{1,0:T(8,128)(2,1)S(1)}, bf16[192,128]{1,0:T(8,128)(2,1)S(1)}, u32[]{:S(2)}, u32[]{:S(2)}) collective-permute-start(bf16[192,128]{1,0:T(8,128)(2,1)S(1)} %get-tuple-element.71), channel_id=1, source_target_pairs={{0,2},{2,4},{4,6},{6,0},{1,3},{3,5},{5,7},{7,1},{8,10},{10,12},{12... | collective-permute-start | bytes 147464 | tf_op jit(solution)/shard_map/ppermute | solution.py:361
  13.9 5.8 %collective-permute-start.4 = (bf16[192,128]{1,0:T(8,128)(2,1)S(1)}, bf16[192,128]{1,0:T(8,128)(2,1)S(1)}, u32[]{:S(2)}, u32[]{:S(2)}) collective-permute-start(bf16[192,128]{1,0:T(8,128)(2,1)S(1)} %get-tuple-element.72), channel_id=1, source_target_pairs={{0,4},{2,6},{4,0},{6,2},{1,5},{3,7},{5,1},{7,3},{8,12},{10,14},{12... | collective-permute-start | bytes 147464 | tf_op jit(solution)/shard_map/ppermute | solution.py:361
  16.5 4.1 %collective-permute-start.5 = (bf16[192,128]{1,0:T(8,128)(2,1)S(1)}, bf16[192,128]{1,0:T(8,128)(2,1)S(1)}, u32[]{:S(2)}, u32[]{:S(2)}) collective-permute-start(bf16[192,128]{1,0:T(8,128)(2,1)S(1)} %get-tuple-element.73), channel_id=1, source_target_pairs={{0,6},{2,0},{4,2},{6,4},{1,7},{3,1},{5,3},{7,5},{8,14},{10,8},{12,... | collective-permute-start | bytes 147464 | tf_op jit(solution)/shard_map/ppermute | solution.py:361
  20.7 1.3 %collective-permute-start.6 = (bf16[320,128]{1,0:T(8,128)(2,1)S(1)}, bf16[320,128]{1,0:T(8,128)(2,1)S(1)}, u32[]{:S(2)}, u32[]{:S(2)}) collective-permute-start(bf16[320,128]{1,0:T(8,128)(2,1)S(1)} %get-tuple-element.83), channel_id=1, source_target_pairs={{0,1},{1,0},{2,3},{3,2},{4,5},{5,4},{6,7},{7,6},{8,9},{9,8},{10,11... | collective-permute-start | bytes 245768 | tf_op jit(solution)/shard_map/ppermute | solution.py:356
  22.3 6.2 %collective-permute-start.7 = (bf16[320,128]{1,0:T(8,128)(2,1)S(1)}, bf16[320,128]{1,0:T(8,128)(2,1)S(1)}, u32[]{:S(2)}, u32[]{:S(2)}) collective-permute-start(bf16[320,128]{1,0:T(8,128)(2,1)S(1)} %get-tuple-element.102), channel_id=1, source_target_pairs={{0,8},{8,0},{16,24},{24,16},{1,9},{9,1},{17,25},{25,17},{2,10},{10... | collective-permute-start | bytes 245768 | tf_op jit(solution)/shard_map/ppermute | solution.py:356
  23.6 6.2 %collective-permute-start.8 = (bf16[320,128]{1,0:T(8,128)(2,1)S(1)}, bf16[320,128]{1,0:T(8,128)(2,1)S(1)}, u32[]{:S(2)}, u32[]{:S(2)}) collective-permute-start(bf16[320,128]{1,0:T(8,128)(2,1)S(1)} %get-tuple-element.103), channel_id=1, source_target_pairs={{0,16},{8,24},{16,0},{24,8},{1,17},{9,25},{17,1},{25,9},{2,18},{10... | collective-permute-start | bytes 245768 | tf_op jit(solution)/shard_map/ppermute | solution.py:356
  24.4 5.4 %collective-permute-start.9 = (bf16[320,128]{1,0:T(8,128)(2,1)S(1)}, bf16[320,128]{1,0:T(8,128)(2,1)S(1)}, u32[]{:S(2)}, u32[]{:S(2)}) collective-permute-start(bf16[320,128]{1,0:T(8,128)(2,1)S(1)} %get-tuple-element.104), channel_id=1, source_target_pairs={{0,24},{8,16},{16,8},{24,0},{1,25},{9,17},{17,9},{25,1},{2,26},{10... | collective-permute-start | bytes 245768 | tf_op jit(solution)/shard_map/ppermute | solution.py:356
  25.8 4.0 %copy-start = (bf16[1,256,256]{2,1,0:T(8,128)(2,1)S(1)}, bf16[1,256,256]{2,1,0:T(8,128)(2,1)}, u32[]{:S(2)}) copy-start(bf16[1,256,256]{2,1,0:T(8,128)(2,1)} %refs_5_.3) | copy-start | bytes 393220
  25.8 4.0 %copy-start.1 = (bf16[1,256,256]{2,1,0:T(8,128)(2,1)S(1)}, bf16[1,256,256]{2,1,0:T(8,128)(2,1)}, u32[]{:S(2)}) copy-start(bf16[1,256,256]{2,1,0:T(8,128)(2,1)} %refs_6_.3) | copy-start | bytes 393220

commit v13 on v12

--- a/solution.py
+++ b/solution.py
@@ -91,10 +91,10 @@
                 at, of, :
             ].astype(BF16)
 
+    copies[0].wait()
+    copies[1].wait()
     for copy in copies[10:]:
         copy.start()
-    copies[0].wait()
-    copies[1].wait()
     piece = jnp.concatenate([pgates[0], jnp.zeros((H, slots - tokens), F32)], axis=1)
     gate_rows = [gates[i] for i in range(count)] + [piece, jnp.zeros((16 - H * (count + 1), slots), F32)]
     cum = lane_cumsum(jnp.concatenate(gate_rows, axis=0))
@@ -312,7 +312,7 @@
     n, count, cols_ref, q_ref, grad_ref, po_ref, pdq_ref, keys_ref, values_ref, later_ref, *refs
 ):
     got, refs = refs[:n], refs[n + 1 :]
-    out_hbm, dq_hbm, dk_hbm, dv_hbm, start, out_buf, dq_buf, dk_buf, dv_buf, sems = refs
+    out_hbm, dq_hbm, dk_hbm, dv_hbm, start, turned, out_buf, dq_buf, dk_buf, dv_buf, sems = refs
     part = DH // n
     block = H * part
     place = partners(n)
@@ -325,23 +325,25 @@
         copies[-1].start()
 
     start[...] = jnp.zeros_like(start)
+    turned[...] = jnp.zeros_like(turned)
     for r in range(count + 1):
-        for k in range(n):
-            for h in range(H):
+        for h in range(H):
+            lanes = slice(h * DH, (h + 1) * DH)
+            for k in range(n):
                 of = pl.ds(pl.multiple_of(h * DH + place[k] * part, part), part)
-                rows = got[k][r * block + h * part : r * block + (h + 1) * part, :]
-                start[r, of, h * DH : (h + 1) * DH] = rows
+                start[r, of, lanes] = got[k][r * block + h * part : r * block + (h + 1) * part, :]
+            turned[r, lanes, lanes] = start[r, lanes, lanes].T
     for r in range(count):
         for t in range(0, slots, HALF):
             at = slice(t, t + HALF)
             out_buf[r, at, :] = (po_ref[r, at, :] + mm(q_ref[r, at, :], start[r])).astype(BF16)
-            dq_buf[r, at, :] = (pdq_ref[r, at, :] + mm_nt(grad_ref[r, at, :], start[r])).astype(BF16)
+            dq_buf[r, at, :] = (pdq_ref[r, at, :] + mm(grad_ref[r, at, :], turned[r])).astype(BF16)
         send(out_buf.at[r], out_hbm.at[r])
         send(dq_buf.at[r], dq_hbm.at[r])
     factor = [
         jnp.exp(cols_ref[:tokens, 8 * count + h : 8 * count + h + 1] + later_ref[h : h + 1, 0:1]) for h in range(H)
     ]
-    for buf, x in ((dk_buf, mm_nt(values_ref[0], start[count])), (dv_buf, mm(keys_ref[0], start[count]))):
+    for buf, x in ((dk_buf, mm(values_ref[0], turned[count])), (dv_buf, mm(keys_ref[0], start[count]))):
         for h in range(H):
             lanes = slice(h * DH, (h + 1) * DH)
             buf[:, lanes] = (factor[h] * x[:, lanes]).astype(BF16)
@@ -492,6 +494,7 @@
         out_specs=[ANY] * 4,
         scratch_shapes=[
             pltpu.VMEM((responses + 1, width, width), BF16),
+            pltpu.VMEM((responses + 1, width, width), BF16),
             pltpu.VMEM(queries.shape, BF16),
             pltpu.VMEM(queries.shape, BF16),
             pltpu.VMEM(keys.shape[1:], BF16),

time: 31.9 us -> 32.2 us (level)
  no operation moved by 1% of the time
where the time goes in v13:
time: 32.2 us; the launch traced here: 32 us
  starting transfers between devices  13.8 us (43%)
  Pallas kernels  13.4 us (42%)
  waiting for transfers between devices  4.01 us (12%)
  between operations  0.74 us (2%)
    ppermute x7, starting transfers between devices, exchange(): lax.ppermute(xs[k], axis, [(s, s ^ k) for s in range(n)])  8.23 us
    ppermute x3, starting transfers between devices, exchange_ring(): lax.ppermute(xs[k], axis, [(s, (s + k) % n) for s in range(n)])  5.57 us
    pallas_call x3, Pallas kernels, sweep(): pl.pallas_call(lambda *refs: sweep_kernel(units, done, *refs), out_shape=...  5.41 us
    ppermute x7, waiting for transfers between devices, exchange(): lax.ppermute(xs[k], axis, [(s, s ^ k) for s in range(n)])  3.08 us
    pallas_call x1, Pallas kernels, first_sweep(): pl.pallas_call(lambda *refs: sweep_kernel(units, (), *refs[:5], None, *re...  2.86 us
    pallas_call x1, Pallas kernels, shards(): pl.pallas_call(lambda *refs: first_kernel(n, *refs), out_shape=[shape((bl...  2.63 us
    pallas_call x1, Pallas kernels, shards(): pl.pallas_call(lambda *refs: last_kernel(n, responses, *refs), out_shape=...  2.02 us
    ppermute x3, waiting for transfers between devices, exchange_ring(): lax.ppermute(xs[k], axis, [(s, (s + k) % n) for s in range(n)])  0.92 us
  transfers between devices with their start and end apart: 10, of which 5 were waited for; matrix products, arithmetic and copies ran while one was open for 0% of the time, Pallas kernels for 26%

profile of v13, /device:TPU:0, one launch (start us, length us, event | category | flops | bytes accessed | tf_op | source)
XLA Modules:
  0.0 32.0 jit_solution(17352770247798336315)
XLA Ops:
  0.6 2.6 %first.1 = (bf16[336,128]{1,0:T(8,128)(2,1)S(1)}, bf16[336,128]{1,0:T(8,128)(2,1)S(1)}, bf16[336,128]{1,0:T(8,128)(2,1)S(1)}, bf16[336,128]{1,0:T(8,128)(2,1)S(1...) custom-call(s32[4]{0:T(128)} %refs_0_.1, ...), custom_call_target="tpu_custom_call" | custom-call | tf_op jit(solution)/shard_map/first/pallas_call | solution.py:396
  3.3 4.0 %collective-permute-start = (bf16[336,128]{1,0:T(8,128)(2,1)S(1)}, bf16[336,128]{1,0:T(8,128)(2,1)S(1)}, u32[]{:S(2)}, u32[]{:S(2)}) collective-permute-start(bf16[336,128]{1,0:T(8,128)(2,1)S(1)} %get-tuple-element.66), channel_id=1, source_target_pairs={{0,24},{8,16},{16,8},{24,0},{1,25},{9,17},{17,9},{25,1},{2,26},{10... | collective-permute-start | bytes 258056 | tf_op jit(solution)/shard_map/ppermute | solution.py:358
  7.2 0.5 %collective-permute-start.1 = (bf16[336,128]{1,0:T(8,128)(2,1)S(1)}, bf16[336,128]{1,0:T(8,128)(2,1)S(1)}, u32[]{:S(2)}, u32[]{:S(2)}) collective-permute-start(bf16[336,128]{1,0:T(8,128)(2,1)S(1)} %get-tuple-element.67), channel_id=1, source_target_pairs={{0,16},{8,24},{16,0},{24,8},{1,17},{9,25},{17,1},{25,9},{2,18},{10... | collective-permute-start | bytes 258056 | tf_op jit(solution)/shard_map/ppermute | solution.py:358
  7.7 0.1 collective-permute-start.2
  7.9 2.9 %sweep.4 = (f32[512,128]{1,0:T(8,128)S(1)}, f32[4,512,256]{2,1,0:T(8,128)S(1)}, f32[4,512,256]{2,1,0:T(8,128)S(1)}, bf16[4,512,256]{2,1,0:T(8,128)(2,1)S(1)}, bf...) custom-call(f32[40,512]{1,0:T(8,128)S(1)} %get-tuple-element.59.refs, ...), custom_call_target="tpu_custom_call" | custom-call | tf_op jit(solution)/shard_map/sweep/pallas_call | solution.py:429
  10.7 0.0 collective-permute-done.refs_1_
  10.7 1.0 %collective-permute-done.1.refs_2_ = bf16[336,128]{1,0:T(8,128)(2,1)S(1)} collective-permute-done((bf16[336,128]{1,0:T(8,128)(2,1)S(1)}, bf16[336,128]{1,0:T(8,128)(2,1)S(1)}, u32[]{:S(2)}, u32[]{:S(2)}) %collective-permute-start.1) | collective-permute-done | bytes 86048 | tf_op jit(solution)/shard_map/ppermute | solution.py:358
  11.7 0.5 %collective-permute-done.2.refs_3_ = bf16[336,128]{1,0:T(8,128)(2,1)S(1)} collective-permute-done((bf16[336,128]{1,0:T(8,128)(2,1)S(1)}, bf16[336,128]{1,0:T(8,128)(2,1)S(1)}, u32[]{:S(2)}, u32[]{:S(2)}) %collective-permute-start.2) | collective-permute-done | bytes 86048 | tf_op jit(solution)/shard_map/ppermute | solution.py:358
  12.2 0.2 second.1
  12.5 1.6 %collective-permute-start.3 = (bf16[192,128]{1,0:T(8,128)(2,1)S(1)}, bf16[192,128]{1,0:T(8,128)(2,1)S(1)}, u32[]{:S(2)}, u32[]{:S(2)}) collective-permute-start(bf16[192,128]{1,0:T(8,128)(2,1)S(1)} %get-tuple-element.71), channel_id=1, source_target_pairs={{0,2},{2,4},{4,6},{6,0},{1,3},{3,5},{5,7},{7,1},{8,10},{10,12},{12... | collective-permute-start | bytes 147464 | tf_op jit(solution)/shard_map/ppermute | solution.py:363
  14.1 2.6 %collective-permute-start.4 = (bf16[192,128]{1,0:T(8,128)(2,1)S(1)}, bf16[192,128]{1,0:T(8,128)(2,1)S(1)}, u32[]{:S(2)}, u32[]{:S(2)}) collective-permute-start(bf16[192,128]{1,0:T(8,128)(2,1)S(1)} %get-tuple-element.72), channel_id=1, source_target_pairs={{0,4},{2,6},{4,0},{6,2},{1,5},{3,7},{5,1},{7,3},{8,12},{10,14},{12... | collective-permute-start | bytes 147464 | tf_op jit(solution)/shard_map/ppermute | solution.py:363
  16.7 1.3 %collective-permute-start.5 = (bf16[192,128]{1,0:T(8,128)(2,1)S(1)}, bf16[192,128]{1,0:T(8,128)(2,1)S(1)}, u32[]{:S(2)}, u32[]{:S(2)}) collective-permute-start(bf16[192,128]{1,0:T(8,128)(2,1)S(1)} %get-tuple-element.73), channel_id=1, source_target_pairs={{0,6},{2,0},{4,2},{6,4},{1,7},{3,1},{5,3},{7,5},{8,14},{10,8},{12,... | collective-permute-start | bytes 147464 | tf_op jit(solution)/shard_map/ppermute | solution.py:363
  18.0 1.8 %sweep.5 = (f32[4,512,256]{2,1,0:T(8,128)S(1)}, f32[4,512,256]{2,1,0:T(8,128)S(1)}, bf16[4,512,256]{2,1,0:T(8,128)(2,1)S(1)}, bf16[4,512,256]{2,1,0:T(8,128)(2,1...) custom-call(f32[40,512]{1,0:T(8,128)S(1)} %get-tuple-element.59.refs, ...), custom_call_target="tpu_custom_call", output_to_operand_aliasing={{0}: (7, {}), {1}: (8, {}), {2}: (9, {}), {3}: (10, {}), {4... | custom-call | tf_op jit(solution)/shard_map/sweep/pallas_call | solution.py:441
  19.8 0.0 collective-permute-done.3.refs_1_
  19.9 0.0 collective-permute-done.4.refs_2_
  19.9 0.9 %collective-permute-done.5.refs_3_ = bf16[192,128]{1,0:T(8,128)(2,1)S(1)} collective-permute-done((bf16[192,128]{1,0:T(8,128)(2,1)S(1)}, bf16[192,128]{1,0:T(8,128)(2,1)S(1)}, u32[]{:S(2)}, u32[]{:S(2)}) %collective-permute-start.5) | collective-permute-done | bytes 49184 | tf_op jit(solution)/shard_map/ppermute | solution.py:363
  20.8 0.1 collective-permute-start.6
  20.9 1.0 %sweep.6 = (f32[4,512,256]{2,1,0:T(8,128)S(1)}, f32[4,512,256]{2,1,0:T(8,128)S(1)}, bf16[4,512,256]{2,1,0:T(8,128)(2,1)S(1)}, bf16[4,512,256]{2,1,0:T(8,128)(2,1...) custom-call(f32[40,512]{1,0:T(8,128)S(1)} %get-tuple-element.59.refs, ...), custom_call_target="tpu_custom_call", output_to_operand_aliasing={{0}: (7, {}), {1}: (8, {}), {2}: (9, {}), {3}: (10, {}), {4... | custom-call | tf_op jit(solution)/shard_map/sweep/pallas_call | solution.py:441
  21.9 0.3 collective-permute-done.6.refs_5_
  22.2 0.3 third.1
  22.4 1.3 %collective-permute-start.7 = (bf16[320,128]{1,0:T(8,128)(2,1)S(1)}, bf16[320,128]{1,0:T(8,128)(2,1)S(1)}, u32[]{:S(2)}, u32[]{:S(2)}) collective-permute-start(bf16[320,128]{1,0:T(8,128)(2,1)S(1)} %get-tuple-element.102), channel_id=1, source_target_pairs={{0,8},{8,0},{16,24},{24,16},{1,9},{9,1},{17,25},{25,17},{2,10},{10... | collective-permute-start | bytes 245768 | tf_op jit(solution)/shard_map/ppermute | solution.py:358
  23.8 0.8 %collective-permute-start.8 = (bf16[320,128]{1,0:T(8,128)(2,1)S(1)}, bf16[320,128]{1,0:T(8,128)(2,1)S(1)}, u32[]{:S(2)}, u32[]{:S(2)}) collective-permute-start(bf16[320,128]{1,0:T(8,128)(2,1)S(1)} %get-tuple-element.103), channel_id=1, source_target_pairs={{0,16},{8,24},{16,0},{24,8},{1,17},{9,25},{17,1},{25,9},{2,18},{10... | collective-permute-start | bytes 245768 | tf_op jit(solution)/shard_map/ppermute | solution.py:358
  24.5 1.4 %collective-permute-start.9 = (bf16[320,128]{1,0:T(8,128)(2,1)S(1)}, bf16[320,128]{1,0:T(8,128)(2,1)S(1)}, u32[]{:S(2)}, u32[]{:S(2)}) collective-permute-start(bf16[320,128]{1,0:T(8,128)(2,1)S(1)} %get-tuple-element.104), channel_id=1, source_target_pairs={{0,24},{8,16},{16,8},{24,0},{1,25},{9,17},{17,9},{25,1},{2,26},{10... | collective-permute-start | bytes 245768 | tf_op jit(solution)/shard_map/ppermute | solution.py:358
  26.0 0.0 copy-start
  26.0 0.0 copy-start.1
  26.0 2.6 %sweep.7 = (f32[4,512,256]{2,1,0:T(8,128)S(1)}, f32[4,512,256]{2,1,0:T(8,128)S(1)}, bf16[4,512,256]{2,1,0:T(8,128)(2,1)S(1)}, bf16[4,512,256]{2,1,0:T(8,128)(2,1...) custom-call(f32[40,512]{1,0:T(8,128)S(1)} %get-tuple-element.59.refs, ...), custom_call_target="tpu_custom_call", output_to_operand_aliasing={{0}: (7, {}), {1}: (8, {}), {2}: (9, {}), {3}: (10, {}), {4... | custom-call | tf_op jit(solution)/shard_map/sweep/pallas_call | solution.py:441
  28.6 0.0 collective-permute-done.7.refs_9_
  28.6 1.3 %collective-permute-done.8.refs_10_ = bf16[320,128]{1,0:T(8,128)(2,1)S(1)} collective-permute-done((bf16[320,128]{1,0:T(8,128)(2,1)S(1)}, bf16[320,128]{1,0:T(8,128)(2,1)S(1)}, u32[]{:S(2)}, u32[]{:S(2)}) %collective-permute-start.8) | collective-permute-done | bytes 81952 | tf_op jit(solution)/shard_map/ppermute | solution.py:358
  30.0 0.0 collective-permute-done.9.refs_11_
  30.0 0.0 copy-done
  30.0 0.0 copy-done.1
  30.0 2.0 %last.1 = (bf16[4,512,256]{2,1,0:T(8,128)(2,1)}, bf16[4,512,256]{2,1,0:T(8,128)(2,1)}, bf16[1,256,256]{2,1,0:T(8,128)(2,1)}, bf16[1,256,256]{2,1,0:T(8,128)(2,1)}) custom-call(f32[512,128]{1,0:T(8,128)S(1)} %get-tuple-element.64.refs_5_.refs_0_, bf16[4,512,256]{2,1,0:T(8,128)(2,1)S(1)} %get-tuple-element.98.refs_1_, ...), custom_call_target="tpu_custom_call" | custom-call | tf_op jit(solution)/shard_map/last/pallas_call | solution.py:490
  (1 shorter events, 0.0 us)
Async XLA Ops:
  3.3 7.5 %collective-permute-start = (bf16[336,128]{1,0:T(8,128)(2,1)S(1)}, bf16[336,128]{1,0:T(8,128)(2,1)S(1)}, u32[]{:S(2)}, u32[]{:S(2)}) collective-permute-start(bf16[336,128]{1,0:T(8,128)(2,1)S(1)} %get-tuple-element.66), channel_id=1, source_target_pairs={{0,24},{8,16},{16,8},{24,0},{1,25},{9,17},{17,9},{25,1},{2,26},{10... | collective-permute-start | bytes 258056 | tf_op jit(solution)/shard_map/ppermute | solution.py:358
  7.2 4.5 %collective-permute-start.1 = (bf16[336,128]{1,0:T(8,128)(2,1)S(1)}, bf16[336,128]{1,0:T(8,128)(2,1)S(1)}, u32[]{:S(2)}, u32[]{:S(2)}) collective-permute-start(bf16[336,128]{1,0:T(8,128)(2,1)S(1)} %get-tuple-element.67), channel_id=1, source_target_pairs={{0,16},{8,24},{16,0},{24,8},{1,17},{9,25},{17,1},{25,9},{2,18},{10... | collective-permute-start | bytes 258056 | tf_op jit(solution)/shard_map/ppermute | solution.py:358
  7.7 4.5 %collective-permute-start.2 = (bf16[336,128]{1,0:T(8,128)(2,1)S(1)}, bf16[336,128]{1,0:T(8,128)(2,1)S(1)}, u32[]{:S(2)}, u32[]{:S(2)}) collective-permute-start(bf16[336,128]{1,0:T(8,128)(2,1)S(1)} %get-tuple-element.68), channel_id=1, source_target_pairs={{0,8},{8,0},{16,24},{24,16},{1,9},{9,1},{17,25},{25,17},{2,10},{10... | collective-permute-start | bytes 258056 | tf_op jit(solution)/shard_map/ppermute | solution.py:358
  12.5 7.4 %collective-permute-start.3 = (bf16[192,128]{1,0:T(8,128)(2,1)S(1)}, bf16[192,128]{1,0:T(8,128)(2,1)S(1)}, u32[]{:S(2)}, u32[]{:S(2)}) collective-permute-start(bf16[192,128]{1,0:T(8,128)(2,1)S(1)} %get-tuple-element.71), channel_id=1, source_target_pairs={{0,2},{2,4},{4,6},{6,0},{1,3},{3,5},{5,7},{7,1},{8,10},{10,12},{12... | collective-permute-start | bytes 147464 | tf_op jit(solution)/shard_map/ppermute | solution.py:363
  14.1 5.8 %collective-permute-start.4 = (bf16[192,128]{1,0:T(8,128)(2,1)S(1)}, bf16[192,128]{1,0:T(8,128)(2,1)S(1)}, u32[]{:S(2)}, u32[]{:S(2)}) collective-permute-start(bf16[192,128]{1,0:T(8,128)(2,1)S(1)} %get-tuple-element.72), channel_id=1, source_target_pairs={{0,4},{2,6},{4,0},{6,2},{1,5},{3,7},{5,1},{7,3},{8,12},{10,14},{12... | collective-permute-start | bytes 147464 | tf_op jit(solution)/shard_map/ppermute | solution.py:363
  16.7 4.1 %collective-permute-start.5 = (bf16[192,128]{1,0:T(8,128)(2,1)S(1)}, bf16[192,128]{1,0:T(8,128)(2,1)S(1)}, u32[]{:S(2)}, u32[]{:S(2)}) collective-permute-start(bf16[192,128]{1,0:T(8,128)(2,1)S(1)} %get-tuple-element.73), channel_id=1, source_target_pairs={{0,6},{2,0},{4,2},{6,4},{1,7},{3,1},{5,3},{7,5},{8,14},{10,8},{12,... | collective-permute-start | bytes 147464 | tf_op jit(solution)/shard_map/ppermute | solution.py:363
  20.8 1.3 %collective-permute-start.6 = (bf16[320,128]{1,0:T(8,128)(2,1)S(1)}, bf16[320,128]{1,0:T(8,128)(2,1)S(1)}, u32[]{:S(2)}, u32[]{:S(2)}) collective-permute-start(bf16[320,128]{1,0:T(8,128)(2,1)S(1)} %get-tuple-element.83), channel_id=1, source_target_pairs={{0,1},{1,0},{2,3},{3,2},{4,5},{5,4},{6,7},{7,6},{8,9},{9,8},{10,11... | collective-permute-start | bytes 245768 | tf_op jit(solution)/shard_map/ppermute | solution.py:358
  22.4 6.2 %collective-permute-start.7 = (bf16[320,128]{1,0:T(8,128)(2,1)S(1)}, bf16[320,128]{1,0:T(8,128)(2,1)S(1)}, u32[]{:S(2)}, u32[]{:S(2)}) collective-permute-start(bf16[320,128]{1,0:T(8,128)(2,1)S(1)} %get-tuple-element.102), channel_id=1, source_target_pairs={{0,8},{8,0},{16,24},{24,16},{1,9},{9,1},{17,25},{25,17},{2,10},{10... | collective-permute-start | bytes 245768 | tf_op jit(solution)/shard_map/ppermute | solution.py:358
  23.8 6.2 %collective-permute-start.8 = (bf16[320,128]{1,0:T(8,128)(2,1)S(1)}, bf16[320,128]{1,0:T(8,128)(2,1)S(1)}, u32[]{:S(2)}, u32[]{:S(2)}) collective-permute-start(bf16[320,128]{1,0:T(8,128)(2,1)S(1)} %get-tuple-element.103), channel_id=1, source_target_pairs={{0,16},{8,24},{16,0},{24,8},{1,17},{9,25},{17,1},{25,9},{2,18},{10... | collective-permute-start | bytes 245768 | tf_op jit(solution)/shard_map/ppermute | solution.py:358
  24.5 5.4 %collective-permute-start.9 = (bf16[320,128]{1,0:T(8,128)(2,1)S(1)}, bf16[320,128]{1,0:T(8,128)(2,1)S(1)}, u32[]{:S(2)}, u32[]{:S(2)}) collective-permute-start(bf16[320,128]{1,0:T(8,128)(2,1)S(1)} %get-tuple-element.104), channel_id=1, source_target_pairs={{0,24},{8,16},{16,8},{24,0},{1,25},{9,17},{17,9},{25,1},{2,26},{10... | collective-permute-start | bytes 245768 | tf_op jit(solution)/shard_map/ppermute | solution.py:358
  26.0 4.0 %copy-start = (bf16[1,256,256]{2,1,0:T(8,128)(2,1)S(1)}, bf16[1,256,256]{2,1,0:T(8,128)(2,1)}, u32[]{:S(2)}) copy-start(bf16[1,256,256]{2,1,0:T(8,128)(2,1)} %refs_5_.3) | copy-start | bytes 393220
  26.0 4.0 %copy-start.1 = (bf16[1,256,256]{2,1,0:T(8,128)(2,1)S(1)}, bf16[1,256,256]{2,1,0:T(8,128)(2,1)}, u32[]{:S(2)}) copy-start(bf16[1,256,256]{2,1,0:T(8,128)(2,1)} %refs_6_.3) | copy-start | bytes 393220

commit v14 on v12

--- a/solution.py
+++ b/solution.py
@@ -66,16 +66,15 @@
 
 
 def first_kernel(
-    n, ids_hbm, lens_hbm, adv_hbm, keys_hbm, values_hbm, pgates_hbm, gates_hbm, mask_hbm, q_hbm, c_hbm, k_hbm, v_hbm,
+    n, ids_hbm, lens_hbm, adv_hbm, keys_hbm, values_hbm, pgates_hbm, gates_hbm, mask_hbm, q_hbm, c_hbm,
     *refs,
 ):
-    msgs, (rows_ref, q, c, k_out, v_out) = refs[:n], refs[n : n + 5]
-    keys, values, pgates, gates, mask, ids_ref, lens_ref, adv_ref, matrices, sems = refs[n + 5 :]
+    msgs, (rows_ref, q, c) = refs[:n], refs[n : n + 3]
+    keys, values, pgates, gates, mask, ids_ref, lens_ref, adv_ref, matrices, sems = refs[n + 3 :]
     pairs = [(pgates_hbm, pgates), (gates_hbm, gates), (lens_hbm, lens_ref), (adv_hbm, adv_ref), (mask_hbm, mask)]
     pairs += [(keys_hbm, keys), (values_hbm, values), (q_hbm, q), (c_hbm, c), (ids_hbm, ids_ref)]
-    pairs += [(k_hbm, k_out), (v_hbm, v_out)]
     copies = [pltpu.make_async_copy(a, b, sems.at[i]) for i, (a, b) in enumerate(pairs)]
-    for copy in copies[:10]:
+    for copy in copies:
         copy.start()
     count = gates.shape[0]
     slots = gates.shape[2]
@@ -91,8 +90,6 @@
                 at, of, :
             ].astype(BF16)
 
-    for copy in copies[10:]:
-        copy.start()
     copies[0].wait()
     copies[1].wait()
     piece = jnp.concatenate([pgates[0], jnp.zeros((H, slots - tokens), F32)], axis=1)
@@ -144,8 +141,6 @@
     notes = jnp.concatenate(notes, axis=0).astype(BF16)
     for k in range(n):
         msgs[k][block : block + 16, :] = notes
-    for copy in copies[10:]:
-        copy.wait()
 
 
 def noted_prompt(notes, i):
@@ -395,9 +390,9 @@
         lambda *refs: first_kernel(n, *refs),
         out_shape=[shape((block * (1 + responses) + 16, DH), BF16)] * n
         + [shape((8 * (responses + 1), slots), F32)]
-        + [shape(queries.shape, BF16)] * 4,
-        in_specs=[ANY] * 12,
-        out_specs=[VMEM] * (n + 5),
+        + [shape(queries.shape, BF16)] * 2,
+        in_specs=[ANY] * 10,
+        out_specs=[VMEM] * (n + 3),
         scratch_shapes=[
             pltpu.VMEM(keys.shape, BF16),
             pltpu.VMEM(values.shape, BF16),
@@ -408,15 +403,15 @@
             pltpu.SMEM(resp_lengths.shape, jnp.int32),
             pltpu.SMEM(advantages.shape, jnp.int32),
             pltpu.VMEM((H * (1 + responses), DH, DH), F32),
-            pltpu.SemaphoreType.DMA((12,)),
+            pltpu.SemaphoreType.DMA((10,)),
         ],
         compiler_params=params(32),
         name="first",
     )(
         *[in_hbm(x) for x in (group_ids, resp_lengths, advantages, keys, values, prompt_gates, resp_gates)],
-        *[in_hbm(x) for x in (loss_mask, queries, cotangent, resp_keys, resp_values)],
+        *[in_hbm(x) for x in (loss_mask, queries, cotangent)],
     )
-    msgs, (rows, queries, cotangent, resp_keys, resp_values) = outs[:n], outs[n:]
+    msgs, (rows, queries, cotangent) = outs[:n], outs[n:]
 
     like = shape(queries.shape, F32)
     like_out = shape(queries.shape, BF16)

time: 31.9 us -> 32 us (level)
  no operation moved by 1% of the time
where the time goes in v14:
time: 32 us; the launch traced here: 31.8 us
  starting transfers between devices  13.8 us (43%)
  Pallas kernels  13.2 us (41%)
  waiting for transfers between devices  4.04 us (13%)
  between operations  0.76 us (2%)
    ppermute x7, starting transfers between devices, exchange(): lax.ppermute(xs[k], axis, [(s, s ^ k) for s in range(n)])  8.22 us
    ppermute x3, starting transfers between devices, exchange_ring(): lax.ppermute(xs[k], axis, [(s, (s + k) % n) for s in range(n)])  5.57 us
    pallas_call x3, Pallas kernels, sweep(): pl.pallas_call(lambda *refs: sweep_kernel(units, done, *refs), out_shape=...  5.39 us
    ppermute x7, waiting for transfers between devices, exchange(): lax.ppermute(xs[k], axis, [(s, s ^ k) for s in range(n)])  3.1 us
    pallas_call x1, Pallas kernels, first_sweep(): pl.pallas_call(lambda *refs: sweep_kernel(units, (), *refs[:5], None, *re...  2.84 us
    pallas_call x1, Pallas kernels, shards(): pl.pallas_call(lambda *refs: first_kernel(n, *refs), out_shape=[shape((bl...  2.55 us
    pallas_call x1, Pallas kernels, shards(): pl.pallas_call(lambda *refs: last_kernel(n, responses, *refs), out_shape=...  1.89 us
    ppermute x3, waiting for transfers between devices, exchange_ring(): lax.ppermute(xs[k], axis, [(s, (s + k) % n) for s in range(n)])  0.94 us
  transfers between devices with their start and end apart: 10, of which 5 were waited for; matrix products, arithmetic and copies ran while one was open for 0% of the time, Pallas kernels for 26%

profile of v14, /device:TPU:0, one launch (start us, length us, event | category | flops | bytes accessed | tf_op | source)
XLA Modules:
  0.0 31.8 jit_solution(13139153297944071322)
XLA Ops:
  0.6 0.0 copy-start.1
  0.6 0.0 copy-start
  0.7 2.6 %first.1 = (bf16[336,128]{1,0:T(8,128)(2,1)S(1)}, bf16[336,128]{1,0:T(8,128)(2,1)S(1)}, bf16[336,128]{1,0:T(8,128)(2,1)S(1)}, bf16[336,128]{1,0:T(8,128)(2,1)S(1...) custom-call(s32[4]{0:T(128)} %refs_0_.1, s32[1,4]{1,0:T(1,128)} %refs_1_.1, ...), custom_call_target="tpu_custom_call" | custom-call | tf_op jit(solution)/shard_map/first/pallas_call | solution.py:389
  3.2 4.0 %collective-permute-start = (bf16[336,128]{1,0:T(8,128)(2,1)S(1)}, bf16[336,128]{1,0:T(8,128)(2,1)S(1)}, u32[]{:S(2)}, u32[]{:S(2)}) collective-permute-start(bf16[336,128]{1,0:T(8,128)(2,1)S(1)} %get-tuple-element.62), channel_id=1, source_target_pairs={{0,24},{8,16},{16,8},{24,0},{1,25},{9,17},{17,9},{25,1},{2,26},{10... | collective-permute-start | bytes 258056 | tf_op jit(solution)/shard_map/ppermute | solution.py:351
  7.2 0.5 %collective-permute-start.1 = (bf16[336,128]{1,0:T(8,128)(2,1)S(1)}, bf16[336,128]{1,0:T(8,128)(2,1)S(1)}, u32[]{:S(2)}, u32[]{:S(2)}) collective-permute-start(bf16[336,128]{1,0:T(8,128)(2,1)S(1)} %get-tuple-element.63), channel_id=1, source_target_pairs={{0,16},{8,24},{16,0},{24,8},{1,17},{9,25},{17,1},{25,9},{2,18},{10... | collective-permute-start | bytes 258056 | tf_op jit(solution)/shard_map/ppermute | solution.py:351
  7.7 0.1 collective-permute-start.2
  7.8 0.0 copy-done.1
  7.8 0.0 copy-done
  7.8 2.8 %sweep.4 = (f32[512,128]{1,0:T(8,128)S(1)}, f32[4,512,256]{2,1,0:T(8,128)S(1)}, f32[4,512,256]{2,1,0:T(8,128)S(1)}, bf16[4,512,256]{2,1,0:T(8,128)(2,1)S(1)}, bf...) custom-call(f32[40,512]{1,0:T(8,128)S(1)} %get-tuple-element.57.refs, ...), custom_call_target="tpu_custom_call" | custom-call | tf_op jit(solution)/shard_map/sweep/pallas_call | solution.py:422
  10.7 0.0 collective-permute-done.refs_1_
  10.7 1.0 %collective-permute-done.1.refs_2_ = bf16[336,128]{1,0:T(8,128)(2,1)S(1)} collective-permute-done((bf16[336,128]{1,0:T(8,128)(2,1)S(1)}, bf16[336,128]{1,0:T(8,128)(2,1)S(1)}, u32[]{:S(2)}, u32[]{:S(2)}) %collective-permute-start.1) | collective-permute-done | bytes 86048 | tf_op jit(solution)/shard_map/ppermute | solution.py:351
  11.7 0.5 %collective-permute-done.2.refs_3_ = bf16[336,128]{1,0:T(8,128)(2,1)S(1)} collective-permute-done((bf16[336,128]{1,0:T(8,128)(2,1)S(1)}, bf16[336,128]{1,0:T(8,128)(2,1)S(1)}, u32[]{:S(2)}, u32[]{:S(2)}) %collective-permute-start.2) | collective-permute-done | bytes 86048 | tf_op jit(solution)/shard_map/ppermute | solution.py:351
  12.2 0.2 second.1
  12.4 1.6 %collective-permute-start.3 = (bf16[192,128]{1,0:T(8,128)(2,1)S(1)}, bf16[192,128]{1,0:T(8,128)(2,1)S(1)}, u32[]{:S(2)}, u32[]{:S(2)}) collective-permute-start(bf16[192,128]{1,0:T(8,128)(2,1)S(1)} %get-tuple-element.67), channel_id=1, source_target_pairs={{0,2},{2,4},{4,6},{6,0},{1,3},{3,5},{5,7},{7,1},{8,10},{10,12},{12... | collective-permute-start | bytes 147464 | tf_op jit(solution)/shard_map/ppermute | solution.py:356
  14.0 2.6 %collective-permute-start.4 = (bf16[192,128]{1,0:T(8,128)(2,1)S(1)}, bf16[192,128]{1,0:T(8,128)(2,1)S(1)}, u32[]{:S(2)}, u32[]{:S(2)}) collective-permute-start(bf16[192,128]{1,0:T(8,128)(2,1)S(1)} %get-tuple-element.68), channel_id=1, source_target_pairs={{0,4},{2,6},{4,0},{6,2},{1,5},{3,7},{5,1},{7,3},{8,12},{10,14},{12... | collective-permute-start | bytes 147464 | tf_op jit(solution)/shard_map/ppermute | solution.py:356
  16.6 1.3 %collective-permute-start.5 = (bf16[192,128]{1,0:T(8,128)(2,1)S(1)}, bf16[192,128]{1,0:T(8,128)(2,1)S(1)}, u32[]{:S(2)}, u32[]{:S(2)}) collective-permute-start(bf16[192,128]{1,0:T(8,128)(2,1)S(1)} %get-tuple-element.69), channel_id=1, source_target_pairs={{0,6},{2,0},{4,2},{6,4},{1,7},{3,1},{5,3},{7,5},{8,14},{10,8},{12,... | collective-permute-start | bytes 147464 | tf_op jit(solution)/shard_map/ppermute | solution.py:356
  18.0 1.8 %sweep.5 = (f32[4,512,256]{2,1,0:T(8,128)S(1)}, f32[4,512,256]{2,1,0:T(8,128)S(1)}, bf16[4,512,256]{2,1,0:T(8,128)(2,1)S(1)}, bf16[4,512,256]{2,1,0:T(8,128)(2,1...) custom-call(f32[40,512]{1,0:T(8,128)S(1)} %get-tuple-element.57.refs, ...), custom_call_target="tpu_custom_call", output_to_operand_aliasing={{0}: (7, {}), {1}: (8, {}), {2}: (9, {}), {3}: (10, {}), {4... | custom-call | tf_op jit(solution)/shard_map/sweep/pallas_call | solution.py:434
  19.8 0.0 collective-permute-done.3.refs_1_
  19.8 0.0 collective-permute-done.4.refs_2_
  19.8 0.9 %collective-permute-done.5.refs_3_ = bf16[192,128]{1,0:T(8,128)(2,1)S(1)} collective-permute-done((bf16[192,128]{1,0:T(8,128)(2,1)S(1)}, bf16[192,128]{1,0:T(8,128)(2,1)S(1)}, u32[]{:S(2)}, u32[]{:S(2)}) %collective-permute-start.5) | collective-permute-done | bytes 49184 | tf_op jit(solution)/shard_map/ppermute | solution.py:356
  20.8 0.1 collective-permute-start.6
  20.8 1.0 %sweep.6 = (f32[4,512,256]{2,1,0:T(8,128)S(1)}, f32[4,512,256]{2,1,0:T(8,128)S(1)}, bf16[4,512,256]{2,1,0:T(8,128)(2,1)S(1)}, bf16[4,512,256]{2,1,0:T(8,128)(2,1...) custom-call(f32[40,512]{1,0:T(8,128)S(1)} %get-tuple-element.57.refs, ...), custom_call_target="tpu_custom_call", output_to_operand_aliasing={{0}: (7, {}), {1}: (8, {}), {2}: (9, {}), {3}: (10, {}), {4... | custom-call | tf_op jit(solution)/shard_map/sweep/pallas_call | solution.py:434
  21.8 0.3 collective-permute-done.6.refs_5_
  22.1 0.3 third.1
  22.4 1.3 %collective-permute-start.7 = (bf16[320,128]{1,0:T(8,128)(2,1)S(1)}, bf16[320,128]{1,0:T(8,128)(2,1)S(1)}, u32[]{:S(2)}, u32[]{:S(2)}) collective-permute-start(bf16[320,128]{1,0:T(8,128)(2,1)S(1)} %get-tuple-element.98), channel_id=1, source_target_pairs={{0,8},{8,0},{16,24},{24,16},{1,9},{9,1},{17,25},{25,17},{2,10},{10... | collective-permute-start | bytes 245768 | tf_op jit(solution)/shard_map/ppermute | solution.py:351
  23.7 0.8 %collective-permute-start.8 = (bf16[320,128]{1,0:T(8,128)(2,1)S(1)}, bf16[320,128]{1,0:T(8,128)(2,1)S(1)}, u32[]{:S(2)}, u32[]{:S(2)}) collective-permute-start(bf16[320,128]{1,0:T(8,128)(2,1)S(1)} %get-tuple-element.99), channel_id=1, source_target_pairs={{0,16},{8,24},{16,0},{24,8},{1,17},{9,25},{17,1},{25,9},{2,18},{10... | collective-permute-start | bytes 245768 | tf_op jit(solution)/shard_map/ppermute | solution.py:351
  24.5 1.4 %collective-permute-start.9 = (bf16[320,128]{1,0:T(8,128)(2,1)S(1)}, bf16[320,128]{1,0:T(8,128)(2,1)S(1)}, u32[]{:S(2)}, u32[]{:S(2)}) collective-permute-start(bf16[320,128]{1,0:T(8,128)(2,1)S(1)} %get-tuple-element.100), channel_id=1, source_target_pairs={{0,24},{8,16},{16,8},{24,0},{1,25},{9,17},{17,9},{25,1},{2,26},{10... | collective-permute-start | bytes 245768 | tf_op jit(solution)/shard_map/ppermute | solution.py:351
  25.9 0.0 copy-start.2
  25.9 0.0 copy-start.3
  25.9 2.6 %sweep.7 = (f32[4,512,256]{2,1,0:T(8,128)S(1)}, f32[4,512,256]{2,1,0:T(8,128)S(1)}, bf16[4,512,256]{2,1,0:T(8,128)(2,1)S(1)}, bf16[4,512,256]{2,1,0:T(8,128)(2,1...) custom-call(f32[40,512]{1,0:T(8,128)S(1)} %get-tuple-element.57.refs, ...), custom_call_target="tpu_custom_call", output_to_operand_aliasing={{0}: (7, {}), {1}: (8, {}), {2}: (9, {}), {3}: (10, {}), {4... | custom-call | tf_op jit(solution)/shard_map/sweep/pallas_call | solution.py:434
  28.6 0.0 collective-permute-done.7.refs_9_
  28.6 1.3 %collective-permute-done.8.refs_10_ = bf16[320,128]{1,0:T(8,128)(2,1)S(1)} collective-permute-done((bf16[320,128]{1,0:T(8,128)(2,1)S(1)}, bf16[320,128]{1,0:T(8,128)(2,1)S(1)}, u32[]{:S(2)}, u32[]{:S(2)}) %collective-permute-start.8) | collective-permute-done | bytes 81952 | tf_op jit(solution)/shard_map/ppermute | solution.py:351
  29.9 0.0 collective-permute-done.9.refs_11_
  29.9 0.0 copy-done.2
  29.9 0.0 copy-done.3
  29.9 1.9 %last.1 = (bf16[4,512,256]{2,1,0:T(8,128)(2,1)}, bf16[4,512,256]{2,1,0:T(8,128)(2,1)}, bf16[1,256,256]{2,1,0:T(8,128)(2,1)}, bf16[1,256,256]{2,1,0:T(8,128)(2,1)}) custom-call(f32[512,128]{1,0:T(8,128)S(1)} %get-tuple-element.60.refs_5_.refs_0_, bf16[4,512,256]{2,1,0:T(8,128)(2,1)S(1)} %get-tuple-element.94.refs_1_, ...), custom_call_target="tpu_custom_call" | custom-call | tf_op jit(solution)/shard_map/last/pallas_call | solution.py:483
  (1 shorter events, 0.0 us)
Async XLA Ops:
  0.6 7.2 %copy-start.1 = (bf16[4,512,256]{2,1,0:T(8,128)(2,1)S(1)}, bf16[4,512,256]{2,1,0:T(8,128)(2,1)}, u32[]{:S(2)}) copy-start(bf16[4,512,256]{2,1,0:T(8,128)(2,1)} %refs_3_.9) | copy-start | bytes 3145732
  0.6 7.2 %copy-start = (bf16[4,512,256]{2,1,0:T(8,128)(2,1)S(1)}, bf16[4,512,256]{2,1,0:T(8,128)(2,1)}, u32[]{:S(2)}) copy-start(bf16[4,512,256]{2,1,0:T(8,128)(2,1)} %refs_2_.9) | copy-start | bytes 3145732
  3.2 7.5 %collective-permute-start = (bf16[336,128]{1,0:T(8,128)(2,1)S(1)}, bf16[336,128]{1,0:T(8,128)(2,1)S(1)}, u32[]{:S(2)}, u32[]{:S(2)}) collective-permute-start(bf16[336,128]{1,0:T(8,128)(2,1)S(1)} %get-tuple-element.62), channel_id=1, source_target_pairs={{0,24},{8,16},{16,8},{24,0},{1,25},{9,17},{17,9},{25,1},{2,26},{10... | collective-permute-start | bytes 258056 | tf_op jit(solution)/shard_map/ppermute | solution.py:351
  7.2 4.5 %collective-permute-start.1 = (bf16[336,128]{1,0:T(8,128)(2,1)S(1)}, bf16[336,128]{1,0:T(8,128)(2,1)S(1)}, u32[]{:S(2)}, u32[]{:S(2)}) collective-permute-start(bf16[336,128]{1,0:T(8,128)(2,1)S(1)} %get-tuple-element.63), channel_id=1, source_target_pairs={{0,16},{8,24},{16,0},{24,8},{1,17},{9,25},{17,1},{25,9},{2,18},{10... | collective-permute-start | bytes 258056 | tf_op jit(solution)/shard_map/ppermute | solution.py:351
  7.7 4.5 %collective-permute-start.2 = (bf16[336,128]{1,0:T(8,128)(2,1)S(1)}, bf16[336,128]{1,0:T(8,128)(2,1)S(1)}, u32[]{:S(2)}, u32[]{:S(2)}) collective-permute-start(bf16[336,128]{1,0:T(8,128)(2,1)S(1)} %get-tuple-element.64), channel_id=1, source_target_pairs={{0,8},{8,0},{16,24},{24,16},{1,9},{9,1},{17,25},{25,17},{2,10},{10... | collective-permute-start | bytes 258056 | tf_op jit(solution)/shard_map/ppermute | solution.py:351
  12.4 7.4 %collective-permute-start.3 = (bf16[192,128]{1,0:T(8,128)(2,1)S(1)}, bf16[192,128]{1,0:T(8,128)(2,1)S(1)}, u32[]{:S(2)}, u32[]{:S(2)}) collective-permute-start(bf16[192,128]{1,0:T(8,128)(2,1)S(1)} %get-tuple-element.67), channel_id=1, source_target_pairs={{0,2},{2,4},{4,6},{6,0},{1,3},{3,5},{5,7},{7,1},{8,10},{10,12},{12... | collective-permute-start | bytes 147464 | tf_op jit(solution)/shard_map/ppermute | solution.py:356
  14.0 5.7 %collective-permute-start.4 = (bf16[192,128]{1,0:T(8,128)(2,1)S(1)}, bf16[192,128]{1,0:T(8,128)(2,1)S(1)}, u32[]{:S(2)}, u32[]{:S(2)}) collective-permute-start(bf16[192,128]{1,0:T(8,128)(2,1)S(1)} %get-tuple-element.68), channel_id=1, source_target_pairs={{0,4},{2,6},{4,0},{6,2},{1,5},{3,7},{5,1},{7,3},{8,12},{10,14},{12... | collective-permute-start | bytes 147464 | tf_op jit(solution)/shard_map/ppermute | solution.py:356
  16.6 4.1 %collective-permute-start.5 = (bf16[192,128]{1,0:T(8,128)(2,1)S(1)}, bf16[192,128]{1,0:T(8,128)(2,1)S(1)}, u32[]{:S(2)}, u32[]{:S(2)}) collective-permute-start(bf16[192,128]{1,0:T(8,128)(2,1)S(1)} %get-tuple-element.69), channel_id=1, source_target_pairs={{0,6},{2,0},{4,2},{6,4},{1,7},{3,1},{5,3},{7,5},{8,14},{10,8},{12,... | collective-permute-start | bytes 147464 | tf_op jit(solution)/shard_map/ppermute | solution.py:356
  20.8 1.3 %collective-permute-start.6 = (bf16[320,128]{1,0:T(8,128)(2,1)S(1)}, bf16[320,128]{1,0:T(8,128)(2,1)S(1)}, u32[]{:S(2)}, u32[]{:S(2)}) collective-permute-start(bf16[320,128]{1,0:T(8,128)(2,1)S(1)} %get-tuple-element.79), channel_id=1, source_target_pairs={{0,1},{1,0},{2,3},{3,2},{4,5},{5,4},{6,7},{7,6},{8,9},{9,8},{10,11... | collective-permute-start | bytes 245768 | tf_op jit(solution)/shard_map/ppermute | solution.py:351
  22.4 6.2 %collective-permute-start.7 = (bf16[320,128]{1,0:T(8,128)(2,1)S(1)}, bf16[320,128]{1,0:T(8,128)(2,1)S(1)}, u32[]{:S(2)}, u32[]{:S(2)}) collective-permute-start(bf16[320,128]{1,0:T(8,128)(2,1)S(1)} %get-tuple-element.98), channel_id=1, source_target_pairs={{0,8},{8,0},{16,24},{24,16},{1,9},{9,1},{17,25},{25,17},{2,10},{10... | collective-permute-start | bytes 245768 | tf_op jit(solution)/shard_map/ppermute | solution.py:351
  23.7 6.2 %collective-permute-start.8 = (bf16[320,128]{1,0:T(8,128)(2,1)S(1)}, bf16[320,128]{1,0:T(8,128)(2,1)S(1)}, u32[]{:S(2)}, u32[]{:S(2)}) collective-permute-start(bf16[320,128]{1,0:T(8,128)(2,1)S(1)} %get-tuple-element.99), channel_id=1, source_target_pairs={{0,16},{8,24},{16,0},{24,8},{1,17},{9,25},{17,1},{25,9},{2,18},{10... | collective-permute-start | bytes 245768 | tf_op jit(solution)/shard_map/ppermute | solution.py:351
  24.5 5.4 %collective-permute-start.9 = (bf16[320,128]{1,0:T(8,128)(2,1)S(1)}, bf16[320,128]{1,0:T(8,128)(2,1)S(1)}, u32[]{:S(2)}, u32[]{:S(2)}) collective-permute-start(bf16[320,128]{1,0:T(8,128)(2,1)S(1)} %get-tuple-element.100), channel_id=1, source_target_pairs={{0,24},{8,16},{16,8},{24,0},{1,25},{9,17},{17,9},{25,1},{2,26},{10... | collective-permute-start | bytes 245768 | tf_op jit(solution)/shard_map/ppermute | solution.py:351
  25.9 4.0 %copy-start.2 = (bf16[1,256,256]{2,1,0:T(8,128)(2,1)S(1)}, bf16[1,256,256]{2,1,0:T(8,128)(2,1)}, u32[]{:S(2)}) copy-start(bf16[1,256,256]{2,1,0:T(8,128)(2,1)} %refs_5_.3) | copy-start | bytes 393220
  25.9 4.0 %copy-start.3 = (bf16[1,256,256]{2,1,0:T(8,128)(2,1)S(1)}, bf16[1,256,256]{2,1,0:T(8,128)(2,1)}, u32[]{:S(2)}) copy-start(bf16[1,256,256]{2,1,0:T(8,128)(2,1)} %refs_6_.3) | copy-start | bytes 393220

commit v15 on v14

--- a/solution.py
+++ b/solution.py
@@ -222,9 +222,18 @@
     if writes:
         *refs, dk_hbm, dv_hbm, sems = refs
     out_ref, dq_ref, query_ref, grad_ref, dk_ref, dv_ref, token_ref = refs[-7:]
+    fetches = []
     if cols_ref is None:
-        cols_ref = refs[0]
+        cols_ref, k_vmem, v_vmem = refs[:3]
+        sems = refs[-8]
+        for r in range(k_ref.shape[0]):
+            for a, b in ((k_ref, k_vmem), (v_ref, v_vmem)):
+                fetches.append(pltpu.make_async_copy(a.at[r], b.at[r], sems.at[len(fetches)]))
+                fetches[-1].start()
         cols_ref[...] = to_columns(rows_ref[...])
+        k_ref, v_ref = k_vmem, v_vmem
+        for fetch in fetches[:2]:
+            fetch.wait()
     copies = []
 
     def send(r):
@@ -299,7 +308,7 @@
             dv_ref[r, of, lanes] = dv[s].astype(BF16).T
         if writes and h == H - 1:
             send(r)
-    for copy in copies:
+    for copy in copies + fetches[2:]:
         copy.wait()
 
 
@@ -420,14 +429,15 @@
 
     def first_sweep(units):
         outs = pl.pallas_call(
-            lambda *refs: sweep_kernel(units, (), *refs[:5], None, *refs[5:]),
-            out_shape=[shape((slots, 128), F32)] + held_shapes,
-            in_specs=[VMEM] * 5,
-            out_specs=[VMEM] * 8,
+            lambda *refs: sweep_kernel(units, (), *refs[:5], None, *refs[5:8], refs[-1], *refs[8:-1]),
+            out_shape=[shape((slots, 128), F32), like_out, like_out] + held_shapes,
+            in_specs=[VMEM, VMEM, ANY, ANY, VMEM],
+            out_specs=[VMEM] * 10,
+            scratch_shapes=[pltpu.SemaphoreType.DMA((2 * responses,))],
             compiler_params=params(),
             name="sweep",
-        )(rows, queries, resp_keys, resp_values, cotangent)
-        return outs[0], outs[1:7], outs[7]
+        )(rows, queries, in_hbm(resp_keys), in_hbm(resp_values), cotangent)
+        return outs[0], outs[1], outs[2], outs[3:9], outs[9]
 
     def sweep(units, before, token, done=()):
         writes = len(done) > 0
@@ -445,7 +455,7 @@
 
     units = [(r, h) for r in range(responses) for h in range(H)]
     got1 = far_first(exchange(msgs, "prompt"))
-    cols, held, token = first_sweep(units[:3])
+    cols, resp_keys, resp_values, held, token = first_sweep(units[:2])
     outs = pl.pallas_call(
         lambda *refs: second_kernel(n, chips, cores, *refs),
         out_shape=[shape(((1 + cores) * block, DH), BF16)] * chips + [shape((8, DH), F32)],
@@ -457,7 +467,7 @@
     )(*got1, token)
     msgs, later = outs[:chips], outs[chips]
     got2 = exchange_ring(msgs, "z")
-    held, token = sweep(units[3:5], held, later)
+    held, token = sweep(units[2:5], held, later)
     sent, kept = pl.pallas_call(
         lambda *refs: swap_kernel(chips, *refs),
         out_shape=[shape(((chips + 1) * block, DH), BF16)] * 2,

time: 32 us -> 31.8 us (level)
  waiting for transfers between devices: 4.04 us -> 3.17 us
  Pallas kernels: 13.2 us -> 13.9 us
    ppermute x3, waiting for transfers between devices: 0.94 us -> 0.12 us  [exchange_ring(): lax.ppermute(xs[k], axis, [(s, (s + k) % n) for s in range(n)])]
    pallas_call x3, Pallas kernels: 5.39 us -> 6.2 us  [sweep(): pl.pallas_call(lambda *refs: sweep_kernel(units, done, *refs), out_shape=...]
  transfers between devices with their start and end apart: 10 -> 10, of which waited for: 5 -> 5; matrix products, arithmetic and copies ran while one was open for 0% -> 0% of each run, Pallas kernels for 26% -> 29%
where the time goes in v15:
time: 31.8 us; the launch traced here: 31.6 us
  Pallas kernels  13.9 us (44%)
  starting transfers between devices  13.8 us (43%)
  waiting for transfers between devices  3.17 us (10%)
  between operations  0.74 us (2%)
    ppermute x7, starting transfers between devices, exchange(): lax.ppermute(xs[k], axis, [(s, s ^ k) for s in range(n)])  8.22 us
    pallas_call x3, Pallas kernels, sweep(): pl.pallas_call(lambda *refs: sweep_kernel(units, done, *refs), out_shape=...  6.2 us
    ppermute x3, starting transfers between devices, exchange_ring(): lax.ppermute(xs[k], axis, [(s, (s + k) % n) for s in range(n)])  5.57 us
    ppermute x7, waiting for transfers between devices, exchange(): lax.ppermute(xs[k], axis, [(s, s ^ k) for s in range(n)])  3.05 us
    pallas_call x1, Pallas kernels, first_sweep(): pl.pallas_call(lambda *refs: sweep_kernel(units, (), *refs[:5], None, *re...  2.89 us
    pallas_call x1, Pallas kernels, shards(): pl.pallas_call(lambda *refs: first_kernel(n, *refs), out_shape=[shape((bl...  2.41 us
    pallas_call x1, Pallas kernels, shards(): pl.pallas_call(lambda *refs: last_kernel(n, responses, *refs), out_shape=...  1.88 us
  transfers between devices with their start and end apart: 10, of which 5 were waited for; matrix products, arithmetic and copies ran while one was open for 0% of the time, Pallas kernels for 29%

profile of v15, /device:TPU:0, one launch (start us, length us, event | category | flops | bytes accessed | tf_op | source)
XLA Modules:
  0.0 31.6 jit_solution(6300204564425451604)
XLA Ops:
  0.6 2.4 %first.1 = (bf16[336,128]{1,0:T(8,128)(2,1)S(1)}, bf16[336,128]{1,0:T(8,128)(2,1)S(1)}, bf16[336,128]{1,0:T(8,128)(2,1)S(1)}, bf16[336,128]{1,0:T(8,128)(2,1)S(1...) custom-call(s32[4]{0:T(128)} %refs_0_.1, s32[1,4]{1,0:T(1,128)} %refs_1_.1, ...), custom_call_target="tpu_custom_call" | custom-call | tf_op jit(solution)/shard_map/first/pallas_call | solution.py:398
  3.1 4.0 %collective-permute-start = (bf16[336,128]{1,0:T(8,128)(2,1)S(1)}, bf16[336,128]{1,0:T(8,128)(2,1)S(1)}, u32[]{:S(2)}, u32[]{:S(2)}) collective-permute-start(bf16[336,128]{1,0:T(8,128)(2,1)S(1)} %get-tuple-element.66), channel_id=1, source_target_pairs={{0,24},{8,16},{16,8},{24,0},{1,25},{9,17},{17,9},{25,1},{2,26},{10... | collective-permute-start | bytes 258056 | tf_op jit(solution)/shard_map/ppermute | solution.py:360
  7.0 0.5 %collective-permute-start.1 = (bf16[336,128]{1,0:T(8,128)(2,1)S(1)}, bf16[336,128]{1,0:T(8,128)(2,1)S(1)}, u32[]{:S(2)}, u32[]{:S(2)}) collective-permute-start(bf16[336,128]{1,0:T(8,128)(2,1)S(1)} %get-tuple-element.67), channel_id=1, source_target_pairs={{0,16},{8,24},{16,0},{24,8},{1,17},{9,25},{17,1},{25,9},{2,18},{10... | collective-permute-start | bytes 258056 | tf_op jit(solution)/shard_map/ppermute | solution.py:360
  7.5 0.1 collective-permute-start.2
  7.7 2.9 %sweep.4 = (f32[512,128]{1,0:T(8,128)S(1)}, bf16[4,512,256]{2,1,0:T(8,128)(2,1)S(1)}, bf16[4,512,256]{2,1,0:T(8,128)(2,1)S(1)}, f32[4,512,256]{2,1,0:T(8,128)S(1...) custom-call(f32[40,512]{1,0:T(8,128)S(1)} %get-tuple-element.59.refs, ...), custom_call_target="tpu_custom_call" | custom-call | tf_op jit(solution)/shard_map/sweep/pallas_call | solution.py:431
  10.6 0.0 collective-permute-done.refs_1_
  10.6 0.9 %collective-permute-done.1.refs_2_ = bf16[336,128]{1,0:T(8,128)(2,1)S(1)} collective-permute-done((bf16[336,128]{1,0:T(8,128)(2,1)S(1)}, bf16[336,128]{1,0:T(8,128)(2,1)S(1)}, u32[]{:S(2)}, u32[]{:S(2)}) %collective-permute-start.1) | collective-permute-done | bytes 86048 | tf_op jit(solution)/shard_map/ppermute | solution.py:360
  11.5 0.5 %collective-permute-done.2.refs_3_ = bf16[336,128]{1,0:T(8,128)(2,1)S(1)} collective-permute-done((bf16[336,128]{1,0:T(8,128)(2,1)S(1)}, bf16[336,128]{1,0:T(8,128)(2,1)S(1)}, u32[]{:S(2)}, u32[]{:S(2)}) %collective-permute-start.2) | collective-permute-done | bytes 86048 | tf_op jit(solution)/shard_map/ppermute | solution.py:360
  12.0 0.2 second.1
  12.2 1.6 %collective-permute-start.3 = (bf16[192,128]{1,0:T(8,128)(2,1)S(1)}, bf16[192,128]{1,0:T(8,128)(2,1)S(1)}, u32[]{:S(2)}, u32[]{:S(2)}) collective-permute-start(bf16[192,128]{1,0:T(8,128)(2,1)S(1)} %get-tuple-element.71), channel_id=1, source_target_pairs={{0,2},{2,4},{4,6},{6,0},{1,3},{3,5},{5,7},{7,1},{8,10},{10,12},{12... | collective-permute-start | bytes 147464 | tf_op jit(solution)/shard_map/ppermute | solution.py:365
  13.9 2.6 %collective-permute-start.4 = (bf16[192,128]{1,0:T(8,128)(2,1)S(1)}, bf16[192,128]{1,0:T(8,128)(2,1)S(1)}, u32[]{:S(2)}, u32[]{:S(2)}) collective-permute-start(bf16[192,128]{1,0:T(8,128)(2,1)S(1)} %get-tuple-element.72), channel_id=1, source_target_pairs={{0,4},{2,6},{4,0},{6,2},{1,5},{3,7},{5,1},{7,3},{8,12},{10,14},{12... | collective-permute-start | bytes 147464 | tf_op jit(solution)/shard_map/ppermute | solution.py:365
  16.5 1.3 %collective-permute-start.5 = (bf16[192,128]{1,0:T(8,128)(2,1)S(1)}, bf16[192,128]{1,0:T(8,128)(2,1)S(1)}, u32[]{:S(2)}, u32[]{:S(2)}) collective-permute-start(bf16[192,128]{1,0:T(8,128)(2,1)S(1)} %get-tuple-element.73), channel_id=1, source_target_pairs={{0,6},{2,0},{4,2},{6,4},{1,7},{3,1},{5,3},{7,5},{8,14},{10,8},{12,... | collective-permute-start | bytes 147464 | tf_op jit(solution)/shard_map/ppermute | solution.py:365
  17.8 2.6 %sweep.5 = (f32[4,512,256]{2,1,0:T(8,128)S(1)}, f32[4,512,256]{2,1,0:T(8,128)S(1)}, bf16[4,512,256]{2,1,0:T(8,128)(2,1)S(1)}, bf16[4,512,256]{2,1,0:T(8,128)(2,1...) custom-call(f32[40,512]{1,0:T(8,128)S(1)} %get-tuple-element.59.refs, ...), custom_call_target="tpu_custom_call", output_to_operand_aliasing={{0}: (7, {}), {1}: (8, {}), {2}: (9, {}), {3}: (10, {}), {4... | custom-call | tf_op jit(solution)/shard_map/sweep/pallas_call | solution.py:444
  20.4 0.0 collective-permute-done.3.refs_1_
  20.4 0.0 collective-permute-done.4.refs_2_
  20.4 0.1 collective-permute-done.5.refs_3_
  20.6 0.1 collective-permute-start.6
  20.7 1.0 %sweep.6 = (f32[4,512,256]{2,1,0:T(8,128)S(1)}, f32[4,512,256]{2,1,0:T(8,128)S(1)}, bf16[4,512,256]{2,1,0:T(8,128)(2,1)S(1)}, bf16[4,512,256]{2,1,0:T(8,128)(2,1...) custom-call(f32[40,512]{1,0:T(8,128)S(1)} %get-tuple-element.59.refs, ...), custom_call_target="tpu_custom_call", output_to_operand_aliasing={{0}: (7, {}), {1}: (8, {}), {2}: (9, {}), {3}: (10, {}), {4... | custom-call | tf_op jit(solution)/shard_map/sweep/pallas_call | solution.py:444
  21.7 0.3 collective-permute-done.6.refs_5_
  21.9 0.3 third.1
  22.2 1.3 %collective-permute-start.7 = (bf16[320,128]{1,0:T(8,128)(2,1)S(1)}, bf16[320,128]{1,0:T(8,128)(2,1)S(1)}, u32[]{:S(2)}, u32[]{:S(2)}) collective-permute-start(bf16[320,128]{1,0:T(8,128)(2,1)S(1)} %get-tuple-element.102), channel_id=1, source_target_pairs={{0,8},{8,0},{16,24},{24,16},{1,9},{9,1},{17,25},{25,17},{2,10},{10... | collective-permute-start | bytes 245768 | tf_op jit(solution)/shard_map/ppermute | solution.py:360
  23.5 0.8 %collective-permute-start.8 = (bf16[320,128]{1,0:T(8,128)(2,1)S(1)}, bf16[320,128]{1,0:T(8,128)(2,1)S(1)}, u32[]{:S(2)}, u32[]{:S(2)}) collective-permute-start(bf16[320,128]{1,0:T(8,128)(2,1)S(1)} %get-tuple-element.103), channel_id=1, source_target_pairs={{0,16},{8,24},{16,0},{24,8},{1,17},{9,25},{17,1},{25,9},{2,18},{10... | collective-permute-start | bytes 245768 | tf_op jit(solution)/shard_map/ppermute | solution.py:360
  24.3 1.4 %collective-permute-start.9 = (bf16[320,128]{1,0:T(8,128)(2,1)S(1)}, bf16[320,128]{1,0:T(8,128)(2,1)S(1)}, u32[]{:S(2)}, u32[]{:S(2)}) collective-permute-start(bf16[320,128]{1,0:T(8,128)(2,1)S(1)} %get-tuple-element.104), channel_id=1, source_target_pairs={{0,24},{8,16},{16,8},{24,0},{1,25},{9,17},{17,9},{25,1},{2,26},{10... | collective-permute-start | bytes 245768 | tf_op jit(solution)/shard_map/ppermute | solution.py:360
  25.8 0.0 copy-start
  25.8 0.0 copy-start.1
  25.8 2.6 %sweep.7 = (f32[4,512,256]{2,1,0:T(8,128)S(1)}, f32[4,512,256]{2,1,0:T(8,128)S(1)}, bf16[4,512,256]{2,1,0:T(8,128)(2,1)S(1)}, bf16[4,512,256]{2,1,0:T(8,128)(2,1...) custom-call(f32[40,512]{1,0:T(8,128)S(1)} %get-tuple-element.59.refs, ...), custom_call_target="tpu_custom_call", output_to_operand_aliasing={{0}: (7, {}), {1}: (8, {}), {2}: (9, {}), {3}: (10, {}), {4... | custom-call | tf_op jit(solution)/shard_map/sweep/pallas_call | solution.py:444
  28.4 0.0 collective-permute-done.7.refs_9_
  28.4 1.3 %collective-permute-done.8.refs_10_ = bf16[320,128]{1,0:T(8,128)(2,1)S(1)} collective-permute-done((bf16[320,128]{1,0:T(8,128)(2,1)S(1)}, bf16[320,128]{1,0:T(8,128)(2,1)S(1)}, u32[]{:S(2)}, u32[]{:S(2)}) %collective-permute-start.8) | collective-permute-done | bytes 81952 | tf_op jit(solution)/shard_map/ppermute | solution.py:360
  29.7 0.0 collective-permute-done.9.refs_11_
  29.7 0.0 copy-done
  29.7 0.0 copy-done.1
  29.8 1.9 %last.1 = (bf16[4,512,256]{2,1,0:T(8,128)(2,1)}, bf16[4,512,256]{2,1,0:T(8,128)(2,1)}, bf16[1,256,256]{2,1,0:T(8,128)(2,1)}, bf16[1,256,256]{2,1,0:T(8,128)(2,1)}) custom-call(f32[512,128]{1,0:T(8,128)S(1)} %get-tuple-element.62.refs_5_.refs_0_, bf16[4,512,256]{2,1,0:T(8,128)(2,1)S(1)} %get-tuple-element.98.refs_1_, ...), custom_call_target="tpu_custom_call" | custom-call | tf_op jit(solution)/shard_map/last/pallas_call | solution.py:493
  (1 shorter events, 0.0 us)
Async XLA Ops:
  3.1 7.5 %collective-permute-start = (bf16[336,128]{1,0:T(8,128)(2,1)S(1)}, bf16[336,128]{1,0:T(8,128)(2,1)S(1)}, u32[]{:S(2)}, u32[]{:S(2)}) collective-permute-start(bf16[336,128]{1,0:T(8,128)(2,1)S(1)} %get-tuple-element.66), channel_id=1, source_target_pairs={{0,24},{8,16},{16,8},{24,0},{1,25},{9,17},{17,9},{25,1},{2,26},{10... | collective-permute-start | bytes 258056 | tf_op jit(solution)/shard_map/ppermute | solution.py:360
  7.0 4.5 %collective-permute-start.1 = (bf16[336,128]{1,0:T(8,128)(2,1)S(1)}, bf16[336,128]{1,0:T(8,128)(2,1)S(1)}, u32[]{:S(2)}, u32[]{:S(2)}) collective-permute-start(bf16[336,128]{1,0:T(8,128)(2,1)S(1)} %get-tuple-element.67), channel_id=1, source_target_pairs={{0,16},{8,24},{16,0},{24,8},{1,17},{9,25},{17,1},{25,9},{2,18},{10... | collective-permute-start | bytes 258056 | tf_op jit(solution)/shard_map/ppermute | solution.py:360
  7.5 4.5 %collective-permute-start.2 = (bf16[336,128]{1,0:T(8,128)(2,1)S(1)}, bf16[336,128]{1,0:T(8,128)(2,1)S(1)}, u32[]{:S(2)}, u32[]{:S(2)}) collective-permute-start(bf16[336,128]{1,0:T(8,128)(2,1)S(1)} %get-tuple-element.68), channel_id=1, source_target_pairs={{0,8},{8,0},{16,24},{24,16},{1,9},{9,1},{17,25},{25,17},{2,10},{10... | collective-permute-start | bytes 258056 | tf_op jit(solution)/shard_map/ppermute | solution.py:360
  12.2 8.2 %collective-permute-start.3 = (bf16[192,128]{1,0:T(8,128)(2,1)S(1)}, bf16[192,128]{1,0:T(8,128)(2,1)S(1)}, u32[]{:S(2)}, u32[]{:S(2)}) collective-permute-start(bf16[192,128]{1,0:T(8,128)(2,1)S(1)} %get-tuple-element.71), channel_id=1, source_target_pairs={{0,2},{2,4},{4,6},{6,0},{1,3},{3,5},{5,7},{7,1},{8,10},{10,12},{12... | collective-permute-start | bytes 147464 | tf_op jit(solution)/shard_map/ppermute | solution.py:365
  13.9 6.6 %collective-permute-start.4 = (bf16[192,128]{1,0:T(8,128)(2,1)S(1)}, bf16[192,128]{1,0:T(8,128)(2,1)S(1)}, u32[]{:S(2)}, u32[]{:S(2)}) collective-permute-start(bf16[192,128]{1,0:T(8,128)(2,1)S(1)} %get-tuple-element.72), channel_id=1, source_target_pairs={{0,4},{2,6},{4,0},{6,2},{1,5},{3,7},{5,1},{7,3},{8,12},{10,14},{12... | collective-permute-start | bytes 147464 | tf_op jit(solution)/shard_map/ppermute | solution.py:365
  16.5 4.1 %collective-permute-start.5 = (bf16[192,128]{1,0:T(8,128)(2,1)S(1)}, bf16[192,128]{1,0:T(8,128)(2,1)S(1)}, u32[]{:S(2)}, u32[]{:S(2)}) collective-permute-start(bf16[192,128]{1,0:T(8,128)(2,1)S(1)} %get-tuple-element.73), channel_id=1, source_target_pairs={{0,6},{2,0},{4,2},{6,4},{1,7},{3,1},{5,3},{7,5},{8,14},{10,8},{12,... | collective-permute-start | bytes 147464 | tf_op jit(solution)/shard_map/ppermute | solution.py:365
  20.6 1.3 %collective-permute-start.6 = (bf16[320,128]{1,0:T(8,128)(2,1)S(1)}, bf16[320,128]{1,0:T(8,128)(2,1)S(1)}, u32[]{:S(2)}, u32[]{:S(2)}) collective-permute-start(bf16[320,128]{1,0:T(8,128)(2,1)S(1)} %get-tuple-element.83), channel_id=1, source_target_pairs={{0,1},{1,0},{2,3},{3,2},{4,5},{5,4},{6,7},{7,6},{8,9},{9,8},{10,11... | collective-permute-start | bytes 245768 | tf_op jit(solution)/shard_map/ppermute | solution.py:360
  22.2 6.2 %collective-permute-start.7 = (bf16[320,128]{1,0:T(8,128)(2,1)S(1)}, bf16[320,128]{1,0:T(8,128)(2,1)S(1)}, u32[]{:S(2)}, u32[]{:S(2)}) collective-permute-start(bf16[320,128]{1,0:T(8,128)(2,1)S(1)} %get-tuple-element.102), channel_id=1, source_target_pairs={{0,8},{8,0},{16,24},{24,16},{1,9},{9,1},{17,25},{25,17},{2,10},{10... | collective-permute-start | bytes 245768 | tf_op jit(solution)/shard_map/ppermute | solution.py:360
  23.5 6.2 %collective-permute-start.8 = (bf16[320,128]{1,0:T(8,128)(2,1)S(1)}, bf16[320,128]{1,0:T(8,128)(2,1)S(1)}, u32[]{:S(2)}, u32[]{:S(2)}) collective-permute-start(bf16[320,128]{1,0:T(8,128)(2,1)S(1)} %get-tuple-element.103), channel_id=1, source_target_pairs={{0,16},{8,24},{16,0},{24,8},{1,17},{9,25},{17,1},{25,9},{2,18},{10... | collective-permute-start | bytes 245768 | tf_op jit(solution)/shard_map/ppermute | solution.py:360
  24.3 5.4 %collective-permute-start.9 = (bf16[320,128]{1,0:T(8,128)(2,1)S(1)}, bf16[320,128]{1,0:T(8,128)(2,1)S(1)}, u32[]{:S(2)}, u32[]{:S(2)}) collective-permute-start(bf16[320,128]{1,0:T(8,128)(2,1)S(1)} %get-tuple-element.104), channel_id=1, source_target_pairs={{0,24},{8,16},{16,8},{24,0},{1,25},{9,17},{17,9},{25,1},{2,26},{10... | collective-permute-start | bytes 245768 | tf_op jit(solution)/shard_map/ppermute | solution.py:360
  25.8 4.0 %copy-start = (bf16[1,256,256]{2,1,0:T(8,128)(2,1)S(1)}, bf16[1,256,256]{2,1,0:T(8,128)(2,1)}, u32[]{:S(2)}) copy-start(bf16[1,256,256]{2,1,0:T(8,128)(2,1)} %refs_5_.3) | copy-start | bytes 393220
  25.8 4.0 %copy-start.1 = (bf16[1,256,256]{2,1,0:T(8,128)(2,1)S(1)}, bf16[1,256,256]{2,1,0:T(8,128)(2,1)}, u32[]{:S(2)}) copy-start(bf16[1,256,256]{2,1,0:T(8,128)(2,1)} %refs_6_.3) | copy-start | bytes 393220

commit v16 on v15

--- a/solution.py
+++ b/solution.py
@@ -113,8 +113,8 @@
     rows += [suffix, jnp.zeros((8 - H, slots), F32)]
     rows_ref[...] = jnp.concatenate(rows, axis=0)
 
-    copies[5].wait()
-    copies[6].wait()
+    for copy in copies[5:]:
+        copy.wait()
     turned = keys[0].T
     later = jnp.exp(suffix[:, :tokens])
     for h in range(H):
@@ -125,8 +125,6 @@
         both = mm(jnp.concatenate([high, low], axis=0), values[0, :, lanes])
         matrices[h] = both[:DH] + both[DH:]
         spread(h)
-    copies[7].wait()
-    copies[8].wait()
     for i in range(count):
         turned = q[i].T
         for h in range(H):
@@ -134,7 +132,6 @@
             scaled = (turned[lanes].astype(F32) * factors[i][h : h + 1]).astype(BF16)
             matrices[H * (1 + i) + h] = mm(scaled, c[i, :, lanes])
             spread(H * (1 + i) + h)
-    copies[9].wait()
     notes = [jnp.broadcast_to(x[h : h + 1].astype(F32), (1, DH)) for x in three_terms(total) for h in range(H)]
     notes += [jnp.full((1, DH), ids_ref[i].astype(F32)) for i in range(count)]
     notes.append(jnp.zeros((16 - len(notes), DH), F32))
@@ -340,8 +337,9 @@
             at = slice(t, t + HALF)
             out_buf[r, at, :] = (po_ref[r, at, :] + mm(q_ref[r, at, :], start[r])).astype(BF16)
             dq_buf[r, at, :] = (pdq_ref[r, at, :] + mm_nt(grad_ref[r, at, :], start[r])).astype(BF16)
-        send(out_buf.at[r], out_hbm.at[r])
-        send(dq_buf.at[r], dq_hbm.at[r])
+        for ready in ([r - 1] if r > 0 else []) + ([r] if r == count - 1 else []):
+            send(out_buf.at[ready], out_hbm.at[ready])
+            send(dq_buf.at[ready], dq_hbm.at[ready])
     factor = [
         jnp.exp(cols_ref[:tokens, 8 * count + h : 8 * count + h + 1] + later_ref[h : h + 1, 0:1]) for h in range(H)
     ]

time: 31.8 us -> 32 us (level)
  no operation moved by 1% of the time
where the time goes in v16:
time: 32 us; the launch traced here: 31.8 us
  Pallas kernels  14.1 us (44%)
  starting transfers between devices  13.8 us (43%)
  waiting for transfers between devices  3.19 us (10%)
  between operations  0.74 us (2%)
    ppermute x7, starting transfers between devices, exchange(): lax.ppermute(xs[k], axis, [(s, s ^ k) for s in range(n)])  8.24 us
    pallas_call x3, Pallas kernels, sweep(): pl.pallas_call(lambda *refs: sweep_kernel(units, done, *refs), out_shape=...  6.2 us
    ppermute x3, starting transfers between devices, exchange_ring(): lax.ppermute(xs[k], axis, [(s, (s + k) % n) for s in range(n)])  5.56 us
    ppermute x7, waiting for transfers between devices, exchange(): lax.ppermute(xs[k], axis, [(s, s ^ k) for s in range(n)])  3.07 us
    pallas_call x1, Pallas kernels, first_sweep(): pl.pallas_call(lambda *refs: sweep_kernel(units, (), *refs[:5], None, *re...  2.9 us
    pallas_call x1, Pallas kernels, shards(): pl.pallas_call(lambda *refs: first_kernel(n, *refs), out_shape=[shape((bl...  2.4 us
    pallas_call x1, Pallas kernels, shards(): pl.pallas_call(lambda *refs: last_kernel(n, responses, *refs), out_shape=...  2.05 us
  transfers between devices with their start and end apart: 10, of which 5 were waited for; matrix products, arithmetic and copies ran while one was open for 0% of the time, Pallas kernels for 29%

profile of v16, /device:TPU:0, one launch (start us, length us, event | category | flops | bytes accessed | tf_op | source)
XLA Modules:
  0.0 31.8 jit_solution(16195381577318124639)
XLA Ops:
  0.6 2.4 %first.1 = (bf16[336,128]{1,0:T(8,128)(2,1)S(1)}, bf16[336,128]{1,0:T(8,128)(2,1)S(1)}, bf16[336,128]{1,0:T(8,128)(2,1)S(1)}, bf16[336,128]{1,0:T(8,128)(2,1)S(1...) custom-call(s32[4]{0:T(128)} %refs_0_.1, s32[1,4]{1,0:T(1,128)} %refs_1_.1, ...), custom_call_target="tpu_custom_call" | custom-call | tf_op jit(solution)/shard_map/first/pallas_call | solution.py:396
  3.0 4.0 %collective-permute-start = (bf16[336,128]{1,0:T(8,128)(2,1)S(1)}, bf16[336,128]{1,0:T(8,128)(2,1)S(1)}, u32[]{:S(2)}, u32[]{:S(2)}) collective-permute-start(bf16[336,128]{1,0:T(8,128)(2,1)S(1)} %get-tuple-element.66), channel_id=1, source_target_pairs={{0,24},{8,16},{16,8},{24,0},{1,25},{9,17},{17,9},{25,1},{2,26},{10... | collective-permute-start | bytes 258056 | tf_op jit(solution)/shard_map/ppermute | solution.py:358
  7.0 0.5 %collective-permute-start.1 = (bf16[336,128]{1,0:T(8,128)(2,1)S(1)}, bf16[336,128]{1,0:T(8,128)(2,1)S(1)}, u32[]{:S(2)}, u32[]{:S(2)}) collective-permute-start(bf16[336,128]{1,0:T(8,128)(2,1)S(1)} %get-tuple-element.67), channel_id=1, source_target_pairs={{0,16},{8,24},{16,0},{24,8},{1,17},{9,25},{17,1},{25,9},{2,18},{10... | collective-permute-start | bytes 258056 | tf_op jit(solution)/shard_map/ppermute | solution.py:358
  7.5 0.1 collective-permute-start.2
  7.7 2.9 %sweep.4 = (f32[512,128]{1,0:T(8,128)S(1)}, bf16[4,512,256]{2,1,0:T(8,128)(2,1)S(1)}, bf16[4,512,256]{2,1,0:T(8,128)(2,1)S(1)}, f32[4,512,256]{2,1,0:T(8,128)S(1...) custom-call(f32[40,512]{1,0:T(8,128)S(1)} %get-tuple-element.59.refs, ...), custom_call_target="tpu_custom_call" | custom-call | tf_op jit(solution)/shard_map/sweep/pallas_call | solution.py:429
  10.6 0.0 collective-permute-done.refs_1_
  10.6 0.9 %collective-permute-done.1.refs_2_ = bf16[336,128]{1,0:T(8,128)(2,1)S(1)} collective-permute-done((bf16[336,128]{1,0:T(8,128)(2,1)S(1)}, bf16[336,128]{1,0:T(8,128)(2,1)S(1)}, u32[]{:S(2)}, u32[]{:S(2)}) %collective-permute-start.1) | collective-permute-done | bytes 86048 | tf_op jit(solution)/shard_map/ppermute | solution.py:358
  11.5 0.5 %collective-permute-done.2.refs_3_ = bf16[336,128]{1,0:T(8,128)(2,1)S(1)} collective-permute-done((bf16[336,128]{1,0:T(8,128)(2,1)S(1)}, bf16[336,128]{1,0:T(8,128)(2,1)S(1)}, u32[]{:S(2)}, u32[]{:S(2)}) %collective-permute-start.2) | collective-permute-done | bytes 86048 | tf_op jit(solution)/shard_map/ppermute | solution.py:358
  12.0 0.2 second.1
  12.2 1.6 %collective-permute-start.3 = (bf16[192,128]{1,0:T(8,128)(2,1)S(1)}, bf16[192,128]{1,0:T(8,128)(2,1)S(1)}, u32[]{:S(2)}, u32[]{:S(2)}) collective-permute-start(bf16[192,128]{1,0:T(8,128)(2,1)S(1)} %get-tuple-element.71), channel_id=1, source_target_pairs={{0,2},{2,4},{4,6},{6,0},{1,3},{3,5},{5,7},{7,1},{8,10},{10,12},{12... | collective-permute-start | bytes 147464 | tf_op jit(solution)/shard_map/ppermute | solution.py:363
  13.9 2.6 %collective-permute-start.4 = (bf16[192,128]{1,0:T(8,128)(2,1)S(1)}, bf16[192,128]{1,0:T(8,128)(2,1)S(1)}, u32[]{:S(2)}, u32[]{:S(2)}) collective-permute-start(bf16[192,128]{1,0:T(8,128)(2,1)S(1)} %get-tuple-element.72), channel_id=1, source_target_pairs={{0,4},{2,6},{4,0},{6,2},{1,5},{3,7},{5,1},{7,3},{8,12},{10,14},{12... | collective-permute-start | bytes 147464 | tf_op jit(solution)/shard_map/ppermute | solution.py:363
  16.5 1.3 %collective-permute-start.5 = (bf16[192,128]{1,0:T(8,128)(2,1)S(1)}, bf16[192,128]{1,0:T(8,128)(2,1)S(1)}, u32[]{:S(2)}, u32[]{:S(2)}) collective-permute-start(bf16[192,128]{1,0:T(8,128)(2,1)S(1)} %get-tuple-element.73), channel_id=1, source_target_pairs={{0,6},{2,0},{4,2},{6,4},{1,7},{3,1},{5,3},{7,5},{8,14},{10,8},{12,... | collective-permute-start | bytes 147464 | tf_op jit(solution)/shard_map/ppermute | solution.py:363
  17.8 2.6 %sweep.5 = (f32[4,512,256]{2,1,0:T(8,128)S(1)}, f32[4,512,256]{2,1,0:T(8,128)S(1)}, bf16[4,512,256]{2,1,0:T(8,128)(2,1)S(1)}, bf16[4,512,256]{2,1,0:T(8,128)(2,1...) custom-call(f32[40,512]{1,0:T(8,128)S(1)} %get-tuple-element.59.refs, ...), custom_call_target="tpu_custom_call", output_to_operand_aliasing={{0}: (7, {}), {1}: (8, {}), {2}: (9, {}), {3}: (10, {}), {4... | custom-call | tf_op jit(solution)/shard_map/sweep/pallas_call | solution.py:442
  20.4 0.0 collective-permute-done.3.refs_1_
  20.4 0.0 collective-permute-done.4.refs_2_
  20.4 0.1 collective-permute-done.5.refs_3_
  20.6 0.1 collective-permute-start.6
  20.7 1.0 %sweep.6 = (f32[4,512,256]{2,1,0:T(8,128)S(1)}, f32[4,512,256]{2,1,0:T(8,128)S(1)}, bf16[4,512,256]{2,1,0:T(8,128)(2,1)S(1)}, bf16[4,512,256]{2,1,0:T(8,128)(2,1...) custom-call(f32[40,512]{1,0:T(8,128)S(1)} %get-tuple-element.59.refs, ...), custom_call_target="tpu_custom_call", output_to_operand_aliasing={{0}: (7, {}), {1}: (8, {}), {2}: (9, {}), {3}: (10, {}), {4... | custom-call | tf_op jit(solution)/shard_map/sweep/pallas_call | solution.py:442
  21.6 0.3 collective-permute-done.6.refs_5_
  21.9 0.3 third.1
  22.2 1.4 %collective-permute-start.7 = (bf16[320,128]{1,0:T(8,128)(2,1)S(1)}, bf16[320,128]{1,0:T(8,128)(2,1)S(1)}, u32[]{:S(2)}, u32[]{:S(2)}) collective-permute-start(bf16[320,128]{1,0:T(8,128)(2,1)S(1)} %get-tuple-element.102), channel_id=1, source_target_pairs={{0,8},{8,0},{16,24},{24,16},{1,9},{9,1},{17,25},{25,17},{2,10},{10... | collective-permute-start | bytes 245768 | tf_op jit(solution)/shard_map/ppermute | solution.py:358
  23.6 0.8 %collective-permute-start.8 = (bf16[320,128]{1,0:T(8,128)(2,1)S(1)}, bf16[320,128]{1,0:T(8,128)(2,1)S(1)}, u32[]{:S(2)}, u32[]{:S(2)}) collective-permute-start(bf16[320,128]{1,0:T(8,128)(2,1)S(1)} %get-tuple-element.103), channel_id=1, source_target_pairs={{0,16},{8,24},{16,0},{24,8},{1,17},{9,25},{17,1},{25,9},{2,18},{10... | collective-permute-start | bytes 245768 | tf_op jit(solution)/shard_map/ppermute | solution.py:358
  24.3 1.4 %collective-permute-start.9 = (bf16[320,128]{1,0:T(8,128)(2,1)S(1)}, bf16[320,128]{1,0:T(8,128)(2,1)S(1)}, u32[]{:S(2)}, u32[]{:S(2)}) collective-permute-start(bf16[320,128]{1,0:T(8,128)(2,1)S(1)} %get-tuple-element.104), channel_id=1, source_target_pairs={{0,24},{8,16},{16,8},{24,0},{1,25},{9,17},{17,9},{25,1},{2,26},{10... | collective-permute-start | bytes 245768 | tf_op jit(solution)/shard_map/ppermute | solution.py:358
  25.8 0.0 copy-start
  25.8 0.0 copy-start.1
  25.8 2.6 %sweep.7 = (f32[4,512,256]{2,1,0:T(8,128)S(1)}, f32[4,512,256]{2,1,0:T(8,128)S(1)}, bf16[4,512,256]{2,1,0:T(8,128)(2,1)S(1)}, bf16[4,512,256]{2,1,0:T(8,128)(2,1...) custom-call(f32[40,512]{1,0:T(8,128)S(1)} %get-tuple-element.59.refs, ...), custom_call_target="tpu_custom_call", output_to_operand_aliasing={{0}: (7, {}), {1}: (8, {}), {2}: (9, {}), {3}: (10, {}), {4... | custom-call | tf_op jit(solution)/shard_map/sweep/pallas_call | solution.py:442
  28.4 0.0 collective-permute-done.7.refs_9_
  28.4 1.3 %collective-permute-done.8.refs_10_ = bf16[320,128]{1,0:T(8,128)(2,1)S(1)} collective-permute-done((bf16[320,128]{1,0:T(8,128)(2,1)S(1)}, bf16[320,128]{1,0:T(8,128)(2,1)S(1)}, u32[]{:S(2)}, u32[]{:S(2)}) %collective-permute-start.8) | collective-permute-done | bytes 81952 | tf_op jit(solution)/shard_map/ppermute | solution.py:358
  29.7 0.0 collective-permute-done.9.refs_11_
  29.8 0.0 copy-done
  29.8 0.0 copy-done.1
  29.8 2.0 %last.1 = (bf16[4,512,256]{2,1,0:T(8,128)(2,1)}, bf16[4,512,256]{2,1,0:T(8,128)(2,1)}, bf16[1,256,256]{2,1,0:T(8,128)(2,1)}, bf16[1,256,256]{2,1,0:T(8,128)(2,1)}) custom-call(f32[512,128]{1,0:T(8,128)S(1)} %get-tuple-element.62.refs_5_.refs_0_, bf16[4,512,256]{2,1,0:T(8,128)(2,1)S(1)} %get-tuple-element.98.refs_1_, ...), custom_call_target="tpu_custom_call" | custom-call | tf_op jit(solution)/shard_map/last/pallas_call | solution.py:491
  (1 shorter events, 0.0 us)
Async XLA Ops:
  3.0 7.5 %collective-permute-start = (bf16[336,128]{1,0:T(8,128)(2,1)S(1)}, bf16[336,128]{1,0:T(8,128)(2,1)S(1)}, u32[]{:S(2)}, u32[]{:S(2)}) collective-permute-start(bf16[336,128]{1,0:T(8,128)(2,1)S(1)} %get-tuple-element.66), channel_id=1, source_target_pairs={{0,24},{8,16},{16,8},{24,0},{1,25},{9,17},{17,9},{25,1},{2,26},{10... | collective-permute-start | bytes 258056 | tf_op jit(solution)/shard_map/ppermute | solution.py:358
  7.0 4.5 %collective-permute-start.1 = (bf16[336,128]{1,0:T(8,128)(2,1)S(1)}, bf16[336,128]{1,0:T(8,128)(2,1)S(1)}, u32[]{:S(2)}, u32[]{:S(2)}) collective-permute-start(bf16[336,128]{1,0:T(8,128)(2,1)S(1)} %get-tuple-element.67), channel_id=1, source_target_pairs={{0,16},{8,24},{16,0},{24,8},{1,17},{9,25},{17,1},{25,9},{2,18},{10... | collective-permute-start | bytes 258056 | tf_op jit(solution)/shard_map/ppermute | solution.py:358
  7.5 4.5 %collective-permute-start.2 = (bf16[336,128]{1,0:T(8,128)(2,1)S(1)}, bf16[336,128]{1,0:T(8,128)(2,1)S(1)}, u32[]{:S(2)}, u32[]{:S(2)}) collective-permute-start(bf16[336,128]{1,0:T(8,128)(2,1)S(1)} %get-tuple-element.68), channel_id=1, source_target_pairs={{0,8},{8,0},{16,24},{24,16},{1,9},{9,1},{17,25},{25,17},{2,10},{10... | collective-permute-start | bytes 258056 | tf_op jit(solution)/shard_map/ppermute | solution.py:358
  12.2 8.2 %collective-permute-start.3 = (bf16[192,128]{1,0:T(8,128)(2,1)S(1)}, bf16[192,128]{1,0:T(8,128)(2,1)S(1)}, u32[]{:S(2)}, u32[]{:S(2)}) collective-permute-start(bf16[192,128]{1,0:T(8,128)(2,1)S(1)} %get-tuple-element.71), channel_id=1, source_target_pairs={{0,2},{2,4},{4,6},{6,0},{1,3},{3,5},{5,7},{7,1},{8,10},{10,12},{12... | collective-permute-start | bytes 147464 | tf_op jit(solution)/shard_map/ppermute | solution.py:363
  13.9 6.6 %collective-permute-start.4 = (bf16[192,128]{1,0:T(8,128)(2,1)S(1)}, bf16[192,128]{1,0:T(8,128)(2,1)S(1)}, u32[]{:S(2)}, u32[]{:S(2)}) collective-permute-start(bf16[192,128]{1,0:T(8,128)(2,1)S(1)} %get-tuple-element.72), channel_id=1, source_target_pairs={{0,4},{2,6},{4,0},{6,2},{1,5},{3,7},{5,1},{7,3},{8,12},{10,14},{12... | collective-permute-start | bytes 147464 | tf_op jit(solution)/shard_map/ppermute | solution.py:363
  16.5 4.1 %collective-permute-start.5 = (bf16[192,128]{1,0:T(8,128)(2,1)S(1)}, bf16[192,128]{1,0:T(8,128)(2,1)S(1)}, u32[]{:S(2)}, u32[]{:S(2)}) collective-permute-start(bf16[192,128]{1,0:T(8,128)(2,1)S(1)} %get-tuple-element.73), channel_id=1, source_target_pairs={{0,6},{2,0},{4,2},{6,4},{1,7},{3,1},{5,3},{7,5},{8,14},{10,8},{12,... | collective-permute-start | bytes 147464 | tf_op jit(solution)/shard_map/ppermute | solution.py:363
  20.6 1.3 %collective-permute-start.6 = (bf16[320,128]{1,0:T(8,128)(2,1)S(1)}, bf16[320,128]{1,0:T(8,128)(2,1)S(1)}, u32[]{:S(2)}, u32[]{:S(2)}) collective-permute-start(bf16[320,128]{1,0:T(8,128)(2,1)S(1)} %get-tuple-element.83), channel_id=1, source_target_pairs={{0,1},{1,0},{2,3},{3,2},{4,5},{5,4},{6,7},{7,6},{8,9},{9,8},{10,11... | collective-permute-start | bytes 245768 | tf_op jit(solution)/shard_map/ppermute | solution.py:358
  22.2 6.2 %collective-permute-start.7 = (bf16[320,128]{1,0:T(8,128)(2,1)S(1)}, bf16[320,128]{1,0:T(8,128)(2,1)S(1)}, u32[]{:S(2)}, u32[]{:S(2)}) collective-permute-start(bf16[320,128]{1,0:T(8,128)(2,1)S(1)} %get-tuple-element.102), channel_id=1, source_target_pairs={{0,8},{8,0},{16,24},{24,16},{1,9},{9,1},{17,25},{25,17},{2,10},{10... | collective-permute-start | bytes 245768 | tf_op jit(solution)/shard_map/ppermute | solution.py:358
  23.6 6.2 %collective-permute-start.8 = (bf16[320,128]{1,0:T(8,128)(2,1)S(1)}, bf16[320,128]{1,0:T(8,128)(2,1)S(1)}, u32[]{:S(2)}, u32[]{:S(2)}) collective-permute-start(bf16[320,128]{1,0:T(8,128)(2,1)S(1)} %get-tuple-element.103), channel_id=1, source_target_pairs={{0,16},{8,24},{16,0},{24,8},{1,17},{9,25},{17,1},{25,9},{2,18},{10... | collective-permute-start | bytes 245768 | tf_op jit(solution)/shard_map/ppermute | solution.py:358
  24.3 5.4 %collective-permute-start.9 = (bf16[320,128]{1,0:T(8,128)(2,1)S(1)}, bf16[320,128]{1,0:T(8,128)(2,1)S(1)}, u32[]{:S(2)}, u32[]{:S(2)}) collective-permute-start(bf16[320,128]{1,0:T(8,128)(2,1)S(1)} %get-tuple-element.104), channel_id=1, source_target_pairs={{0,24},{8,16},{16,8},{24,0},{1,25},{9,17},{17,9},{25,1},{2,26},{10... | collective-permute-start | bytes 245768 | tf_op jit(solution)/shard_map/ppermute | solution.py:358
  25.8 4.0 %copy-start = (bf16[1,256,256]{2,1,0:T(8,128)(2,1)S(1)}, bf16[1,256,256]{2,1,0:T(8,128)(2,1)}, u32[]{:S(2)}) copy-start(bf16[1,256,256]{2,1,0:T(8,128)(2,1)} %refs_5_.3) | copy-start | bytes 393220
  25.8 4.0 %copy-start.1 = (bf16[1,256,256]{2,1,0:T(8,128)(2,1)S(1)}, bf16[1,256,256]{2,1,0:T(8,128)(2,1)}, u32[]{:S(2)}) copy-start(bf16[1,256,256]{2,1,0:T(8,128)(2,1)} %refs_6_.3) | copy-start | bytes 393220

commit v17 on v15

--- a/solution.py
+++ b/solution.py
@@ -339,9 +339,9 @@
         for t in range(0, slots, HALF):
             at = slice(t, t + HALF)
             out_buf[r, at, :] = (po_ref[r, at, :] + mm(q_ref[r, at, :], start[r])).astype(BF16)
+            send(out_buf.at[r, at], out_hbm.at[r, at])
             dq_buf[r, at, :] = (pdq_ref[r, at, :] + mm_nt(grad_ref[r, at, :], start[r])).astype(BF16)
-        send(out_buf.at[r], out_hbm.at[r])
-        send(dq_buf.at[r], dq_hbm.at[r])
+            send(dq_buf.at[r, at], dq_hbm.at[r, at])
     factor = [
         jnp.exp(cols_ref[:tokens, 8 * count + h : 8 * count + h + 1] + later_ref[h : h + 1, 0:1]) for h in range(H)
     ]
@@ -501,7 +501,7 @@
             pltpu.VMEM(queries.shape, BF16),
             pltpu.VMEM(keys.shape[1:], BF16),
             pltpu.VMEM(keys.shape[1:], BF16),
-            pltpu.SemaphoreType.DMA((2 + 2 * responses,)),
+            pltpu.SemaphoreType.DMA((2 + 2 * responses * (slots // HALF),)),
         ],
         compiler_params=params(),
         name="last",

time: 31.8 us -> 31.8 us (level)
  no operation moved by 1% of the time
where the time goes in v17:
time: 31.8 us; the launch traced here: 31.6 us
  Pallas kernels  13.9 us (44%)
  starting transfers between devices  13.8 us (43%)
  waiting for transfers between devices  3.17 us (10%)
  between operations  0.74 us (2%)
    ppermute x7, starting transfers between devices, exchange(): lax.ppermute(xs[k], axis, [(s, s ^ k) for s in range(n)])  8.22 us
    pallas_call x3, Pallas kernels, sweep(): pl.pallas_call(lambda *refs: sweep_kernel(units, done, *refs), out_shape=...  6.2 us
    ppermute x3, starting transfers between devices, exchange_ring(): lax.ppermute(xs[k], axis, [(s, (s + k) % n) for s in range(n)])  5.57 us
    ppermute x7, waiting for transfers between devices, exchange(): lax.ppermute(xs[k], axis, [(s, s ^ k) for s in range(n)])  3.05 us
    pallas_call x1, Pallas kernels, first_sweep(): pl.pallas_call(lambda *refs: sweep_kernel(units, (), *refs[:5], None, *re...  2.89 us
    pallas_call x1, Pallas kernels, shards(): pl.pallas_call(lambda *refs: first_kernel(n, *refs), out_shape=[shape((bl...  2.41 us
    pallas_call x1, Pallas kernels, shards(): pl.pallas_call(lambda *refs: last_kernel(n, responses, *refs), out_shape=...  1.87 us
  transfers between devices with their start and end apart: 10, of which 5 were waited for; matrix products, arithmetic and copies ran while one was open for 0% of the time, Pallas kernels for 29%

profile of v17, /device:TPU:0, one launch (start us, length us, event | category | flops | bytes accessed | tf_op | source)
XLA Modules:
  0.0 31.6 jit_solution(3153219950304589898)
XLA Ops:
  0.6 2.4 %first.1 = (bf16[336,128]{1,0:T(8,128)(2,1)S(1)}, bf16[336,128]{1,0:T(8,128)(2,1)S(1)}, bf16[336,128]{1,0:T(8,128)(2,1)S(1)}, bf16[336,128]{1,0:T(8,128)(2,1)S(1...) custom-call(s32[4]{0:T(128)} %refs_0_.1, s32[1,4]{1,0:T(1,128)} %refs_1_.1, ...), custom_call_target="tpu_custom_call" | custom-call | tf_op jit(solution)/shard_map/first/pallas_call | solution.py:398
  3.1 4.0 %collective-permute-start = (bf16[336,128]{1,0:T(8,128)(2,1)S(1)}, bf16[336,128]{1,0:T(8,128)(2,1)S(1)}, u32[]{:S(2)}, u32[]{:S(2)}) collective-permute-start(bf16[336,128]{1,0:T(8,128)(2,1)S(1)} %get-tuple-element.66), channel_id=1, source_target_pairs={{0,24},{8,16},{16,8},{24,0},{1,25},{9,17},{17,9},{25,1},{2,26},{10... | collective-permute-start | bytes 258056 | tf_op jit(solution)/shard_map/ppermute | solution.py:360
  7.0 0.5 %collective-permute-start.1 = (bf16[336,128]{1,0:T(8,128)(2,1)S(1)}, bf16[336,128]{1,0:T(8,128)(2,1)S(1)}, u32[]{:S(2)}, u32[]{:S(2)}) collective-permute-start(bf16[336,128]{1,0:T(8,128)(2,1)S(1)} %get-tuple-element.67), channel_id=1, source_target_pairs={{0,16},{8,24},{16,0},{24,8},{1,17},{9,25},{17,1},{25,9},{2,18},{10... | collective-permute-start | bytes 258056 | tf_op jit(solution)/shard_map/ppermute | solution.py:360
  7.5 0.1 collective-permute-start.2
  7.7 2.9 %sweep.4 = (f32[512,128]{1,0:T(8,128)S(1)}, bf16[4,512,256]{2,1,0:T(8,128)(2,1)S(1)}, bf16[4,512,256]{2,1,0:T(8,128)(2,1)S(1)}, f32[4,512,256]{2,1,0:T(8,128)S(1...) custom-call(f32[40,512]{1,0:T(8,128)S(1)} %get-tuple-element.59.refs, ...), custom_call_target="tpu_custom_call" | custom-call | tf_op jit(solution)/shard_map/sweep/pallas_call | solution.py:431
  10.6 0.0 collective-permute-done.refs_1_
  10.6 0.9 %collective-permute-done.1.refs_2_ = bf16[336,128]{1,0:T(8,128)(2,1)S(1)} collective-permute-done((bf16[336,128]{1,0:T(8,128)(2,1)S(1)}, bf16[336,128]{1,0:T(8,128)(2,1)S(1)}, u32[]{:S(2)}, u32[]{:S(2)}) %collective-permute-start.1) | collective-permute-done | bytes 86048 | tf_op jit(solution)/shard_map/ppermute | solution.py:360
  11.5 0.5 %collective-permute-done.2.refs_3_ = bf16[336,128]{1,0:T(8,128)(2,1)S(1)} collective-permute-done((bf16[336,128]{1,0:T(8,128)(2,1)S(1)}, bf16[336,128]{1,0:T(8,128)(2,1)S(1)}, u32[]{:S(2)}, u32[]{:S(2)}) %collective-permute-start.2) | collective-permute-done | bytes 86048 | tf_op jit(solution)/shard_map/ppermute | solution.py:360
  12.0 0.2 second.1
  12.2 1.6 %collective-permute-start.3 = (bf16[192,128]{1,0:T(8,128)(2,1)S(1)}, bf16[192,128]{1,0:T(8,128)(2,1)S(1)}, u32[]{:S(2)}, u32[]{:S(2)}) collective-permute-start(bf16[192,128]{1,0:T(8,128)(2,1)S(1)} %get-tuple-element.71), channel_id=1, source_target_pairs={{0,2},{2,4},{4,6},{6,0},{1,3},{3,5},{5,7},{7,1},{8,10},{10,12},{12... | collective-permute-start | bytes 147464 | tf_op jit(solution)/shard_map/ppermute | solution.py:365
  13.9 2.6 %collective-permute-start.4 = (bf16[192,128]{1,0:T(8,128)(2,1)S(1)}, bf16[192,128]{1,0:T(8,128)(2,1)S(1)}, u32[]{:S(2)}, u32[]{:S(2)}) collective-permute-start(bf16[192,128]{1,0:T(8,128)(2,1)S(1)} %get-tuple-element.72), channel_id=1, source_target_pairs={{0,4},{2,6},{4,0},{6,2},{1,5},{3,7},{5,1},{7,3},{8,12},{10,14},{12... | collective-permute-start | bytes 147464 | tf_op jit(solution)/shard_map/ppermute | solution.py:365
  16.5 1.3 %collective-permute-start.5 = (bf16[192,128]{1,0:T(8,128)(2,1)S(1)}, bf16[192,128]{1,0:T(8,128)(2,1)S(1)}, u32[]{:S(2)}, u32[]{:S(2)}) collective-permute-start(bf16[192,128]{1,0:T(8,128)(2,1)S(1)} %get-tuple-element.73), channel_id=1, source_target_pairs={{0,6},{2,0},{4,2},{6,4},{1,7},{3,1},{5,3},{7,5},{8,14},{10,8},{12,... | collective-permute-start | bytes 147464 | tf_op jit(solution)/shard_map/ppermute | solution.py:365
  17.8 2.6 %sweep.5 = (f32[4,512,256]{2,1,0:T(8,128)S(1)}, f32[4,512,256]{2,1,0:T(8,128)S(1)}, bf16[4,512,256]{2,1,0:T(8,128)(2,1)S(1)}, bf16[4,512,256]{2,1,0:T(8,128)(2,1...) custom-call(f32[40,512]{1,0:T(8,128)S(1)} %get-tuple-element.59.refs, ...), custom_call_target="tpu_custom_call", output_to_operand_aliasing={{0}: (7, {}), {1}: (8, {}), {2}: (9, {}), {3}: (10, {}), {4... | custom-call | tf_op jit(solution)/shard_map/sweep/pallas_call | solution.py:444
  20.4 0.0 collective-permute-done.3.refs_1_
  20.4 0.0 collective-permute-done.4.refs_2_
  20.4 0.1 collective-permute-done.5.refs_3_
  20.6 0.1 collective-permute-start.6
  20.7 1.0 %sweep.6 = (f32[4,512,256]{2,1,0:T(8,128)S(1)}, f32[4,512,256]{2,1,0:T(8,128)S(1)}, bf16[4,512,256]{2,1,0:T(8,128)(2,1)S(1)}, bf16[4,512,256]{2,1,0:T(8,128)(2,1...) custom-call(f32[40,512]{1,0:T(8,128)S(1)} %get-tuple-element.59.refs, ...), custom_call_target="tpu_custom_call", output_to_operand_aliasing={{0}: (7, {}), {1}: (8, {}), {2}: (9, {}), {3}: (10, {}), {4... | custom-call | tf_op jit(solution)/shard_map/sweep/pallas_call | solution.py:444
  21.7 0.3 collective-permute-done.6.refs_5_
  21.9 0.3 third.1
  22.2 1.3 %collective-permute-start.7 = (bf16[320,128]{1,0:T(8,128)(2,1)S(1)}, bf16[320,128]{1,0:T(8,128)(2,1)S(1)}, u32[]{:S(2)}, u32[]{:S(2)}) collective-permute-start(bf16[320,128]{1,0:T(8,128)(2,1)S(1)} %get-tuple-element.102), channel_id=1, source_target_pairs={{0,8},{8,0},{16,24},{24,16},{1,9},{9,1},{17,25},{25,17},{2,10},{10... | collective-permute-start | bytes 245768 | tf_op jit(solution)/shard_map/ppermute | solution.py:360
  23.5 0.8 %collective-permute-start.8 = (bf16[320,128]{1,0:T(8,128)(2,1)S(1)}, bf16[320,128]{1,0:T(8,128)(2,1)S(1)}, u32[]{:S(2)}, u32[]{:S(2)}) collective-permute-start(bf16[320,128]{1,0:T(8,128)(2,1)S(1)} %get-tuple-element.103), channel_id=1, source_target_pairs={{0,16},{8,24},{16,0},{24,8},{1,17},{9,25},{17,1},{25,9},{2,18},{10... | collective-permute-start | bytes 245768 | tf_op jit(solution)/shard_map/ppermute | solution.py:360
  24.3 1.4 %collective-permute-start.9 = (bf16[320,128]{1,0:T(8,128)(2,1)S(1)}, bf16[320,128]{1,0:T(8,128)(2,1)S(1)}, u32[]{:S(2)}, u32[]{:S(2)}) collective-permute-start(bf16[320,128]{1,0:T(8,128)(2,1)S(1)} %get-tuple-element.104), channel_id=1, source_target_pairs={{0,24},{8,16},{16,8},{24,0},{1,25},{9,17},{17,9},{25,1},{2,26},{10... | collective-permute-start | bytes 245768 | tf_op jit(solution)/shard_map/ppermute | solution.py:360
  25.8 0.0 copy-start
  25.8 0.0 copy-start.1
  25.8 2.6 %sweep.7 = (f32[4,512,256]{2,1,0:T(8,128)S(1)}, f32[4,512,256]{2,1,0:T(8,128)S(1)}, bf16[4,512,256]{2,1,0:T(8,128)(2,1)S(1)}, bf16[4,512,256]{2,1,0:T(8,128)(2,1...) custom-call(f32[40,512]{1,0:T(8,128)S(1)} %get-tuple-element.59.refs, ...), custom_call_target="tpu_custom_call", output_to_operand_aliasing={{0}: (7, {}), {1}: (8, {}), {2}: (9, {}), {3}: (10, {}), {4... | custom-call | tf_op jit(solution)/shard_map/sweep/pallas_call | solution.py:444
  28.4 0.0 collective-permute-done.7.refs_9_
  28.4 1.3 %collective-permute-done.8.refs_10_ = bf16[320,128]{1,0:T(8,128)(2,1)S(1)} collective-permute-done((bf16[320,128]{1,0:T(8,128)(2,1)S(1)}, bf16[320,128]{1,0:T(8,128)(2,1)S(1)}, u32[]{:S(2)}, u32[]{:S(2)}) %collective-permute-start.8) | collective-permute-done | bytes 81952 | tf_op jit(solution)/shard_map/ppermute | solution.py:360
  29.7 0.0 collective-permute-done.9.refs_11_
  29.7 0.0 copy-done
  29.7 0.0 copy-done.1
  29.7 1.9 %last.1 = (bf16[4,512,256]{2,1,0:T(8,128)(2,1)}, bf16[4,512,256]{2,1,0:T(8,128)(2,1)}, bf16[1,256,256]{2,1,0:T(8,128)(2,1)}, bf16[1,256,256]{2,1,0:T(8,128)(2,1)}) custom-call(f32[512,128]{1,0:T(8,128)S(1)} %get-tuple-element.62.refs_5_.refs_0_, bf16[4,512,256]{2,1,0:T(8,128)(2,1)S(1)} %get-tuple-element.98.refs_1_, ...), custom_call_target="tpu_custom_call" | custom-call | tf_op jit(solution)/shard_map/last/pallas_call | solution.py:493
  (1 shorter events, 0.0 us)
Async XLA Ops:
  3.1 7.5 %collective-permute-start = (bf16[336,128]{1,0:T(8,128)(2,1)S(1)}, bf16[336,128]{1,0:T(8,128)(2,1)S(1)}, u32[]{:S(2)}, u32[]{:S(2)}) collective-permute-start(bf16[336,128]{1,0:T(8,128)(2,1)S(1)} %get-tuple-element.66), channel_id=1, source_target_pairs={{0,24},{8,16},{16,8},{24,0},{1,25},{9,17},{17,9},{25,1},{2,26},{10... | collective-permute-start | bytes 258056 | tf_op jit(solution)/shard_map/ppermute | solution.py:360
  7.0 4.5 %collective-permute-start.1 = (bf16[336,128]{1,0:T(8,128)(2,1)S(1)}, bf16[336,128]{1,0:T(8,128)(2,1)S(1)}, u32[]{:S(2)}, u32[]{:S(2)}) collective-permute-start(bf16[336,128]{1,0:T(8,128)(2,1)S(1)} %get-tuple-element.67), channel_id=1, source_target_pairs={{0,16},{8,24},{16,0},{24,8},{1,17},{9,25},{17,1},{25,9},{2,18},{10... | collective-permute-start | bytes 258056 | tf_op jit(solution)/shard_map/ppermute | solution.py:360
  7.5 4.5 %collective-permute-start.2 = (bf16[336,128]{1,0:T(8,128)(2,1)S(1)}, bf16[336,128]{1,0:T(8,128)(2,1)S(1)}, u32[]{:S(2)}, u32[]{:S(2)}) collective-permute-start(bf16[336,128]{1,0:T(8,128)(2,1)S(1)} %get-tuple-element.68), channel_id=1, source_target_pairs={{0,8},{8,0},{16,24},{24,16},{1,9},{9,1},{17,25},{25,17},{2,10},{10... | collective-permute-start | bytes 258056 | tf_op jit(solution)/shard_map/ppermute | solution.py:360
  12.2 8.2 %collective-permute-start.3 = (bf16[192,128]{1,0:T(8,128)(2,1)S(1)}, bf16[192,128]{1,0:T(8,128)(2,1)S(1)}, u32[]{:S(2)}, u32[]{:S(2)}) collective-permute-start(bf16[192,128]{1,0:T(8,128)(2,1)S(1)} %get-tuple-element.71), channel_id=1, source_target_pairs={{0,2},{2,4},{4,6},{6,0},{1,3},{3,5},{5,7},{7,1},{8,10},{10,12},{12... | collective-permute-start | bytes 147464 | tf_op jit(solution)/shard_map/ppermute | solution.py:365
  13.9 6.5 %collective-permute-start.4 = (bf16[192,128]{1,0:T(8,128)(2,1)S(1)}, bf16[192,128]{1,0:T(8,128)(2,1)S(1)}, u32[]{:S(2)}, u32[]{:S(2)}) collective-permute-start(bf16[192,128]{1,0:T(8,128)(2,1)S(1)} %get-tuple-element.72), channel_id=1, source_target_pairs={{0,4},{2,6},{4,0},{6,2},{1,5},{3,7},{5,1},{7,3},{8,12},{10,14},{12... | collective-permute-start | bytes 147464 | tf_op jit(solution)/shard_map/ppermute | solution.py:365
  16.5 4.1 %collective-permute-start.5 = (bf16[192,128]{1,0:T(8,128)(2,1)S(1)}, bf16[192,128]{1,0:T(8,128)(2,1)S(1)}, u32[]{:S(2)}, u32[]{:S(2)}) collective-permute-start(bf16[192,128]{1,0:T(8,128)(2,1)S(1)} %get-tuple-element.73), channel_id=1, source_target_pairs={{0,6},{2,0},{4,2},{6,4},{1,7},{3,1},{5,3},{7,5},{8,14},{10,8},{12,... | collective-permute-start | bytes 147464 | tf_op jit(solution)/shard_map/ppermute | solution.py:365
  20.6 1.3 %collective-permute-start.6 = (bf16[320,128]{1,0:T(8,128)(2,1)S(1)}, bf16[320,128]{1,0:T(8,128)(2,1)S(1)}, u32[]{:S(2)}, u32[]{:S(2)}) collective-permute-start(bf16[320,128]{1,0:T(8,128)(2,1)S(1)} %get-tuple-element.83), channel_id=1, source_target_pairs={{0,1},{1,0},{2,3},{3,2},{4,5},{5,4},{6,7},{7,6},{8,9},{9,8},{10,11... | collective-permute-start | bytes 245768 | tf_op jit(solution)/shard_map/ppermute | solution.py:360
  22.2 6.2 %collective-permute-start.7 = (bf16[320,128]{1,0:T(8,128)(2,1)S(1)}, bf16[320,128]{1,0:T(8,128)(2,1)S(1)}, u32[]{:S(2)}, u32[]{:S(2)}) collective-permute-start(bf16[320,128]{1,0:T(8,128)(2,1)S(1)} %get-tuple-element.102), channel_id=1, source_target_pairs={{0,8},{8,0},{16,24},{24,16},{1,9},{9,1},{17,25},{25,17},{2,10},{10... | collective-permute-start | bytes 245768 | tf_op jit(solution)/shard_map/ppermute | solution.py:360
  23.5 6.2 %collective-permute-start.8 = (bf16[320,128]{1,0:T(8,128)(2,1)S(1)}, bf16[320,128]{1,0:T(8,128)(2,1)S(1)}, u32[]{:S(2)}, u32[]{:S(2)}) collective-permute-start(bf16[320,128]{1,0:T(8,128)(2,1)S(1)} %get-tuple-element.103), channel_id=1, source_target_pairs={{0,16},{8,24},{16,0},{24,8},{1,17},{9,25},{17,1},{25,9},{2,18},{10... | collective-permute-start | bytes 245768 | tf_op jit(solution)/shard_map/ppermute | solution.py:360
  24.3 5.4 %collective-permute-start.9 = (bf16[320,128]{1,0:T(8,128)(2,1)S(1)}, bf16[320,128]{1,0:T(8,128)(2,1)S(1)}, u32[]{:S(2)}, u32[]{:S(2)}) collective-permute-start(bf16[320,128]{1,0:T(8,128)(2,1)S(1)} %get-tuple-element.104), channel_id=1, source_target_pairs={{0,24},{8,16},{16,8},{24,0},{1,25},{9,17},{17,9},{25,1},{2,26},{10... | collective-permute-start | bytes 245768 | tf_op jit(solution)/shard_map/ppermute | solution.py:360
  25.8 4.0 %copy-start = (bf16[1,256,256]{2,1,0:T(8,128)(2,1)S(1)}, bf16[1,256,256]{2,1,0:T(8,128)(2,1)}, u32[]{:S(2)}) copy-start(bf16[1,256,256]{2,1,0:T(8,128)(2,1)} %refs_5_.3) | copy-start | bytes 393220
  25.8 4.0 %copy-start.1 = (bf16[1,256,256]{2,1,0:T(8,128)(2,1)S(1)}, bf16[1,256,256]{2,1,0:T(8,128)(2,1)}, u32[]{:S(2)}) copy-start(bf16[1,256,256]{2,1,0:T(8,128)(2,1)} %refs_6_.3) | copy-start | bytes 393220

commit v18 on v15

--- a/solution.py
+++ b/solution.py
@@ -477,7 +477,6 @@
         name="swap",
     )(*got2, token)
     swapped = exchange([kept, sent], "core")[1]
-    held, token = sweep(units[5:6], held, kept)
     msgs = pl.pallas_call(
         lambda *refs: third_kernel(n, chips, *refs),
         out_shape=[shape(((responses + 1) * block, DH), BF16)] * n,
@@ -487,7 +486,7 @@
         name="third",
     )(*got1, kept, swapped, token)
     got3 = exchange(msgs, "prompt")
-    held, token = sweep(units[6:], held, msgs[0], range(responses - 1))
+    held, token = sweep(units[5:], held, msgs[0], range(responses - 2))
     partial_out, partial_dq, query, grad_out, resp_dk, resp_dv = held
 
     resp_out, resp_dq, prompt_dk, prompt_dv = pl.pallas_call(

time: 31.8 us -> 31.8 us (level)
    pallas_call x3 -> x2, Pallas kernels: 6.2 us -> 6.08 us  [sweep(): pl.pallas_call(lambda *refs: sweep_kernel(units, done, *refs), out_shape=...]
  transfers between devices with their start and end apart: 10 -> 10, of which waited for: 5 -> 5; matrix products, arithmetic and copies ran while one was open for 0% -> 0% of each run, Pallas kernels for 29% -> 28%
where the time goes in v18:
time: 31.8 us; the launch traced here: 31.6 us
  Pallas kernels  13.8 us (43%)
  starting transfers between devices  13.8 us (43%)
  waiting for transfers between devices  3.3 us (10%)
  between operations  0.73 us (2%)
    ppermute x7, starting transfers between devices, exchange(): lax.ppermute(xs[k], axis, [(s, s ^ k) for s in range(n)])  8.22 us
    pallas_call x2, Pallas kernels, sweep(): pl.pallas_call(lambda *refs: sweep_kernel(units, done, *refs), out_shape=...  6.08 us
    ppermute x3, starting transfers between devices, exchange_ring(): lax.ppermute(xs[k], axis, [(s, (s + k) % n) for s in range(n)])  5.57 us
    ppermute x7, waiting for transfers between devices, exchange(): lax.ppermute(xs[k], axis, [(s, s ^ k) for s in range(n)])  3.18 us
    pallas_call x1, Pallas kernels, first_sweep(): pl.pallas_call(lambda *refs: sweep_kernel(units, (), *refs[:5], None, *re...  2.89 us
    pallas_call x1, Pallas kernels, shards(): pl.pallas_call(lambda *refs: first_kernel(n, *refs), out_shape=[shape((bl...  2.41 us
    pallas_call x1, Pallas kernels, shards(): pl.pallas_call(lambda *refs: last_kernel(n, responses, *refs), out_shape=...  1.88 us
  transfers between devices with their start and end apart: 10, of which 5 were waited for; matrix products, arithmetic and copies ran while one was open for 0% of the time, Pallas kernels for 28%

profile of v18, /device:TPU:0, one launch (start us, length us, event | category | flops | bytes accessed | tf_op | source)
XLA Modules:
  0.0 31.6 jit_solution(6188275894696057637)
XLA Ops:
  0.6 2.4 %first.1 = (bf16[336,128]{1,0:T(8,128)(2,1)S(1)}, bf16[336,128]{1,0:T(8,128)(2,1)S(1)}, bf16[336,128]{1,0:T(8,128)(2,1)S(1)}, bf16[336,128]{1,0:T(8,128)(2,1)S(1...) custom-call(s32[4]{0:T(128)} %refs_0_.1, s32[1,4]{1,0:T(1,128)} %refs_1_.1, ...), custom_call_target="tpu_custom_call" | custom-call | tf_op jit(solution)/shard_map/first/pallas_call | solution.py:398
  3.1 4.0 %collective-permute-start = (bf16[336,128]{1,0:T(8,128)(2,1)S(1)}, bf16[336,128]{1,0:T(8,128)(2,1)S(1)}, u32[]{:S(2)}, u32[]{:S(2)}) collective-permute-start(bf16[336,128]{1,0:T(8,128)(2,1)S(1)} %get-tuple-element.59), channel_id=1, source_target_pairs={{0,24},{8,16},{16,8},{24,0},{1,25},{9,17},{17,9},{25,1},{2,26},{10... | collective-permute-start | bytes 258056 | tf_op jit(solution)/shard_map/ppermute | solution.py:360
  7.0 0.5 %collective-permute-start.1 = (bf16[336,128]{1,0:T(8,128)(2,1)S(1)}, bf16[336,128]{1,0:T(8,128)(2,1)S(1)}, u32[]{:S(2)}, u32[]{:S(2)}) collective-permute-start(bf16[336,128]{1,0:T(8,128)(2,1)S(1)} %get-tuple-element.60), channel_id=1, source_target_pairs={{0,16},{8,24},{16,0},{24,8},{1,17},{9,25},{17,1},{25,9},{2,18},{10... | collective-permute-start | bytes 258056 | tf_op jit(solution)/shard_map/ppermute | solution.py:360
  7.5 0.1 collective-permute-start.2
  7.7 2.9 %sweep.3 = (f32[512,128]{1,0:T(8,128)S(1)}, bf16[4,512,256]{2,1,0:T(8,128)(2,1)S(1)}, bf16[4,512,256]{2,1,0:T(8,128)(2,1)S(1)}, f32[4,512,256]{2,1,0:T(8,128)S(1...) custom-call(f32[40,512]{1,0:T(8,128)S(1)} %get-tuple-element.52.refs, ...), custom_call_target="tpu_custom_call" | custom-call | tf_op jit(solution)/shard_map/sweep/pallas_call | solution.py:431
  10.6 0.0 collective-permute-done.refs_1_
  10.6 0.9 %collective-permute-done.1.refs_2_ = bf16[336,128]{1,0:T(8,128)(2,1)S(1)} collective-permute-done((bf16[336,128]{1,0:T(8,128)(2,1)S(1)}, bf16[336,128]{1,0:T(8,128)(2,1)S(1)}, u32[]{:S(2)}, u32[]{:S(2)}) %collective-permute-start.1) | collective-permute-done | bytes 86048 | tf_op jit(solution)/shard_map/ppermute | solution.py:360
  11.5 0.5 %collective-permute-done.2.refs_3_ = bf16[336,128]{1,0:T(8,128)(2,1)S(1)} collective-permute-done((bf16[336,128]{1,0:T(8,128)(2,1)S(1)}, bf16[336,128]{1,0:T(8,128)(2,1)S(1)}, u32[]{:S(2)}, u32[]{:S(2)}) %collective-permute-start.2) | collective-permute-done | bytes 86048 | tf_op jit(solution)/shard_map/ppermute | solution.py:360
  12.0 0.2 second.1
  12.2 1.6 %collective-permute-start.3 = (bf16[192,128]{1,0:T(8,128)(2,1)S(1)}, bf16[192,128]{1,0:T(8,128)(2,1)S(1)}, u32[]{:S(2)}, u32[]{:S(2)}) collective-permute-start(bf16[192,128]{1,0:T(8,128)(2,1)S(1)} %get-tuple-element.64), channel_id=1, source_target_pairs={{0,2},{2,4},{4,6},{6,0},{1,3},{3,5},{5,7},{7,1},{8,10},{10,12},{12... | collective-permute-start | bytes 147464 | tf_op jit(solution)/shard_map/ppermute | solution.py:365
  13.9 2.6 %collective-permute-start.4 = (bf16[192,128]{1,0:T(8,128)(2,1)S(1)}, bf16[192,128]{1,0:T(8,128)(2,1)S(1)}, u32[]{:S(2)}, u32[]{:S(2)}) collective-permute-start(bf16[192,128]{1,0:T(8,128)(2,1)S(1)} %get-tuple-element.65), channel_id=1, source_target_pairs={{0,4},{2,6},{4,0},{6,2},{1,5},{3,7},{5,1},{7,3},{8,12},{10,14},{12... | collective-permute-start | bytes 147464 | tf_op jit(solution)/shard_map/ppermute | solution.py:365
  16.5 1.3 %collective-permute-start.5 = (bf16[192,128]{1,0:T(8,128)(2,1)S(1)}, bf16[192,128]{1,0:T(8,128)(2,1)S(1)}, u32[]{:S(2)}, u32[]{:S(2)}) collective-permute-start(bf16[192,128]{1,0:T(8,128)(2,1)S(1)} %get-tuple-element.66), channel_id=1, source_target_pairs={{0,6},{2,0},{4,2},{6,4},{1,7},{3,1},{5,3},{7,5},{8,14},{10,8},{12,... | collective-permute-start | bytes 147464 | tf_op jit(solution)/shard_map/ppermute | solution.py:365
  17.8 2.6 %sweep.4 = (f32[4,512,256]{2,1,0:T(8,128)S(1)}, f32[4,512,256]{2,1,0:T(8,128)S(1)}, bf16[4,512,256]{2,1,0:T(8,128)(2,1)S(1)}, bf16[4,512,256]{2,1,0:T(8,128)(2,1...) custom-call(f32[40,512]{1,0:T(8,128)S(1)} %get-tuple-element.52.refs, ...), custom_call_target="tpu_custom_call", output_to_operand_aliasing={{0}: (7, {}), {1}: (8, {}), {2}: (9, {}), {3}: (10, {}), {4... | custom-call | tf_op jit(solution)/shard_map/sweep/pallas_call | solution.py:444
  20.4 0.0 collective-permute-done.3.refs_1_
  20.4 0.0 collective-permute-done.4.refs_2_
  20.4 0.1 collective-permute-done.5.refs_3_
  20.6 0.1 collective-permute-start.6
  20.7 1.3 %collective-permute-done.6.refs_5_ = bf16[320,128]{1,0:T(8,128)(2,1)S(1)} collective-permute-done((bf16[320,128]{1,0:T(8,128)(2,1)S(1)}, bf16[320,128]{1,0:T(8,128)(2,1)S(1)}, u32[]{:S(2)}, u32[]{:S(2)}) %collective-permute-start.6) | collective-permute-done | bytes 81952 | tf_op jit(solution)/shard_map/ppermute | solution.py:360
  21.9 0.3 third.1
  22.2 1.3 %collective-permute-start.7 = (bf16[320,128]{1,0:T(8,128)(2,1)S(1)}, bf16[320,128]{1,0:T(8,128)(2,1)S(1)}, u32[]{:S(2)}, u32[]{:S(2)}) collective-permute-start(bf16[320,128]{1,0:T(8,128)(2,1)S(1)} %get-tuple-element.88), channel_id=1, source_target_pairs={{0,8},{8,0},{16,24},{24,16},{1,9},{9,1},{17,25},{25,17},{2,10},{10... | collective-permute-start | bytes 245768 | tf_op jit(solution)/shard_map/ppermute | solution.py:360
  23.5 0.8 %collective-permute-start.8 = (bf16[320,128]{1,0:T(8,128)(2,1)S(1)}, bf16[320,128]{1,0:T(8,128)(2,1)S(1)}, u32[]{:S(2)}, u32[]{:S(2)}) collective-permute-start(bf16[320,128]{1,0:T(8,128)(2,1)S(1)} %get-tuple-element.89), channel_id=1, source_target_pairs={{0,16},{8,24},{16,0},{24,8},{1,17},{9,25},{17,1},{25,9},{2,18},{10... | collective-permute-start | bytes 245768 | tf_op jit(solution)/shard_map/ppermute | solution.py:360
  24.3 1.4 %collective-permute-start.9 = (bf16[320,128]{1,0:T(8,128)(2,1)S(1)}, bf16[320,128]{1,0:T(8,128)(2,1)S(1)}, u32[]{:S(2)}, u32[]{:S(2)}) collective-permute-start(bf16[320,128]{1,0:T(8,128)(2,1)S(1)} %get-tuple-element.90), channel_id=1, source_target_pairs={{0,24},{8,16},{16,8},{24,0},{1,25},{9,17},{17,9},{25,1},{2,26},{10... | collective-permute-start | bytes 245768 | tf_op jit(solution)/shard_map/ppermute | solution.py:360
  25.8 0.0 copy-start
  25.8 0.0 copy-start.1
  25.8 3.5 %sweep.5 = (f32[4,512,256]{2,1,0:T(8,128)S(1)}, f32[4,512,256]{2,1,0:T(8,128)S(1)}, bf16[4,512,256]{2,1,0:T(8,128)(2,1)S(1)}, bf16[4,512,256]{2,1,0:T(8,128)(2,1...) custom-call(f32[40,512]{1,0:T(8,128)S(1)} %get-tuple-element.52.refs, ...), custom_call_target="tpu_custom_call", output_to_operand_aliasing={{0}: (7, {}), {1}: (8, {}), {2}: (9, {}), {3}: (10, {}), {4... | custom-call | tf_op jit(solution)/shard_map/sweep/pallas_call | solution.py:444
  29.2 0.0 collective-permute-done.7.refs_9_
  29.3 0.5 %collective-permute-done.8.refs_10_ = bf16[320,128]{1,0:T(8,128)(2,1)S(1)} collective-permute-done((bf16[320,128]{1,0:T(8,128)(2,1)S(1)}, bf16[320,128]{1,0:T(8,128)(2,1)S(1)}, u32[]{:S(2)}, u32[]{:S(2)}) %collective-permute-start.8) | collective-permute-done | bytes 81952 | tf_op jit(solution)/shard_map/ppermute | solution.py:360
  29.7 0.0 collective-permute-done.9.refs_11_
  29.7 0.0 copy-done
  29.7 0.0 copy-done.1
  29.7 1.9 %last.1 = (bf16[4,512,256]{2,1,0:T(8,128)(2,1)}, bf16[4,512,256]{2,1,0:T(8,128)(2,1)}, bf16[1,256,256]{2,1,0:T(8,128)(2,1)}, bf16[1,256,256]{2,1,0:T(8,128)(2,1)}) custom-call(f32[512,128]{1,0:T(8,128)S(1)} %get-tuple-element.55.refs_5_.refs_0_, bf16[4,512,256]{2,1,0:T(8,128)(2,1)S(1)} %get-tuple-element.84.refs_1_, ...), custom_call_target="tpu_custom_call" | custom-call | tf_op jit(solution)/shard_map/last/pallas_call | solution.py:492
  (1 shorter events, 0.0 us)
Async XLA Ops:
  3.1 7.5 %collective-permute-start = (bf16[336,128]{1,0:T(8,128)(2,1)S(1)}, bf16[336,128]{1,0:T(8,128)(2,1)S(1)}, u32[]{:S(2)}, u32[]{:S(2)}) collective-permute-start(bf16[336,128]{1,0:T(8,128)(2,1)S(1)} %get-tuple-element.59), channel_id=1, source_target_pairs={{0,24},{8,16},{16,8},{24,0},{1,25},{9,17},{17,9},{25,1},{2,26},{10... | collective-permute-start | bytes 258056 | tf_op jit(solution)/shard_map/ppermute | solution.py:360
  7.0 4.5 %collective-permute-start.1 = (bf16[336,128]{1,0:T(8,128)(2,1)S(1)}, bf16[336,128]{1,0:T(8,128)(2,1)S(1)}, u32[]{:S(2)}, u32[]{:S(2)}) collective-permute-start(bf16[336,128]{1,0:T(8,128)(2,1)S(1)} %get-tuple-element.60), channel_id=1, source_target_pairs={{0,16},{8,24},{16,0},{24,8},{1,17},{9,25},{17,1},{25,9},{2,18},{10... | collective-permute-start | bytes 258056 | tf_op jit(solution)/shard_map/ppermute | solution.py:360
  7.5 4.5 %collective-permute-start.2 = (bf16[336,128]{1,0:T(8,128)(2,1)S(1)}, bf16[336,128]{1,0:T(8,128)(2,1)S(1)}, u32[]{:S(2)}, u32[]{:S(2)}) collective-permute-start(bf16[336,128]{1,0:T(8,128)(2,1)S(1)} %get-tuple-element.61), channel_id=1, source_target_pairs={{0,8},{8,0},{16,24},{24,16},{1,9},{9,1},{17,25},{25,17},{2,10},{10... | collective-permute-start | bytes 258056 | tf_op jit(solution)/shard_map/ppermute | solution.py:360
  12.2 8.2 %collective-permute-start.3 = (bf16[192,128]{1,0:T(8,128)(2,1)S(1)}, bf16[192,128]{1,0:T(8,128)(2,1)S(1)}, u32[]{:S(2)}, u32[]{:S(2)}) collective-permute-start(bf16[192,128]{1,0:T(8,128)(2,1)S(1)} %get-tuple-element.64), channel_id=1, source_target_pairs={{0,2},{2,4},{4,6},{6,0},{1,3},{3,5},{5,7},{7,1},{8,10},{10,12},{12... | collective-permute-start | bytes 147464 | tf_op jit(solution)/shard_map/ppermute | solution.py:365
  13.9 6.6 %collective-permute-start.4 = (bf16[192,128]{1,0:T(8,128)(2,1)S(1)}, bf16[192,128]{1,0:T(8,128)(2,1)S(1)}, u32[]{:S(2)}, u32[]{:S(2)}) collective-permute-start(bf16[192,128]{1,0:T(8,128)(2,1)S(1)} %get-tuple-element.65), channel_id=1, source_target_pairs={{0,4},{2,6},{4,0},{6,2},{1,5},{3,7},{5,1},{7,3},{8,12},{10,14},{12... | collective-permute-start | bytes 147464 | tf_op jit(solution)/shard_map/ppermute | solution.py:365
  16.5 4.1 %collective-permute-start.5 = (bf16[192,128]{1,0:T(8,128)(2,1)S(1)}, bf16[192,128]{1,0:T(8,128)(2,1)S(1)}, u32[]{:S(2)}, u32[]{:S(2)}) collective-permute-start(bf16[192,128]{1,0:T(8,128)(2,1)S(1)} %get-tuple-element.66), channel_id=1, source_target_pairs={{0,6},{2,0},{4,2},{6,4},{1,7},{3,1},{5,3},{7,5},{8,14},{10,8},{12,... | collective-permute-start | bytes 147464 | tf_op jit(solution)/shard_map/ppermute | solution.py:365
  20.6 1.3 %collective-permute-start.6 = (bf16[320,128]{1,0:T(8,128)(2,1)S(1)}, bf16[320,128]{1,0:T(8,128)(2,1)S(1)}, u32[]{:S(2)}, u32[]{:S(2)}) collective-permute-start(bf16[320,128]{1,0:T(8,128)(2,1)S(1)} %get-tuple-element.76), channel_id=1, source_target_pairs={{0,1},{1,0},{2,3},{3,2},{4,5},{5,4},{6,7},{7,6},{8,9},{9,8},{10,11... | collective-permute-start | bytes 245768 | tf_op jit(solution)/shard_map/ppermute | solution.py:360
  22.2 7.0 %collective-permute-start.7 = (bf16[320,128]{1,0:T(8,128)(2,1)S(1)}, bf16[320,128]{1,0:T(8,128)(2,1)S(1)}, u32[]{:S(2)}, u32[]{:S(2)}) collective-permute-start(bf16[320,128]{1,0:T(8,128)(2,1)S(1)} %get-tuple-element.88), channel_id=1, source_target_pairs={{0,8},{8,0},{16,24},{24,16},{1,9},{9,1},{17,25},{25,17},{2,10},{10... | collective-permute-start | bytes 245768 | tf_op jit(solution)/shard_map/ppermute | solution.py:360
  23.5 6.2 %collective-permute-start.8 = (bf16[320,128]{1,0:T(8,128)(2,1)S(1)}, bf16[320,128]{1,0:T(8,128)(2,1)S(1)}, u32[]{:S(2)}, u32[]{:S(2)}) collective-permute-start(bf16[320,128]{1,0:T(8,128)(2,1)S(1)} %get-tuple-element.89), channel_id=1, source_target_pairs={{0,16},{8,24},{16,0},{24,8},{1,17},{9,25},{17,1},{25,9},{2,18},{10... | collective-permute-start | bytes 245768 | tf_op jit(solution)/shard_map/ppermute | solution.py:360
  24.3 5.4 %collective-permute-start.9 = (bf16[320,128]{1,0:T(8,128)(2,1)S(1)}, bf16[320,128]{1,0:T(8,128)(2,1)S(1)}, u32[]{:S(2)}, u32[]{:S(2)}) collective-permute-start(bf16[320,128]{1,0:T(8,128)(2,1)S(1)} %get-tuple-element.90), channel_id=1, source_target_pairs={{0,24},{8,16},{16,8},{24,0},{1,25},{9,17},{17,9},{25,1},{2,26},{10... | collective-permute-start | bytes 245768 | tf_op jit(solution)/shard_map/ppermute | solution.py:360
  25.8 4.0 %copy-start = (bf16[1,256,256]{2,1,0:T(8,128)(2,1)S(1)}, bf16[1,256,256]{2,1,0:T(8,128)(2,1)}, u32[]{:S(2)}) copy-start(bf16[1,256,256]{2,1,0:T(8,128)(2,1)} %refs_5_.3) | copy-start | bytes 393220
  25.8 4.0 %copy-start.1 = (bf16[1,256,256]{2,1,0:T(8,128)(2,1)S(1)}, bf16[1,256,256]{2,1,0:T(8,128)(2,1)}, u32[]{:S(2)}) copy-start(bf16[1,256,256]{2,1,0:T(8,128)(2,1)} %refs_6_.3) | copy-start | bytes 393220
